TPU v7x, 32 devices: a whole 2x2x4 slice. The times are simulated.
32 devices in a mesh: blk: 8 (over z, x), head: 4 (over y, core).
Axes of the slice: x: 2, y: 2, z: 4, core: 2. Of those that a mesh axis runs over, the one named last changes fastest.
Arguments:
- block_input: bfloat16 [2, 2048, 2048], P(None, ('blk', 'head')), may hold values from -6 to 6
- cotangent: bfloat16 [2, 2048, 2048], P(None, ('blk', 'head')), may hold values from -6 to 6
- w_query: bfloat16 [2048, 2048], P('blk', 'head'), may hold values from -0.125 to 0.125
- w_key: bfloat16 [2048, 2048], P('blk', 'head'), may hold values from -0.125 to 0.125
- w_value: bfloat16 [2048, 2048], P('blk', 'head'), may hold values from -0.125 to 0.125
- w_out: bfloat16 [2048, 2048], P('head', 'blk'), may hold values from -3 to 3
- w_gate: bfloat16 [2048, 8192], P('blk', 'head'), may hold values from -0.125 to 0.125
- w_up: bfloat16 [2048, 8192], P('blk', 'head'), may hold values from -0.125 to 0.125
- w_down: bfloat16 [8192, 2048], P('head', 'blk'), may hold values from -0.0625 to 0.0625
Outputs:
- block_output: bfloat16 [2, 2048, 2048], P(None, ('blk', 'head'))
- input_grad: bfloat16 [2, 2048, 2048], P(None, ('blk', 'head'))
- grad_query: float32 [2048, 2048], P('blk', 'head')
- grad_key: float32 [2048, 2048], P('blk', 'head')
- grad_value: float32 [2048, 2048], P('blk', 'head')
- grad_out: float32 [2048, 2048], P('head', 'blk')
- grad_gate: float32 [2048, 8192], P('blk', 'head')
- grad_up: float32 [2048, 8192], P('blk', 'head')
- grad_down: float32 [8192, 2048], P('head', 'blk')
All inputs are finite; a program needn't handle non-finite values.
Results may differ from a plain program's by a relative error of at most 0.025.
Values may be sent and summed in bfloat16 or wider, within the bound.
No kernel may reach another device: no remote copies, remote signals or barrier semaphores. Data moves between devices by JAX's collectives and lax.ppermute only.
A program may use at most 256 MiB of HBM per device.

v0:
```python
import jax
import jax.numpy as jnp
from jax import lax
from jax.sharding import PartitionSpec as P

HEADS = 16
HEAD_DIM = 128
FF = 8192


epsilon = 1e-05


def layer_norm(values):
    center = values - jnp.mean(values, axis=-1, keepdims=True)
    spread = jnp.mean(center * center, axis=-1, keepdims=True)
    return center * lax.rsqrt(spread + epsilon)


def rotary(values, places):
    half = values.shape[-1] // 2
    rates = 10000.0 ** (-jnp.arange(half, dtype=jnp.float32) * 2.0 / values.shape[-1])
    angles = places[:, None] * rates[None, :]
    cosine = jnp.cos(angles)[:, None, :]
    sine = jnp.sin(angles)[:, None, :]
    first = values[..., :half]
    second = values[..., half:]
    return jnp.concatenate(
        [first * cosine - second * sine, second * cosine + first * sine], axis=-1
    )


def arrange(gathered):
    joined = jnp.concatenate([gathered[0], gathered[1], gathered[2]], axis=1)
    paired = jnp.concatenate([gathered[4], gathered[5]], axis=1)
    return (joined, gathered[3], paired, gathered[6])


def local(block_input, cotangent, w_query, w_key, w_value, w_out, w_gate, w_up, w_down):
    micro = block_input.shape[0]
    tok_rows = block_input.shape[1]
    groups = lax.axis_size("head")
    rows = tok_rows * groups
    head_count = HEADS // groups
    width_part = head_count * HEAD_DIM
    hidden_part = FF // groups
    scale = HEAD_DIM ** (-0.5)
    first_row = lax.axis_index("blk") * rows
    places = first_row + jnp.arange(rows, dtype=jnp.int32)
    last_place = first_row + rows - 1
    place_float = places.astype(jnp.float32)
    shards = (w_query, w_key, w_value, w_out, w_gate, w_up, w_down)
    model_width = block_input.shape[2]
    projection_grad = jnp.zeros((model_width, 3 * width_part), jnp.float32)
    output_grad = jnp.zeros((width_part, model_width), jnp.float32)
    feed_grad = jnp.zeros((model_width, 2 * hidden_part), jnp.float32)
    down_grad = jnp.zeros((hidden_part, model_width), jnp.float32)
    outputs = []
    input_grads = []
    for index in range(micro):
        w_joined, w_out_rows, w_paired, w_down_rows = arrange(
            (
                lax.all_gather(shards[0], "blk", axis=0, tiled=True),
                lax.all_gather(shards[1], "blk", axis=0, tiled=True),
                lax.all_gather(shards[2], "blk", axis=0, tiled=True),
                lax.all_gather(shards[3], "blk", axis=1, tiled=True),
                lax.all_gather(shards[4], "blk", axis=0, tiled=True),
                lax.all_gather(shards[5], "blk", axis=0, tiled=True),
                lax.all_gather(shards[6], "blk", axis=1, tiled=True),
            )
        )
        tokens = block_input[index].astype(jnp.float32)
        normed = layer_norm(tokens).astype(jnp.bfloat16)
        normed_all = lax.all_gather(normed, "head", axis=0, tiled=True)
        projected = jnp.dot(normed_all, w_joined, preferred_element_type=jnp.float32)
        query_raw = projected[:, :width_part].reshape(rows, head_count, HEAD_DIM)
        key_raw = projected[:, width_part : 2 * width_part].reshape(rows, head_count, HEAD_DIM)
        query = rotary(query_raw, place_float).astype(jnp.bfloat16)
        key = rotary(key_raw, place_float).astype(jnp.bfloat16)
        value_flat = projected[:, 2 * width_part :].astype(jnp.bfloat16)
        value = value_flat.reshape(rows, head_count, HEAD_DIM)
        key_flat = key.reshape(rows, width_part)
        initial = (
            jnp.full((rows, head_count), -1e30, jnp.float32),
            jnp.zeros((rows, head_count), jnp.float32),
            jnp.zeros((rows, head_count, HEAD_DIM), jnp.float32),
        )
        pieces = (
            lax.all_gather(key_flat, "blk", axis=0, tiled=True),
            lax.all_gather(value_flat, "blk", axis=0, tiled=True),
        )
        count = pieces[0].shape[0]

        def attend_live(state):
            top, total, summed = state
            key_piece = pieces[0].reshape(count, head_count, HEAD_DIM)
            value_piece = pieces[1].reshape(count, head_count, HEAD_DIM)
            scores = (
                jnp.einsum("rhd,nhd->rhn", query, key_piece, preferred_element_type=jnp.float32)
                * scale
            )
            allowed = jnp.arange(count, dtype=jnp.int32)[None, None, :] <= places[:, None, None]
            scores = jnp.where(allowed, scores, -1e30)
            new_top = jnp.maximum(top, jnp.max(scores, axis=-1))
            weights = jnp.where(allowed, jnp.exp(scores - new_top[..., None]), 0.0)
            total = jnp.sum(weights, axis=-1)
            summed = jnp.einsum(
                "rhn,nhd->rhd",
                weights.astype(jnp.bfloat16),
                value_piece,
                preferred_element_type=jnp.float32,
            )
            return (new_top, total, summed)

        top, total, summed = lax.cond(
            jnp.int32(0) <= last_place, attend_live, lambda state: state, initial
        )
        attended = summed / total[..., None]
        log_total = top + jnp.log(total)
        attended_low = attended.reshape(rows, width_part).astype(jnp.bfloat16)
        mid = tokens + lax.psum_scatter(
            jnp.dot(attended_low, w_out_rows, preferred_element_type=jnp.float32).astype(
                jnp.bfloat16
            ),
            "head",
            scatter_dimension=0,
            tiled=True,
        ).astype(jnp.float32)
        mid_normed = layer_norm(mid).astype(jnp.bfloat16)
        back_out = cotangent[index]
        mid_all, back_all = (
            lax.all_gather(mid_normed, "head", axis=0, tiled=True),
            lax.all_gather(back_out, "head", axis=0, tiled=True),
        )
        gate_up = jnp.dot(mid_all, w_paired, preferred_element_type=jnp.float32)
        gate = gate_up[:, :hidden_part]
        up = gate_up[:, hidden_part:]
        hidden = (jax.nn.silu(gate) * up).astype(jnp.bfloat16)
        output = mid + lax.psum_scatter(
            jnp.dot(hidden, w_down_rows, preferred_element_type=jnp.float32).astype(jnp.bfloat16),
            "head",
            scatter_dimension=0,
            tiled=True,
        ).astype(jnp.float32)
        outputs.append(output.astype(jnp.bfloat16))
        down_grad = down_grad + jnp.einsum(
            "rf,rd->fd", hidden, back_all, preferred_element_type=jnp.float32
        )
        back_hidden = jnp.einsum(
            "rd,fd->rf", back_all, w_down_rows, preferred_element_type=jnp.float32
        )
        _, swiglu_back = jax.vjp(lambda left, right: jax.nn.silu(left) * right, gate, up)
        back_gate, back_up = swiglu_back(back_hidden)
        back_paired = jnp.concatenate([back_gate, back_up], axis=1).astype(jnp.bfloat16)
        feed_grad = feed_grad + jnp.einsum(
            "rc,rg->cg", mid_all, back_paired, preferred_element_type=jnp.float32
        )
        back_mid_normed = lax.psum_scatter(
            jnp.einsum(
                "rg,cg->rc", back_paired, w_paired, preferred_element_type=jnp.float32
            ).astype(jnp.bfloat16),
            "head",
            scatter_dimension=0,
            tiled=True,
        ).astype(jnp.float32)
        _, norm_back_mid = jax.vjp(layer_norm, mid)
        back_mid = back_out.astype(jnp.float32) + norm_back_mid(back_mid_normed)[0]
        back_attn = back_mid.astype(jnp.bfloat16)
        back_attn_all = lax.all_gather(back_attn, "head", axis=0, tiled=True)
        output_grad = output_grad + jnp.einsum(
            "re,rd->ed", attended_low, back_attn_all, preferred_element_type=jnp.float32
        )
        back_attended = jnp.einsum(
            "rd,ed->re", back_attn_all, w_out_rows, preferred_element_type=jnp.float32
        ).astype(jnp.bfloat16)
        back_attended = back_attended.reshape(rows, head_count, HEAD_DIM)
        delta = jnp.sum(back_attended.astype(jnp.float32) * attended, axis=-1)

        def query_piece(carry, pieces, start):
            count = pieces[0].shape[0]

            def query_live(running):
                key_piece = pieces[0].reshape(count, head_count, HEAD_DIM)
                value_piece = pieces[1].reshape(count, head_count, HEAD_DIM)
                scores = (
                    jnp.einsum("rhd,nhd->rhn", query, key_piece, preferred_element_type=jnp.float32)
                    * scale
                )
                allowed = jnp.arange(count, dtype=jnp.int32)[None, None, :] <= places[:, None, None]
                probs = jnp.where(allowed, jnp.exp(scores - log_total[..., None]), 0.0)
                dots = jnp.einsum(
                    "rhd,nhd->rhn", back_attended, value_piece, preferred_element_type=jnp.float32
                )
                back_scores = (probs * (dots - delta[..., None])).astype(jnp.bfloat16)
                return (
                    jnp.einsum(
                        "rhn,nhd->rhd", back_scores, key_piece, preferred_element_type=jnp.float32
                    )
                    * scale
                )

            return lax.cond(start <= last_place, query_live, lambda running: running, carry)

        zero_heads = jnp.zeros((rows, head_count, HEAD_DIM), jnp.float32)
        back_query_rot = query_piece(
            zero_heads,
            (
                lax.all_gather(key_flat, "blk", axis=0, tiled=True),
                lax.all_gather(value_flat, "blk", axis=0, tiled=True),
            ),
            jnp.int32(0),
        )
        all_log_total, all_delta = (
            lax.all_gather(log_total, "blk", axis=0, tiled=True),
            lax.all_gather(delta, "blk", axis=0, tiled=True),
        )
        sent = (query.reshape(rows, width_part), back_attended.reshape(rows, width_part))
        key_pieces = (
            lax.all_gather(sent[0], "blk", axis=0, tiled=True),
            lax.all_gather(sent[1], "blk", axis=0, tiled=True),
        )
        key_count = key_pieces[0].shape[0]

        def key_live(state):
            query_piece = key_pieces[0].reshape(key_count, head_count, HEAD_DIM)
            grad_piece = key_pieces[1].reshape(key_count, head_count, HEAD_DIM)
            scores = (
                jnp.einsum("nhd,rhd->nhr", query_piece, key, preferred_element_type=jnp.float32)
                * scale
            )
            allowed = jnp.arange(key_count, dtype=jnp.int32)[:, None, None] >= places[None, None, :]
            probs = jnp.where(allowed, jnp.exp(scores - all_log_total[..., None]), 0.0)
            back_value = jnp.einsum(
                "nhr,nhd->rhd",
                probs.astype(jnp.bfloat16),
                grad_piece,
                preferred_element_type=jnp.float32,
            )
            dots = jnp.einsum("nhd,rhd->nhr", grad_piece, value, preferred_element_type=jnp.float32)
            back_scores = (probs * (dots - all_delta[..., None])).astype(jnp.bfloat16)
            back_key = (
                jnp.einsum(
                    "nhr,nhd->rhd", back_scores, query_piece, preferred_element_type=jnp.float32
                )
                * scale
            )
            return (back_key, back_value)

        back_key_rot, back_value = lax.cond(
            jnp.int32(0) + key_count > first_row,
            key_live,
            lambda state: state,
            (zero_heads, zero_heads),
        )
        _, rotate_back = jax.vjp(lambda block: rotary(block, place_float), query_raw)
        back_query = rotate_back(back_query_rot)[0].reshape(rows, width_part).astype(jnp.bfloat16)
        back_key = rotate_back(back_key_rot)[0].reshape(rows, width_part).astype(jnp.bfloat16)
        back_joined = jnp.concatenate(
            [back_query, back_key, back_value.reshape(rows, width_part).astype(jnp.bfloat16)],
            axis=1,
        )
        projection_grad = projection_grad + jnp.einsum(
            "rc,rg->cg", normed_all, back_joined, preferred_element_type=jnp.float32
        )
        back_normed = lax.psum_scatter(
            jnp.einsum(
                "rg,cg->rc", back_joined, w_joined, preferred_element_type=jnp.float32
            ).astype(jnp.bfloat16),
            "head",
            scatter_dimension=0,
            tiled=True,
        ).astype(jnp.float32)
        _, norm_back_input = jax.vjp(layer_norm, tokens)
        input_grads.append((back_mid + norm_back_input(back_normed)[0]).astype(jnp.bfloat16))
    summed_grads = (
        lax.psum_scatter(
            projection_grad[:, :width_part].astype(jnp.bfloat16),
            "blk",
            scatter_dimension=0,
            tiled=True,
        ).astype(jnp.float32),
        lax.psum_scatter(
            projection_grad[:, width_part : 2 * width_part].astype(jnp.bfloat16),
            "blk",
            scatter_dimension=0,
            tiled=True,
        ).astype(jnp.float32),
        lax.psum_scatter(
            projection_grad[:, 2 * width_part :].astype(jnp.bfloat16),
            "blk",
            scatter_dimension=0,
            tiled=True,
        ).astype(jnp.float32),
        lax.psum_scatter(
            output_grad.astype(jnp.bfloat16), "blk", scatter_dimension=1, tiled=True
        ).astype(jnp.float32),
        lax.psum_scatter(
            feed_grad[:, :hidden_part].astype(jnp.bfloat16), "blk", scatter_dimension=0, tiled=True
        ).astype(jnp.float32),
        lax.psum_scatter(
            feed_grad[:, hidden_part:].astype(jnp.bfloat16), "blk", scatter_dimension=0, tiled=True
        ).astype(jnp.float32),
        lax.psum_scatter(
            down_grad.astype(jnp.bfloat16), "blk", scatter_dimension=1, tiled=True
        ).astype(jnp.float32),
    )
    return (
        jnp.stack(outputs),
        jnp.stack(input_grads),
        summed_grads[0],
        summed_grads[1],
        summed_grads[2],
        summed_grads[3],
        summed_grads[4],
        summed_grads[5],
        summed_grads[6],
    )


def solution(mesh):
    placed = (
        P(None, ("blk", "head"), None),
        P(None, ("blk", "head"), None),
        P("blk", "head"),
        P("blk", "head"),
        P("blk", "head"),
        P("head", "blk"),
        P("blk", "head"),
        P("blk", "head"),
        P("head", "blk"),
    )
    return jax.shard_map(
        local,
        mesh=mesh,
        in_specs=placed,
        out_specs=(
            P(None, ("blk", "head"), None),
            P(None, ("blk", "head"), None),
            P("blk", "head"),
            P("blk", "head"),
            P("blk", "head"),
            P("head", "blk"),
            P("blk", "head"),
            P("blk", "head"),
            P("head", "blk"),
        ),
        check_vma=False,
    )
```

profile of v0, /device:TPU:0, one launch (start us, length us, event | category | flops | bytes accessed | tf_op | source)
XLA Modules:
  0.0 2234.8 jit_solution(9846319537801684786)
XLA Ops:
  14.6 47.6 %all-gather.28.cloned.1.call-done = bf16[2048,512]{1,0:T(8,128)(2,1)} async-done(((bf16[256,512]{1,0:T(8,128)(2,1)}), bf16[2048,512]{1,0:T(8,128)(2,1)}) %all-gather.28.cloned.1.call-update) | async-done | bytes 2097168 | tf_op jit(solution)/shard_map/all_gather | solution.py:63
  65.3 46.8 %all-gather.30.cloned.1.call-done = bf16[2048,512]{1,0:T(8,128)(2,1)} async-done(((bf16[256,512]{1,0:T(8,128)(2,1)}), bf16[2048,512]{1,0:T(8,128)(2,1)}) %all-gather.30.cloned.1.call-update) | async-done | bytes 2097168 | tf_op jit(solution)/shard_map/all_gather | solution.py:64
  115.2 46.8 %all-gather.32.cloned.1.call-done = bf16[2048,512]{1,0:T(8,128)(2,1)} async-done(((bf16[256,512]{1,0:T(8,128)(2,1)}), bf16[2048,512]{1,0:T(8,128)(2,1)}) %all-gather.32.cloned.1.call-update) | async-done | bytes 2097168 | tf_op jit(solution)/shard_map/all_gather | solution.py:65
  165.2 14.1 all-gather.26.cloned.1.call-done
  187.9 48.9 %all-gather.34.cloned.1.call-done = bf16[2048,512]{0,1:T(8,128)(2,1)} async-done(((bf16[256,512]{0,1:T(8,128)(2,1)}), bf16[2048,512]{0,1:T(8,128)(2,1)}) %all-gather.34.cloned.1.call-update) | async-done | bytes 2097168 | tf_op jit(solution)/shard_map/all_gather | solution.py:89
  236.8 50.1 %all-gather.36.cloned.1.call-done = bf16[2048,512]{1,0:T(8,128)(2,1)} async-done(((bf16[256,512]{1,0:T(8,128)(2,1)}), bf16[2048,512]{1,0:T(8,128)(2,1)}) %all-gather.36.cloned.1.call-update) | async-done | bytes 2097168 | tf_op jit(solution)/shard_map/all_gather | solution.py:90
  286.8 12.6 conditional.6
  300.7 37.7 %all-gather.38.cloned.1.call-done = bf16[512,2048]{1,0:T(8,128)(2,1)} async-done(((bf16[512,256]{1,0:T(8,128)(2,1)}), bf16[512,2048]{1,0:T(8,128)(2,1)}) %all-gather.38.cloned.1.call-update) | async-done | bytes 2097168 | tf_op jit(solution)/shard_map/all_gather | solution.py:66
  343.2 21.9 reduce-scatter.16.cloned.1.call-done
  371.1 121.2 %all-gather.42.cloned.1.call-done = bf16[2048,2048]{1,0:T(8,128)(2,1)} async-done(((bf16[256,2048]{1,0:T(8,128)(2,1)}), bf16[2048,2048]{1,0:T(8,128)(2,1)}) %all-gather.42.cloned.1.call-update) | async-done | bytes 8388624 | tf_op jit(solution)/shard_map/all_gather | solution.py:67
  492.4 8.4 constant_dynamic-update-slice_fusion.4
  500.8 116.9 %all-gather.44.cloned.1.call-done = bf16[2048,2048]{1,0:T(8,128)(2,1)} async-done(((bf16[256,2048]{1,0:T(8,128)(2,1)}), bf16[2048,2048]{1,0:T(8,128)(2,1)}) %all-gather.44.cloned.1.call-update) | async-done | bytes 8388624 | tf_op jit(solution)/shard_map/all_gather | solution.py:68
  617.7 8.2 constant_dynamic-update-slice_fusion.3
  626.0 8.9 all-gather.40.cloned.1.call-done
  634.9 12.7 fusion.201
  647.6 6.2 all-gather.68.cloned.1.call-done
  653.7 127.7 %all-gather.46.cloned.1.call-done = bf16[2048,2048]{1,0:T(8,128)(2,1)} async-done(((bf16[2048,256]{1,0:T(8,128)(2,1)}), bf16[2048,2048]{1,0:T(8,128)(2,1)}) %all-gather.46.cloned.1.call-update) | async-done | bytes 8388624 | tf_op jit(solution)/shard_map/all_gather | solution.py:69
  781.4 8.1 fusion.116
  794.4 9.7 convolution_convert_fusion.1
  804.2 12.9 reduce-scatter.18.cloned.1.call-done
  817.1 27.9 %reduce-scatter.24.cloned.1.call-done = bf16[64,2048]{1,0:T(8,128)(2,1)} async-done(((bf16[256,2048]{1,0:T(8,128)(2,1)}), bf16[64,2048]{1,0:T(8,128)(2,1)}) %reduce-scatter.24.cloned.1.call-update) | async-done | bytes 262160 | tf_op jit(solution)/shard_map/reduce_scatter | solution.py:158
  852.3 16.2 all-gather.56.cloned.1.call-done
  872.7 32.4 %all_gather.110 = f32[2048,4]{0,1:T(4,128)} all-gather(f32[256,4]{0,1:T(4,128)S(1)} %add.185), channel_id=1, replica_groups=mesh['blk'=8,'head'=4] {'blk'}, dimensions={0}, use_global_device_ids=true | all-gather | bytes 36864 | tf_op jit(solution)/shard_map/all_gather | solution.py:214
  908.5 17.6 conditional.8
  915.3 8.9 fusion.44
  926.1 37.2 %all_gather.112 = f32[2048,4]{1,0:T(8,128)} all-gather(f32[256,4]{1,0:T(8,128)} %multiply_reduce_fusion.1), channel_id=1, replica_groups=mesh['blk'=8,'head'=4] {'blk'}, dimensions={0}, use_global_device_ids=true | all-gather | bytes 36864 | tf_op jit(solution)/shard_map/all_gather | solution.py:215
  963.3 15.0 all-gather.60.cloned.1.call-done
  978.3 29.7 %conditional.9 = (f32[256,4,64]{0,2,1:T(8,128)S(1)}, f32[256,4,64]{0,2,1:T(8,128)}, f32[256,4,64]{0,2,1:T(8,128)}, bf16[256,512]{0,1:T(8,128)(2,1)S(1)}) conditional(s32[]{:T(128)} %convert_element_type.329, () %tuple.97, (s32[256]{0:T(256)S(1)}, bf16[2048,512]{0,1:T(8,128)(2,1)}, bf16[256,4,128]{0,2,1:T(8,128)(2,1)S(1)}, f32[2048,4]{0,1:T(4,128)}, ...), branch_computations={%region_26.27_spmd, %region_27.28_spmd} | conditional | flops 2169307136 | bytes 52593752 | solution.py:249
  991.1 9.0 fusion.61
  1016.0 23.7 %reduce-scatter.26.cloned.1.call-done = bf16[64,2048]{1,0:T(8,128)(2,1)} async-done(((bf16[256,2048]{1,0:T(8,128)(2,1)}), bf16[64,2048]{1,0:T(8,128)(2,1)}) %reduce-scatter.26.cloned.1.call-update) | async-done | bytes 262160 | tf_op jit(solution)/shard_map/reduce_scatter | solution.py:265
  1043.0 16.8 all-gather.48.cloned.1.call-done
  1070.1 48.4 %all-gather.50.cloned.1.call-done = bf16[2048,512]{0,1:T(8,128)(2,1)} async-done(((bf16[256,512]{0,1:T(8,128)(2,1)}), bf16[2048,512]{0,1:T(8,128)(2,1)}) %all-gather.50.cloned.1.call-update) | async-done | bytes 2097168 | tf_op jit(solution)/shard_map/all_gather | solution.py:89
  1118.4 49.6 %all-gather.52.cloned.1.call-done = bf16[2048,512]{1,0:T(8,128)(2,1)} async-done(((bf16[256,512]{1,0:T(8,128)(2,1)}), bf16[2048,512]{1,0:T(8,128)(2,1)}) %all-gather.52.cloned.1.call-update) | async-done | bytes 2097168 | tf_op jit(solution)/shard_map/all_gather | solution.py:90
  1168.1 12.8 conditional.7
  1187.4 22.3 reduce-scatter.20.cloned.1.call-done
  1215.8 15.7 all-gather.54.cloned.1.call-done
  1231.5 12.7 fusion.203
  1244.2 6.3 all-gather.70.cloned.1.call-done
  1250.5 9.6 fusion.119
  1260.1 11.9 convolution_convert_fusion
  1272.3 7.1 convolution_convert_fusion.6
  1279.4 17.7 reduce-scatter.28.cloned.1.call-done
  1299.5 25.5 %reduce-scatter.22.cloned.1.call-done = bf16[64,2048]{1,0:T(8,128)(2,1)} async-done(((bf16[256,2048]{1,0:T(8,128)(2,1)}), bf16[64,2048]{1,0:T(8,128)(2,1)}) %reduce-scatter.22.cloned.1.call-update) | async-done | bytes 262160 | tf_op jit(solution)/shard_map/reduce_scatter | solution.py:139
  1330.4 16.1 all-gather.62.cloned.1.call-done
  1355.6 32.5 %all_gather.116 = f32[2048,4]{0,1:T(4,128)} all-gather(f32[256,4]{0,1:T(4,128)S(1)} %add.188), channel_id=1, replica_groups=mesh['blk'=8,'head'=4] {'blk'}, dimensions={0}, use_global_device_ids=true | all-gather | bytes 36864 | tf_op jit(solution)/shard_map/all_gather | solution.py:214
  1392.0 17.7 conditional.10
  1399.0 8.9 fusion.85
  1409.8 37.3 %all_gather.118 = f32[2048,4]{1,0:T(8,128)} all-gather(f32[256,4]{1,0:T(8,128)} %multiply_reduce_fusion), channel_id=1, replica_groups=mesh['blk'=8,'head'=4] {'blk'}, dimensions={0}, use_global_device_ids=true | all-gather | bytes 36864 | tf_op jit(solution)/shard_map/all_gather | solution.py:215
  1447.1 10.2 all-gather.66.cloned.1.call-done
  1457.3 30.1 %conditional.11 = (f32[256,4,64]{0,2,1:T(8,128)S(1)}, f32[256,4,64]{0,2,1:T(8,128)}, f32[256,4,64]{0,2,1:T(8,128)}, bf16[256,512]{0,1:T(8,128)(2,1)S(1)}) conditional(s32[]{:T(128)} %convert_element_type.329, () %tuple.101, (s32[256]{0:T(256)S(1)}, bf16[2048,512]{0,1:T(8,128)(2,1)}, bf16[256,4,128]{0,2,1:T(8,128)(2,1)S(1)}, f32[2048,4]{0,1:T(4,128)}, ...), branch_computations={%region_37.38_spmd, %region_38.39_spmd} | conditional | flops 2169307136 | bytes 52593752 | solution.py:249
  1457.3 6.2 fusion.199
  1470.3 9.1 fusion.102
  1481.2 6.2 fusion.103
  1506.6 14.7 fusion.122
  1521.3 17.5 add_convert_fusion
  1538.9 12.1 fusion.191
  1552.6 8.2 fusion.126
  1560.9 11.5 add_convert_fusion.1
  1581.0 46.7 %reduce-scatter.32.cloned.1.call-done = bf16[256,512]{1,0:T(8,128)(2,1)} async-done(((bf16[2048,512]{1,0:T(8,128)(2,1)}), bf16[256,512]{1,0:T(8,128)(2,1)}) %reduce-scatter.32.cloned.1.call-update) | async-done | bytes 262160 | tf_op jit(solution)/shard_map/reduce_scatter | solution.py:276
  1629.5 69.1 %reduce-scatter.34.cloned.1.call-done = bf16[256,512]{1,0:T(8,128)(2,1)} async-done(((bf16[2048,512]{1,0:T(8,128)(2,1)}), bf16[256,512]{1,0:T(8,128)(2,1)}) %reduce-scatter.34.cloned.1.call-update) | async-done | bytes 262160 | tf_op jit(solution)/shard_map/reduce_scatter | solution.py:282
  1700.4 69.2 %reduce-scatter.36.cloned.1.call-done = bf16[256,512]{1,0:T(8,128)(2,1)} async-done(((bf16[2048,512]{1,0:T(8,128)(2,1)}), bf16[256,512]{1,0:T(8,128)(2,1)}) %reduce-scatter.36.cloned.1.call-update) | async-done | bytes 262160 | tf_op jit(solution)/shard_map/reduce_scatter | solution.py:288
  1771.3 149.7 %reduce-scatter.40.cloned.1.call-done = bf16[256,2048]{1,0:T(8,128)(2,1)} async-done(((bf16[2048,2048]{1,0:T(8,128)(2,1)}), bf16[256,2048]{1,0:T(8,128)(2,1)}) %reduce-scatter.40.cloned.1.call-update) | async-done | bytes 1048592 | tf_op jit(solution)/shard_map/reduce_scatter | solution.py:297
  1923.8 149.2 %reduce-scatter.42.cloned.1.call-done = bf16[256,2048]{1,0:T(8,128)(2,1)} async-done(((bf16[2048,2048]{1,0:T(8,128)(2,1)}), bf16[256,2048]{1,0:T(8,128)(2,1)}) %reduce-scatter.42.cloned.1.call-update) | async-done | bytes 1048592 | tf_op jit(solution)/shard_map/reduce_scatter | solution.py:300
  2075.8 149.2 %reduce-scatter.44.cloned.1.call-done = bf16[2048,256]{1,0:T(8,128)(2,1)} async-done(((bf16[2048,2048]{1,0:T(8,128)(2,1)}), bf16[2048,256]{1,0:T(8,128)(2,1)}) %reduce-scatter.44.cloned.1.call-update) | async-done | bytes 1048592 | tf_op jit(solution)/shard_map/reduce_scatter | solution.py:303
  (360 shorter events, 226.4 us)
Async XLA Ops:
  7.2 55.0 %all-gather.28.cloned.1.call-start = ((), (), s32[]{:S(2)}) async-start(), calls=%async_computation.16 | async-start | bytes 2359296 | tf_op jit(solution)/shard_map/all_gather | solution.py:63
  7.9 104.2 %all-gather.30.cloned.1.call-start = ((), (), s32[]{:S(2)}) async-start(), calls=%async_computation.17 | async-start | bytes 2359296 | tf_op jit(solution)/shard_map/all_gather | solution.py:64
  8.7 153.4 %all-gather.32.cloned.1.call-start = ((), (), s32[]{:S(2)}) async-start(), calls=%async_computation.18 | async-start | bytes 2359296 | tf_op jit(solution)/shard_map/all_gather | solution.py:65
  9.4 169.9 %all-gather.26.cloned.1.call-start = ((), (), s32[]{:S(2)}) async-start(), calls=%async_computation.15 | async-start | bytes 1310720 | tf_op jit(solution)/shard_map/all_gather | solution.py:74
  12.3 102.8 %copy-start.66 = (f32[64]{0:T(128)}, f32[64]{0:T(128)S(1)}, u32[]{:S(2)}) copy-start(f32[64]{0:T(128)S(1)} %fusion.140) | copy-start | bytes 772
  12.4 102.8 %copy-start.54 = (f32[64]{0:T(128)}, f32[64]{0:T(128)S(1)}, u32[]{:S(2)}) copy-start(f32[64]{0:T(128)S(1)} %fusion.170) | copy-start | bytes 772
  14.2 222.6 %all-gather.34.cloned.1.call-start = ((), (), s32[]{:S(2)}) async-start(), calls=%async_computation.19 | async-start | bytes 2359296 | tf_op jit(solution)/shard_map/all_gather | solution.py:89
  185.6 101.3 %all-gather.36.cloned.1.call-start = ((), (), s32[]{:S(2)}) async-start(), calls=%async_computation.20 | async-start | bytes 2359296 | tf_op jit(solution)/shard_map/all_gather | solution.py:90
  186.4 152.1 %all-gather.38.cloned.1.call-start = ((), (), s32[]{:S(2)}) async-start(), calls=%async_computation.21 | async-start | bytes 2359296 | tf_op jit(solution)/shard_map/all_gather | solution.py:66
  187.1 178.0 %reduce-scatter.16.cloned.1.call-start = ((), (), s32[]{:S(2)}) async-start(), calls=%async_computation.22 | async-start | bytes 1310720 | tf_op jit(solution)/shard_map/reduce_scatter | solution.py:121
  299.5 65.6 %copy-start = (bf16[2,64,2048]{2,1,0:T(8,128)(2,1)S(1)}, bf16[2,64,2048]{2,1,0:T(8,128)(2,1)}, u32[]{:S(2)}) copy-start(bf16[2,64,2048]{2,1,0:T(8,128)(2,1)} %param.21) | copy-start | bytes 1572868
  300.4 38.1 %copy-start.22 = (f32[256,4]{1,0:T(8,128)}, f32[256,4]{1,0:T(8,128)S(1)}, u32[]{:S(2)}) copy-start(f32[256,4]{1,0:T(8,128)S(1)} %copy.70) | copy-start | bytes 12292
  300.7 68.5 %copy-start.16 = (bf16[256,4,128]{2,1,0:T(4,128)(2,1)}, bf16[256,4,128]{2,1,0:T(4,128)(2,1)S(1)}, u32[]{:S(2)}) copy-start(bf16[256,4,128]{2,1,0:T(4,128)(2,1)S(1)} %fusion.183) | copy-start | bytes 786436
  338.5 30.8 %copy-start.8 = (bf16[2,64,2048]{2,1,0:T(8,128)(2,1)S(1)}, bf16[2,64,2048]{2,1,0:T(8,128)(2,1)}, u32[]{:S(2)}) copy-start(bf16[2,64,2048]{2,1,0:T(8,128)(2,1)} %param.22) | copy-start | bytes 1572868
  341.8 150.5 %all-gather.42.cloned.1.call-start = ((), (), s32[]{:S(2)}) async-start(), calls=%async_computation.24 | async-start | bytes 9437184 | tf_op jit(solution)/shard_map/all_gather | solution.py:67
  342.6 275.1 %all-gather.44.cloned.1.call-start = ((), (), s32[]{:S(2)}) async-start(), calls=%async_computation.25 | async-start | bytes 9437184 | tf_op jit(solution)/shard_map/all_gather | solution.py:68
  343.2 291.7 %all-gather.40.cloned.1.call-start = ((), (), s32[]{:S(2)}) async-start(), calls=%async_computation.23 | async-start | bytes 1310720 | tf_op jit(solution)/shard_map/all_gather | solution.py:132
  367.4 133.4 %copy-start.71 = (f32[64]{0:T(128)}, f32[64]{0:T(128)S(1)}, u32[]{:S(2)}) copy-start(f32[64]{0:T(128)S(1)} %multiply_reduce_fusion.3) | copy-start | bytes 772
  367.4 133.4 %copy-start.59 = (f32[64]{0:T(128)}, f32[64]{0:T(128)S(1)}, u32[]{:S(2)}) copy-start(f32[64]{0:T(128)S(1)} %fusion.171) | copy-start | bytes 772
  369.2 284.5 %all-gather.68.cloned.1.call-start = ((), (), s32[]{:S(2)}) async-start(), calls=%async_computation.51 | async-start | bytes 1310720 | tf_op jit(solution)/shard_map/all_gather | solution.py:133
  370.1 411.2 %all-gather.46.cloned.1.call-start = ((), (), s32[]{:S(2)}) async-start(), calls=%async_computation.26 | async-start | bytes 9437184 | tf_op jit(solution)/shard_map/all_gather | solution.py:69
  370.9 446.2 %reduce-scatter.18.cloned.1.call-start = ((), (), s32[]{:S(2)}) async-start(), calls=%async_computation.27 | async-start | bytes 1310720 | tf_op jit(solution)/shard_map/reduce_scatter | solution.py:139
  793.9 51.1 %reduce-scatter.24.cloned.1.call-start = ((), (), s32[]{:S(2)}) async-start(), calls=%async_computation.34 | async-start | bytes 1310720 | tf_op jit(solution)/shard_map/reduce_scatter | solution.py:158
  794.4 50.6 %copy-start.4 = (bf16[64,2048]{1,0:T(8,128)(2,1)S(1)}, bf16[64,2048]{1,0:T(8,128)(2,1)}, u32[]{:S(2)}) copy-start(bf16[64,2048]{1,0:T(8,128)(2,1)} %reduce-scatter.16.cloned.1.call-done) | copy-start | bytes 786436
  804.1 64.4 %all-gather.56.cloned.1.call-start = ((), (), s32[]{:S(2)}) async-start(), calls=%async_computation.35 | async-start | bytes 1310720 | tf_op jit(solution)/shard_map/all_gather | solution.py:169
  847.7 60.8 %copy-start.1 = (bf16[2048,512]{0,1:T(8,128)(2,1)S(1)}, bf16[2048,512]{0,1:T(8,128)(2,1)}, u32[]{:S(2)}) copy-start(bf16[2048,512]{0,1:T(8,128)(2,1)} %all-gather.34.cloned.1.call-done) | copy-start | bytes 6291460
  849.1 22.9 %copy-start.60 = (f32[64]{0:T(128)}, f32[64]{0:T(128)S(1)}, u32[]{:S(2)}) copy-start(f32[64]{0:T(128)S(1)} %negate_multiply_fusion.3) | copy-start | bytes 772
  851.7 111.6 %all-gather.58.cloned.1.call-start = ((), (), s32[]{:S(2)}) async-start(), calls=%async_computation.36 | async-start | bytes 2359296 | tf_op jit(solution)/shard_map/all_gather | solution.py:219
  852.3 126.0 %all-gather.60.cloned.1.call-start = ((), (), s32[]{:S(2)}) async-start(), calls=%async_computation.37 | async-start | bytes 2359296 | tf_op jit(solution)/shard_map/all_gather | solution.py:220
  872.0 167.8 %reduce-scatter.26.cloned.1.call-start = ((), (), s32[]{:S(2)}) async-start(), calls=%async_computation.38 | async-start | bytes 1310720 | tf_op jit(solution)/shard_map/reduce_scatter | solution.py:265
  908.5 69.9 %copy-start.14 = (bf16[256,4,128]{0,2,1:T(8,128)(2,1)S(1)}, bf16[256,4,128]{0,2,1:T(8,128)(2,1)}, u32[]{:S(2)}) copy-start(bf16[256,4,128]{0,2,1:T(8,128)(2,1)} %maximum_convert_fusion) | copy-start | bytes 786436
  908.5 69.9 %copy-start.40 = (bf16[256,512]{1,0:T(8,128)(2,1)S(1)}, bf16[256,512]{1,0:T(8,128)(2,1)}, u32[]{:S(2)}) copy-start(bf16[256,512]{1,0:T(8,128)(2,1)} %slice.201) | copy-start | bytes 786436
  926.1 52.2 %copy-start.46 = (f32[256,4,64]{0,2,1:T(8,128)}, f32[256,4,64]{0,2,1:T(8,128)S(1)}, u32[]{:S(2)}) copy-start(f32[256,4,64]{0,2,1:T(8,128)S(1)} %get-tuple-element.221) | copy-start | bytes 786436
  1015.9 43.9 %all-gather.48.cloned.1.call-start = ((), (), s32[]{:S(2)}) async-start(), calls=%async_computation.28 | async-start | bytes 1310720 | tf_op jit(solution)/shard_map/all_gather | solution.py:74
  1016.0 48.8 %copy-start.52 = (f32[64]{0:T(128)}, f32[64]{0:T(128)S(1)}, u32[]{:S(2)}) copy-start(f32[64]{0:T(128)S(1)} %broadcast_multiply_fusion.1) | copy-start | bytes 772
  1043.0 75.5 %all-gather.50.cloned.1.call-start = ((), (), s32[]{:S(2)}) async-start(), calls=%async_computation.29 | async-start | bytes 2359296 | tf_op jit(solution)/shard_map/all_gather | solution.py:89
  1067.2 100.9 %all-gather.52.cloned.1.call-start = ((), (), s32[]{:S(2)}) async-start(), calls=%async_computation.30 | async-start | bytes 2359296 | tf_op jit(solution)/shard_map/all_gather | solution.py:90
  1069.1 140.6 %reduce-scatter.20.cloned.1.call-start = ((), (), s32[]{:S(2)}) async-start(), calls=%async_computation.31 | async-start | bytes 1310720 | tf_op jit(solution)/shard_map/reduce_scatter | solution.py:121
  1180.9 28.8 %copy-start.18 = (bf16[64,2048]{1,0:T(8,128)(2,1)S(1)}, bf16[64,2048]{1,0:T(8,128)(2,1)}, u32[]{:S(2)}) copy-start(bf16[64,2048]{1,0:T(8,128)(2,1)} %reduce-scatter.26.cloned.1.call-done) | copy-start | bytes 786436
  1180.9 28.7 %copy-start.55 = (f32[64]{0:T(128)S(1)}, f32[64]{0:T(128)}, u32[]{:S(2)}) copy-start(f32[64]{0:T(128)} %copy-done.54) | copy-start | bytes 772
  1186.1 45.4 %all-gather.54.cloned.1.call-start = ((), (), s32[]{:S(2)}) async-start(), calls=%async_computation.32 | async-start | bytes 1310720 | tf_op jit(solution)/shard_map/all_gather | solution.py:132
  1212.8 31.4 %copy-start.72 = (f32[64]{0:T(128)}, f32[64]{0:T(128)S(1)}, u32[]{:S(2)}) copy-start(f32[64]{0:T(128)S(1)} %multiply_reduce_fusion.2) | copy-start | bytes 772
  1212.8 31.4 %copy-start.65 = (f32[64]{0:T(128)}, f32[64]{0:T(128)S(1)}, u32[]{:S(2)}) copy-start(f32[64]{0:T(128)S(1)} %fusion.173) | copy-start | bytes 772
  1214.6 35.9 %all-gather.70.cloned.1.call-start = ((), (), s32[]{:S(2)}) async-start(), calls=%async_computation.52 | async-start | bytes 1310720 | tf_op jit(solution)/shard_map/all_gather | solution.py:133
  1215.4 81.7 %reduce-scatter.28.cloned.1.call-start = ((), (), s32[]{:S(2)}) async-start(), calls=%async_computation.39 | async-start | bytes 1310720 | tf_op jit(solution)/shard_map/reduce_scatter | solution.py:158
  1272.1 52.9 %reduce-scatter.22.cloned.1.call-start = ((), (), s32[]{:S(2)}) async-start(), calls=%async_computation.33 | async-start | bytes 1310720 | tf_op jit(solution)/shard_map/reduce_scatter | solution.py:139
  1272.3 24.8 %copy-start.5 = (bf16[64,2048]{1,0:T(8,128)(2,1)S(1)}, bf16[64,2048]{1,0:T(8,128)(2,1)}, u32[]{:S(2)}) copy-start(bf16[64,2048]{1,0:T(8,128)(2,1)} %reduce-scatter.20.cloned.1.call-done) | copy-start | bytes 786436
  1279.4 67.2 %all-gather.62.cloned.1.call-start = ((), (), s32[]{:S(2)}) async-start(), calls=%async_computation.40 | async-start | bytes 1310720 | tf_op jit(solution)/shard_map/all_gather | solution.py:169
  1327.1 24.2 %copy-start.63 = (f32[64]{0:T(128)}, f32[64]{0:T(128)S(1)}, u32[]{:S(2)}) copy-start(f32[64]{0:T(128)S(1)} %negate_multiply_fusion.1) | copy-start | bytes 772
  1329.7 117.4 %all-gather.64.cloned.1.call-start = ((), (), s32[]{:S(2)}) async-start(), calls=%async_computation.41 | async-start | bytes 2359296 | tf_op jit(solution)/shard_map/all_gather | solution.py:219
  1330.4 126.9 %all-gather.66.cloned.1.call-start = ((), (), s32[]{:S(2)}) async-start(), calls=%async_computation.42 | async-start | bytes 2359296 | tf_op jit(solution)/shard_map/all_gather | solution.py:220
  1349.2 225.0 %reduce-scatter.38.cloned.1.call-start = ((), (), s32[]{:S(2)}) async-start(), calls=%async_computation.47 | async-start | bytes 2359296 | tf_op jit(solution)/shard_map/reduce_scatter | solution.py:294
  1351.3 38.5 %copy-start.23 = (f32[256,4]{1,0:T(8,128)S(1)}, f32[256,4]{1,0:T(8,128)}, u32[]{:S(2)}) copy-start(f32[256,4]{1,0:T(8,128)} %copy.78) | copy-start | bytes 12292
  1351.3 40.8 %copy-start.2 = (bf16[2048,512]{0,1:T(8,128)(2,1)S(1)}, bf16[2048,512]{0,1:T(8,128)(2,1)}, u32[]{:S(2)}) copy-start(bf16[2048,512]{0,1:T(8,128)(2,1)} %all-gather.50.cloned.1.call-done) | copy-start | bytes 6291460
  1354.9 221.2 %reduce-scatter.30.cloned.1.call-start = ((), (), s32[]{:S(2)}) async-start(), calls=%async_computation.43 | async-start | bytes 1310720 | tf_op jit(solution)/shard_map/reduce_scatter | solution.py:265
  1392.0 65.3 %copy-start.15 = (bf16[256,4,128]{0,2,1:T(8,128)(2,1)S(1)}, bf16[256,4,128]{0,2,1:T(8,128)(2,1)}, u32[]{:S(2)}) copy-start(bf16[256,4,128]{0,2,1:T(8,128)(2,1)} %maximum_convert_fusion.2) | copy-start | bytes 786436
  1392.0 65.3 %copy-start.41 = (bf16[256,512]{1,0:T(8,128)(2,1)S(1)}, bf16[256,512]{1,0:T(8,128)(2,1)}, u32[]{:S(2)}) copy-start(bf16[256,512]{1,0:T(8,128)(2,1)} %slice.200) | copy-start | bytes 786436
  1409.7 47.6 %copy-start.47 = (f32[256,4,64]{0,2,1:T(8,128)}, f32[256,4,64]{0,2,1:T(8,128)S(1)}, u32[]{:S(2)}) copy-start(f32[256,4,64]{0,2,1:T(8,128)S(1)} %get-tuple-element.230) | copy-start | bytes 786436
  1495.6 132.1 %reduce-scatter.32.cloned.1.call-start = ((), (), s32[]{:S(2)}) async-start(), calls=%async_computation.44 | async-start | bytes 2359296 | tf_op jit(solution)/shard_map/reduce_scatter | solution.py:276
  1505.1 193.5 %reduce-scatter.34.cloned.1.call-start = ((), (), s32[]{:S(2)}) async-start(), calls=%async_computation.45 | async-start | bytes 2359296 | tf_op jit(solution)/shard_map/reduce_scatter | solution.py:282
  1505.8 263.7 %reduce-scatter.36.cloned.1.call-start = ((), (), s32[]{:S(2)}) async-start(), calls=%async_computation.46 | async-start | bytes 2359296 | tf_op jit(solution)/shard_map/reduce_scatter | solution.py:288
  1506.5 414.5 %reduce-scatter.40.cloned.1.call-start = ((), (), s32[]{:S(2)}) async-start(), calls=%async_computation.48 | async-start | bytes 9437184 | tf_op jit(solution)/shard_map/reduce_scatter | solution.py:297
  1551.0 522.0 %reduce-scatter.42.cloned.1.call-start = ((), (), s32[]{:S(2)}) async-start(), calls=%async_computation.49 | async-start | bytes 9437184 | tf_op jit(solution)/shard_map/reduce_scatter | solution.py:300
  1551.6 673.4 %reduce-scatter.44.cloned.1.call-start = ((), (), s32[]{:S(2)}) async-start(), calls=%async_computation.50 | async-start | bytes 9437184 | tf_op jit(solution)/shard_map/reduce_scatter | solution.py:303
  (50 other events, 280.6 us)
Sparse Core Ops, SparseCore 0:
  10.1 51.9 all-gather.27
  64.3 47.7 all-gather.29
  114.2 47.7 all-gather.31
  164.0 15.2 all-gather.25
  185.7 51.0 all-gather.33
  239.3 47.4 all-gather.35
  288.9 49.5 all-gather.37
  342.0 23.0 reduce-scatter.15
  367.4 124.9 all-gather.41
  494.6 123.1 all-gather.43
  619.9 14.9 all-gather.39
  637.0 16.7 all-gather.67
  655.9 125.3 all-gather.45
  794.0 23.0 reduce-scatter.17
  820.0 24.8 reduce-scatter.23
  851.8 16.7 all-gather.55
  871.2 50.8 all-gather.57
  924.9 53.4 all-gather.59
  1016.0 23.6 reduce-scatter.25
  1043.1 16.7 all-gather.47
  1067.3 51.0 all-gather.49
  1120.6 47.4 all-gather.51
  1186.3 23.3 reduce-scatter.19
  1214.7 16.7 all-gather.53
  1233.7 16.7 all-gather.69
  1272.2 24.8 reduce-scatter.27
  1300.0 24.8 reduce-scatter.21
  1329.8 16.7 all-gather.61
  1349.4 52.1 all-gather.63
  1404.4 52.9 all-gather.65
  1461.3 68.1 reduce-scatter.37
  1532.1 23.8 reduce-scatter.29
  1560.0 67.6 reduce-scatter.31
  1631.8 66.7 reduce-scatter.33
  1702.7 66.8 reduce-scatter.35
  1773.0 147.9 reduce-scatter.39
  1924.9 148.0 reduce-scatter.41
  2076.6 148.3 reduce-scatter.43
where the time goes:
time: 2250 us; the launch traced here: 2230 us
  waiting for transfers between devices  1660 us (74%)
  matrix products  257 us (11%)
  blocking collectives  139 us (6%)
  other arithmetic  84.3 us (4%)
  local copies, waits for them, and re-layouts  73.3 us (3%)
    reduce_scatter x1, waiting for transfers between devices, local(): lax.psum_scatter(feed_grad[:, :hidden_part].astype(jnp.bfloat16), 'blk',...  150 us
    reduce_scatter x1, waiting for transfers between devices, local(): lax.psum_scatter(down_grad.astype(jnp.bfloat16), 'blk', scatter_dimension...  149 us
    reduce_scatter x1, waiting for transfers between devices, local(): lax.psum_scatter(feed_grad[:, hidden_part:].astype(jnp.bfloat16), 'blk',...  149 us
    all_gather x1, waiting for transfers between devices, local(): lax.all_gather(shards[6], 'blk', axis=1, tiled=True)  128 us
    all_gather x1, waiting for transfers between devices, local(): lax.all_gather(shards[4], 'blk', axis=0, tiled=True)  121 us
    all_gather x1, waiting for transfers between devices, local(): lax.all_gather(shards[5], 'blk', axis=0, tiled=True)  117 us
    all_gather x2, waiting for transfers between devices, local(): lax.all_gather(value_flat, 'blk', axis=0, tiled=True)  99.7 us
    all_gather x2, waiting for transfers between devices, local(): lax.all_gather(key_flat, 'blk', axis=0, tiled=True)  97.3 us
  transfers between devices with their start and end apart: 38, of which 34 were waited for; matrix products, arithmetic and copies ran while one was open for 13% of the time, Pallas kernels for 0%

commit v1 on v0

v1 whole, which is shorter than its diff:
```python
import functools

import jax
import jax.numpy as jnp
import numpy as np
from jax import lax
from jax.experimental import pallas as pl
from jax.experimental.pallas import tpu as pltpu
from jax.sharding import PartitionSpec as P

HEADS = 16
HEAD_DIM = 128
FF = 8192
AXES = ("blk", "head")
SCALE = HEAD_DIM**-0.5
EPS = 1e-05
F32 = jnp.float32
BF16 = jnp.bfloat16


def swap(value, nb, nh, db, dh):
    pairs = [
        (b * nh + h, (b ^ db) * nh + (h ^ dh)) for b in range(nb) for h in range(nh)
    ]
    return lax.ppermute(value, AXES, pairs)


def norm_stats(values):
    center = values - jnp.mean(values, axis=-1, keepdims=True)
    spread = jnp.mean(center * center, axis=-1, keepdims=True)
    rstd = lax.rsqrt(spread + EPS)
    return center * rstd, rstd


def norm_back(grad, normed, rstd):
    return (
        grad
        - jnp.mean(grad, axis=-1, keepdims=True)
        - normed * jnp.mean(grad * normed, axis=-1, keepdims=True)
    ) * rstd


def attend_kernel(q_ref, k_ref, v_ref, pq_ref, pk_ref, o_ref, lse_ref):
    scores = lax.dot_general(
        q_ref[...], k_ref[...], (((1,), (1,)), ((), ())), preferred_element_type=F32
    )
    scores = jnp.where(pk_ref[...] <= pq_ref[...], scores * SCALE, -1e30)
    top = jnp.max(scores, axis=-1, keepdims=True)
    weights = jnp.exp(scores - top)
    total = jnp.sum(weights, axis=-1, keepdims=True)
    summed = jnp.dot(weights.astype(BF16), v_ref[...], preferred_element_type=F32)
    o_ref[...] = (summed / total).astype(BF16)
    lse_ref[...] = top + jnp.log(total)


def attend_back_kernel(
    q_ref, do_ref, lse_ref, pq_ref, k_ref, v_ref, pk_ref, dq_ref, dk_ref, dv_ref
):
    @pl.when(pl.program_id(0) == 0)
    def _():
        dk_ref[...] = jnp.zeros_like(dk_ref)
        dv_ref[...] = jnp.zeros_like(dv_ref)

    q, k, v, do = q_ref[...], k_ref[...], v_ref[...], do_ref[...]
    scores = lax.dot_general(q, k, (((1,), (1,)), ((), ())), preferred_element_type=F32)
    probs = jnp.where(
        pk_ref[...] <= pq_ref[...], jnp.exp(scores * SCALE - lse_ref[...]), 0.0
    )
    dots = lax.dot_general(do, v, (((1,), (1,)), ((), ())), preferred_element_type=F32)
    delta = jnp.sum(probs * dots, axis=-1, keepdims=True)
    back = (probs * (dots - delta)).astype(BF16)
    dq_ref[...] = jnp.dot(back, k, preferred_element_type=F32) * SCALE
    dk_ref[...] += (
        lax.dot_general(back, q, (((0,), (0,)), ((), ())), preferred_element_type=F32)
        * SCALE
    )
    dv_ref[...] += lax.dot_general(
        probs.astype(BF16), do, (((0,), (0,)), ((), ())), preferred_element_type=F32
    )


def attend(q, k, v, pos_q, pos_k):
    rows, keys = q.shape[0], k.shape[0]
    bq = min(rows, max(64, (256 * 2048) // keys))
    row = lambda w: pl.BlockSpec((bq, w), lambda i: (i, 0))
    whole = lambda shape: pl.BlockSpec(shape, lambda i: (0, 0))
    return pl.pallas_call(
        attend_kernel,
        grid=(rows // bq,),
        in_specs=[
            row(HEAD_DIM),
            whole((keys, HEAD_DIM)),
            whole((keys, HEAD_DIM)),
            row(1),
            whole((1, keys)),
        ],
        out_specs=[row(HEAD_DIM), row(1)],
        out_shape=[
            jax.ShapeDtypeStruct((rows, HEAD_DIM), BF16),
            jax.ShapeDtypeStruct((rows, 1), F32),
        ],
        compiler_params=pltpu.CompilerParams(vmem_limit_bytes=48 * 2**20),
        cost_estimate=pl.CostEstimate(
            flops=4 * rows * keys * HEAD_DIM,
            bytes_accessed=8 * rows * HEAD_DIM,
            transcendentals=rows * keys,
        ),
        name="attend",
    )(q, k, v, pos_q, pos_k)


def attend_back(q, do, lse, pos_q, k, v, pos_k):
    rows, keys = q.shape[0], k.shape[0]
    bq = min(rows, max(64, (256 * 2048) // keys))
    row = lambda w: pl.BlockSpec((bq, w), lambda i: (i, 0))
    whole = lambda shape: pl.BlockSpec(shape, lambda i: (0, 0))
    kv = whole((keys, HEAD_DIM))
    return pl.pallas_call(
        attend_back_kernel,
        grid=(rows // bq,),
        in_specs=[row(HEAD_DIM), row(HEAD_DIM), row(1), row(1), kv, kv, whole((1, keys))],
        out_specs=[row(HEAD_DIM), kv, kv],
        out_shape=[
            jax.ShapeDtypeStruct((rows, HEAD_DIM), F32),
            jax.ShapeDtypeStruct((keys, HEAD_DIM), F32),
            jax.ShapeDtypeStruct((keys, HEAD_DIM), F32),
        ],
        compiler_params=pltpu.CompilerParams(vmem_limit_bytes=48 * 2**20),
        cost_estimate=pl.CostEstimate(
            flops=10 * rows * keys * HEAD_DIM,
            bytes_accessed=16 * rows * HEAD_DIM,
            transcendentals=rows * keys,
        ),
        name="attend_back",
    )(q, do, lse, pos_q, k, v, pos_k)


def rope(values, cosine, sine):
    half = HEAD_DIM // 2
    first, second = values[:, :half], values[:, half:]
    return jnp.concatenate(
        [first * cosine - second * sine, second * cosine + first * sine], axis=1
    )


def local(nb, nh, block_input, cotangent, w_query, w_key, w_value, w_out, w_gate, w_up, w_down):
    tok_rows, width = block_input.shape[1:]
    slices = HEADS // nh
    half = nb // 2
    spread = half // slices
    kin = width // nb
    unit = FF // HEADS
    b, h = lax.axis_index("blk"), lax.axis_index("head")
    low = b % slices
    second = b >= half
    mine = 2 * tok_rows
    move = functools.partial(swap, nb=nb, nh=nh)

    exchanges = ((1, 0), (2, 0), (0, 2))
    orders = [
        (exchanges[0], exchanges[2], exchanges[1], (0, 1)),
        (exchanges[2], exchanges[1], exchanges[0], (0, 1)),
        (exchanges[1], exchanges[0], exchanges[2], (0, 1)),
    ]
    cut = (3 * mine // 8) // 16 * 16
    counts = (cut, cut, mine - 2 * cut)
    starts = (0, cut, 2 * cut)

    def gather(value):
        parts = [value[s : s + n] for s, n in zip(starts, counts)]
        for step in range(4):
            arrived = [move(p, db=o[step][0], dh=o[step][1]) for p, o in zip(parts, orders)]
            parts = [jnp.concatenate([p, r], axis=0) for p, r in zip(parts, arrived)]
        return jnp.concatenate(parts, axis=0)

    def scatter(value):
        parts = [value[16 * s : 16 * (s + n)] for s, n in zip(starts, counts)]
        for step in (3, 2, 1, 0):
            kept = [p[: p.shape[0] // 2] for p in parts]
            sent = [p[p.shape[0] // 2 :] for p in parts]
            arrived = [move(p, db=o[step][0], dh=o[step][1]) for p, o in zip(sent, orders)]
            parts = [
                (p.astype(F32) + r.astype(F32)).astype(BF16) if step else p.astype(F32) + r.astype(F32)
                for p, r in zip(kept, arrived)
            ]
        return jnp.concatenate(parts, axis=0)

    flip_b, flip_h, place = [], [], []
    for order, s, n in zip(orders, starts, counts):
        db, dh = np.zeros(1, np.int32), np.zeros(1, np.int32)
        for x, y in order:
            db, dh = np.concatenate([db, db ^ x]), np.concatenate([dh, dh ^ y])
        rows = np.tile(np.arange(s, s + n), 16)
        flip_b.append(np.repeat(db, n) ^ np.where(rows >= tok_rows, half, 0))
        flip_h.append(np.repeat(dh, n))
        place.append(rows % tok_rows)
    flip_b, flip_h, place = map(np.concatenate, (flip_b, flip_h, place))

    def positions(block):
        return ((block ^ flip_b) * nh + (h ^ flip_h)) * tok_rows + place

    pos = positions(b)
    rates = 10000.0 ** (-jnp.arange(HEAD_DIM // 2, dtype=F32) * 2.0 / HEAD_DIM)
    angles = pos.astype(F32)[:, None] * rates[None, :]
    cosine, sine = jnp.cos(angles), jnp.sin(angles)

    def to_micro(pair):
        keep = jnp.where(second, pair[1], pair[0])
        send = jnp.where(second, pair[0], pair[1])
        return jnp.concatenate([keep, move(send, db=half, dh=0)], axis=0)

    def from_micro(rows):
        arrived = move(rows[tok_rows:], db=half, dh=0)
        kept = rows[:tok_rows]
        return jnp.stack(
            [jnp.where(second, arrived, kept), jnp.where(second, kept, arrived)]
        )

    def spread_weights(source):
        pieces = [lax.dynamic_index_in_dim(source, low, 0, False)]
        for d in range(1, slices):
            pieces.append(
                move(lax.dynamic_index_in_dim(source, low ^ d, 0, False), db=d, dh=0)
            )
        step = slices
        while step < nb:
            arrived = move(jnp.stack(pieces), db=step, dh=0)
            pieces = pieces + [arrived[i] for i in range(len(pieces))]
            step *= 2
        return pieces

    def in_order(pieces, lo, hi):
        result = jnp.zeros((len(pieces), kin, hi - lo), BF16)
        for j, piece in enumerate(pieces):
            result = lax.dynamic_update_index_in_dim(result, piece[:, lo:hi], b ^ j, 0)
        return result

    def by_slice(weight):
        return weight.reshape(kin, slices, -1).transpose(1, 0, 2)

    def fold_rows(block, tall):
        n = block.shape[0]
        if tall >= kin:
            return block.reshape(n, tall // kin, kin, kin).transpose(0, 2, 1, 3).reshape(n, kin, tall)
        return block.reshape(n, tall, kin // tall, tall).transpose(0, 2, 1, 3).reshape(n, kin, tall)

    def unfold_rows(block, tall):
        n = block.shape[0]
        if tall >= kin:
            return block.reshape(n, kin, tall // kin, kin).transpose(2, 1, 0, 3).reshape(tall, n * kin)
        return block.reshape(n, kin // tall, tall, tall).transpose(2, 0, 1, 3).reshape(tall, n * kin)

    def refold_rows(grad, tall):
        if tall >= kin:
            return grad.reshape(tall // kin, kin, nb, kin).transpose(2, 1, 0, 3).reshape(nb, kin, tall)
        return grad.reshape(tall, nb, kin // tall, tall).transpose(1, 2, 0, 3).reshape(nb, kin, tall)

    def from_fold(block, tall):
        n = block.shape[0]
        if tall >= kin:
            return block.reshape(n, kin, tall // kin, kin).transpose(0, 2, 1, 3).reshape(n, tall, kin)
        return block.reshape(n, kin // tall, tall, tall).transpose(0, 2, 1, 3).reshape(n, tall, kin)

    tokens = to_micro(block_input).astype(F32)
    attn_source = jnp.concatenate(
        [
            by_slice(w_query),
            by_slice(w_key),
            by_slice(w_value),
            fold_rows(w_out.reshape(slices, HEAD_DIM, kin), HEAD_DIM),
        ],
        axis=2,
    )
    attn_pieces = spread_weights(attn_source)
    back_rows = to_micro(cotangent)
    feed_source = jnp.concatenate(
        [by_slice(w_gate), by_slice(w_up), fold_rows(w_down.reshape(slices, unit, kin), unit)],
        axis=2,
    )
    feed_pieces = spread_weights(feed_source)

    w_joined = in_order(attn_pieces, 0, 3 * HEAD_DIM).reshape(width, 3 * HEAD_DIM)
    w_out_rows = unfold_rows(in_order(attn_pieces, 3 * HEAD_DIM, 4 * HEAD_DIM), HEAD_DIM)
    w_paired = in_order(feed_pieces, 0, 2 * unit).reshape(width, 2 * unit)
    w_down_rows = unfold_rows(in_order(feed_pieces, 2 * unit, 3 * unit), unit)

    normed_f, rstd_in = norm_stats(tokens)
    normed_all = gather(normed_f.astype(BF16))
    projected = jnp.dot(normed_all, w_joined, preferred_element_type=F32)
    query = rope(projected[:, :HEAD_DIM], cosine, sine).astype(BF16)
    key = rope(projected[:, HEAD_DIM : 2 * HEAD_DIM], cosine, sine).astype(BF16)
    value = projected[:, 2 * HEAD_DIM :].astype(BF16)

    if spread > 1:
        teams = [
            [(((m * spread + s) * slices + l) * nh + k) for s in range(spread)]
            for m in range(2)
            for l in range(slices)
            for k in range(nh)
        ]
        everyone = lambda t: lax.all_gather(t, AXES, axis=0, tiled=True, axis_index_groups=teams)
        keys, values = everyone(key), everyone(value)
        first = b - (b // slices % spread) * slices
        pos_k = jnp.concatenate([positions(first + s * slices) for s in range(spread)])
    else:
        keys, values, pos_k = key, value, pos

    attended, lse = attend(query, keys, values, pos[:, None], pos_k[None, :])
    mixed = scatter(jnp.dot(attended, w_out_rows, preferred_element_type=F32).astype(BF16))
    mid = tokens + mixed
    mid_f, rstd_mid = norm_stats(mid)
    back_all = gather(back_rows)
    mid_all = gather(mid_f.astype(BF16))
    gate_up = jnp.dot(mid_all, w_paired, preferred_element_type=F32)
    gate, up = gate_up[:, :unit], gate_up[:, unit:]
    sig = 1.0 / (1.0 + jnp.exp(-gate))
    hidden = (gate * sig * up).astype(BF16)
    back_hidden = lax.dot_general(
        back_all, w_down_rows, (((1,), (1,)), ((), ())), preferred_element_type=F32
    )
    back_gate = back_hidden * up * sig * (1.0 + gate * (1.0 - sig))
    back_up = back_hidden * gate * sig
    back_paired = jnp.concatenate([back_gate, back_up], axis=1).astype(BF16)
    back_mid_normed = scatter(
        lax.dot_general(
            back_paired, w_paired, (((1,), (1,)), ((), ())), preferred_element_type=F32
        ).astype(BF16)
    )
    output = mid + scatter(
        jnp.dot(hidden, w_down_rows, preferred_element_type=F32).astype(BF16)
    )
    block_output = from_micro(output.astype(BF16))

    over_rows = (((0,), (0,)), ((), ()))
    grad_down = lax.dot_general(hidden, back_all, over_rows, preferred_element_type=F32)
    grad_feed = lax.dot_general(mid_all, back_paired, over_rows, preferred_element_type=F32)

    def collect(grads):
        step = half
        while step >= slices:
            grads = grads.reshape((2, grads.shape[0] // 2) + grads.shape[1:])
            bit = (b // step) % 2
            kept = lax.dynamic_index_in_dim(grads, bit, 0, False)
            sent = lax.dynamic_index_in_dim(grads, 1 - bit, 0, False)
            grads = (kept.astype(F32) + move(sent, db=step, dh=0).astype(F32)).astype(BF16)
            step //= 2
        result = lax.dynamic_update_index_in_dim(
            jnp.zeros_like(grads), lax.dynamic_index_in_dim(grads, low, 0, False), low, 0
        )
        for d in range(1, slices):
            arrived = move(lax.dynamic_index_in_dim(grads, low ^ d, 0, False), db=d, dh=0)
            result = lax.dynamic_update_index_in_dim(result, arrived, low ^ d, 0)
        return result

    def to_shard(block):
        return block.transpose(1, 0, 2).reshape(kin, -1).astype(F32)

    feed_sum = collect(
        jnp.concatenate(
            [
                grad_feed.astype(BF16).reshape(nb, kin, 2 * unit),
                refold_rows(grad_down.astype(BF16), unit),
            ],
            axis=2,
        )
    )
    grad_gate = to_shard(feed_sum[:, :, :unit])
    grad_up = to_shard(feed_sum[:, :, unit : 2 * unit])
    grad_down_shard = from_fold(feed_sum[:, :, 2 * unit :], unit).reshape(slices * unit, kin).astype(F32)

    back_mid = back_rows.astype(F32) + norm_back(back_mid_normed, mid_f, rstd_mid)
    back_attn_all = gather(back_mid.astype(BF16))
    grad_out = lax.dot_general(attended, back_attn_all, over_rows, preferred_element_type=F32)
    back_attended = lax.dot_general(
        back_attn_all, w_out_rows, (((1,), (1,)), ((), ())), preferred_element_type=F32
    ).astype(BF16)
    back_q, back_k, back_v = attend_back(
        query, back_attended, lse, pos[:, None], keys, values, pos_k[None, :]
    )
    if spread > 1:
        shared = lambda t: lax.psum_scatter(
            t, AXES, scatter_dimension=0, tiled=True, axis_index_groups=teams
        )
        back_k, back_v = shared(back_k), shared(back_v)
    back_joined = jnp.concatenate(
        [rope(back_q, cosine, -sine), rope(back_k, cosine, -sine), back_v], axis=1
    ).astype(BF16)
    back_normed = scatter(
        lax.dot_general(
            back_joined, w_joined, (((1,), (1,)), ((), ())), preferred_element_type=F32
        ).astype(BF16)
    )
    grad_joined = lax.dot_general(normed_all, back_joined, over_rows, preferred_element_type=F32)
    attn_sum = collect(
        jnp.concatenate(
            [
                grad_joined.astype(BF16).reshape(nb, kin, 3 * HEAD_DIM),
                refold_rows(grad_out.astype(BF16), HEAD_DIM),
            ],
            axis=2,
        )
    )
    input_grad = from_micro((back_mid + norm_back(back_normed, normed_f, rstd_in)).astype(BF16))
    return (
        block_output,
        input_grad,
        to_shard(attn_sum[:, :, :HEAD_DIM]),
        to_shard(attn_sum[:, :, HEAD_DIM : 2 * HEAD_DIM]),
        to_shard(attn_sum[:, :, 2 * HEAD_DIM : 3 * HEAD_DIM]),
        from_fold(attn_sum[:, :, 3 * HEAD_DIM :], HEAD_DIM)
        .reshape(slices * HEAD_DIM, kin)
        .astype(F32),
        grad_gate,
        grad_up,
        grad_down_shard,
    )


def solution(mesh):
    rows = P(None, AXES, None)
    placed = (rows, rows) + (P("blk", "head"),) * 3 + (P("head", "blk"),) + (P("blk", "head"),) * 2 + (P("head", "blk"),)
    return jax.shard_map(
        functools.partial(local, mesh.shape["blk"], mesh.shape["head"]),
        mesh=mesh,
        in_specs=placed,
        out_specs=placed,
        check_vma=False,
    )
```

time: 2250 us -> 1140 us (0.51)
  waiting for transfers between devices: 1660 us -> 491 us
  local copies, waits for them, and re-layouts: 73.3 us -> 276 us
  matrix products: 257 us -> 96.8 us
  blocking collectives: 139 us -> 0 us
  starting transfers between devices: 3.49 us -> 121 us
  Pallas kernels: 0 us -> 26.8 us
  other arithmetic: 84.3 us -> 107 us
    all_gather x23 -> x0, waiting for transfers between devices: 867 us -> none  [the longest x1 128 us: local(): lax.all_gather(shards[6], 'blk', axis=1, tiled=True)]
    reduce_scatter x15 -> x0, waiting for transfers between devices: 785 us -> none  [the longest x1 150 us: local(): lax.psum_scatter(feed_grad[:, :hidden_part].astype(jnp.bfloat16), 'blk',...]
    ppermute x0 -> x116, waiting for transfers between devices: none -> 491 us  [swap(): return lax.ppermute(value, AXES, pairs)]
    dot_general x38 -> x12, matrix products: 257 us -> 96.8 us  [the longest x1 15.1 us: local(): gate_up = jnp.dot(mid_all, w_paired, preferred_element_type=F32)]
    all_gather x4 -> x0, blocking collectives: 139 us -> none  [the longest x2 74.5 us: local(): lax.all_gather(delta, 'blk', axis=0, tiled=True)]
    ppermute x0 -> x116, starting transfers between devices: none -> 121 us  [swap(): return lax.ppermute(value, AXES, pairs)]
    unnamed x139 -> x249, local copies, waits for them, and re-layouts: 22.7 us -> 77.9 us
    dynamic_update_slice x0 -> x38, local copies, waits for them, and re-layouts: none -> 45.8 us  [the longest x32 40.1 us: in_order(): result = lax.dynamic_update_index_in_dim(result, piece[:, lo:hi], b ^ j, 0)]
  transfers between devices with their start and end apart: 38 -> 116, of which waited for: 34 -> 51; matrix products, arithmetic and copies ran while one was open for 13% -> 32% of each run, Pallas kernels for 0% -> 1%
where the time goes in v1:
time: 1140 us; the launch traced here: 1120 us
  waiting for transfers between devices  491 us (43%)
  local copies, waits for them, and re-layouts  276 us (24%)
  starting transfers between devices  121 us (11%)
  other arithmetic  107 us (9%)
  matrix products  96.8 us (8%)
  Pallas kernels  26.8 us (2%)
    ppermute x116, waiting for transfers between devices, swap(): return lax.ppermute(value, AXES, pairs)  491 us
    ppermute x116, starting transfers between devices, swap(): return lax.ppermute(value, AXES, pairs)  121 us
    unnamed x249, local copies, waits for them, and re-layouts  77.9 us
    dynamic_update_slice x32, local copies, waits for them, and re-layouts, in_order(): result = lax.dynamic_update_index_in_dim(result, piece[:, lo:hi], b ^ j, 0)  40.1 us
    concatenate x36, other arithmetic, gather(): parts = [jnp.concatenate([p, r], axis=0) for p, r in zip(parts, arrived)]  36.1 us
    convert_element_type x32, other arithmetic, scatter(): (p.astype(F32) + r.astype(F32)).astype(BF16)  23.7 us
  transfers between devices with their start and end apart: 116, of which 51 were waited for; matrix products, arithmetic and copies ran while one was open for 32% of the time, Pallas kernels for 1%

profile of v1, /device:TPU:0, one launch (start us, length us, event | category | flops | bytes accessed | tf_op | source)
XLA Modules:
  0.0 1121.6 jit_solution(818893687531659799)
XLA Ops:
  75.3 19.3 %collective-permute-done.1 = bf16[48,2048]{1,0:T(8,128)(2,1)S(1)} collective-permute-done((bf16[48,2048]{1,0:T(8,128)(2,1)S(1)}, bf16[48,2048]{1,0:T(8,128)(2,1)S(1)}, u32[]{:S(2)}, u32[]{:S(2)}) %collective-permute-start.1) | collective-permute-done | bytes 196640 | tf_op jit(solution)/shard_map/ppermute | solution.py:25
  96.9 3.8 collective-permute-done.5
  104.6 5.5 collective-permute-done.60
  145.9 3.1 pad_maximum_fusion.2
  180.0 62.3 %collective-permute-done.3 = bf16[192,2048]{1,0:T(8,128)(2,1)} collective-permute-done((bf16[192,2048]{1,0:T(8,128)(2,1)}, bf16[192,2048]{1,0:T(8,128)(2,1)}, u32[]{:S(2)}, u32[]{:S(2)}) %collective-permute-start.3) | collective-permute-done | bytes 786464 | tf_op jit(solution)/shard_map/ppermute | solution.py:25
  272.0 19.1 %collective-permute-done.9 = bf16[32,2048]{1,0:T(8,128)(2,1)S(1)} collective-permute-done((bf16[32,2048]{1,0:T(8,128)(2,1)S(1)}, bf16[32,2048]{1,0:T(8,128)(2,1)S(1)}, u32[]{:S(2)}, u32[]{:S(2)}) %collective-permute-start.9) | collective-permute-done | bytes 131104 | tf_op jit(solution)/shard_map/ppermute | solution.py:25
  291.2 3.6 collective-permute-start.10
  296.2 5.0 collective-permute-done.10
  307.1 7.5 collective-permute-done.11
  315.7 3.2 fusion.94
  329.5 7.7 fusion.103
  337.3 5.1 fusion.47
  343.0 9.8 attend.1
  369.4 7.7 collective-permute-done.26
  379.9 4.2 add_convert_fusion.7
  389.0 16.4 %collective-permute-done.28 = bf16[32,2048]{1,0:T(8,128)(2,1)S(1)} collective-permute-done((bf16[32,2048]{1,0:T(8,128)(2,1)S(1)}, bf16[32,2048]{1,0:T(8,128)(2,1)S(1)}, u32[]{:S(2)}, u32[]{:S(2)}) %collective-permute-start.28) | collective-permute-done | bytes 131104 | tf_op jit(solution)/shard_map/ppermute | solution.py:25
  409.9 4.9 collective-permute-done.19
  415.5 3.4 collective-permute-done.23
  420.7 4.1 collective-permute-done.24
  437.5 4.6 collective-permute-done.30
  447.5 15.0 %collective-permute-done.67 = bf16[32,2048]{1,0:T(8,128)(2,1)S(1)} collective-permute-done((bf16[32,2048]{1,0:T(8,128)(2,1)S(1)}, bf16[32,2048]{1,0:T(8,128)(2,1)S(1)}, u32[]{:S(2)}, u32[]{:S(2)}) %collective-permute-start.67) | collective-permute-done | bytes 131104 | tf_op jit(solution)/shard_map/ppermute | solution.py:25
  476.4 11.4 %collective-permute-done.35 = bf16[192,2048]{1,0:T(8,128)(2,1)} collective-permute-done((bf16[192,2048]{1,0:T(8,128)(2,1)}, bf16[192,2048]{1,0:T(8,128)(2,1)}, u32[]{:S(2)}, u32[]{:S(2)}) %collective-permute-start.35) | collective-permute-done | bytes 786464 | tf_op jit(solution)/shard_map/ppermute | solution.py:25
  501.5 3.7 collective-permute-done.37
  509.3 3.9 collective-permute-done.38
  516.3 3.5 copy.178
  523.0 4.0 collective-permute-done.39
  536.8 15.1 %fusion.104 = f32[2048,1024]{0,1:T(8,128)} fusion(bf16[2048,2048]{1,0:T(8,128)(2,1)} %constant_dynamic-update-slice_fusion.15, bf16[2048,1024]{1,0:T(8,128)(2,1)} %bitcast.69), kind=kOutput, calls=%fused_computation.386 | convolution fusion | flops 8589934592 | bytes 20971520 | tf_op jit(solution)/shard_map/dot_general | solution.py:314
  552.0 8.4 multiply_convert_fusion.1
  560.4 4.8 convolution_convert_fusion.5
  565.2 7.0 convolution_convert_fusion.2
  572.2 12.6 %convolution_convert_fusion.4 = bf16[2048,1024]{1,0:T(8,128)(2,1)} fusion(bf16[2048,2048]{1,0:T(8,128)(2,1)} %constant_dynamic-update-slice_fusion.15, bf16[2048,512]{0,1:T(8,128)(2,1)S(1)} %get-tuple-element.57, bf16[2048,512]{0,1:T(8,128)(2,1)S(1)} %get-tuple-element.56), kind=kOutput, calls=%fused_computation.15 | convolution fusion | flops 8600420352 | bytes 16777216 | tf_op jit(solution)/shard_map/dot_general | solution.py:336
  584.8 13.6 %convolution_convert_fusion.1 = bf16[2048,2048]{1,0:T(8,128)(2,1)} fusion(bf16[2048,1024]{1,0:T(8,128)(2,1)} %bitcast.69, bf16[2048,512]{0,1:T(8,128)(2,1)} %copy-done.85, bf16[2048,512]{0,1:T(8,128)(2,1)S(1)} %get-tuple-element.56), kind=kOutput, calls=%fused_computation.3 | convolution fusion | flops 8602517504 | bytes 16777216 | tf_op jit(solution)/shard_map/dot_general | solution.py:325
  603.6 6.6 copy.191
  610.2 3.6 fusion.2
  632.5 11.3 %collective-permute-done.54 = bf16[128,2048]{1,0:T(8,128)(2,1)} collective-permute-done((bf16[128,2048]{1,0:T(8,128)(2,1)}, bf16[128,2048]{1,0:T(8,128)(2,1)}, u32[]{:S(2)}, u32[]{:S(2)}) %collective-permute-start.54) | collective-permute-done | bytes 524320 | tf_op jit(solution)/shard_map/ppermute | solution.py:25
  649.9 4.5 collective-permute-done.80
  656.5 13.0 %collective-permute-done.55 = bf16[64,2048]{1,0:T(8,128)(2,1)S(1)} collective-permute-done((bf16[64,2048]{1,0:T(8,128)(2,1)S(1)}, bf16[64,2048]{1,0:T(8,128)(2,1)S(1)}, u32[]{:S(2)}, u32[]{:S(2)}) %collective-permute-start.55) | collective-permute-done | bytes 262176 | tf_op jit(solution)/shard_map/ppermute | solution.py:25
  670.6 5.4 collective-permute-done.81
  677.3 42.9 %collective-permute-done.56 = bf16[32,2048]{1,0:T(8,128)(2,1)S(1)} collective-permute-done((bf16[32,2048]{1,0:T(8,128)(2,1)S(1)}, bf16[32,2048]{1,0:T(8,128)(2,1)S(1)}, u32[]{:S(2)}, u32[]{:S(2)}) %collective-permute-start.56) | collective-permute-done | bytes 131104 | tf_op jit(solution)/shard_map/ppermute | solution.py:25
  722.7 32.9 %collective-permute-done.82 = bf16[32,2048]{1,0:T(8,128)(2,1)S(1)} collective-permute-done((bf16[32,2048]{1,0:T(8,128)(2,1)S(1)}, bf16[32,2048]{1,0:T(8,128)(2,1)S(1)}, u32[]{:S(2)}, u32[]{:S(2)}) %collective-permute-start.82) | collective-permute-done | bytes 131104 | tf_op jit(solution)/shard_map/ppermute | solution.py:25
  759.8 15.3 %collective-permute-done.76 = bf16[192,2048]{1,0:T(8,128)(2,1)S(1)} collective-permute-done((bf16[192,2048]{1,0:T(8,128)(2,1)S(1)}, bf16[192,2048]{1,0:T(8,128)(2,1)S(1)}, u32[]{:S(2)}, u32[]{:S(2)}) %collective-permute-start.76) | collective-permute-done | bytes 786464 | tf_op jit(solution)/shard_map/ppermute | solution.py:25
  779.6 6.0 collective-permute-done.77
  787.4 4.1 collective-permute-done.78
  796.6 4.7 collective-permute-done.83
  802.9 7.6 collective-permute-done.84
  814.7 3.1 collective-permute-start.57
  819.9 14.6 %collective-permute-done.85 = bf16[192,2048]{1,0:T(8,128)(2,1)} collective-permute-done((bf16[192,2048]{1,0:T(8,128)(2,1)}, bf16[192,2048]{1,0:T(8,128)(2,1)}, u32[]{:S(2)}, u32[]{:S(2)}) %collective-permute-start.85) | collective-permute-done | bytes 786464 | tf_op jit(solution)/shard_map/ppermute | solution.py:25
  843.4 12.7 %collective-permute-done.89 = bf16[192,2048]{1,0:T(8,128)(2,1)S(1)} collective-permute-done((bf16[192,2048]{1,0:T(8,128)(2,1)S(1)}, bf16[192,2048]{1,0:T(8,128)(2,1)S(1)}, u32[]{:S(2)}, u32[]{:S(2)}) %collective-permute-start.89) | collective-permute-done | bytes 786464 | tf_op jit(solution)/shard_map/ppermute | solution.py:25
  881.3 8.3 collective-permute-done.113
  891.9 19.7 %collective-permute-done.92 = bf16[64,2048]{1,0:T(8,128)(2,1)S(1)} collective-permute-done((bf16[64,2048]{1,0:T(8,128)(2,1)}, bf16[64,2048]{1,0:T(8,128)(2,1)S(1)}, u32[]{:S(2)}, u32[]{:S(2)}) %collective-permute-start.92) | collective-permute-done | bytes 262176 | tf_op jit(solution)/shard_map/ppermute | solution.py:25
  923.1 4.2 collective-permute-done.93
  935.4 5.8 convolution_convert_fusion.8.do_ref
  941.3 17.0 %attend_back.1 = (f32[2048,128]{1,0:T(8,128)S(1)}, f32[2048,128]{1,0:T(8,128)S(1)}, f32[2048,128]{1,0:T(8,128)S(1)}) custom-call(bf16[2048,128]{1,0:T(8,128)(2,1)S(1)} %copy-done.6, bf16[2048,128]{1,0:T(8,128)(2,1)S(1)} %convolution_convert_fusion.8.do_ref, f32[2048,1]{1,0:T(8,128)} %copy-done.9, s32[2048,1]{1,0:T(8,128)} %copy-done.2, ...), custom_call_target="tpu_custom_call" | custom-call | flops 5368709120 | bytes 4194304 | tf_op jit(solution)/shard_map/attend_back/pallas_call | solution.py:118
  958.4 5.1 fusion.41
  965.9 9.7 convolution_convert_fusion.6
  975.6 8.3 convolution_convert_fusion
  993.7 3.9 fusion.89
  1002.5 37.3 %collective-permute-done.108 = bf16[4,256,512]{1,2,0:T(8,128)(2,1)S(1)} collective-permute-done((bf16[4,256,512]{1,2,0:T(8,128)(2,1)S(1)}, bf16[4,256,512]{1,2,0:T(8,128)(2,1)S(1)}, u32[]{:S(2)}, u32[]{:S(2)}) %collective-permute-start.108) | collective-permute-done | bytes 1048608 | tf_op jit(solution)/shard_map/ppermute | solution.py:25
  1047.8 3.0 copy.202
  1061.4 4.2 add_convert_fusion.1
  1073.2 14.0 %collective-permute-done.106 = bf16[32,2048]{1,0:T(8,128)(2,1)} collective-permute-done((bf16[32,2048]{1,0:T(8,128)(2,1)S(1)}, bf16[32,2048]{1,0:T(8,128)(2,1)}, u32[]{:S(2)}, u32[]{:S(2)}) %collective-permute-start.106) | collective-permute-done | bytes 131104 | tf_op jit(solution)/shard_map/ppermute | solution.py:25
  1092.0 6.0 collective-permute-done.97
  1103.9 3.1 collective-permute-done.102
  1115.2 4.1 collective-permute-done.107
  (734 shorter events, 472.9 us)
Async XLA Ops:
  3.3 45.6 %collective-permute-start.59 = (bf16[48,2048]{1,0:T(8,128)(2,1)}, bf16[48,2048]{1,0:T(8,128)(2,1)}, u32[]{:S(2)}, u32[]{:S(2)}) collective-permute-start(bf16[48,2048]{1,0:T(8,128)(2,1)} %slice_bitcast_fusion.16), channel_id=1, source_target_pairs={{0,4},{1,5},{2,6},{3,7},{4,0},{5,1},{6,2},{7,3},{8,12},{9,13},{10,... | collective-permute-start | bytes 589832 | tf_op jit(solution)/shard_map/ppermute | solution.py:25
  6.2 251.0 %collective-permute-start.58 = (bf16[64,2048]{1,0:T(8,128)(2,1)}, bf16[64,2048]{1,0:T(8,128)(2,1)}, u32[]{:S(2)}, u32[]{:S(2)}) collective-permute-start(bf16[64,2048]{1,0:T(8,128)(2,1)} %get-tuple-element.124), channel_id=1, source_target_pairs={{0,16},{1,17},{2,18},{3,19},{4,20},{5,21},{6,22},{7,23},{8,24},{9,... | collective-permute-start | bytes 786440 | tf_op jit(solution)/shard_map/ppermute | solution.py:25
  10.6 43.1 %collective-permute-start = (bf16[64,2048]{1,0:T(8,128)(2,1)}, bf16[64,2048]{1,0:T(8,128)(2,1)S(1)}, u32[]{:S(2)}, u32[]{:S(2)}) collective-permute-start(bf16[64,2048]{1,0:T(8,128)(2,1)} %get-tuple-element.137), channel_id=1, source_target_pairs={{0,16},{1,17},{2,18},{3,19},{4,20},{5,21},{6,22},{7,23},{8,24},{9,... | collective-permute-start | bytes 786440 | tf_op jit(solution)/shard_map/ppermute | solution.py:25
  13.7 40.8 %collective-permute-start.13 = (bf16[256,512]{1,0:T(8,128)(2,1)}, bf16[256,512]{1,0:T(8,128)(2,1)}, u32[]{:S(2)}, u32[]{:S(2)}) collective-permute-start(bf16[256,512]{1,0:T(8,128)(2,1)} %bitcast.12), channel_id=1, source_target_pairs={{0,4},{1,5},{2,6},{3,7},{4,0},{5,1},{6,2},{7,3},{8,12},{9,13},{10,... | collective-permute-start | bytes 786440 | tf_op jit(solution)/shard_map/ppermute | solution.py:25
  14.8 43.3 %collective-permute-start.14 = (bf16[256,512]{1,0:T(8,128)(2,1)}, bf16[256,512]{1,0:T(8,128)(2,1)}, u32[]{:S(2)}, u32[]{:S(2)}) collective-permute-start(bf16[256,512]{1,0:T(8,128)(2,1)} %bitcast.14), channel_id=1, source_target_pairs={{0,8},{1,9},{2,10},{3,11},{4,12},{5,13},{6,14},{7,15},{8,0},{9,1},... | collective-permute-start | bytes 786440 | tf_op jit(solution)/shard_map/ppermute | solution.py:25
  53.6 61.6 %collective-permute-start.41 = (bf16[256,1536]{1,0:T(8,128)(2,1)}, bf16[256,1536]{1,0:T(8,128)(2,1)}, u32[]{:S(2)}, u32[]{:S(2)}) collective-permute-start(bf16[256,1536]{1,0:T(8,128)(2,1)} %bitcast.341), channel_id=1, source_target_pairs={{0,4},{1,5},{2,6},{3,7},{4,0},{5,1},{6,2},{7,3},{8,12},{9,13},{10,... | collective-permute-start | bytes 2359304 | tf_op jit(solution)/shard_map/ppermute | solution.py:25
  54.4 65.8 %collective-permute-start.42 = (bf16[256,1536]{1,0:T(8,128)(2,1)}, bf16[256,1536]{1,0:T(8,128)(2,1)}, u32[]{:S(2)}, u32[]{:S(2)}) collective-permute-start(bf16[256,1536]{1,0:T(8,128)(2,1)} %bitcast.340), channel_id=1, source_target_pairs={{0,8},{1,9},{2,10},{3,11},{4,12},{5,13},{6,14},{7,15},{8,0},{9,1},... | collective-permute-start | bytes 2359304 | tf_op jit(solution)/shard_map/ppermute | solution.py:25
  58.1 65.7 %collective-permute-start.43 = (bf16[256,1536]{1,0:T(8,128)(2,1)}, bf16[256,1536]{1,0:T(8,128)(2,1)}, u32[]{:S(2)}, u32[]{:S(2)}) collective-permute-start(bf16[256,1536]{1,0:T(8,128)(2,1)} %bitcast.339), channel_id=1, source_target_pairs={{0,12},{1,13},{2,14},{3,15},{4,8},{5,9},{6,10},{7,11},{8,4},{9,5},... | collective-permute-start | bytes 2359304 | tf_op jit(solution)/shard_map/ppermute | solution.py:25
  63.3 31.3 %collective-permute-start.1 = (bf16[48,2048]{1,0:T(8,128)(2,1)S(1)}, bf16[48,2048]{1,0:T(8,128)(2,1)S(1)}, u32[]{:S(2)}, u32[]{:S(2)}) collective-permute-start(bf16[48,2048]{1,0:T(8,128)(2,1)S(1)} %get-tuple-element.135), channel_id=1, source_target_pairs={{0,4},{1,5},{2,6},{3,7},{4,0},{5,1},{6,2},{7,3},{8,12},{9,13},{10,... | collective-permute-start | bytes 589832 | tf_op jit(solution)/shard_map/ppermute | solution.py:25
  110.1 45.6 %collective-permute-start.16 = (bf16[4,256,512]{1,2,0:T(8,128)(2,1)}, bf16[4,256,512]{1,2,0:T(8,128)(2,1)}, u32[]{:S(2)}, u32[]{:S(2)}) collective-permute-start(bf16[4,256,512]{1,2,0:T(8,128)(2,1)} %pad_maximum_fusion.15), channel_id=1, source_target_pairs={{0,16},{1,17},{2,18},{3,19},{4,20},{5,21},{6,22},{7,23},{8,24},{9,... | collective-permute-start | bytes 3145736 | tf_op jit(solution)/shard_map/ppermute | solution.py:25
  115.2 33.8 %collective-permute-start.2 = (bf16[96,2048]{1,0:T(8,128)(2,1)}, bf16[96,2048]{1,0:T(8,128)(2,1)}, u32[]{:S(2)}, u32[]{:S(2)}) collective-permute-start(bf16[96,2048]{1,0:T(8,128)(2,1)} %pad_maximum_fusion.39), channel_id=1, source_target_pairs={{0,2},{1,3},{2,0},{3,1},{4,6},{5,7},{6,4},{7,5},{8,10},{9,11},{10,... | collective-permute-start | bytes 1179656 | tf_op jit(solution)/shard_map/ppermute | solution.py:25
  120.2 34.1 %collective-permute-start.6 = (bf16[96,2048]{1,0:T(8,128)(2,1)}, bf16[96,2048]{1,0:T(8,128)(2,1)S(1)}, u32[]{:S(2)}, u32[]{:S(2)}) collective-permute-start(bf16[96,2048]{1,0:T(8,128)(2,1)} %pad_maximum_fusion.40), channel_id=1, source_target_pairs={{0,8},{1,9},{2,10},{3,11},{4,12},{5,13},{6,14},{7,15},{8,0},{9,1},... | collective-permute-start | bytes 1179656 | tf_op jit(solution)/shard_map/ppermute | solution.py:25
  123.7 51.0 %collective-permute-start.61 = (bf16[192,2048]{1,0:T(8,128)(2,1)}, bf16[192,2048]{1,0:T(8,128)(2,1)}, u32[]{:S(2)}, u32[]{:S(2)}) collective-permute-start(bf16[192,2048]{1,0:T(8,128)(2,1)} %pad_maximum_fusion.25), channel_id=1, source_target_pairs={{0,8},{1,9},{2,10},{3,11},{4,12},{5,13},{6,14},{7,15},{8,0},{9,1},... | collective-permute-start | bytes 2359304 | tf_op jit(solution)/shard_map/ppermute | solution.py:25
  149.0 166.7 %collective-permute-start.44 = (bf16[4,256,1536]{1,2,0:T(8,128)(2,1)}, bf16[4,256,1536]{1,2,0:T(8,128)(2,1)}, u32[]{:S(2)}, u32[]{:S(2)}) collective-permute-start(bf16[4,256,1536]{1,2,0:T(8,128)(2,1)} %pad_maximum_fusion.2), channel_id=1, source_target_pairs={{0,16},{1,17},{2,18},{3,19},{4,20},{5,21},{6,22},{7,23},{8,24},{9,... | collective-permute-start | bytes 9437192 | tf_op jit(solution)/shard_map/ppermute | solution.py:25
  154.3 87.9 %collective-permute-start.3 = (bf16[192,2048]{1,0:T(8,128)(2,1)}, bf16[192,2048]{1,0:T(8,128)(2,1)}, u32[]{:S(2)}, u32[]{:S(2)}) collective-permute-start(bf16[192,2048]{1,0:T(8,128)(2,1)} %pad_maximum_fusion.21), channel_id=1, source_target_pairs={{0,8},{1,9},{2,10},{3,11},{4,12},{5,13},{6,14},{7,15},{8,0},{9,1},... | collective-permute-start | bytes 2359304 | tf_op jit(solution)/shard_map/ppermute | solution.py:25
  155.8 94.6 %collective-permute-start.7 = (bf16[192,2048]{1,0:T(8,128)(2,1)}, bf16[192,2048]{1,0:T(8,128)(2,1)}, u32[]{:S(2)}, u32[]{:S(2)}) collective-permute-start(bf16[192,2048]{1,0:T(8,128)(2,1)} %pad_maximum_fusion.22), channel_id=1, source_target_pairs={{0,4},{1,5},{2,6},{3,7},{4,0},{5,1},{6,2},{7,3},{8,12},{9,13},{10,... | collective-permute-start | bytes 2359304 | tf_op jit(solution)/shard_map/ppermute | solution.py:25
  177.4 77.0 %collective-permute-start.62 = (bf16[384,2048]{1,0:T(8,128)(2,1)}, bf16[384,2048]{1,0:T(8,128)(2,1)}, u32[]{:S(2)}, u32[]{:S(2)}) collective-permute-start(bf16[384,2048]{1,0:T(8,128)(2,1)} %pad_maximum_fusion.9), channel_id=1, source_target_pairs={{0,1},{1,0},{2,3},{3,2},{4,5},{5,4},{6,7},{7,6},{8,9},{9,8},{10,11... | collective-permute-start | bytes 4718600 | tf_op jit(solution)/shard_map/ppermute | solution.py:25
  269.4 21.7 %collective-permute-start.9 = (bf16[32,2048]{1,0:T(8,128)(2,1)S(1)}, bf16[32,2048]{1,0:T(8,128)(2,1)S(1)}, u32[]{:S(2)}, u32[]{:S(2)}) collective-permute-start(bf16[32,2048]{1,0:T(8,128)(2,1)S(1)} %get-tuple-element.131), channel_id=1, source_target_pairs={{0,8},{1,9},{2,10},{3,11},{4,12},{5,13},{6,14},{7,15},{8,0},{9,1},... | collective-permute-start | bytes 393224 | tf_op jit(solution)/shard_map/ppermute | solution.py:25
  271.9 30.9 %collective-permute-start.64 = (bf16[96,2048]{1,0:T(8,128)(2,1)S(1)}, bf16[96,2048]{1,0:T(8,128)(2,1)S(1)}, u32[]{:S(2)}, u32[]{:S(2)}) collective-permute-start(bf16[96,2048]{1,0:T(8,128)(2,1)S(1)} %pad_maximum_fusion.44), channel_id=1, source_target_pairs={{0,8},{1,9},{2,10},{3,11},{4,12},{5,13},{6,14},{7,15},{8,0},{9,1},... | collective-permute-start | bytes 1179656 | tf_op jit(solution)/shard_map/ppermute | solution.py:25
  303.8 82.6 %collective-permute-start.65 = (bf16[192,2048]{1,0:T(8,128)(2,1)}, bf16[192,2048]{1,0:T(8,128)(2,1)}, u32[]{:S(2)}, u32[]{:S(2)}) collective-permute-start(bf16[192,2048]{1,0:T(8,128)(2,1)} %pad_maximum_fusion.26), channel_id=1, source_target_pairs={{0,4},{1,5},{2,6},{3,7},{4,0},{5,1},{6,2},{7,3},{8,12},{9,13},{10,... | collective-permute-start | bytes 2359304 | tf_op jit(solution)/shard_map/ppermute | solution.py:25
  361.2 18.7 %collective-permute-start.17 = (bf16[384,2048]{1,0:T(8,128)(2,1)}, bf16[384,2048]{1,0:T(8,128)(2,1)}, u32[]{:S(2)}, u32[]{:S(2)}) collective-permute-start(bf16[384,2048]{1,0:T(8,128)(2,1)} %get-tuple-element.73), channel_id=1, source_target_pairs={{0,1},{1,0},{2,3},{3,2},{4,5},{5,4},{6,7},{7,6},{8,9},{9,8},{10,11... | collective-permute-start | bytes 4718600 | tf_op jit(solution)/shard_map/ppermute | solution.py:25
  361.2 18.7 %collective-permute-start.21 = (bf16[384,2048]{1,0:T(8,128)(2,1)}, bf16[384,2048]{1,0:T(8,128)(2,1)}, u32[]{:S(2)}, u32[]{:S(2)}) collective-permute-start(bf16[384,2048]{1,0:T(8,128)(2,1)} %get-tuple-element.74), channel_id=1, source_target_pairs={{0,1},{1,0},{2,3},{3,2},{4,5},{5,4},{6,7},{7,6},{8,9},{9,8},{10,11... | collective-permute-start | bytes 4718600 | tf_op jit(solution)/shard_map/ppermute | solution.py:25
  384.1 21.2 %collective-permute-start.18 = (bf16[192,2048]{1,0:T(8,128)(2,1)S(1)}, bf16[192,2048]{1,0:T(8,128)(2,1)S(1)}, u32[]{:S(2)}, u32[]{:S(2)}) collective-permute-start(bf16[192,2048]{1,0:T(8,128)(2,1)S(1)} %slice.778), channel_id=1, source_target_pairs={{0,8},{1,9},{2,10},{3,11},{4,12},{5,13},{6,14},{7,15},{8,0},{9,1},... | collective-permute-start | bytes 2359304 | tf_op jit(solution)/shard_map/ppermute | solution.py:25
  385.9 19.4 %collective-permute-start.28 = (bf16[32,2048]{1,0:T(8,128)(2,1)S(1)}, bf16[32,2048]{1,0:T(8,128)(2,1)S(1)}, u32[]{:S(2)}, u32[]{:S(2)}) collective-permute-start(bf16[32,2048]{1,0:T(8,128)(2,1)S(1)} %slice.798), channel_id=1, source_target_pairs={{0,8},{1,9},{2,10},{3,11},{4,12},{5,13},{6,14},{7,15},{8,0},{9,1},... | collective-permute-start | bytes 393224 | tf_op jit(solution)/shard_map/ppermute | solution.py:25
  387.7 48.1 %collective-permute-start.66 = (bf16[384,2048]{1,0:T(8,128)(2,1)S(1)}, bf16[384,2048]{1,0:T(8,128)(2,1)S(1)}, u32[]{:S(2)}, u32[]{:S(2)}) collective-permute-start(bf16[384,2048]{1,0:T(8,128)(2,1)S(1)} %pad_maximum_fusion.10), channel_id=1, source_target_pairs={{0,1},{1,0},{2,3},{3,2},{4,5},{5,4},{6,7},{7,6},{8,9},{9,8},{10,11... | collective-permute-start | bytes 4718600 | tf_op jit(solution)/shard_map/ppermute | solution.py:25
  387.9 20.0 %collective-permute-start.22 = (bf16[192,2048]{1,0:T(8,128)(2,1)S(1)}, bf16[192,2048]{1,0:T(8,128)(2,1)S(1)}, u32[]{:S(2)}, u32[]{:S(2)}) collective-permute-start(bf16[192,2048]{1,0:T(8,128)(2,1)S(1)} %slice.786), channel_id=1, source_target_pairs={{0,4},{1,5},{2,6},{3,7},{4,0},{5,1},{6,2},{7,3},{8,12},{9,13},{10,... | collective-permute-start | bytes 2359304 | tf_op jit(solution)/shard_map/ppermute | solution.py:25
  442.2 23.0 %collective-permute-start.31 = (bf16[192,2048]{1,0:T(8,128)(2,1)S(1)}, bf16[192,2048]{1,0:T(8,128)(2,1)S(1)}, u32[]{:S(2)}, u32[]{:S(2)}) collective-permute-start(bf16[192,2048]{1,0:T(8,128)(2,1)S(1)} %pad_maximum_fusion.23), channel_id=1, source_target_pairs={{0,8},{1,9},{2,10},{3,11},{4,12},{5,13},{6,14},{7,15},{8,0},{9,1},... | collective-permute-start | bytes 2359304 | tf_op jit(solution)/shard_map/ppermute | solution.py:25
  445.4 17.2 %collective-permute-start.67 = (bf16[32,2048]{1,0:T(8,128)(2,1)S(1)}, bf16[32,2048]{1,0:T(8,128)(2,1)S(1)}, u32[]{:S(2)}, u32[]{:S(2)}) collective-permute-start(bf16[32,2048]{1,0:T(8,128)(2,1)S(1)} %get-tuple-element.138), channel_id=1, source_target_pairs={{0,8},{1,9},{2,10},{3,11},{4,12},{5,13},{6,14},{7,15},{8,0},{9,1},... | collective-permute-start | bytes 393224 | tf_op jit(solution)/shard_map/ppermute | solution.py:25
  445.9 20.9 %collective-permute-start.34 = (bf16[96,2048]{1,0:T(8,128)(2,1)S(1)}, bf16[96,2048]{1,0:T(8,128)(2,1)S(1)}, u32[]{:S(2)}, u32[]{:S(2)}) collective-permute-start(bf16[96,2048]{1,0:T(8,128)(2,1)S(1)} %pad_maximum_fusion.42), channel_id=1, source_target_pairs={{0,8},{1,9},{2,10},{3,11},{4,12},{5,13},{6,14},{7,15},{8,0},{9,1},... | collective-permute-start | bytes 1179656 | tf_op jit(solution)/shard_map/ppermute | solution.py:25
  466.6 23.6 %collective-permute-start.32 = (bf16[384,2048]{1,0:T(8,128)(2,1)}, bf16[384,2048]{1,0:T(8,128)(2,1)}, u32[]{:S(2)}, u32[]{:S(2)}) collective-permute-start(bf16[384,2048]{1,0:T(8,128)(2,1)} %pad_maximum_fusion.7), channel_id=1, source_target_pairs={{0,1},{1,0},{2,3},{3,2},{4,5},{5,4},{6,7},{7,6},{8,9},{9,8},{10,11... | collective-permute-start | bytes 4718600 | tf_op jit(solution)/shard_map/ppermute | solution.py:25
  467.7 20.1 %collective-permute-start.35 = (bf16[192,2048]{1,0:T(8,128)(2,1)}, bf16[192,2048]{1,0:T(8,128)(2,1)}, u32[]{:S(2)}, u32[]{:S(2)}) collective-permute-start(bf16[192,2048]{1,0:T(8,128)(2,1)} %pad_maximum_fusion.24), channel_id=1, source_target_pairs={{0,4},{1,5},{2,6},{3,7},{4,0},{5,1},{6,2},{7,3},{8,12},{9,13},{10,... | collective-permute-start | bytes 2359304 | tf_op jit(solution)/shard_map/ppermute | solution.py:25
  473.4 33.7 %collective-permute-start.69 = (bf16[128,2048]{1,0:T(8,128)(2,1)}, bf16[128,2048]{1,0:T(8,128)(2,1)}, u32[]{:S(2)}, u32[]{:S(2)}) collective-permute-start(bf16[128,2048]{1,0:T(8,128)(2,1)} %pad_maximum_fusion.36), channel_id=1, source_target_pairs={{0,2},{1,3},{2,0},{3,1},{4,6},{5,7},{6,4},{7,5},{8,10},{9,11},{10,... | collective-permute-start | bytes 1572872 | tf_op jit(solution)/shard_map/ppermute | solution.py:25
  509.3 20.8 %collective-permute-start.70 = (bf16[256,2048]{1,0:T(8,128)(2,1)}, bf16[256,2048]{1,0:T(8,128)(2,1)}, u32[]{:S(2)}, u32[]{:S(2)}) collective-permute-start(bf16[256,2048]{1,0:T(8,128)(2,1)} %pad_maximum_fusion.17), channel_id=1, source_target_pairs={{0,1},{1,0},{2,3},{3,2},{4,5},{5,4},{6,7},{7,6},{8,9},{9,8},{10,11... | collective-permute-start | bytes 3145736 | tf_op jit(solution)/shard_map/ppermute | solution.py:25
  613.8 225.9 %collective-permute-start.112 = (bf16[4,256,1536]{1,2,0:T(8,128)(2,1)}, bf16[4,256,1536]{1,2,0:T(8,128)(2,1)}, u32[]{:S(2)}, u32[]{:S(2)}) collective-permute-start(bf16[4,256,1536]{1,2,0:T(8,128)(2,1)} %fusion.2), channel_id=1, source_target_pairs={{0,16},{1,17},{2,18},{3,19},{4,20},{5,21},{6,22},{7,23},{8,24},{9,... | collective-permute-start | bytes 9437192 | tf_op jit(solution)/shard_map/ppermute | solution.py:25
  622.5 23.5 %collective-permute-start.71 = (bf16[384,2048]{1,0:T(8,128)(2,1)S(1)}, bf16[384,2048]{1,0:T(8,128)(2,1)S(1)}, u32[]{:S(2)}, u32[]{:S(2)}) collective-permute-start(bf16[384,2048]{1,0:T(8,128)(2,1)S(1)} %get-tuple-element.64), channel_id=1, source_target_pairs={{0,1},{1,0},{2,3},{3,2},{4,5},{5,4},{6,7},{7,6},{8,9},{9,8},{10,11... | collective-permute-start | bytes 4718600 | tf_op jit(solution)/shard_map/ppermute | solution.py:25
  627.3 19.8 %collective-permute-start.75 = (bf16[384,2048]{1,0:T(8,128)(2,1)S(1)}, bf16[384,2048]{1,0:T(8,128)(2,1)S(1)}, u32[]{:S(2)}, u32[]{:S(2)}) collective-permute-start(bf16[384,2048]{1,0:T(8,128)(2,1)S(1)} %get-tuple-element.65), channel_id=1, source_target_pairs={{0,1},{1,0},{2,3},{3,2},{4,5},{5,4},{6,7},{7,6},{8,9},{9,8},{10,11... | collective-permute-start | bytes 4718600 | tf_op jit(solution)/shard_map/ppermute | solution.py:25
  630.2 24.2 %collective-permute-start.80 = (bf16[128,2048]{1,0:T(8,128)(2,1)}, bf16[128,2048]{1,0:T(8,128)(2,1)}, u32[]{:S(2)}, u32[]{:S(2)}) collective-permute-start(bf16[128,2048]{1,0:T(8,128)(2,1)} %slice.873), channel_id=1, source_target_pairs={{0,2},{1,3},{2,0},{3,1},{4,6},{5,7},{6,4},{7,5},{8,10},{9,11},{10,... | collective-permute-start | bytes 1572872 | tf_op jit(solution)/shard_map/ppermute | solution.py:25
  643.7 112.8 %collective-permute-start.46 = (bf16[192,2048]{1,0:T(8,128)(2,1)S(1)}, bf16[192,2048]{1,0:T(8,128)(2,1)S(1)}, u32[]{:S(2)}, u32[]{:S(2)}) collective-permute-start(bf16[192,2048]{1,0:T(8,128)(2,1)S(1)} %slice.827), channel_id=1, source_target_pairs={{0,8},{1,9},{2,10},{3,11},{4,12},{5,13},{6,14},{7,15},{8,0},{9,1},... | collective-permute-start | bytes 2359304 | tf_op jit(solution)/shard_map/ppermute | solution.py:25
  646.1 112.4 %collective-permute-start.50 = (bf16[192,2048]{1,0:T(8,128)(2,1)S(1)}, bf16[192,2048]{1,0:T(8,128)(2,1)S(1)}, u32[]{:S(2)}, u32[]{:S(2)}) collective-permute-start(bf16[192,2048]{1,0:T(8,128)(2,1)S(1)} %slice.835), channel_id=1, source_target_pairs={{0,4},{1,5},{2,6},{3,7},{4,0},{5,1},{6,2},{7,3},{8,12},{9,13},{10,... | collective-permute-start | bytes 2359304 | tf_op jit(solution)/shard_map/ppermute | solution.py:25
  647.1 22.4 %collective-permute-start.55 = (bf16[64,2048]{1,0:T(8,128)(2,1)S(1)}, bf16[64,2048]{1,0:T(8,128)(2,1)S(1)}, u32[]{:S(2)}, u32[]{:S(2)}) collective-permute-start(bf16[64,2048]{1,0:T(8,128)(2,1)S(1)} %slice.845), channel_id=1, source_target_pairs={{0,4},{1,5},{2,6},{3,7},{4,0},{5,1},{6,2},{7,3},{8,12},{9,13},{10,... | collective-permute-start | bytes 786440 | tf_op jit(solution)/shard_map/ppermute | solution.py:25
  654.4 104.4 %collective-permute-start.72 = (bf16[192,2048]{1,0:T(8,128)(2,1)S(1)}, bf16[192,2048]{1,0:T(8,128)(2,1)S(1)}, u32[]{:S(2)}, u32[]{:S(2)}) collective-permute-start(bf16[192,2048]{1,0:T(8,128)(2,1)S(1)} %slice.857), channel_id=1, source_target_pairs={{0,8},{1,9},{2,10},{3,11},{4,12},{5,13},{6,14},{7,15},{8,0},{9,1},... | collective-permute-start | bytes 2359304 | tf_op jit(solution)/shard_map/ppermute | solution.py:25
  675.9 44.3 %collective-permute-start.56 = (bf16[32,2048]{1,0:T(8,128)(2,1)S(1)}, bf16[32,2048]{1,0:T(8,128)(2,1)S(1)}, u32[]{:S(2)}, u32[]{:S(2)}) collective-permute-start(bf16[32,2048]{1,0:T(8,128)(2,1)S(1)} %slice.847), channel_id=1, source_target_pairs={{0,8},{1,9},{2,10},{3,11},{4,12},{5,13},{6,14},{7,15},{8,0},{9,1},... | collective-permute-start | bytes 393224 | tf_op jit(solution)/shard_map/ppermute | solution.py:25
  720.2 35.4 %collective-permute-start.82 = (bf16[32,2048]{1,0:T(8,128)(2,1)S(1)}, bf16[32,2048]{1,0:T(8,128)(2,1)S(1)}, u32[]{:S(2)}, u32[]{:S(2)}) collective-permute-start(bf16[32,2048]{1,0:T(8,128)(2,1)S(1)} %slice.877), channel_id=1, source_target_pairs={{0,8},{1,9},{2,10},{3,11},{4,12},{5,13},{6,14},{7,15},{8,0},{9,1},... | collective-permute-start | bytes 393224 | tf_op jit(solution)/shard_map/ppermute | solution.py:25
  755.6 19.5 %collective-permute-start.76 = (bf16[192,2048]{1,0:T(8,128)(2,1)S(1)}, bf16[192,2048]{1,0:T(8,128)(2,1)S(1)}, u32[]{:S(2)}, u32[]{:S(2)}) collective-permute-start(bf16[192,2048]{1,0:T(8,128)(2,1)S(1)} %slice.865), channel_id=1, source_target_pairs={{0,4},{1,5},{2,6},{3,7},{4,0},{5,1},{6,2},{7,3},{8,12},{9,13},{10,... | collective-permute-start | bytes 2359304 | tf_op jit(solution)/shard_map/ppermute | solution.py:25
  756.9 18.5 %collective-permute-start.47 = (bf16[96,2048]{1,0:T(8,128)(2,1)S(1)}, bf16[96,2048]{1,0:T(8,128)(2,1)S(1)}, u32[]{:S(2)}, u32[]{:S(2)}) collective-permute-start(bf16[96,2048]{1,0:T(8,128)(2,1)S(1)} %slice.829), channel_id=1, source_target_pairs={{0,2},{1,3},{2,0},{3,1},{4,6},{5,7},{6,4},{7,5},{8,10},{9,11},{10,... | collective-permute-start | bytes 1179656 | tf_op jit(solution)/shard_map/ppermute | solution.py:25
  758.8 17.8 %collective-permute-start.51 = (bf16[96,2048]{1,0:T(8,128)(2,1)S(1)}, bf16[96,2048]{1,0:T(8,128)(2,1)S(1)}, u32[]{:S(2)}, u32[]{:S(2)}) collective-permute-start(bf16[96,2048]{1,0:T(8,128)(2,1)S(1)} %slice.837), channel_id=1, source_target_pairs={{0,8},{1,9},{2,10},{3,11},{4,12},{5,13},{6,14},{7,15},{8,0},{9,1},... | collective-permute-start | bytes 1179656 | tf_op jit(solution)/shard_map/ppermute | solution.py:25
  759.2 19.1 %collective-permute-start.73 = (bf16[96,2048]{1,0:T(8,128)(2,1)S(1)}, bf16[96,2048]{1,0:T(8,128)(2,1)S(1)}, u32[]{:S(2)}, u32[]{:S(2)}) collective-permute-start(bf16[96,2048]{1,0:T(8,128)(2,1)S(1)} %slice.859), channel_id=1, source_target_pairs={{0,2},{1,3},{2,0},{3,1},{4,6},{5,7},{6,4},{7,5},{8,10},{9,11},{10,... | collective-permute-start | bytes 1179656 | tf_op jit(solution)/shard_map/ppermute | solution.py:25
  811.4 23.1 %collective-permute-start.85 = (bf16[192,2048]{1,0:T(8,128)(2,1)}, bf16[192,2048]{1,0:T(8,128)(2,1)}, u32[]{:S(2)}, u32[]{:S(2)}) collective-permute-start(bf16[192,2048]{1,0:T(8,128)(2,1)} %pad_maximum_fusion.27), channel_id=1, source_target_pairs={{0,8},{1,9},{2,10},{3,11},{4,12},{5,13},{6,14},{7,15},{8,0},{9,1},... | collective-permute-start | bytes 2359304 | tf_op jit(solution)/shard_map/ppermute | solution.py:25
  814.7 64.7 %collective-permute-start.57 = (bf16[64,2048]{1,0:T(8,128)(2,1)}, bf16[64,2048]{1,0:T(8,128)(2,1)}, u32[]{:S(2)}, u32[]{:S(2)}) collective-permute-start(bf16[64,2048]{1,0:T(8,128)(2,1)} %slice.848), channel_id=1, source_target_pairs={{0,16},{1,17},{2,18},{3,19},{4,20},{5,21},{6,22},{7,23},{8,24},{9,... | collective-permute-start | bytes 786440 | tf_op jit(solution)/shard_map/ppermute | solution.py:25
  817.9 20.7 %collective-permute-start.88 = (bf16[96,2048]{1,0:T(8,128)(2,1)S(1)}, bf16[96,2048]{1,0:T(8,128)(2,1)S(1)}, u32[]{:S(2)}, u32[]{:S(2)}) collective-permute-start(bf16[96,2048]{1,0:T(8,128)(2,1)S(1)} %pad_maximum_fusion.46), channel_id=1, source_target_pairs={{0,8},{1,9},{2,10},{3,11},{4,12},{5,13},{6,14},{7,15},{8,0},{9,1},... | collective-permute-start | bytes 1179656 | tf_op jit(solution)/shard_map/ppermute | solution.py:25
  835.9 22.5 %collective-permute-start.86 = (bf16[384,2048]{1,0:T(8,128)(2,1)S(1)}, bf16[384,2048]{1,0:T(8,128)(2,1)S(1)}, u32[]{:S(2)}, u32[]{:S(2)}) collective-permute-start(bf16[384,2048]{1,0:T(8,128)(2,1)S(1)} %pad_maximum_fusion.11), channel_id=1, source_target_pairs={{0,1},{1,0},{2,3},{3,2},{4,5},{5,4},{6,7},{7,6},{8,9},{9,8},{10,11... | collective-permute-start | bytes 4718600 | tf_op jit(solution)/shard_map/ppermute | solution.py:25
  838.6 17.4 %collective-permute-start.89 = (bf16[192,2048]{1,0:T(8,128)(2,1)S(1)}, bf16[192,2048]{1,0:T(8,128)(2,1)S(1)}, u32[]{:S(2)}, u32[]{:S(2)}) collective-permute-start(bf16[192,2048]{1,0:T(8,128)(2,1)S(1)} %pad_maximum_fusion.28), channel_id=1, source_target_pairs={{0,4},{1,5},{2,6},{3,7},{4,0},{5,1},{6,2},{7,3},{8,12},{9,13},{10,... | collective-permute-start | bytes 2359304 | tf_op jit(solution)/shard_map/ppermute | solution.py:25
  869.0 20.7 %collective-permute-start.113 = (bf16[256,1536]{1,0:T(8,128)(2,1)}, bf16[256,1536]{1,0:T(8,128)(2,1)}, u32[]{:S(2)}, u32[]{:S(2)}) collective-permute-start(bf16[256,1536]{1,0:T(8,128)(2,1)} %bitcast.344), channel_id=1, source_target_pairs={{0,4},{1,5},{2,6},{3,7},{4,0},{5,1},{6,2},{7,3},{8,12},{9,13},{10,... | collective-permute-start | bytes 2359304 | tf_op jit(solution)/shard_map/ppermute | solution.py:25
  872.2 43.8 %collective-permute-start.114 = (bf16[256,1536]{1,0:T(8,128)(2,1)}, bf16[256,1536]{1,0:T(8,128)(2,1)}, u32[]{:S(2)}, u32[]{:S(2)}) collective-permute-start(bf16[256,1536]{1,0:T(8,128)(2,1)} %bitcast.342), channel_id=1, source_target_pairs={{0,8},{1,9},{2,10},{3,11},{4,12},{5,13},{6,14},{7,15},{8,0},{9,1},... | collective-permute-start | bytes 2359304 | tf_op jit(solution)/shard_map/ppermute | solution.py:25
  876.5 41.8 %collective-permute-start.115 = (bf16[256,1536]{1,0:T(8,128)(2,1)}, bf16[256,1536]{1,0:T(8,128)(2,1)}, u32[]{:S(2)}, u32[]{:S(2)}) collective-permute-start(bf16[256,1536]{1,0:T(8,128)(2,1)} %bitcast.343), channel_id=1, source_target_pairs={{0,12},{1,13},{2,14},{3,15},{4,8},{5,9},{6,10},{7,11},{8,4},{9,5},... | collective-permute-start | bytes 2359304 | tf_op jit(solution)/shard_map/ppermute | solution.py:25
  878.4 33.2 %collective-permute-start.92 = (bf16[64,2048]{1,0:T(8,128)(2,1)}, bf16[64,2048]{1,0:T(8,128)(2,1)S(1)}, u32[]{:S(2)}, u32[]{:S(2)}) collective-permute-start(bf16[64,2048]{1,0:T(8,128)(2,1)} %pad_maximum_fusion.50), channel_id=1, source_target_pairs={{0,4},{1,5},{2,6},{3,7},{4,0},{5,1},{6,2},{7,3},{8,12},{9,13},{10,... | collective-permute-start | bytes 786440 | tf_op jit(solution)/shard_map/ppermute | solution.py:25
  991.2 48.5 %collective-permute-start.108 = (bf16[4,256,512]{1,2,0:T(8,128)(2,1)S(1)}, bf16[4,256,512]{1,2,0:T(8,128)(2,1)S(1)}, u32[]{:S(2)}, u32[]{:S(2)}) collective-permute-start(bf16[4,256,512]{1,2,0:T(8,128)(2,1)S(1)} %fusion.51), channel_id=1, source_target_pairs={{0,16},{1,17},{2,18},{3,19},{4,20},{5,21},{6,22},{7,23},{8,24},{9,... | collective-permute-start | bytes 3145736 | tf_op jit(solution)/shard_map/ppermute | solution.py:25
  997.7 63.7 %collective-permute-start.95 = (bf16[384,2048]{1,0:T(8,128)(2,1)}, bf16[384,2048]{1,0:T(8,128)(2,1)}, u32[]{:S(2)}, u32[]{:S(2)}) collective-permute-start(bf16[384,2048]{1,0:T(8,128)(2,1)} %get-tuple-element.60), channel_id=1, source_target_pairs={{0,1},{1,0},{2,3},{3,2},{4,5},{5,4},{6,7},{7,6},{8,9},{9,8},{10,11... | collective-permute-start | bytes 4718600 | tf_op jit(solution)/shard_map/ppermute | solution.py:25
  997.7 63.7 %collective-permute-start.99 = (bf16[384,2048]{1,0:T(8,128)(2,1)}, bf16[384,2048]{1,0:T(8,128)(2,1)}, u32[]{:S(2)}, u32[]{:S(2)}) collective-permute-start(bf16[384,2048]{1,0:T(8,128)(2,1)} %get-tuple-element.61), channel_id=1, source_target_pairs={{0,1},{1,0},{2,3},{3,2},{4,5},{5,4},{6,7},{7,6},{8,9},{9,8},{10,11... | collective-permute-start | bytes 4718600 | tf_op jit(solution)/shard_map/ppermute | solution.py:25
  1001.0 58.2 %collective-permute-start.104 = (bf16[128,2048]{1,0:T(8,128)(2,1)}, bf16[128,2048]{1,0:T(8,128)(2,1)}, u32[]{:S(2)}, u32[]{:S(2)}) collective-permute-start(bf16[128,2048]{1,0:T(8,128)(2,1)} %slice.900), channel_id=1, source_target_pairs={{0,2},{1,3},{2,0},{3,1},{4,6},{5,7},{6,4},{7,5},{8,10},{9,11},{10,... | collective-permute-start | bytes 1572872 | tf_op jit(solution)/shard_map/ppermute | solution.py:25
  1053.7 16.5 %collective-permute-start.111 = (bf16[256,512]{1,0:T(8,128)(2,1)}, bf16[256,512]{1,0:T(8,128)(2,1)}, u32[]{:S(2)}, u32[]{:S(2)}) collective-permute-start(bf16[256,512]{1,0:T(8,128)(2,1)} %bitcast.95), channel_id=1, source_target_pairs={{0,12},{1,13},{2,14},{3,15},{4,8},{5,9},{6,10},{7,11},{8,4},{9,5},... | collective-permute-start | bytes 786440 | tf_op jit(solution)/shard_map/ppermute | solution.py:25
  1066.5 21.7 %collective-permute-start.96 = (bf16[192,2048]{1,0:T(8,128)(2,1)}, bf16[192,2048]{1,0:T(8,128)(2,1)}, u32[]{:S(2)}, u32[]{:S(2)}) collective-permute-start(bf16[192,2048]{1,0:T(8,128)(2,1)} %slice.884), channel_id=1, source_target_pairs={{0,8},{1,9},{2,10},{3,11},{4,12},{5,13},{6,14},{7,15},{8,0},{9,1},... | collective-permute-start | bytes 2359304 | tf_op jit(solution)/shard_map/ppermute | solution.py:25
  1067.7 19.6 %collective-permute-start.106 = (bf16[32,2048]{1,0:T(8,128)(2,1)S(1)}, bf16[32,2048]{1,0:T(8,128)(2,1)}, u32[]{:S(2)}, u32[]{:S(2)}) collective-permute-start(bf16[32,2048]{1,0:T(8,128)(2,1)S(1)} %slice.904), channel_id=1, source_target_pairs={{0,8},{1,9},{2,10},{3,11},{4,12},{5,13},{6,14},{7,15},{8,0},{9,1},... | collective-permute-start | bytes 393224 | tf_op jit(solution)/shard_map/ppermute | solution.py:25
  1072.1 19.2 %collective-permute-start.100 = (bf16[192,2048]{1,0:T(8,128)(2,1)S(1)}, bf16[192,2048]{1,0:T(8,128)(2,1)S(1)}, u32[]{:S(2)}, u32[]{:S(2)}) collective-permute-start(bf16[192,2048]{1,0:T(8,128)(2,1)S(1)} %slice.892), channel_id=1, source_target_pairs={{0,4},{1,5},{2,6},{3,7},{4,0},{5,1},{6,2},{7,3},{8,12},{9,13},{10,... | collective-permute-start | bytes 2359304 | tf_op jit(solution)/shard_map/ppermute | solution.py:25
  (146 other events, 3468.8 us)

commit v2 on v1

v2 whole, which is shorter than its diff:
```python
import functools

import jax
import jax.numpy as jnp
import numpy as np
from jax import lax
from jax.experimental import pallas as pl
from jax.experimental.pallas import tpu as pltpu
from jax.sharding import PartitionSpec as P

HEADS = 16
HEAD_DIM = 128
FF = 8192
AXES = ("blk", "head")
SCALE = HEAD_DIM**-0.5
EPS = 1e-05
F32 = jnp.float32
BF16 = jnp.bfloat16
VMEM = pl.BlockSpec(memory_space=pltpu.VMEM)
SMEM = pl.BlockSpec(memory_space=pltpu.SMEM)
NN = (((1,), (0,)), ((), ()))
NT = (((1,), (1,)), ((), ()))
TN = (((0,), (0,)), ((), ()))


def dot(a, b, dims=NN):
    return lax.dot_general(a, b, dims, preferred_element_type=F32)


def shape(rows, columns, kind=BF16):
    return jax.ShapeDtypeStruct((rows, columns), kind)


def call(kernel, outs, name, flops=0, moved=0, grid=None, **more):
    settings = dict(
        out_shape=outs,
        compiler_params=pltpu.CompilerParams(vmem_limit_bytes=56 * 2**20),
        name=name,
    )
    if flops:
        settings["cost_estimate"] = pl.CostEstimate(
            flops=int(flops), bytes_accessed=int(moved), transcendentals=0
        )
    settings.update(more)
    if grid is not None:
        settings["grid"] = grid
    return pl.pallas_call(kernel, **settings)


def swap(value, nb, nh, db, dh):
    pairs = [
        (b * nh + h, (b ^ db) * nh + (h ^ dh)) for b in range(nb) for h in range(nh)
    ]
    return lax.ppermute(value, AXES, pairs)


def norm_stats(values):
    center = values - jnp.mean(values, axis=-1, keepdims=True)
    spread = jnp.mean(center * center, axis=-1, keepdims=True)
    rstd = lax.rsqrt(spread + EPS)
    return center * rstd, rstd


def norm_back(grad, normed, rstd):
    return (
        grad
        - jnp.mean(grad, axis=-1, keepdims=True)
        - normed * jnp.mean(grad * normed, axis=-1, keepdims=True)
    ) * rstd


def turn(values, table, back=False):
    half = HEAD_DIM // 2
    other = jnp.concatenate([values[:, half:], values[:, :half]], axis=1)
    other = other * table[:, HEAD_DIM:]
    return values * table[:, :HEAD_DIM] + (-other if back else other)


def after(value, *others):
    return lax.optimization_barrier((value,) + others)[0]


def pack(low, weights, slices, kin):
    wide = [w.shape[1] // slices for w in weights[:-1]]
    wide.append(weights[-1].shape[0] // slices)
    total = sum(wide)

    def kernel(low_ref, *refs):
        sources, outs = refs[: len(weights)], refs[len(weights) :]
        for d in range(slices):
            at = 0
            which = low_ref[0] ^ d
            for i, (source, w) in enumerate(zip(sources, wide)):
                where = pl.ds(pl.multiple_of(which * w, 128), w)
                if i < len(wide) - 1:
                    outs[d][:, at : at + w] = source[:, where]
                else:
                    outs[d][:, at : at + w] = source[where, :].T
                at += w

    return call(
        kernel,
        [shape(kin, total)] * slices,
        "pack",
        in_specs=[SMEM] + [VMEM] * len(weights),
        out_specs=[VMEM] * slices,
    )(low, *weights)


def assemble(low, pieces, kin, slices):
    groups = pieces[0][0].shape[0] // (kin * len(pieces[0][1]))
    total = pieces[0][0].shape[1]

    def kernel(low_ref, *refs):
        out = refs[-1]
        for (_, which), piece in zip(pieces, refs):
            for g in range(groups):
                for i, d in enumerate(which):
                    block = g * slices + (low_ref[0] ^ d)
                    rows = pl.ds(pl.multiple_of(block * kin, kin), kin)
                    at = (g * len(which) + i) * kin
                    out[rows, :] = piece[at : at + kin, :]

    return call(
        kernel,
        shape(groups * slices * kin, total),
        "assemble",
        in_specs=[SMEM] + [VMEM] * len(pieces),
        out_specs=VMEM,
    )(low, *[p for p, _ in pieces])


def unpack(low, pieces, wide):
    kin, slices = pieces[0].shape[0], len(pieces)

    def kernel(low_ref, *refs):
        sources, outs = refs[:slices], refs[slices:]
        for d in range(slices):
            at = 0
            which = low_ref[0] ^ d
            for i, (out, w) in enumerate(zip(outs, wide)):
                where = pl.ds(pl.multiple_of(which * w, 128), w)
                part = sources[d][:, at : at + w].astype(F32)
                if i < len(wide) - 1:
                    out[:, where] = part
                else:
                    out[where, :] = part.T
                at += w

    outs = [shape(kin, slices * w, F32) for w in wide[:-1]]
    outs.append(shape(slices * wide[-1], kin, F32))
    return call(
        kernel,
        outs,
        "unpack",
        in_specs=[SMEM] + [VMEM] * slices,
        out_specs=[VMEM] * len(wide),
    )(low, *pieces)


def join(refs):
    return jnp.concatenate([r[...] for r in refs], axis=0)


def project(pieces, weights, table):
    section = pieces[0].shape[0] * 2
    sections = len(pieces) // 2
    rows = section * sections

    def kernel(*refs):
        parts, (w, t, q, k, v) = refs[: len(pieces)], refs[len(pieces) :]
        for s in range(sections):
            out = dot(join(parts[2 * s : 2 * s + 2]), w[:, : 3 * HEAD_DIM])
            at = pl.ds(s * section, section)
            angles = t[at, :]
            q[at, :] = turn(out[:, :HEAD_DIM], angles).astype(BF16)
            k[at, :] = turn(out[:, HEAD_DIM : 2 * HEAD_DIM], angles).astype(BF16)
            v[at, :] = out[:, 2 * HEAD_DIM :].astype(BF16)

    width = weights.shape[0]
    return call(
        kernel,
        [shape(rows, HEAD_DIM)] * 3,
        "project",
        6 * rows * width * HEAD_DIM,
        2 * rows * width,
        in_specs=[VMEM] * (len(pieces) + 2),
        out_specs=[VMEM] * 3,
    )(*pieces, weights, table)


def row_block(keys):
    return max(64, 256 * 2048 // keys)


def split_rows(rows, step, width):
    n = rows // 2 // step
    return (
        n,
        [
            pl.BlockSpec((step, width), lambda i: (jnp.minimum(i, n - 1), 0)),
            pl.BlockSpec((step, width), lambda i: (jnp.maximum(i - n, 0), 0)),
        ],
        [shape(rows // 2, width)] * 2,
    )


def put(n, kept, sent, value):
    @pl.when(pl.program_id(0) < n)
    def _():
        kept[...] = value

    @pl.when(pl.program_id(0) >= n)
    def _():
        sent[...] = value


def attend(q, k, v, weights, pos_q, pos_k, half):
    rows, keys, width = q.shape[0] // 2, k.shape[0], weights.shape[0]
    bq = min(rows // 2, row_block(keys))
    first = half * rows // bq
    n, split, shapes = split_rows(rows, bq, width)

    def kernel(q_ref, k_ref, v_ref, w_ref, pq_ref, pk_ref, o_ref, lse_ref, kept, sent):
        scores = dot(q_ref[...], k_ref[...], NT)
        scores = jnp.where(pk_ref[...] <= pq_ref[...], scores * SCALE, -1e30)
        top = jnp.max(scores, axis=-1, keepdims=True)
        probs = jnp.exp(scores - top)
        total = jnp.sum(probs, axis=-1, keepdims=True)
        low = (dot(probs.astype(BF16), v_ref[...]) / total).astype(BF16)
        o_ref[...] = low
        lse_ref[...] = top + jnp.log(total)
        put(n, kept, sent, dot(low, w_ref[:, 3 * HEAD_DIM :], NT).astype(BF16))

    there = lambda w: pl.BlockSpec((bq, w), lambda i: (i + first, 0))
    here = lambda w: pl.BlockSpec((bq, w), lambda i: (i, 0))
    whole = lambda a: pl.BlockSpec(a.shape, lambda i: (0, 0))
    return call(
        kernel,
        [shape(rows, HEAD_DIM), shape(rows, 1, F32)] + shapes,
        "attend",
        4 * rows * keys * HEAD_DIM + 2 * rows * width * HEAD_DIM,
        2 * rows * width,
        grid=(rows // bq,),
        in_specs=[there(HEAD_DIM), whole(k), whole(v), whole(weights), there(1), whole(pos_k)],
        out_specs=[here(HEAD_DIM), here(1)] + split,
    )(q, k, v, weights, pos_q, pos_k)


def feed(tokens, backs, weights):
    rows, width = sum(p.shape[0] for p in tokens), weights.shape[0]
    unit = weights.shape[1] // 3
    count = len(tokens)
    step = min(256, rows // 2)

    def kernel(*refs):
        xs, gs = refs[:count], refs[count : 2 * count]
        w, paired, hidden, kept, sent, x_all, g_all = refs[2 * count :]
        at = 0
        for x, g in zip(xs, gs):
            x_all[at : at + x.shape[0], :] = x[...]
            g_all[at : at + x.shape[0], :] = g[...]
            at += x.shape[0]

        for first, part in ((0, kept), (rows // 2, sent)):

            @pl.loop(0, rows // 2 // step)
            def _(i):
                at = pl.ds(pl.multiple_of(first + i * step, step), step)
                gate_up = dot(x_all[at, :], w[:, : 2 * unit])
                back = dot(g_all[at, :], w[:, 2 * unit :])
                gate, up = gate_up[:, :unit], gate_up[:, unit:]
                sig = 1.0 / (1.0 + jnp.exp(-gate))
                act = gate * sig
                hidden[at, :] = (act * up).astype(BF16)
                paired[at, :unit] = (back * up * sig * (1.0 + gate * (1.0 - sig))).astype(BF16)
                paired[at, unit:] = (back * act).astype(BF16)
                there = pl.ds(pl.multiple_of(i * step, step), step)
                part[there, :] = dot(paired[at, :], w[:, : 2 * unit], NT).astype(BF16)

    return call(
        kernel,
        [shape(rows, 2 * unit), shape(rows, unit)] + [shape(rows // 2, width)] * 2,
        "feed",
        10 * rows * unit * width,
        2 * rows * width,
        in_specs=[VMEM] * (2 * count + 1),
        out_specs=[VMEM] * 4,
        scratch_shapes=[pltpu.VMEM((rows, width), BF16)] * 2,
    )(*tokens, *backs, weights)


def feed_out(hidden, weights):
    rows, unit = hidden.shape
    width = weights.shape[0]
    step = min(256, rows // 2)
    n, split, shapes = split_rows(rows, step, width)

    def kernel(hidden_ref, w_ref, kept, sent):
        put(n, kept, sent, dot(hidden_ref[...], w_ref[:, 2 * unit :], NT).astype(BF16))

    return call(
        kernel,
        shapes,
        "feed_out",
        2 * rows * unit * width,
        2 * rows * width,
        grid=(rows // step,),
        in_specs=[
            pl.BlockSpec((step, unit), lambda i: (i, 0)),
            pl.BlockSpec(weights.shape, lambda i: (0, 0)),
        ],
        out_specs=split,
    )(hidden, weights)


def weight_grads(pairs, width):
    columns = [sides[0].shape[1] for _, sides in pairs]
    total = sum(columns)
    block = 256
    flat = []
    for pieces, sides in pairs:
        flat += list(pieces) + list(sides)

    def kernel(*refs):
        out = refs[-1]
        at, start = 0, 0
        for (pieces, sides), wide in zip(pairs, columns):
            left = join(refs[at : at + len(pieces)])
            at += len(pieces)
            right = join(refs[at : at + len(sides)])
            at += len(sides)
            out[:, start : start + wide] = dot(left, right, TN).astype(BF16)
            start += wide

    specs = []
    for pieces, sides in pairs:
        specs += [pl.BlockSpec((p.shape[0], block), lambda j: (0, j)) for p in pieces]
        specs += [pl.BlockSpec(s.shape, lambda j: (0, 0)) for s in sides]
    rows = sum(p.shape[0] for p in pairs[0][0])
    return call(
        kernel,
        shape(width, total),
        "weight_grads",
        2 * rows * width * total,
        2 * rows * (width + total),
        grid=(width // block,),
        in_specs=specs,
        out_specs=pl.BlockSpec((block, total), lambda j: (j, 0)),
    )(*flat)


def back_project(pieces, weights):
    rows, width = sum(p.shape[0] for p in pieces), weights.shape[0]

    def kernel(*refs):
        w, out = refs[-2:]
        at = 0
        for s in range(len(pieces) // 2):
            x = join(refs[2 * s : 2 * s + 2])
            out[at : at + x.shape[0], :] = dot(x, w[:, 3 * HEAD_DIM :]).astype(BF16)
            at += x.shape[0]

    return call(
        kernel,
        shape(rows, HEAD_DIM),
        "back_project",
        2 * rows * width * HEAD_DIM,
        2 * rows * width,
        in_specs=[VMEM] * (len(pieces) + 1),
        out_specs=VMEM,
    )(*pieces, weights)


def attend_back(q, do, lse, pos_q, k, v, pos_k):
    rows, keys = q.shape[0], k.shape[0]
    bq = min(rows, row_block(keys))

    def kernel(q_ref, do_ref, lse_ref, pq_ref, k_ref, v_ref, pk_ref, dq_ref, dk_ref, dv_ref):
        @pl.when(pl.program_id(0) == 0)
        def _():
            dk_ref[...] = jnp.zeros_like(dk_ref)
            dv_ref[...] = jnp.zeros_like(dv_ref)

        q, k, v, do = q_ref[...], k_ref[...], v_ref[...], do_ref[...]
        scores = dot(q, k, NT)
        probs = jnp.where(
            pk_ref[...] <= pq_ref[...], jnp.exp(scores * SCALE - lse_ref[...]), 0.0
        )
        dots = dot(do, v, NT)
        delta = jnp.sum(probs * dots, axis=-1, keepdims=True)
        back = (probs * (dots - delta)).astype(BF16)
        dq_ref[...] = dot(back, k) * SCALE
        dk_ref[...] += dot(back, q, TN) * SCALE
        dv_ref[...] += dot(probs.astype(BF16), do, TN)

    row = lambda w: pl.BlockSpec((bq, w), lambda i: (i, 0))
    whole = lambda s: pl.BlockSpec(s, lambda i: (0, 0))
    kv = whole((keys, HEAD_DIM))
    return call(
        kernel,
        [shape(rows, HEAD_DIM, F32), shape(keys, HEAD_DIM, F32), shape(keys, HEAD_DIM, F32)],
        "attend_back",
        10 * rows * keys * HEAD_DIM,
        16 * rows * HEAD_DIM,
        grid=(rows // bq,),
        in_specs=[row(HEAD_DIM), row(HEAD_DIM), row(1), row(1), kv, kv, whole((1, keys))],
        out_specs=[row(HEAD_DIM), kv, kv],
    )(q, do, lse, pos_q, k, v, pos_k)


def back_input(dq, dk, dv, table, weights, half):
    rows, width = dq.shape[0] // 2, weights.shape[0]
    step = min(256, rows // 2)
    first = half * rows // step
    n, split, shapes = split_rows(rows, step, width)

    def kernel(dq_ref, dk_ref, dv_ref, t_ref, w_ref, joined, kept, sent):
        joined[:, :HEAD_DIM] = turn(dq_ref[...], t_ref[...], True).astype(BF16)
        joined[:, HEAD_DIM : 2 * HEAD_DIM] = turn(dk_ref[...], t_ref[...], True).astype(BF16)
        joined[:, 2 * HEAD_DIM :] = dv_ref[...].astype(BF16)
        put(n, kept, sent, dot(joined[...], w_ref[:, : 3 * HEAD_DIM], NT).astype(BF16))

    there = lambda w: pl.BlockSpec((step, w), lambda i: (i + first, 0))
    here = lambda w: pl.BlockSpec((step, w), lambda i: (i, 0))
    return call(
        kernel,
        [shape(rows, 3 * HEAD_DIM)] + shapes,
        "back_input",
        6 * rows * width * HEAD_DIM,
        2 * rows * width,
        grid=(rows // step,),
        in_specs=[there(HEAD_DIM)] * 3
        + [there(2 * HEAD_DIM), pl.BlockSpec(weights.shape, lambda i: (0, 0))],
        out_specs=[here(3 * HEAD_DIM)] + split,
    )(dq, dk, dv, table, weights)


def local(nb, nh, block_input, cotangent, w_query, w_key, w_value, w_out, w_gate, w_up, w_down):
    tok_rows, width = block_input.shape[1:]
    slices = HEADS // nh
    half = nb // 2
    groups = nb // slices
    spread = groups // 2
    kin = width // nb
    unit = FF // HEADS
    b, h = lax.axis_index("blk"), lax.axis_index("head")
    low, group = b % slices, b // slices
    second = b >= half
    mine = 2 * tok_rows
    move = functools.partial(swap, nb=nb, nh=nh)
    scalar = lambda v: v.astype(jnp.int32).reshape(1)

    opening, core = (2, 0), (0, 1)
    orders = [((1, 0), (0, 2)), ((0, 2), (1, 0))]

    def exchange(values, step):
        return [move(v, db=o[step][0], dh=o[step][1]) for v, o in zip(values, orders)]

    def across(value, way):
        return move(value, db=way[0], dh=way[1])

    def tied(values, beside):
        return [after(v, *beside) for v in values] if beside else values

    class Gather:
        def __init__(self, value):
            self.parts = value
            self.sent = across(value, opening)

        def open(self, *beside):
            arrived = tied([self.sent], beside)[0]
            n = tok_rows
            self.parts = [
                jnp.concatenate([self.parts[:n], arrived[:n]], axis=0),
                jnp.concatenate([self.parts[n:], arrived[n:]], axis=0),
            ]
            self.sent = exchange(self.parts, 0)

        def take(self, *beside):
            arrived = tied(self.sent, beside)
            self.parts = [jnp.concatenate([p, r], axis=0) for p, r in zip(self.parts, arrived)]
            self.sent = exchange(self.parts, 1)
            self.near = self.parts + [across(p, core) for p in self.parts]

        def far(self, *beside):
            pieces = tied(self.sent, beside)
            return pieces + [across(p, core) for p in pieces]

    def gather(value):
        work = Gather(value)
        work.open()
        work.take()
        return work.near, work.far()

    class Scatter:
        def __init__(self, kept, sent):
            self.kept, self.sent = kept, across(sent, core)

        def add(self, *beside):
            arrived = tied([self.sent], beside)[0]
            n = self.kept.shape[0] // 2
            return [
                (self.kept[r].astype(F32) + arrived[r].astype(F32)).astype(BF16)
                for r in (slice(0, n), slice(n, 2 * n))
            ]

        def open(self, *beside):
            self.far = self.add(*beside)
            self.sent_far = exchange(self.far, 1)

        def near(self, kept, sent):
            self.kept, self.sent = kept, across(sent, core)

        def take_near(self, *beside):
            self.parts = self.add(*beside)

        def take(self, *beside):
            arrived = tied(self.sent_far, beside)
            sums = [p.astype(F32) + r.astype(F32) for p, r in zip(self.parts, arrived)]
            n = 2 * tok_rows
            self.parts = [p[:n] for p in sums]
            self.sent = exchange([p[n:].astype(BF16) for p in sums], 0)

        def pair(self, *beside):
            arrived = tied(self.sent, beside)
            sums = [p + r.astype(F32) for p, r in zip(self.parts, arrived)]
            n = tok_rows
            self.parts = jnp.concatenate([p[:n] for p in sums], axis=0)
            self.sent = across(
                jnp.concatenate([p[n:] for p in sums], axis=0).astype(BF16), opening
            )

        def close(self, *beside):
            return self.parts + tied([self.sent], beside)[0].astype(F32)

    flip_b, flip_h, place = [], [], []
    for last in range(2):
        for other in range(2):
            for r, (one, two) in enumerate(orders):
                db, dh = np.array([0, opening[0]]), np.array([0, opening[1]])
                db, dh = np.concatenate([db, db ^ one[0]]), np.concatenate([dh, dh ^ one[1]])
                if last:
                    db, dh = db ^ two[0], dh ^ two[1]
                dh = dh ^ other
                flip_b.append(np.repeat(db, tok_rows) ^ (half if r else 0))
                flip_h.append(np.repeat(dh, tok_rows))
                place.append(np.tile(np.arange(tok_rows), 4))
    flip_b, flip_h, place = (np.concatenate(t).astype(np.int32) for t in (flip_b, flip_h, place))

    def positions(block):
        return ((block ^ flip_b) * nh + (h ^ flip_h)) * tok_rows + place

    pos = positions(b)
    rates = 10000.0 ** (-jnp.arange(HEAD_DIM // 2, dtype=F32) * 2.0 / HEAD_DIM)
    angles = pos.astype(F32)[:, None] * rates[None, :]
    cosine, sine = jnp.cos(angles), jnp.sin(angles)
    table = jnp.concatenate([cosine, cosine, -sine, sine], axis=1)

    def to_micro(pair, *beside):
        keep = jnp.where(second, pair[1], pair[0])
        send = jnp.where(second, pair[0], pair[1])
        arrived = tied([move(send, db=half, dh=0)], beside)[0]
        return jnp.concatenate([keep, arrived], axis=0)

    def from_micro(rows):
        arrived = move(rows[tok_rows:], db=half, dh=0)
        kept = rows[:tok_rows]
        return jnp.stack(
            [jnp.where(second, arrived, kept), jnp.where(second, kept, arrived)]
        )

    alike = [[g * slices + l for g in range(groups)] for l in range(slices)]

    def to_groups(piece):
        return lax.all_gather(piece, "blk", axis=0, tiled=True, axis_index_groups=alike)

    def from_slices(pieces):
        return [move(p, db=d + 1, dh=0) for d, p in enumerate(pieces[1:])]

    def from_groups(grads):
        return lax.psum_scatter(
            grads, "blk", scatter_dimension=0, tiled=True, axis_index_groups=alike
        )

    def collect(whole):
        whole = whole.reshape(slices, kin, -1)
        pick = lambda d: lax.dynamic_index_in_dim(whole, low ^ d, 0, False)
        return [pick(0)] + [move(pick(d), db=d, dh=0) for d in range(1, slices)]

    every = tuple(range(slices))
    attn_own = pack(scalar(low), (w_query, w_key, w_value, w_out), slices, kin)
    feed_own = pack(scalar(low), (w_gate, w_up, w_down), slices, kin)
    tokens = to_micro(block_input, table, *attn_own, *feed_own).astype(F32)
    attn_rest = from_slices(attn_own)
    feed_all = [to_groups(feed_own[0])]
    attn_all = to_groups(
        after(jnp.concatenate([attn_own[0]] + attn_rest, axis=0), *feed_all)
    )
    w_attn = assemble(scalar(low), [(attn_all, every)], kin, slices)
    normed_f, rstd_in = norm_stats(tokens)
    first = Gather(normed_f.astype(BF16))
    first.open(*attn_rest)
    feed_rest = from_slices(feed_own)
    first.take(feed_rest[1])
    normed = first.near + first.far(feed_rest[0], feed_rest[2])
    for piece in (feed_rest[1], feed_rest[0], feed_rest[2]):
        feed_all.append(to_groups(piece))
    back_rows = to_micro(cotangent)
    cots = Gather(after(back_rows, *normed[:2]))
    query, key, value = project(normed, w_attn, table)
    cots.open(query)
    if spread > 1:
        teams = [
            [(((m * spread + s) * slices + l) * nh + k) for s in range(spread)]
            for m in range(2)
            for l in range(slices)
            for k in range(nh)
        ]
        everyone = lambda t: lax.all_gather(t, AXES, axis=0, tiled=True, axis_index_groups=teams)
        keys, values = everyone(key), everyone(value)
        first = b - (group % spread) * slices
        pos_k = jnp.concatenate([positions(first + s * slices) for s in range(spread)])
    else:
        keys, values, pos_k = key, value, pos

    pos_q, pos_k = pos[:, None], pos_k[None, :]
    low1, lse1, kept, sent = attend(query, keys, values, w_attn, pos_q, pos_k, 1)
    mixing = Scatter(kept, sent)
    mixing.open()
    low0, lse0, kept, sent = attend(
        after(query, *mixing.far), keys, values, w_attn, pos_q, pos_k, 0
    )
    mixing.near(kept, sent)
    mixing.take_near()
    mixing.take(feed_all[1])
    cots.take(*mixing.parts)
    mixing.pair()
    mid = tokens + mixing.close(feed_all[2])
    mid_f, rstd_mid = norm_stats(mid)

    mids = Gather(mid_f.astype(BF16))
    mids.open(*cots.sent)
    backs_far = cots.far(*mids.parts)
    backs_near = cots.near
    mids.take(*backs_far, feed_all[3])
    w_feed = assemble(
        scalar(low),
        [(a, d) for a, d in zip(feed_all, ((0,), (2,), (1,), (3,)))],
        kin,
        slices,
    )
    paired0, hidden0, kept0, sent0 = feed(mids.near, backs_near, w_feed)
    mids_far = mids.far(hidden0)
    paired1, hidden1, kept, sent = feed(mids_far, backs_far, w_feed)
    giving = Scatter(kept, sent)
    giving.open()
    giving.near(kept0, sent0)
    feed_grads = weight_grads(
        [
            (mids.near + mids_far, [paired0, after(paired1, *giving.far)]),
            (backs_near + backs_far, [hidden0, hidden1]),
        ],
        width,
    )
    giving.take_near()
    giving.take(feed_grads)
    feed_whole = from_groups(feed_grads)
    out1 = feed_out(after(hidden1, *giving.parts), w_feed)
    giving.pair(*out1)
    out0 = feed_out(after(hidden0, giving.parts), w_feed)
    back_mid_normed = giving.close(*out0)

    back_mid = back_rows.astype(F32) + norm_back(back_mid_normed, mid_f, rstd_mid)
    turned = gather(back_mid.astype(BF16))
    back_attn = turned[0] + turned[1]

    finishing = Scatter(*(after(o, *turned[1][:2]) for o in out1))
    back_attended = back_project(back_attn, w_attn)
    finishing.open(back_attended)
    finishing.near(*out0)
    lse = jnp.concatenate([lse0, lse1], axis=0)
    back_q, back_k, back_v = attend_back(
        query, after(back_attended, *finishing.far), lse, pos_q, keys, values, pos_k
    )
    finishing.take_near(back_q)
    finishing.take()
    if spread > 1:
        shared = lambda t: lax.psum_scatter(
            t, AXES, scatter_dimension=0, tiled=True, axis_index_groups=teams
        )
        back_k, back_v = shared(back_k), shared(back_v)
    joined1, kept, sent = back_input(
        after(back_q, *finishing.parts), back_k, back_v, table, w_attn, 1
    )
    entering = Scatter(kept, sent)
    entering.open()
    finishing.pair(joined1)
    joined0, kept, sent = back_input(
        after(back_q, finishing.parts), back_k, back_v, table, w_attn, 0
    )
    entering.near(kept, sent)
    output = mid + finishing.close(joined0)
    block_output = from_micro(output.astype(BF16))
    attn_grads = weight_grads(
        [(normed, [joined0, joined1]), (back_attn, [low0, low1])], width
    )
    entering.take_near(attn_grads)
    entering.take()
    entering.pair()
    feed_sum = collect(after(feed_whole, entering.parts))
    back_normed = entering.close()
    grad_gate, grad_up, grad_down = unpack(scalar(low), feed_sum, (unit,) * 3)
    attn_sum = collect(after(from_groups(after(attn_grads, feed_whole)), back_normed))
    grad_query, grad_key, grad_value, grad_out = unpack(
        scalar(low), attn_sum, (HEAD_DIM,) * 4
    )
    input_grad = from_micro((back_mid + norm_back(back_normed, normed_f, rstd_in)).astype(BF16))
    return (
        block_output,
        input_grad,
        grad_query,
        grad_key,
        grad_value,
        grad_out,
        grad_gate,
        grad_up,
        grad_down,
    )


def solution(mesh):
    rows = P(None, AXES, None)
    tall, wide = P("blk", "head"), P("head", "blk")
    placed = (rows, rows, tall, tall, tall, wide, tall, tall, wide)
    return jax.shard_map(
        functools.partial(local, mesh.shape["blk"], mesh.shape["head"]),
        mesh=mesh,
        in_specs=placed,
        out_specs=placed,
        check_vma=False,
    )
```

time: 1140 us -> 766 us (0.67)
  local copies, waits for them, and re-layouts: 276 us -> 25.2 us
  Pallas kernels: 26.8 us -> 183 us
  matrix products: 96.8 us -> 0 us
  waiting for transfers between devices: 491 us -> 397 us
  starting transfers between devices: 121 us -> 72 us
  other arithmetic: 107 us -> 65.5 us
  between operations: 3.27 us -> 15.4 us
    pallas_call x2 -> x19, Pallas kernels: 26.8 us -> 183 us  [the longest x2 38.7 us: feed(): call(kernel, [shape(rows, 2 * unit), shape(rows, unit)] + [shape(rows //...]
    ppermute x116 -> x80, waiting for transfers between devices: 491 us -> 383 us  [swap(): return lax.ppermute(value, AXES, pairs)]
    dot_general x12 -> x0, matrix products: 96.8 us -> none  [the longest x1 15.1 us: local(): gate_up = jnp.dot(mid_all, w_paired, preferred_element_type=F32)]
    unnamed x249 -> x104, local copies, waits for them, and re-layouts: 77.9 us -> 8.31 us
    ppermute x116 -> x80, starting transfers between devices: 121 us -> 71.1 us  [swap(): return lax.ppermute(value, AXES, pairs)]
    dynamic_update_slice x38 -> x0, local copies, waits for them, and re-layouts: 45.8 us -> none  [the longest x32 40.1 us: in_order(): result = lax.dynamic_update_index_in_dim(result, piece[:, lo:hi], b ^ j, 0)]
    broadcast_in_dim x29 -> x1, local copies, waits for them, and re-layouts: 37.8 us -> 1.36 us  [local(): pos_q, pos_k = (pos[:, None], pos_k[None, :])]
    slice x63 -> x35, local copies, waits for them, and re-layouts: 41.9 us -> 8.1 us  [the longest x6 3.63 us: take(): self.sent = exchange([p[n:].astype(BF16) for p in sums], 0)]
  transfers between devices with their start and end apart: 116 -> 87, of which waited for: 51 -> 49; matrix products, arithmetic and copies ran while one was open for 32% -> 10% of each run, Pallas kernels for 1% -> 19%
where the time goes in v2:
time: 766 us; the launch traced here: 759 us
  waiting for transfers between devices  397 us (52%)
  Pallas kernels  183 us (24%)
  starting transfers between devices  72 us (9%)
  other arithmetic  65.5 us (9%)
  local copies, waits for them, and re-layouts  25.2 us (3%)
  between operations  15.4 us (2%)
    ppermute x80, waiting for transfers between devices, swap(): return lax.ppermute(value, AXES, pairs)  383 us
    ppermute x80, starting transfers between devices, swap(): return lax.ppermute(value, AXES, pairs)  71.1 us
    pallas_call x2, Pallas kernels, feed(): call(kernel, [shape(rows, 2 * unit), shape(rows, unit)] + [shape(rows //...  38.7 us
    pallas_call x2, Pallas kernels, weight_grads(): call(kernel, shape(width, total), 'weight_grads', 2 * rows * width * tota...  33.5 us
    pallas_call x2, Pallas kernels, attend(): call(kernel, [shape(rows, HEAD_DIM), shape(rows, 1, F32)] + shapes, 'atte...  20.7 us
    pallas_call x1, Pallas kernels, attend_back(): call(kernel, [shape(rows, HEAD_DIM, F32), shape(keys, HEAD_DIM, F32), sha...  18.8 us
    pallas_call x2, Pallas kernels, feed_out(): call(kernel, shapes, 'feed_out', 2 * rows * unit * width, 2 * rows * widt...  15.9 us
    pallas_call x2, Pallas kernels, back_input(): call(kernel, [shape(rows, 3 * HEAD_DIM)] + shapes, 'back_input', 6 * rows...  15.5 us
  transfers between devices with their start and end apart: 87, of which 49 were waited for; matrix products, arithmetic and copies ran while one was open for 10% of the time, Pallas kernels for 19%

profile of v2, /device:TPU:0, one launch (start us, length us, event | category | flops | bytes accessed | tf_op | source)
XLA Modules:
  0.0 758.9 jit_solution(17402597535270516340)
XLA Ops:
  8.3 4.1 collective-permute-start
  13.2 3.7 multiply_cosine_fusion
  16.9 3.8 pack.3
  31.7 3.6 collective-permute-done.2
  35.3 15.9 %collective-permute-done.3 = bf16[256,512]{1,0:T(8,128)(2,1)S(1)} collective-permute-done((bf16[256,512]{1,0:T(8,128)(2,1)}, bf16[256,512]{1,0:T(8,128)(2,1)S(1)}, u32[]{:S(2)}, u32[]{:S(2)}) %collective-permute-start.3) | collective-permute-done | bytes 262176 | tf_op jit(solution)/shard_map/ppermute | solution.py:54
  51.2 12.0 %collective-permute-done.4 = bf16[256,512]{1,0:T(8,128)(2,1)} collective-permute-done((bf16[256,512]{1,0:T(8,128)(2,1)}, bf16[256,512]{1,0:T(8,128)(2,1)}, u32[]{:S(2)}, u32[]{:S(2)}) %collective-permute-start.4) | collective-permute-done | bytes 262176 | tf_op jit(solution)/shard_map/ppermute | solution.py:54
  67.7 16.7 %collective-permute-done.6 = bf16[256,1536]{1,0:T(8,128)(2,1)S(1)} collective-permute-done((bf16[256,1536]{1,0:T(8,128)(2,1)}, bf16[256,1536]{1,0:T(8,128)(2,1)S(1)}, u32[]{:S(2)}, u32[]{:S(2)}) %collective-permute-start.6) | collective-permute-done | bytes 786464 | tf_op jit(solution)/shard_map/ppermute | solution.py:54
  94.4 49.6 %collective-permute-done.11 = bf16[256,1536]{1,0:T(8,128)(2,1)} collective-permute-done((bf16[256,1536]{1,0:T(8,128)(2,1)}, bf16[256,1536]{1,0:T(8,128)(2,1)}, u32[]{:S(2)}, u32[]{:S(2)}) %collective-permute-start.11) | collective-permute-done | bytes 786464 | tf_op jit(solution)/shard_map/ppermute | solution.py:54
  146.1 3.0 assemble.2.refs_8_.w_ref
  150.0 10.4 %project.1 = (bf16[2048,128]{1,0:T(8,128)(2,1)}, bf16[2048,128]{1,0:T(8,128)(2,1)}, bf16[2048,128]{1,0:T(8,128)(2,1)}) custom-call(bf16[256,2048]{1,0:T(8,128)(2,1)} %copy-done.1, bf16[256,2048]{1,0:T(8,128)(2,1)} %copy-done, bf16[256,2048]{1,0:T(8,128)(2,1)} %collective-permute-done.8.refs_2_, bf16[256,2048]{1,0:T(8,128)(2,1)} %collective-permute-done.9.refs_3_, ...), custom_call_target="tpu_custom_call" | custom-call | flops 3221225472 | bytes 8388608 | tf_op jit(solution)/shard_map/project/pallas_call | solution.py:181
  160.4 10.2 %attend.2 = (bf16[1024,128]{1,0:T(8,128)(2,1)}, f32[1024,1]{1,0:T(8,128)}, bf16[512,2048]{1,0:T(8,128)(2,1)}, bf16[512,2048]{1,0:T(8,128)(2,1)}) custom-call(bf16[2048,128]{1,0:T(8,128)(2,1)} %get-tuple-element.120.q_ref, bf16[2048,128]{1,0:T(8,128)(2,1)} %get-tuple-element.116.k_ref, bf16[2048,128]{1,0:T(8,128)(2,1)} %get-tuple-element.117.v_ref, ...), custom_call_target="tpu_custom_call" | custom-call | flops 1610612736 | bytes 4194304 | tf_op jit(solution)/shard_map/attend/pallas_call | solution.py:238
  170.9 4.2 collective-permute-done.16
  175.0 3.7 add_convert_fusion.15
  178.8 10.5 %attend.3 = (bf16[1024,128]{1,0:T(8,128)(2,1)}, f32[1024,1]{1,0:T(8,128)}, bf16[512,2048]{1,0:T(8,128)(2,1)}, bf16[512,2048]{1,0:T(8,128)(2,1)}) custom-call(bf16[2048,128]{1,0:T(8,128)(2,1)} %get-tuple-element.120.q_ref, bf16[2048,128]{1,0:T(8,128)(2,1)} %get-tuple-element.116.k_ref, bf16[2048,128]{1,0:T(8,128)(2,1)} %get-tuple-element.117.v_ref, ...), custom_call_target="tpu_custom_call" | custom-call | flops 1610612736 | bytes 4194304 | tf_op jit(solution)/shard_map/attend/pallas_call | solution.py:238
  189.5 2.9 collective-permute-start.24
  192.4 25.7 %collective-permute-done.24 = bf16[64,2048]{1,0:T(8,128)(2,1)S(1)} collective-permute-done((bf16[64,2048]{1,0:T(8,128)(2,1)S(1)}, bf16[64,2048]{1,0:T(8,128)(2,1)S(1)}, u32[]{:S(2)}, u32[]{:S(2)}) %collective-permute-start.24) | collective-permute-done | bytes 262176 | tf_op jit(solution)/shard_map/ppermute | solution.py:54
  223.1 16.6 %collective-permute-done.25 = bf16[128,2048]{1,0:T(8,128)(2,1)} collective-permute-done((bf16[128,2048]{1,0:T(8,128)(2,1)}, bf16[128,2048]{1,0:T(8,128)(2,1)}, u32[]{:S(2)}, u32[]{:S(2)}) %collective-permute-start.25) | collective-permute-done | bytes 524320 | tf_op jit(solution)/shard_map/ppermute | solution.py:54
  246.9 3.3 convert_add_fusion.7
  254.1 11.1 %collective-permute-done.19 = bf16[128,2048]{1,0:T(8,128)(2,1)S(1)} collective-permute-done((bf16[128,2048]{1,0:T(8,128)(2,1)S(1)}, bf16[128,2048]{1,0:T(8,128)(2,1)S(1)}, u32[]{:S(2)}, u32[]{:S(2)}) %collective-permute-start.19) | collective-permute-done | bytes 524320 | tf_op jit(solution)/shard_map/ppermute | solution.py:54
  265.4 2.9 collective-permute-done.21
  276.1 9.1 %collective-permute-done.22 = bf16[128,2048]{1,0:T(8,128)(2,1)} collective-permute-done((bf16[128,2048]{1,0:T(8,128)(2,1)S(1)}, bf16[128,2048]{1,0:T(8,128)(2,1)}, u32[]{:S(2)}, u32[]{:S(2)}) %collective-permute-start.22) | collective-permute-done | bytes 524320 | tf_op jit(solution)/shard_map/ppermute | solution.py:54
  287.4 9.0 %collective-permute-done.29.refs_5_.refs_15_ = bf16[256,2048]{1,0:T(8,128)(2,1)} collective-permute-done((bf16[256,2048]{1,0:T(8,128)(2,1)}, bf16[256,2048]{1,0:T(8,128)(2,1)}, u32[]{:S(2)}, u32[]{:S(2)}) %collective-permute-start.29) | collective-permute-done | bytes 1048608 | tf_op jit(solution)/shard_map/ppermute | solution.py:54
  297.7 5.6 collective-permute-done.23
  307.2 10.7 %collective-permute-done.33 = bf16[128,2048]{1,0:T(8,128)(2,1)S(1)} collective-permute-done((bf16[128,2048]{1,0:T(8,128)(2,1)S(1)}, bf16[128,2048]{1,0:T(8,128)(2,1)S(1)}, u32[]{:S(2)}, u32[]{:S(2)}) %collective-permute-start.33) | collective-permute-done | bytes 524320 | tf_op jit(solution)/shard_map/ppermute | solution.py:54
  318.7 13.2 %all-gather.14.cloned.1.call-done.refs_3_ = bf16[512,1536]{1,0:T(8,128)(2,1)} async-done(((bf16[256,1536]{1,0:T(8,128)(2,1)}), bf16[512,1536]{1,0:T(8,128)(2,1)}) %all-gather.14.cloned.1.call-update) | async-done | bytes 1572880 | tf_op jit(solution)/shard_map/all_gather | solution.py:576
  336.7 5.9 assemble.3.refs_8_.w_ref
  344.7 19.3 %feed.2 = (bf16[1024,1024]{1,0:T(8,128)(2,1)}, bf16[1024,512]{1,0:T(8,128)(2,1)}, bf16[512,2048]{1,0:T(8,128)(2,1)}, bf16[512,2048]{1,0:T(8,128)(2,1)}) custom-call(bf16[256,2048]{1,0:T(8,128)(2,1)} %copy-done.31, bf16[256,2048]{1,0:T(8,128)(2,1)} %copy-done.30, bf16[256,2048]{1,0:T(8,128)(2,1)} %copy-done.47, bf16[256,2048]{1,0:T(8,128)(2,1)} %copy-done.46, ...), custom_call_target="tpu_custom_call" | custom-call | flops 10737418240 | bytes 4194304 | tf_op jit(solution)/shard_map/feed/pallas_call | solution.py:281
  369.2 19.3 %feed.3 = (bf16[1024,1024]{1,0:T(8,128)(2,1)}, bf16[1024,512]{1,0:T(8,128)(2,1)}, bf16[512,2048]{1,0:T(8,128)(2,1)}, bf16[512,2048]{1,0:T(8,128)(2,1)}) custom-call(bf16[256,2048]{1,0:T(8,128)(2,1)} %copy-done.49, bf16[256,2048]{1,0:T(8,128)(2,1)} %copy-done.48, bf16[256,2048]{1,0:T(8,128)(2,1)} %copy-done.51, bf16[256,2048]{1,0:T(8,128)(2,1)} %copy-done.50, ...), custom_call_target="tpu_custom_call" | custom-call | flops 10737418240 | bytes 4194304 | tf_op jit(solution)/shard_map/feed/pallas_call | solution.py:281
  389.1 5.5 collective-permute-done.43
  394.6 3.6 add_convert_fusion.10
  399.3 19.9 %weight_grads.2 = bf16[2048,1536]{1,0:T(8,128)(2,1)} custom-call(bf16[256,2048]{1,0:T(8,128)(2,1)} %copy-done.31, bf16[256,2048]{1,0:T(8,128)(2,1)} %copy-done.30, bf16[256,2048]{1,0:T(8,128)(2,1)} %copy-done.47, bf16[256,2048]{1,0:T(8,128)(2,1)} %copy-done.46, bf16[256,2048]{1,0:T(8,128)(2,1)} %copy-done.49, bf16[256,2048]{1,0:T(8,128)(2,1)} %copy-done.48, ...), custom_call_target="tpu_custom_call" | custom-call | flops 12884901888 | bytes 14680064 | tf_op jit(solution)/shard_map/weight_grads/pallas_call | solution.py:341
  419.2 4.5 collective-permute-done.46
  424.0 3.3 convert_add_fusion.5
  429.6 7.9 %feed_out.2 = (bf16[512,2048]{1,0:T(8,128)(2,1)}, bf16[512,2048]{1,0:T(8,128)(2,1)}) custom-call(bf16[1024,512]{1,0:T(8,128)(2,1)} %get-tuple-element.148.refs_19_.hidden_ref, bf16[2048,1536]{1,0:T(8,128)(2,1)} %assemble.3.refs_8_.w_ref), custom_call_target="tpu_custom_call" | custom-call | flops 2147483648 | bytes 4194304 | tf_op jit(solution)/shard_map/feed_out/pallas_call | solution.py:302
  437.5 2.8 collective-permute-done.45
  442.6 7.9 %feed_out.3 = (bf16[512,2048]{1,0:T(8,128)(2,1)}, bf16[512,2048]{1,0:T(8,128)(2,1)}) custom-call(bf16[1024,512]{1,0:T(8,128)(2,1)} %get-tuple-element.153.refs_18_.hidden_ref, bf16[2048,1536]{1,0:T(8,128)(2,1)} %assemble.3.refs_8_.w_ref), custom_call_target="tpu_custom_call" | custom-call | flops 2147483648 | bytes 4194304 | tf_op jit(solution)/shard_map/feed_out/pallas_call | solution.py:302
  450.7 3.8 collective-permute-done.49
  456.1 2.7 fusion.16
  459.1 22.1 %collective-permute-done.50 = bf16[128,2048]{1,0:T(8,128)(2,1)S(1)} collective-permute-done((bf16[128,2048]{1,0:T(8,128)(2,1)S(1)}, bf16[128,2048]{1,0:T(8,128)(2,1)S(1)}, u32[]{:S(2)}, u32[]{:S(2)}) %collective-permute-start.50) | collective-permute-done | bytes 524320 | tf_op jit(solution)/shard_map/ppermute | solution.py:54
  482.6 10.5 %collective-permute-done.52 = bf16[128,2048]{1,0:T(8,128)(2,1)S(1)} collective-permute-done((bf16[128,2048]{1,0:T(8,128)(2,1)S(1)}, bf16[128,2048]{1,0:T(8,128)(2,1)S(1)}, u32[]{:S(2)}, u32[]{:S(2)}) %collective-permute-start.52) | collective-permute-done | bytes 524320 | tf_op jit(solution)/shard_map/ppermute | solution.py:54
  493.5 3.3 collective-permute-start.55
  496.9 17.2 %collective-permute-done.56.refs_5_.refs_15_ = bf16[256,2048]{1,0:T(8,128)(2,1)} collective-permute-done((bf16[256,2048]{1,0:T(8,128)(2,1)S(1)}, bf16[256,2048]{1,0:T(8,128)(2,1)}, u32[]{:S(2)}, u32[]{:S(2)}) %collective-permute-start.56) | collective-permute-done | bytes 1048608 | tf_op jit(solution)/shard_map/ppermute | solution.py:54
  521.4 2.6 collective-permute-done.53.refs_2_.refs_12_
  526.1 7.2 back_project.1.do_ref
  533.3 3.8 add_convert_fusion.7
  537.1 18.8 %attend_back.1 = (f32[2048,128]{1,0:T(8,128)}, f32[2048,128]{1,0:T(8,128)}, f32[2048,128]{1,0:T(8,128)}) custom-call(bf16[2048,128]{1,0:T(8,128)(2,1)} %get-tuple-element.120.q_ref, bf16[2048,128]{1,0:T(8,128)(2,1)} %back_project.1.do_ref, f32[2048,1]{1,0:T(8,128)} %copy.35.lse_ref, s32[2048,1]{1,0:T(8,128)} %copy.31.pq_ref, ...), custom_call_target="tpu_custom_call" | custom-call | flops 5368709120 | bytes 4194304 | tf_op jit(solution)/shard_map/attend_back/pallas_call | solution.py:400
  555.9 7.8 %back_input.2 = (bf16[1024,384]{1,0:T(8,128)(2,1)}, bf16[512,2048]{1,0:T(8,128)(2,1)}, bf16[512,2048]{1,0:T(8,128)(2,1)}) custom-call(f32[2048,128]{1,0:T(8,128)} %get-tuple-element.165.dq_ref, f32[2048,128]{1,0:T(8,128)} %get-tuple-element.166.dk_ref, f32[2048,128]{1,0:T(8,128)} %get-tuple-element.167.dv_ref, f32[2048,256]{1,0:T(8,128)} %pad_maximum_fusion.refs_9_.t_ref, ...), custom_call_target="tpu_custom_call" | custom-call | flops 1610612736 | bytes 4194304 | tf_op jit(solution)/shard_map/back_input/pallas_call | solution.py:426
  566.0 7.7 %back_input.3 = (bf16[1024,384]{1,0:T(8,128)(2,1)}, bf16[512,2048]{1,0:T(8,128)(2,1)}, bf16[512,2048]{1,0:T(8,128)(2,1)}) custom-call(f32[2048,128]{1,0:T(8,128)} %get-tuple-element.165.dq_ref, f32[2048,128]{1,0:T(8,128)} %get-tuple-element.166.dk_ref, f32[2048,128]{1,0:T(8,128)} %get-tuple-element.167.dv_ref, f32[2048,256]{1,0:T(8,128)} %pad_maximum_fusion.refs_9_.t_ref, ...), custom_call_target="tpu_custom_call" | custom-call | flops 1610612736 | bytes 4194304 | tf_op jit(solution)/shard_map/back_input/pallas_call | solution.py:426
  578.0 12.3 %collective-permute-done.60 = bf16[256,2048]{1,0:T(8,128)(2,1)} collective-permute-done((bf16[256,2048]{1,0:T(8,128)(2,1)}, bf16[256,2048]{1,0:T(8,128)(2,1)}, u32[]{:S(2)}, u32[]{:S(2)}) %collective-permute-start.60) | collective-permute-done | bytes 1048608 | tf_op jit(solution)/shard_map/ppermute | solution.py:54
  592.2 2.6 convert_add_fusion.3
  598.6 13.6 %weight_grads.3 = bf16[2048,512]{1,0:T(8,128)(2,1)} custom-call(bf16[256,2048]{1,0:T(8,128)(2,1)} %copy-done.1, bf16[256,2048]{1,0:T(8,128)(2,1)} %copy-done, bf16[256,2048]{1,0:T(8,128)(2,1)} %collective-permute-done.8.refs_2_, bf16[256,2048]{1,0:T(8,128)(2,1)} %collective-permute-done.9.refs_3_, bf16[256,2048]{1,0:T(8,128)(2,1)} %collective-permute-done.10.refs_4_, ...), custom_call_target="tpu_custom_call" | custom-call | flops 4294967296 | bytes 10485760 | tf_op jit(solution)/shard_map/weight_grads/pallas_call | solution.py:341
  612.3 12.5 %collective-permute-done.61 = bf16[128,2048]{1,0:T(8,128)(2,1)} collective-permute-done((bf16[128,2048]{1,0:T(8,128)(2,1)}, bf16[128,2048]{1,0:T(8,128)(2,1)}, u32[]{:S(2)}, u32[]{:S(2)}) %collective-permute-start.61) | collective-permute-done | bytes 524320 | tf_op jit(solution)/shard_map/ppermute | solution.py:54
  627.3 3.3 convert_add_fusion.1
  637.5 2.7 collective-permute-start.64
  640.3 4.4 collective-permute-done.69
  650.2 2.9 collective-permute-start.72
  653.1 10.9 %collective-permute-done.64 = bf16[128,2048]{1,0:T(8,128)(2,1)} collective-permute-done((bf16[128,2048]{1,0:T(8,128)(2,1)}, bf16[128,2048]{1,0:T(8,128)(2,1)}, u32[]{:S(2)}, u32[]{:S(2)}) %collective-permute-start.64) | collective-permute-done | bytes 524320 | tf_op jit(solution)/shard_map/ppermute | solution.py:54
  665.4 21.1 %collective-permute-done.72 = bf16[128,2048]{1,0:T(8,128)(2,1)} collective-permute-done((bf16[128,2048]{1,0:T(8,128)(2,1)}, bf16[128,2048]{1,0:T(8,128)(2,1)}, u32[]{:S(2)}, u32[]{:S(2)}) %collective-permute-start.72) | collective-permute-done | bytes 524320 | tf_op jit(solution)/shard_map/ppermute | solution.py:54
  695.2 7.6 %collective-permute-done.65 = bf16[64,2048]{1,0:T(8,128)(2,1)S(1)} collective-permute-done((bf16[64,2048]{1,0:T(8,128)(2,1)S(1)}, bf16[64,2048]{1,0:T(8,128)(2,1)S(1)}, u32[]{:S(2)}, u32[]{:S(2)}) %collective-permute-start.65) | collective-permute-done | bytes 262176 | tf_op jit(solution)/shard_map/ppermute | solution.py:54
  702.8 9.5 %collective-permute-done.73 = bf16[64,2048]{1,0:T(8,128)(2,1)S(1)} collective-permute-done((bf16[64,2048]{1,0:T(8,128)(2,1)S(1)}, bf16[64,2048]{1,0:T(8,128)(2,1)S(1)}, u32[]{:S(2)}, u32[]{:S(2)}) %collective-permute-start.73) | collective-permute-done | bytes 262176 | tf_op jit(solution)/shard_map/ppermute | solution.py:54
  721.0 6.2 collective-permute-done.78.refs_2_
  727.2 15.9 %collective-permute-done.79.refs_3_ = bf16[256,1536]{1,0:T(8,128)(2,1)} collective-permute-done((bf16[256,1536]{1,0:T(8,128)(2,1)S(1)}, bf16[256,1536]{1,0:T(8,128)(2,1)}, u32[]{:S(2)}, u32[]{:S(2)}) %collective-permute-start.79) | collective-permute-done | bytes 786464 | tf_op jit(solution)/shard_map/ppermute | solution.py:54
  743.1 5.0 unpack.3
  749.3 2.6 unpack.2
  (350 shorter events, 141.1 us)
Async XLA Ops:
  7.2 82.0 %all-gather.6.cloned.1.call-start = ((), (), s32[]{:S(2)}) async-start(), calls=%async_computation.2 | async-start | bytes 2359296 | tf_op jit(solution)/shard_map/all_gather | solution.py:576
  8.3 16.9 %collective-permute-start = (bf16[64,2048]{1,0:T(8,128)(2,1)S(1)}, bf16[64,2048]{1,0:T(8,128)(2,1)S(1)}, u32[]{:S(2)}, u32[]{:S(2)}) collective-permute-start(bf16[64,2048]{1,0:T(8,128)(2,1)S(1)} %get-tuple-element.251), channel_id=1, source_target_pairs={{0,16},{1,17},{2,18},{3,19},{4,20},{5,21},{6,22},{7,23},{8,24},{9,... | collective-permute-start | bytes 786440 | tf_op jit(solution)/shard_map/ppermute | solution.py:54
  26.0 37.2 %collective-permute-start.1 = (bf16[128,2048]{1,0:T(8,128)(2,1)S(1)}, bf16[128,2048]{1,0:T(8,128)(2,1)S(1)}, u32[]{:S(2)}, u32[]{:S(2)}) collective-permute-start(bf16[128,2048]{1,0:T(8,128)(2,1)S(1)} %fusion.4), channel_id=1, source_target_pairs={{0,8},{1,9},{2,10},{3,11},{4,12},{5,13},{6,14},{7,15},{8,0},{9,1},... | collective-permute-start | bytes 1572872 | tf_op jit(solution)/shard_map/ppermute | solution.py:54
  29.1 22.1 %collective-permute-start.3 = (bf16[256,512]{1,0:T(8,128)(2,1)}, bf16[256,512]{1,0:T(8,128)(2,1)S(1)}, u32[]{:S(2)}, u32[]{:S(2)}) collective-permute-start(bf16[256,512]{1,0:T(8,128)(2,1)} %get-tuple-element.102), channel_id=1, source_target_pairs={{0,8},{1,9},{2,10},{3,11},{4,12},{5,13},{6,14},{7,15},{8,0},{9,1},... | collective-permute-start | bytes 786440 | tf_op jit(solution)/shard_map/ppermute | solution.py:54
  29.6 33.6 %collective-permute-start.4 = (bf16[256,512]{1,0:T(8,128)(2,1)}, bf16[256,512]{1,0:T(8,128)(2,1)}, u32[]{:S(2)}, u32[]{:S(2)}) collective-permute-start(bf16[256,512]{1,0:T(8,128)(2,1)} %get-tuple-element.103), channel_id=1, source_target_pairs={{0,12},{1,13},{2,14},{3,15},{4,8},{5,9},{6,10},{7,11},{8,4},{9,5},... | collective-permute-start | bytes 786440 | tf_op jit(solution)/shard_map/ppermute | solution.py:54
  31.1 53.3 %collective-permute-start.6 = (bf16[256,1536]{1,0:T(8,128)(2,1)}, bf16[256,1536]{1,0:T(8,128)(2,1)S(1)}, u32[]{:S(2)}, u32[]{:S(2)}) collective-permute-start(bf16[256,1536]{1,0:T(8,128)(2,1)} %get-tuple-element.106), channel_id=1, source_target_pairs={{0,8},{1,9},{2,10},{3,11},{4,12},{5,13},{6,14},{7,15},{8,0},{9,1},... | collective-permute-start | bytes 2359304 | tf_op jit(solution)/shard_map/ppermute | solution.py:54
  31.6 114.5 %all-gather.8.cloned.1.call-start = ((), (), s32[]{:S(2)}) async-start(), calls=%async_computation.3 | async-start | bytes 3145728 | tf_op jit(solution)/shard_map/all_gather | solution.py:576
  63.3 21.1 %collective-permute-start.7 = (bf16[128,2048]{1,0:T(8,128)(2,1)S(1)}, bf16[128,2048]{1,0:T(8,128)(2,1)}, u32[]{:S(2)}, u32[]{:S(2)}) collective-permute-start(bf16[128,2048]{1,0:T(8,128)(2,1)S(1)} %pad_maximum_fusion.15), channel_id=1, source_target_pairs={{0,2},{1,3},{2,0},{3,1},{4,6},{5,7},{6,4},{7,5},{8,10},{9,11},{10,... | collective-permute-start | bytes 1572872 | tf_op jit(solution)/shard_map/ppermute | solution.py:54
  65.0 20.3 %collective-permute-start.5 = (bf16[128,2048]{1,0:T(8,128)(2,1)S(1)}, bf16[128,2048]{1,0:T(8,128)(2,1)}, u32[]{:S(2)}, u32[]{:S(2)}) collective-permute-start(bf16[128,2048]{1,0:T(8,128)(2,1)S(1)} %pad_maximum_fusion.14), channel_id=1, source_target_pairs={{0,4},{1,5},{2,6},{3,7},{4,0},{5,1},{6,2},{7,3},{8,12},{9,13},{10,... | collective-permute-start | bytes 1572872 | tf_op jit(solution)/shard_map/ppermute | solution.py:54
  86.5 57.6 %collective-permute-start.13 = (bf16[256,2048]{1,0:T(8,128)(2,1)S(1)}, bf16[256,2048]{1,0:T(8,128)(2,1)S(1)}, u32[]{:S(2)}, u32[]{:S(2)}) collective-permute-start(bf16[256,2048]{1,0:T(8,128)(2,1)S(1)} %pad_maximum_fusion.2.refs_1_), channel_id=1, source_target_pairs={{0,4},{1,5},{2,6},{3,7},{4,0},{5,1},{6,2},{7,3},{8,12},{9,13},{10,... | collective-permute-start | bytes 3145736 | tf_op jit(solution)/shard_map/ppermute | solution.py:54
  89.2 153.9 %all-gather.10.cloned.1.call-start = ((), (), s32[]{:S(2)}) async-start(), calls=%async_computation.4 | async-start | bytes 2359296 | tf_op jit(solution)/shard_map/all_gather | solution.py:576
  89.8 54.9 %collective-permute-start.10 = (bf16[256,2048]{1,0:T(8,128)(2,1)S(1)}, bf16[256,2048]{1,0:T(8,128)(2,1)}, u32[]{:S(2)}, u32[]{:S(2)}) collective-permute-start(bf16[256,2048]{1,0:T(8,128)(2,1)S(1)} %pad_maximum_fusion.1.refs_0_), channel_id=1, source_target_pairs={{0,2},{1,3},{2,0},{3,1},{4,6},{5,7},{6,4},{7,5},{8,10},{9,11},{10,... | collective-permute-start | bytes 3145736 | tf_op jit(solution)/shard_map/ppermute | solution.py:54
  91.3 52.7 %collective-permute-start.11 = (bf16[256,1536]{1,0:T(8,128)(2,1)}, bf16[256,1536]{1,0:T(8,128)(2,1)}, u32[]{:S(2)}, u32[]{:S(2)}) collective-permute-start(bf16[256,1536]{1,0:T(8,128)(2,1)} %get-tuple-element.105), channel_id=1, source_target_pairs={{0,4},{1,5},{2,6},{3,7},{4,0},{5,1},{6,2},{7,3},{8,12},{9,13},{10,... | collective-permute-start | bytes 2359304 | tf_op jit(solution)/shard_map/ppermute | solution.py:54
  91.9 52.2 %collective-permute-start.12 = (bf16[256,1536]{1,0:T(8,128)(2,1)}, bf16[256,1536]{1,0:T(8,128)(2,1)}, u32[]{:S(2)}, u32[]{:S(2)}) collective-permute-start(bf16[256,1536]{1,0:T(8,128)(2,1)} %get-tuple-element.107), channel_id=1, source_target_pairs={{0,12},{1,13},{2,14},{3,15},{4,8},{5,9},{6,10},{7,11},{8,4},{9,5},... | collective-permute-start | bytes 2359304 | tf_op jit(solution)/shard_map/ppermute | solution.py:54
  94.4 54.8 %collective-permute-start.9 = (bf16[256,2048]{1,0:T(8,128)(2,1)S(1)}, bf16[256,2048]{1,0:T(8,128)(2,1)}, u32[]{:S(2)}, u32[]{:S(2)}) collective-permute-start(bf16[256,2048]{1,0:T(8,128)(2,1)S(1)} %pad_maximum_fusion.2.refs_1_), channel_id=1, source_target_pairs={{0,1},{1,0},{2,3},{3,2},{4,5},{5,4},{6,7},{7,6},{8,9},{9,8},{10,11... | collective-permute-start | bytes 3145736 | tf_op jit(solution)/shard_map/ppermute | solution.py:54
  170.8 105.3 %all-gather.12.cloned.1.call-start = ((), (), s32[]{:S(2)}) async-start(), calls=%async_computation.5 | async-start | bytes 2359296 | tf_op jit(solution)/shard_map/all_gather | solution.py:576
  189.3 57.7 %collective-permute-start.17 = (bf16[512,2048]{1,0:T(8,128)(2,1)}, bf16[512,2048]{1,0:T(8,128)(2,1)}, u32[]{:S(2)}, u32[]{:S(2)}) collective-permute-start(bf16[512,2048]{1,0:T(8,128)(2,1)} %get-tuple-element.122), channel_id=1, source_target_pairs={{0,1},{1,0},{2,3},{3,2},{4,5},{5,4},{6,7},{7,6},{8,9},{9,8},{10,11... | collective-permute-start | bytes 6291464 | tf_op jit(solution)/shard_map/ppermute | solution.py:54
  189.5 28.6 %collective-permute-start.24 = (bf16[64,2048]{1,0:T(8,128)(2,1)S(1)}, bf16[64,2048]{1,0:T(8,128)(2,1)S(1)}, u32[]{:S(2)}, u32[]{:S(2)}) collective-permute-start(bf16[64,2048]{1,0:T(8,128)(2,1)S(1)} %get-tuple-element.245), channel_id=1, source_target_pairs={{0,16},{1,17},{2,18},{3,19},{4,20},{5,21},{6,22},{7,23},{8,24},{9,... | collective-permute-start | bytes 786440 | tf_op jit(solution)/shard_map/ppermute | solution.py:54
  219.0 20.7 %collective-permute-start.25 = (bf16[128,2048]{1,0:T(8,128)(2,1)}, bf16[128,2048]{1,0:T(8,128)(2,1)}, u32[]{:S(2)}, u32[]{:S(2)}) collective-permute-start(bf16[128,2048]{1,0:T(8,128)(2,1)} %pad_maximum_fusion.17), channel_id=1, source_target_pairs={{0,8},{1,9},{2,10},{3,11},{4,12},{5,13},{6,14},{7,15},{8,0},{9,1},... | collective-permute-start | bytes 1572872 | tf_op jit(solution)/shard_map/ppermute | solution.py:54
  219.0 112.9 %all-gather.14.cloned.1.call-start = ((), (), s32[]{:S(2)}) async-start(), calls=%async_computation.6 | async-start | bytes 2359296 | tf_op jit(solution)/shard_map/all_gather | solution.py:576
  219.1 25.7 %collective-permute-start.20 = (bf16[256,2048]{1,0:T(8,128)(2,1)}, bf16[256,2048]{1,0:T(8,128)(2,1)}, u32[]{:S(2)}, u32[]{:S(2)}) collective-permute-start(bf16[256,2048]{1,0:T(8,128)(2,1)} %get-tuple-element.215), channel_id=1, source_target_pairs={{0,4},{1,5},{2,6},{3,7},{4,0},{5,1},{6,2},{7,3},{8,12},{9,13},{10,... | collective-permute-start | bytes 3145736 | tf_op jit(solution)/shard_map/ppermute | solution.py:54
  220.6 26.3 %collective-permute-start.18 = (bf16[256,2048]{1,0:T(8,128)(2,1)}, bf16[256,2048]{1,0:T(8,128)(2,1)}, u32[]{:S(2)}, u32[]{:S(2)}) collective-permute-start(bf16[256,2048]{1,0:T(8,128)(2,1)} %get-tuple-element.214), channel_id=1, source_target_pairs={{0,2},{1,3},{2,0},{3,1},{4,6},{5,7},{6,4},{7,5},{8,10},{9,11},{10,... | collective-permute-start | bytes 3145736 | tf_op jit(solution)/shard_map/ppermute | solution.py:54
  241.6 28.8 %collective-permute-start.28 = (bf16[128,2048]{1,0:T(8,128)(2,1)}, bf16[128,2048]{1,0:T(8,128)(2,1)}, u32[]{:S(2)}, u32[]{:S(2)}) collective-permute-start(bf16[128,2048]{1,0:T(8,128)(2,1)} %pad_maximum_fusion.19), channel_id=1, source_target_pairs={{0,2},{1,3},{2,0},{3,1},{4,6},{5,7},{6,4},{7,5},{8,10},{9,11},{10,... | collective-permute-start | bytes 1572872 | tf_op jit(solution)/shard_map/ppermute | solution.py:54
  250.3 14.9 %collective-permute-start.19 = (bf16[128,2048]{1,0:T(8,128)(2,1)S(1)}, bf16[128,2048]{1,0:T(8,128)(2,1)S(1)}, u32[]{:S(2)}, u32[]{:S(2)}) collective-permute-start(bf16[128,2048]{1,0:T(8,128)(2,1)S(1)} %fusion.19), channel_id=1, source_target_pairs={{0,4},{1,5},{2,6},{3,7},{4,0},{5,1},{6,2},{7,3},{8,12},{9,13},{10,... | collective-permute-start | bytes 1572872 | tf_op jit(solution)/shard_map/ppermute | solution.py:54
  250.5 17.8 %collective-permute-start.21 = (bf16[128,2048]{1,0:T(8,128)(2,1)S(1)}, bf16[128,2048]{1,0:T(8,128)(2,1)S(1)}, u32[]{:S(2)}, u32[]{:S(2)}) collective-permute-start(bf16[128,2048]{1,0:T(8,128)(2,1)S(1)} %fusion.18), channel_id=1, source_target_pairs={{0,2},{1,3},{2,0},{3,1},{4,6},{5,7},{6,4},{7,5},{8,10},{9,11},{10,... | collective-permute-start | bytes 1572872 | tf_op jit(solution)/shard_map/ppermute | solution.py:54
  252.0 21.5 %collective-permute-start.26 = (bf16[128,2048]{1,0:T(8,128)(2,1)S(1)}, bf16[128,2048]{1,0:T(8,128)(2,1)S(1)}, u32[]{:S(2)}, u32[]{:S(2)}) collective-permute-start(bf16[128,2048]{1,0:T(8,128)(2,1)S(1)} %pad_maximum_fusion.18), channel_id=1, source_target_pairs={{0,4},{1,5},{2,6},{3,7},{4,0},{5,1},{6,2},{7,3},{8,12},{9,13},{10,... | collective-permute-start | bytes 1572872 | tf_op jit(solution)/shard_map/ppermute | solution.py:54
  268.5 16.7 %collective-permute-start.22 = (bf16[128,2048]{1,0:T(8,128)(2,1)S(1)}, bf16[128,2048]{1,0:T(8,128)(2,1)}, u32[]{:S(2)}, u32[]{:S(2)}) collective-permute-start(bf16[128,2048]{1,0:T(8,128)(2,1)S(1)} %pad_maximum_fusion.16), channel_id=1, source_target_pairs={{0,8},{1,9},{2,10},{3,11},{4,12},{5,13},{6,14},{7,15},{8,0},{9,1},... | collective-permute-start | bytes 1572872 | tf_op jit(solution)/shard_map/ppermute | solution.py:54
  272.5 23.9 %collective-permute-start.29 = (bf16[256,2048]{1,0:T(8,128)(2,1)}, bf16[256,2048]{1,0:T(8,128)(2,1)}, u32[]{:S(2)}, u32[]{:S(2)}) collective-permute-start(bf16[256,2048]{1,0:T(8,128)(2,1)} %pad_maximum_fusion.5.refs_5_.refs_11_), channel_id=1, source_target_pairs={{0,4},{1,5},{2,6},{3,7},{4,0},{5,1},{6,2},{7,3},{8,12},{9,13},{10,... | collective-permute-start | bytes 3145736 | tf_op jit(solution)/shard_map/ppermute | solution.py:54
  274.6 23.1 %collective-permute-start.27 = (bf16[256,2048]{1,0:T(8,128)(2,1)}, bf16[256,2048]{1,0:T(8,128)(2,1)}, u32[]{:S(2)}, u32[]{:S(2)}) collective-permute-start(bf16[256,2048]{1,0:T(8,128)(2,1)} %pad_maximum_fusion.4.refs_4_.refs_10_), channel_id=1, source_target_pairs={{0,2},{1,3},{2,0},{3,1},{4,6},{5,7},{6,4},{7,5},{8,10},{9,11},{10,... | collective-permute-start | bytes 3145736 | tf_op jit(solution)/shard_map/ppermute | solution.py:54
  287.0 16.3 %collective-permute-start.23 = (bf16[128,2048]{1,0:T(8,128)(2,1)S(1)}, bf16[128,2048]{1,0:T(8,128)(2,1)S(1)}, u32[]{:S(2)}, u32[]{:S(2)}) collective-permute-start(bf16[128,2048]{1,0:T(8,128)(2,1)S(1)} %fusion.11), channel_id=1, source_target_pairs={{0,8},{1,9},{2,10},{3,11},{4,12},{5,13},{6,14},{7,15},{8,0},{9,1},... | collective-permute-start | bytes 1572872 | tf_op jit(solution)/shard_map/ppermute | solution.py:54
  287.1 348.4 %reduce-scatter.3.cloned.1.call-start = ((), (), s32[]{:S(2)}) async-start(), calls=%async_computation.7 | async-start | bytes 9437184 | tf_op jit(solution)/shard_map/reduce_scatter | solution.py:582
  303.5 28.4 %collective-permute-start.32 = (bf16[256,2048]{1,0:T(8,128)(2,1)}, bf16[256,2048]{1,0:T(8,128)(2,1)}, u32[]{:S(2)}, u32[]{:S(2)}) collective-permute-start(bf16[256,2048]{1,0:T(8,128)(2,1)} %collective-permute-done.29.refs_5_.refs_15_), channel_id=1, source_target_pairs={{0,1},{1,0},{2,3},{3,2},{4,5},{5,4},{6,7},{7,6},{8,9},{9,8},{10,11... | collective-permute-start | bytes 3145736 | tf_op jit(solution)/shard_map/ppermute | solution.py:54
  303.5 28.4 %collective-permute-start.31 = (bf16[256,2048]{1,0:T(8,128)(2,1)}, bf16[256,2048]{1,0:T(8,128)(2,1)}, u32[]{:S(2)}, u32[]{:S(2)}) collective-permute-start(bf16[256,2048]{1,0:T(8,128)(2,1)} %collective-permute-done.27.refs_4_.refs_14_), channel_id=1, source_target_pairs={{0,1},{1,0},{2,3},{3,2},{4,5},{5,4},{6,7},{7,6},{8,9},{9,8},{10,11... | collective-permute-start | bytes 3145736 | tf_op jit(solution)/shard_map/ppermute | solution.py:54
  305.7 27.4 %collective-permute-start.30 = (bf16[128,2048]{1,0:T(8,128)(2,1)S(1)}, bf16[128,2048]{1,0:T(8,128)(2,1)S(1)}, u32[]{:S(2)}, u32[]{:S(2)}) collective-permute-start(bf16[128,2048]{1,0:T(8,128)(2,1)S(1)} %pad_maximum_fusion.20), channel_id=1, source_target_pairs={{0,4},{1,5},{2,6},{3,7},{4,0},{5,1},{6,2},{7,3},{8,12},{9,13},{10,... | collective-permute-start | bytes 1572872 | tf_op jit(solution)/shard_map/ppermute | solution.py:54
  307.2 28.0 %collective-permute-start.37 = (bf16[256,2048]{1,0:T(8,128)(2,1)}, bf16[256,2048]{1,0:T(8,128)(2,1)}, u32[]{:S(2)}, u32[]{:S(2)}) collective-permute-start(bf16[256,2048]{1,0:T(8,128)(2,1)} %pad_maximum_fusion.5.refs_5_.refs_11_), channel_id=1, source_target_pairs={{0,1},{1,0},{2,3},{3,2},{4,5},{5,4},{6,7},{7,6},{8,9},{9,8},{10,11... | collective-permute-start | bytes 3145736 | tf_op jit(solution)/shard_map/ppermute | solution.py:54
  318.7 23.9 %collective-permute-start.36 = (bf16[256,2048]{1,0:T(8,128)(2,1)}, bf16[256,2048]{1,0:T(8,128)(2,1)}, u32[]{:S(2)}, u32[]{:S(2)}) collective-permute-start(bf16[256,2048]{1,0:T(8,128)(2,1)} %pad_maximum_fusion.4.refs_4_.refs_10_), channel_id=1, source_target_pairs={{0,1},{1,0},{2,3},{3,2},{4,5},{5,4},{6,7},{7,6},{8,9},{9,8},{10,11... | collective-permute-start | bytes 3145736 | tf_op jit(solution)/shard_map/ppermute | solution.py:54
  333.8 30.2 %collective-permute-start.40 = (bf16[256,2048]{1,0:T(8,128)(2,1)S(1)}, bf16[256,2048]{1,0:T(8,128)(2,1)S(1)}, u32[]{:S(2)}, u32[]{:S(2)}) collective-permute-start(bf16[256,2048]{1,0:T(8,128)(2,1)S(1)} %pad_maximum_fusion.7.refs_1_), channel_id=1, source_target_pairs={{0,4},{1,5},{2,6},{3,7},{4,0},{5,1},{6,2},{7,3},{8,12},{9,13},{10,... | collective-permute-start | bytes 3145736 | tf_op jit(solution)/shard_map/ppermute | solution.py:54
  335.2 28.8 %collective-permute-start.39 = (bf16[256,2048]{1,0:T(8,128)(2,1)S(1)}, bf16[256,2048]{1,0:T(8,128)(2,1)S(1)}, u32[]{:S(2)}, u32[]{:S(2)}) collective-permute-start(bf16[256,2048]{1,0:T(8,128)(2,1)S(1)} %pad_maximum_fusion.6.refs_0_), channel_id=1, source_target_pairs={{0,2},{1,3},{2,0},{3,1},{4,6},{5,7},{6,4},{7,5},{8,10},{9,11},{10,... | collective-permute-start | bytes 3145736 | tf_op jit(solution)/shard_map/ppermute | solution.py:54
  388.7 35.3 %collective-permute-start.38 = (bf16[512,2048]{1,0:T(8,128)(2,1)}, bf16[512,2048]{1,0:T(8,128)(2,1)}, u32[]{:S(2)}, u32[]{:S(2)}) collective-permute-start(bf16[512,2048]{1,0:T(8,128)(2,1)} %get-tuple-element.137), channel_id=1, source_target_pairs={{0,1},{1,0},{2,3},{3,2},{4,5},{5,4},{6,7},{7,6},{8,9},{9,8},{10,11... | collective-permute-start | bytes 6291464 | tf_op jit(solution)/shard_map/ppermute | solution.py:54
  398.2 25.5 %collective-permute-start.46 = (bf16[256,2048]{1,0:T(8,128)(2,1)}, bf16[256,2048]{1,0:T(8,128)(2,1)}, u32[]{:S(2)}, u32[]{:S(2)}) collective-permute-start(bf16[256,2048]{1,0:T(8,128)(2,1)} %get-tuple-element.211), channel_id=1, source_target_pairs={{0,4},{1,5},{2,6},{3,7},{4,0},{5,1},{6,2},{7,3},{8,12},{9,13},{10,... | collective-permute-start | bytes 3145736 | tf_op jit(solution)/shard_map/ppermute | solution.py:54
  398.7 25.2 %collective-permute-start.44 = (bf16[256,2048]{1,0:T(8,128)(2,1)}, bf16[256,2048]{1,0:T(8,128)(2,1)}, u32[]{:S(2)}, u32[]{:S(2)}) collective-permute-start(bf16[256,2048]{1,0:T(8,128)(2,1)} %get-tuple-element.210), channel_id=1, source_target_pairs={{0,2},{1,3},{2,0},{3,1},{4,6},{5,7},{6,4},{7,5},{8,10},{9,11},{10,... | collective-permute-start | bytes 3145736 | tf_op jit(solution)/shard_map/ppermute | solution.py:54
  450.5 263.3 %reduce-scatter.5.cloned.1.call-start = ((), (), s32[]{:S(2)}) async-start(), calls=%async_computation.8 | async-start | bytes 3145728 | tf_op jit(solution)/shard_map/reduce_scatter | solution.py:582
  458.8 22.5 %collective-permute-start.50 = (bf16[128,2048]{1,0:T(8,128)(2,1)S(1)}, bf16[128,2048]{1,0:T(8,128)(2,1)S(1)}, u32[]{:S(2)}, u32[]{:S(2)}) collective-permute-start(bf16[128,2048]{1,0:T(8,128)(2,1)S(1)} %get-tuple-element.196), channel_id=1, source_target_pairs={{0,8},{1,9},{2,10},{3,11},{4,12},{5,13},{6,14},{7,15},{8,0},{9,1},... | collective-permute-start | bytes 1572872 | tf_op jit(solution)/shard_map/ppermute | solution.py:54
  493.1 20.9 %collective-permute-start.56 = (bf16[256,2048]{1,0:T(8,128)(2,1)S(1)}, bf16[256,2048]{1,0:T(8,128)(2,1)}, u32[]{:S(2)}, u32[]{:S(2)}) collective-permute-start(bf16[256,2048]{1,0:T(8,128)(2,1)S(1)} %pad_maximum_fusion.10.refs_1_.refs_11_), channel_id=1, source_target_pairs={{0,4},{1,5},{2,6},{3,7},{4,0},{5,1},{6,2},{7,3},{8,12},{9,13},{10,... | collective-permute-start | bytes 3145736 | tf_op jit(solution)/shard_map/ppermute | solution.py:54
  493.5 20.5 %collective-permute-start.55 = (bf16[256,2048]{1,0:T(8,128)(2,1)S(1)}, bf16[256,2048]{1,0:T(8,128)(2,1)}, u32[]{:S(2)}, u32[]{:S(2)}) collective-permute-start(bf16[256,2048]{1,0:T(8,128)(2,1)S(1)} %pad_maximum_fusion.9.refs_0_.refs_10_), channel_id=1, source_target_pairs={{0,2},{1,3},{2,0},{3,1},{4,6},{5,7},{6,4},{7,5},{8,10},{9,11},{10,... | collective-permute-start | bytes 3145736 | tf_op jit(solution)/shard_map/ppermute | solution.py:54
  514.1 19.2 %collective-permute-start.59 = (bf16[512,2048]{1,0:T(8,128)(2,1)}, bf16[512,2048]{1,0:T(8,128)(2,1)}, u32[]{:S(2)}, u32[]{:S(2)}) collective-permute-start(bf16[512,2048]{1,0:T(8,128)(2,1)} %get-tuple-element.158), channel_id=1, source_target_pairs={{0,1},{1,0},{2,3},{3,2},{4,5},{5,4},{6,7},{7,6},{8,9},{9,8},{10,11... | collective-permute-start | bytes 6291464 | tf_op jit(solution)/shard_map/ppermute | solution.py:54
  521.0 52.7 %collective-permute-start.48 = (bf16[512,2048]{1,0:T(8,128)(2,1)}, bf16[512,2048]{1,0:T(8,128)(2,1)S(1)}, u32[]{:S(2)}, u32[]{:S(2)}) collective-permute-start(bf16[512,2048]{1,0:T(8,128)(2,1)} %get-tuple-element.155), channel_id=1, source_target_pairs={{0,1},{1,0},{2,3},{3,2},{4,5},{5,4},{6,7},{7,6},{8,9},{9,8},{10,11... | collective-permute-start | bytes 6291464 | tf_op jit(solution)/shard_map/ppermute | solution.py:54
  564.0 26.3 %collective-permute-start.60 = (bf16[256,2048]{1,0:T(8,128)(2,1)}, bf16[256,2048]{1,0:T(8,128)(2,1)}, u32[]{:S(2)}, u32[]{:S(2)}) collective-permute-start(bf16[256,2048]{1,0:T(8,128)(2,1)} %get-tuple-element.206), channel_id=1, source_target_pairs={{0,2},{1,3},{2,0},{3,1},{4,6},{5,7},{6,4},{7,5},{8,10},{9,11},{10,... | collective-permute-start | bytes 3145736 | tf_op jit(solution)/shard_map/ppermute | solution.py:54
  565.8 26.4 %collective-permute-start.62 = (bf16[256,2048]{1,0:T(8,128)(2,1)}, bf16[256,2048]{1,0:T(8,128)(2,1)}, u32[]{:S(2)}, u32[]{:S(2)}) collective-permute-start(bf16[256,2048]{1,0:T(8,128)(2,1)} %get-tuple-element.207), channel_id=1, source_target_pairs={{0,4},{1,5},{2,6},{3,7},{4,0},{5,1},{6,2},{7,3},{8,12},{9,13},{10,... | collective-permute-start | bytes 3145736 | tf_op jit(solution)/shard_map/ppermute | solution.py:54
  573.7 53.4 %collective-permute-start.66 = (bf16[512,2048]{1,0:T(8,128)(2,1)}, bf16[512,2048]{1,0:T(8,128)(2,1)}, u32[]{:S(2)}, u32[]{:S(2)}) collective-permute-start(bf16[512,2048]{1,0:T(8,128)(2,1)} %get-tuple-element.175), channel_id=1, source_target_pairs={{0,1},{1,0},{2,3},{3,2},{4,5},{5,4},{6,7},{7,6},{8,9},{9,8},{10,11... | collective-permute-start | bytes 6291464 | tf_op jit(solution)/shard_map/ppermute | solution.py:54
  575.9 51.3 %collective-permute-start.68 = (bf16[256,2048]{1,0:T(8,128)(2,1)}, bf16[256,2048]{1,0:T(8,128)(2,1)}, u32[]{:S(2)}, u32[]{:S(2)}) collective-permute-start(bf16[256,2048]{1,0:T(8,128)(2,1)} %get-tuple-element.202), channel_id=1, source_target_pairs={{0,2},{1,3},{2,0},{3,1},{4,6},{5,7},{6,4},{7,5},{8,10},{9,11},{10,... | collective-permute-start | bytes 3145736 | tf_op jit(solution)/shard_map/ppermute | solution.py:54
  576.6 50.6 %collective-permute-start.70 = (bf16[256,2048]{1,0:T(8,128)(2,1)}, bf16[256,2048]{1,0:T(8,128)(2,1)}, u32[]{:S(2)}, u32[]{:S(2)}) collective-permute-start(bf16[256,2048]{1,0:T(8,128)(2,1)} %get-tuple-element.203), channel_id=1, source_target_pairs={{0,4},{1,5},{2,6},{3,7},{4,0},{5,1},{6,2},{7,3},{8,12},{9,13},{10,... | collective-permute-start | bytes 3145736 | tf_op jit(solution)/shard_map/ppermute | solution.py:54
  597.0 27.8 %collective-permute-start.61 = (bf16[128,2048]{1,0:T(8,128)(2,1)}, bf16[128,2048]{1,0:T(8,128)(2,1)}, u32[]{:S(2)}, u32[]{:S(2)}) collective-permute-start(bf16[128,2048]{1,0:T(8,128)(2,1)} %slice.497), channel_id=1, source_target_pairs={{0,4},{1,5},{2,6},{3,7},{4,0},{5,1},{6,2},{7,3},{8,12},{9,13},{10,... | collective-permute-start | bytes 1572872 | tf_op jit(solution)/shard_map/ppermute | solution.py:54
  598.0 29.1 %collective-permute-start.63 = (bf16[128,2048]{1,0:T(8,128)(2,1)}, bf16[128,2048]{1,0:T(8,128)(2,1)}, u32[]{:S(2)}, u32[]{:S(2)}) collective-permute-start(bf16[128,2048]{1,0:T(8,128)(2,1)} %slice.496), channel_id=1, source_target_pairs={{0,2},{1,3},{2,0},{3,1},{4,6},{5,7},{6,4},{7,5},{8,10},{9,11},{10,... | collective-permute-start | bytes 1572872 | tf_op jit(solution)/shard_map/ppermute | solution.py:54
  637.5 26.5 %collective-permute-start.64 = (bf16[128,2048]{1,0:T(8,128)(2,1)}, bf16[128,2048]{1,0:T(8,128)(2,1)}, u32[]{:S(2)}, u32[]{:S(2)}) collective-permute-start(bf16[128,2048]{1,0:T(8,128)(2,1)} %pad_maximum_fusion.25), channel_id=1, source_target_pairs={{0,8},{1,9},{2,10},{3,11},{4,12},{5,13},{6,14},{7,15},{8,0},{9,1},... | collective-permute-start | bytes 1572872 | tf_op jit(solution)/shard_map/ppermute | solution.py:54
  650.2 36.3 %collective-permute-start.72 = (bf16[128,2048]{1,0:T(8,128)(2,1)}, bf16[128,2048]{1,0:T(8,128)(2,1)}, u32[]{:S(2)}, u32[]{:S(2)}) collective-permute-start(bf16[128,2048]{1,0:T(8,128)(2,1)} %pad_maximum_fusion.27), channel_id=1, source_target_pairs={{0,8},{1,9},{2,10},{3,11},{4,12},{5,13},{6,14},{7,15},{8,0},{9,1},... | collective-permute-start | bytes 1572872 | tf_op jit(solution)/shard_map/ppermute | solution.py:54
  665.3 37.5 %collective-permute-start.65 = (bf16[64,2048]{1,0:T(8,128)(2,1)S(1)}, bf16[64,2048]{1,0:T(8,128)(2,1)S(1)}, u32[]{:S(2)}, u32[]{:S(2)}) collective-permute-start(bf16[64,2048]{1,0:T(8,128)(2,1)S(1)} %slice.412), channel_id=1, source_target_pairs={{0,16},{1,17},{2,18},{3,19},{4,20},{5,21},{6,22},{7,23},{8,24},{9,... | collective-permute-start | bytes 786440 | tf_op jit(solution)/shard_map/ppermute | solution.py:54
  688.5 23.8 %collective-permute-start.73 = (bf16[64,2048]{1,0:T(8,128)(2,1)S(1)}, bf16[64,2048]{1,0:T(8,128)(2,1)S(1)}, u32[]{:S(2)}, u32[]{:S(2)}) collective-permute-start(bf16[64,2048]{1,0:T(8,128)(2,1)S(1)} %slice.424), channel_id=1, source_target_pairs={{0,16},{1,17},{2,18},{3,19},{4,20},{5,21},{6,22},{7,23},{8,24},{9,... | collective-permute-start | bytes 786440 | tf_op jit(solution)/shard_map/ppermute | solution.py:54
  691.3 25.9 %collective-permute-start.77 = (bf16[256,1536]{1,0:T(8,128)(2,1)}, bf16[256,1536]{1,0:T(8,128)(2,1)S(1)}, u32[]{:S(2)}, u32[]{:S(2)}) collective-permute-start(bf16[256,1536]{1,0:T(8,128)(2,1)} %get-tuple-element.218), channel_id=1, source_target_pairs={{0,4},{1,5},{2,6},{3,7},{4,0},{5,1},{6,2},{7,3},{8,12},{9,13},{10,... | collective-permute-start | bytes 2359304 | tf_op jit(solution)/shard_map/ppermute | solution.py:54
  692.1 35.1 %collective-permute-start.78 = (bf16[256,1536]{1,0:T(8,128)(2,1)}, bf16[256,1536]{1,0:T(8,128)(2,1)S(1)}, u32[]{:S(2)}, u32[]{:S(2)}) collective-permute-start(bf16[256,1536]{1,0:T(8,128)(2,1)} %get-tuple-element.217), channel_id=1, source_target_pairs={{0,8},{1,9},{2,10},{3,11},{4,12},{5,13},{6,14},{7,15},{8,0},{9,1},... | collective-permute-start | bytes 2359304 | tf_op jit(solution)/shard_map/ppermute | solution.py:54
  694.6 48.5 %collective-permute-start.79 = (bf16[256,1536]{1,0:T(8,128)(2,1)S(1)}, bf16[256,1536]{1,0:T(8,128)(2,1)}, u32[]{:S(2)}, u32[]{:S(2)}) collective-permute-start(bf16[256,1536]{1,0:T(8,128)(2,1)S(1)} %get-tuple-element.216), channel_id=1, source_target_pairs={{0,12},{1,13},{2,14},{3,15},{4,8},{5,9},{6,10},{7,11},{8,4},{9,5},... | collective-permute-start | bytes 2359304 | tf_op jit(solution)/shard_map/ppermute | solution.py:54
  715.8 32.3 %collective-permute-start.74 = (bf16[256,512]{1,0:T(8,128)(2,1)S(1)}, bf16[256,512]{1,0:T(8,128)(2,1)S(1)}, u32[]{:S(2)}, u32[]{:S(2)}) collective-permute-start(bf16[256,512]{1,0:T(8,128)(2,1)S(1)} %get-tuple-element.226), channel_id=1, source_target_pairs={{0,4},{1,5},{2,6},{3,7},{4,0},{5,1},{6,2},{7,3},{8,12},{9,13},{10,... | collective-permute-start | bytes 786440 | tf_op jit(solution)/shard_map/ppermute | solution.py:54
  717.2 30.8 %collective-permute-start.75 = (bf16[256,512]{1,0:T(8,128)(2,1)S(1)}, bf16[256,512]{1,0:T(8,128)(2,1)S(1)}, u32[]{:S(2)}, u32[]{:S(2)}) collective-permute-start(bf16[256,512]{1,0:T(8,128)(2,1)S(1)} %get-tuple-element.225), channel_id=1, source_target_pairs={{0,8},{1,9},{2,10},{3,11},{4,12},{5,13},{6,14},{7,15},{8,0},{9,1},... | collective-permute-start | bytes 786440 | tf_op jit(solution)/shard_map/ppermute | solution.py:54
  717.2 31.3 %collective-permute-start.76 = (bf16[256,512]{1,0:T(8,128)(2,1)S(1)}, bf16[256,512]{1,0:T(8,128)(2,1)S(1)}, u32[]{:S(2)}, u32[]{:S(2)}) collective-permute-start(bf16[256,512]{1,0:T(8,128)(2,1)S(1)} %get-tuple-element.224), channel_id=1, source_target_pairs={{0,12},{1,13},{2,14},{3,15},{4,8},{5,9},{6,10},{7,11},{8,4},{9,5},... | collective-permute-start | bytes 786440 | tf_op jit(solution)/shard_map/ppermute | solution.py:54
  (78 other events, 1091.6 us)
Sparse Core Ops, SparseCore 0:
  31.7 44.3 all-gather.5
  89.3 56.4 all-gather.7
  171.0 57.6 all-gather.9
  230.1 44.0 all-gather.11
  287.2 44.6 all-gather.13
  450.7 143.2 reduce-scatter.2
  635.6 78.1 reduce-scatter.4

commit v3 on v2

--- a/solution.py
+++ b/solution.py
@@ -575,6 +575,19 @@
     def to_groups(piece):
         return lax.all_gather(piece, "blk", axis=0, tiled=True, axis_index_groups=alike)
 
+    def doubled(piece):
+        step = slices
+        while step < nb:
+            arrived = move(piece, db=step, dh=0)
+            upper = (b // step) % 2 == 1
+            piece = jnp.where(
+                upper,
+                jnp.concatenate([arrived, piece], axis=0),
+                jnp.concatenate([piece, arrived], axis=0),
+            )
+            step *= 2
+        return piece
+
     def from_slices(pieces):
         return [move(p, db=d + 1, dh=0) for d, p in enumerate(pieces[1:])]
 
@@ -600,16 +613,16 @@
     w_attn = assemble(scalar(low), [(attn_all, every)], kin, slices)
     normed_f, rstd_in = norm_stats(tokens)
     first = Gather(normed_f.astype(BF16))
-    first.open(*attn_rest)
+    back_rows = to_micro(cotangent)
+    first.open(*attn_rest, back_rows)
     feed_rest = from_slices(feed_own)
-    first.take(feed_rest[1])
-    normed = first.near + first.far(feed_rest[0], feed_rest[2])
-    for piece in (feed_rest[1], feed_rest[0], feed_rest[2]):
+    first.take()
+    normed = first.near + first.far(*feed_rest)
+    for piece in (feed_rest[1], feed_rest[0]):
         feed_all.append(to_groups(piece))
-    back_rows = to_micro(cotangent)
+    feed_all.append(doubled(feed_rest[2]))
     cots = Gather(after(back_rows, *normed[:2]))
     query, key, value = project(normed, w_attn, table)
-    cots.open(query)
     if spread > 1:
         teams = [
             [(((m * spread + s) * slices + l) * nh + k) for s in range(spread)]
@@ -629,21 +642,22 @@
     mixing = Scatter(kept, sent)
     mixing.open()
     low0, lse0, kept, sent = attend(
-        after(query, *mixing.far), keys, values, w_attn, pos_q, pos_k, 0
-    )
+        after(query, *mixing.far, cots.sent), keys, values, w_attn, pos_q, pos_k, 0
+    )
+    cots.open()
     mixing.near(kept, sent)
     mixing.take_near()
     mixing.take(feed_all[1])
     cots.take(*mixing.parts)
     mixing.pair()
-    mid = tokens + mixing.close(feed_all[2])
+    mid = tokens + mixing.close(feed_all[2], feed_all[3])
     mid_f, rstd_mid = norm_stats(mid)
 
     mids = Gather(mid_f.astype(BF16))
     mids.open(*cots.sent)
     backs_far = cots.far(*mids.parts)
     backs_near = cots.near
-    mids.take(*backs_far, feed_all[3])
+    mids.take(*backs_far)
     w_feed = assemble(
         scalar(low),
         [(a, d) for a, d in zip(feed_all, ((0,), (2,), (1,), (3,)))],
@@ -691,7 +705,7 @@
         )
         back_k, back_v = shared(back_k), shared(back_v)
     joined1, kept, sent = back_input(
-        after(back_q, *finishing.parts), back_k, back_v, table, w_attn, 1
+        after(back_q, *finishing.sent_far), back_k, back_v, table, w_attn, 1
     )
     entering = Scatter(kept, sent)
     entering.open()

time: 766 us -> 728 us (0.950)
  waiting for transfers between devices: 397 us -> 367 us
    ppermute x80 -> x81, waiting for transfers between devices: 383 us -> 322 us  [swap(): return lax.ppermute(value, AXES, pairs)]
    all_gather x5 -> x4, waiting for transfers between devices: 13.2 us -> 43.8 us  [to_groups(): lax.all_gather(piece, 'blk', axis=0, tiled=True, axis_index_groups=alike)]
    ppermute x80 -> x81, starting transfers between devices: 71.1 us -> 63.7 us  [swap(): return lax.ppermute(value, AXES, pairs)]
  transfers between devices with their start and end apart: 87 -> 87, of which waited for: 49 -> 49; matrix products, arithmetic and copies ran while one was open for 10% -> 10% of each run, Pallas kernels for 19% -> 20%
where the time goes in v3:
time: 728 us; the launch traced here: 718 us
  waiting for transfers between devices  367 us (50%)
  Pallas kernels  184 us (25%)
  starting transfers between devices  64.9 us (9%)
  other arithmetic  62.1 us (9%)
  local copies, waits for them, and re-layouts  24.2 us (3%)
  between operations  15.9 us (2%)
    ppermute x81, waiting for transfers between devices, swap(): return lax.ppermute(value, AXES, pairs)  322 us
    ppermute x81, starting transfers between devices, swap(): return lax.ppermute(value, AXES, pairs)  63.7 us
    all_gather x4, waiting for transfers between devices, to_groups(): lax.all_gather(piece, 'blk', axis=0, tiled=True, axis_index_groups=alike)  43.8 us
    pallas_call x2, Pallas kernels, feed(): call(kernel, [shape(rows, 2 * unit), shape(rows, unit)] + [shape(rows //...  38.8 us
    pallas_call x2, Pallas kernels, weight_grads(): call(kernel, shape(width, total), 'weight_grads', 2 * rows * width * tota...  33.6 us
    pallas_call x2, Pallas kernels, attend(): call(kernel, [shape(rows, HEAD_DIM), shape(rows, 1, F32)] + shapes, 'atte...  20.5 us
    pallas_call x1, Pallas kernels, attend_back(): call(kernel, [shape(rows, HEAD_DIM, F32), shape(keys, HEAD_DIM, F32), sha...  18.6 us
    pallas_call x2, Pallas kernels, back_input(): call(kernel, [shape(rows, 3 * HEAD_DIM)] + shapes, 'back_input', 6 * rows...  15.9 us
  transfers between devices with their start and end apart: 87, of which 49 were waited for; matrix products, arithmetic and copies ran while one was open for 10% of the time, Pallas kernels for 20%

profile of v3, /device:TPU:0, one launch (start us, length us, event | category | flops | bytes accessed | tf_op | source)
XLA Modules:
  0.0 717.7 jit_solution(2724784623477731665)
XLA Ops:
  8.4 4.1 collective-permute-start
  18.4 3.8 pack.3
  22.4 3.7 multiply_cosine_fusion
  31.1 8.9 %collective-permute-done.5 = bf16[64,2048]{1,0:T(8,128)(2,1)S(1)} collective-permute-done((bf16[64,2048]{1,0:T(8,128)(2,1)S(1)}, bf16[64,2048]{1,0:T(8,128)(2,1)S(1)}, u32[]{:S(2)}, u32[]{:S(2)}) %collective-permute-start.5) | collective-permute-done | bytes 262176 | tf_op jit(solution)/shard_map/ppermute | solution.py:54
  40.8 3.4 collective-permute-done.4
  44.3 17.8 %collective-permute-done.1 = bf16[128,2048]{1,0:T(8,128)(2,1)S(1)} collective-permute-done((bf16[128,2048]{1,0:T(8,128)(2,1)S(1)}, bf16[128,2048]{1,0:T(8,128)(2,1)S(1)}, u32[]{:S(2)}, u32[]{:S(2)}) %collective-permute-start.1) | collective-permute-done | bytes 524320 | tf_op jit(solution)/shard_map/ppermute | solution.py:54
  66.6 8.4 %collective-permute-done.7 = bf16[128,2048]{1,0:T(8,128)(2,1)S(1)} collective-permute-done((bf16[128,2048]{1,0:T(8,128)(2,1)S(1)}, bf16[128,2048]{1,0:T(8,128)(2,1)S(1)}, u32[]{:S(2)}, u32[]{:S(2)}) %collective-permute-start.7) | collective-permute-done | bytes 524320 | tf_op jit(solution)/shard_map/ppermute | solution.py:54
  82.5 31.6 %collective-permute-done.13 = bf16[256,1536]{1,0:T(8,128)(2,1)} collective-permute-done((bf16[256,1536]{1,0:T(8,128)(2,1)}, bf16[256,1536]{1,0:T(8,128)(2,1)}, u32[]{:S(2)}, u32[]{:S(2)}) %collective-permute-start.13) | collective-permute-done | bytes 786464 | tf_op jit(solution)/shard_map/ppermute | solution.py:54
  114.1 18.6 %collective-permute-done.11 = bf16[256,1536]{1,0:T(8,128)(2,1)} collective-permute-done((bf16[256,1536]{1,0:T(8,128)(2,1)}, bf16[256,1536]{1,0:T(8,128)(2,1)}, u32[]{:S(2)}, u32[]{:S(2)}) %collective-permute-start.11) | collective-permute-done | bytes 786464 | tf_op jit(solution)/shard_map/ppermute | solution.py:54
  132.7 3.9 collective-permute-done.12
  138.4 3.0 assemble.2.refs_8_.w_ref
  141.5 10.4 %project.1 = (bf16[2048,128]{1,0:T(8,128)(2,1)}, bf16[2048,128]{1,0:T(8,128)(2,1)}, bf16[2048,128]{1,0:T(8,128)(2,1)}) custom-call(bf16[256,2048]{1,0:T(8,128)(2,1)} %copy-done.1, bf16[256,2048]{1,0:T(8,128)(2,1)} %copy-done, bf16[256,2048]{1,0:T(8,128)(2,1)} %collective-permute-done.8.refs_2_, bf16[256,2048]{1,0:T(8,128)(2,1)} %collective-permute-done.9.refs_3_, ...), custom_call_target="tpu_custom_call" | custom-call | flops 3221225472 | bytes 8388608 | tf_op jit(solution)/shard_map/project/pallas_call | solution.py:181
  151.9 10.3 %attend.2 = (bf16[1024,128]{1,0:T(8,128)(2,1)}, f32[1024,1]{1,0:T(8,128)}, bf16[512,2048]{1,0:T(8,128)(2,1)}, bf16[512,2048]{1,0:T(8,128)(2,1)}) custom-call(bf16[2048,128]{1,0:T(8,128)(2,1)} %get-tuple-element.116.q_ref, bf16[2048,128]{1,0:T(8,128)(2,1)} %get-tuple-element.111.k_ref, bf16[2048,128]{1,0:T(8,128)(2,1)} %get-tuple-element.112.v_ref, ...), custom_call_target="tpu_custom_call" | custom-call | flops 1610612736 | bytes 4194304 | tf_op jit(solution)/shard_map/attend/pallas_call | solution.py:238
  162.4 4.1 collective-permute-done.17
  166.6 3.8 add_convert_fusion.15
  170.4 11.4 %collective-permute-done.18 = bf16[128,2048]{1,0:T(8,128)(2,1)S(1)} collective-permute-done((bf16[128,2048]{1,0:T(8,128)(2,1)S(1)}, bf16[128,2048]{1,0:T(8,128)(2,1)S(1)}, u32[]{:S(2)}, u32[]{:S(2)}) %collective-permute-start.18) | collective-permute-done | bytes 524320 | tf_op jit(solution)/shard_map/ppermute | solution.py:54
  182.6 10.2 %attend.3 = (bf16[1024,128]{1,0:T(8,128)(2,1)}, f32[1024,1]{1,0:T(8,128)}, bf16[512,2048]{1,0:T(8,128)(2,1)}, bf16[512,2048]{1,0:T(8,128)(2,1)}) custom-call(bf16[2048,128]{1,0:T(8,128)(2,1)} %get-tuple-element.116.q_ref, bf16[2048,128]{1,0:T(8,128)(2,1)} %get-tuple-element.111.k_ref, bf16[2048,128]{1,0:T(8,128)(2,1)} %get-tuple-element.112.v_ref, ...), custom_call_target="tpu_custom_call" | custom-call | flops 1610612736 | bytes 4194304 | tf_op jit(solution)/shard_map/attend/pallas_call | solution.py:238
  198.8 29.7 %all-gather.9.cloned.1.call-done.refs_1_ = bf16[512,1536]{1,0:T(8,128)(2,1)} async-done(((bf16[256,1536]{1,0:T(8,128)(2,1)}), bf16[512,1536]{1,0:T(8,128)(2,1)}) %all-gather.9.cloned.1.call-update) | async-done | bytes 1572880 | tf_op jit(solution)/shard_map/all_gather | solution.py:576
  228.5 3.3 convert_add_fusion.7
  231.9 3.1 collective-permute-start.21
  235.1 2.7 collective-permute-start.23
  237.9 9.9 %collective-permute-done.21 = bf16[128,2048]{1,0:T(8,128)(2,1)S(1)} collective-permute-done((bf16[128,2048]{1,0:T(8,128)(2,1)S(1)}, bf16[128,2048]{1,0:T(8,128)(2,1)S(1)}, u32[]{:S(2)}, u32[]{:S(2)}) %collective-permute-start.21) | collective-permute-done | bytes 524320 | tf_op jit(solution)/shard_map/ppermute | solution.py:54
  249.3 3.5 maximum_select_fusion.refs_3_
  256.0 3.1 collective-permute-done.27
  260.1 2.7 collective-permute-start.28
  262.9 14.1 %all-gather.11.cloned.1.call-done.refs_2_ = bf16[512,1536]{1,0:T(8,128)(2,1)} async-done(((bf16[256,1536]{1,0:T(8,128)(2,1)}), bf16[512,1536]{1,0:T(8,128)(2,1)}) %all-gather.11.cloned.1.call-update) | async-done | bytes 1572880 | tf_op jit(solution)/shard_map/all_gather | solution.py:576
  280.3 3.6 collective-permute-done.28.refs_4_.refs_14_
  283.9 8.5 %collective-permute-done.26 = bf16[128,2048]{1,0:T(8,128)(2,1)S(1)} collective-permute-done((bf16[128,2048]{1,0:T(8,128)(2,1)S(1)}, bf16[128,2048]{1,0:T(8,128)(2,1)S(1)}, u32[]{:S(2)}, u32[]{:S(2)}) %collective-permute-start.26) | collective-permute-done | bytes 524320 | tf_op jit(solution)/shard_map/ppermute | solution.py:54
  296.1 11.0 %collective-permute-done.34 = bf16[128,2048]{1,0:T(8,128)(2,1)S(1)} collective-permute-done((bf16[128,2048]{1,0:T(8,128)(2,1)S(1)}, bf16[128,2048]{1,0:T(8,128)(2,1)S(1)}, u32[]{:S(2)}, u32[]{:S(2)}) %collective-permute-start.34) | collective-permute-done | bytes 524320 | tf_op jit(solution)/shard_map/ppermute | solution.py:54
  311.8 5.9 assemble.3.refs_8_.w_ref
  318.8 19.5 %feed.2 = (bf16[1024,1024]{1,0:T(8,128)(2,1)}, bf16[1024,512]{1,0:T(8,128)(2,1)}, bf16[512,2048]{1,0:T(8,128)(2,1)}, bf16[512,2048]{1,0:T(8,128)(2,1)}) custom-call(bf16[256,2048]{1,0:T(8,128)(2,1)} %copy-done.40, bf16[256,2048]{1,0:T(8,128)(2,1)} %copy-done.39, bf16[256,2048]{1,0:T(8,128)(2,1)} %collective-permute-done.35.refs_2_, ...), custom_call_target="tpu_custom_call" | custom-call | flops 10737418240 | bytes 4194304 | tf_op jit(solution)/shard_map/feed/pallas_call | solution.py:281
  343.5 19.3 %feed.3 = (bf16[1024,1024]{1,0:T(8,128)(2,1)}, bf16[1024,512]{1,0:T(8,128)(2,1)}, bf16[512,2048]{1,0:T(8,128)(2,1)}, bf16[512,2048]{1,0:T(8,128)(2,1)}) custom-call(bf16[256,2048]{1,0:T(8,128)(2,1)} %copy-done.61, bf16[256,2048]{1,0:T(8,128)(2,1)} %copy-done.60, bf16[256,2048]{1,0:T(8,128)(2,1)} %copy-done.63, bf16[256,2048]{1,0:T(8,128)(2,1)} %copy-done.62, ...), custom_call_target="tpu_custom_call" | custom-call | flops 10737418240 | bytes 4194304 | tf_op jit(solution)/shard_map/feed/pallas_call | solution.py:281
  363.3 5.5 collective-permute-done.44
  368.8 3.6 add_convert_fusion.10
  373.6 19.9 %weight_grads.2 = bf16[2048,1536]{1,0:T(8,128)(2,1)} custom-call(bf16[256,2048]{1,0:T(8,128)(2,1)} %copy-done.40, bf16[256,2048]{1,0:T(8,128)(2,1)} %copy-done.39, bf16[256,2048]{1,0:T(8,128)(2,1)} %collective-permute-done.35.refs_2_, bf16[256,2048]{1,0:T(8,128)(2,1)} %collective-permute-done.36.refs_3_, bf16[256,2048]{1,0:T(8,128)(2,1)} %copy-done.61, ...), custom_call_target="tpu_custom_call" | custom-call | flops 12884901888 | bytes 14680064 | tf_op jit(solution)/shard_map/weight_grads/pallas_call | solution.py:341
  393.4 4.5 collective-permute-done.47
  398.3 3.3 convert_add_fusion.5
  403.8 7.9 %feed_out.2 = (bf16[512,2048]{1,0:T(8,128)(2,1)}, bf16[512,2048]{1,0:T(8,128)(2,1)}) custom-call(bf16[1024,512]{1,0:T(8,128)(2,1)} %get-tuple-element.142.refs_19_.hidden_ref, bf16[2048,1536]{1,0:T(8,128)(2,1)} %assemble.3.refs_8_.w_ref), custom_call_target="tpu_custom_call" | custom-call | flops 2147483648 | bytes 4194304 | tf_op jit(solution)/shard_map/feed_out/pallas_call | solution.py:302
  411.8 2.8 collective-permute-done.46
  416.4 7.9 %feed_out.3 = (bf16[512,2048]{1,0:T(8,128)(2,1)}, bf16[512,2048]{1,0:T(8,128)(2,1)}) custom-call(bf16[1024,512]{1,0:T(8,128)(2,1)} %get-tuple-element.147.refs_18_.hidden_ref, bf16[2048,1536]{1,0:T(8,128)(2,1)} %assemble.3.refs_8_.w_ref), custom_call_target="tpu_custom_call" | custom-call | flops 2147483648 | bytes 4194304 | tf_op jit(solution)/shard_map/feed_out/pallas_call | solution.py:302
  424.4 3.3 collective-permute-done.50
  430.1 14.8 %collective-permute-done.51 = bf16[128,2048]{1,0:T(8,128)(2,1)S(1)} collective-permute-done((bf16[128,2048]{1,0:T(8,128)(2,1)S(1)}, bf16[128,2048]{1,0:T(8,128)(2,1)S(1)}, u32[]{:S(2)}, u32[]{:S(2)}) %collective-permute-start.51) | collective-permute-done | bytes 524320 | tf_op jit(solution)/shard_map/ppermute | solution.py:54
  445.3 14.7 %collective-permute-done.53 = bf16[128,2048]{1,0:T(8,128)(2,1)S(1)} collective-permute-done((bf16[128,2048]{1,0:T(8,128)(2,1)S(1)}, bf16[128,2048]{1,0:T(8,128)(2,1)S(1)}, u32[]{:S(2)}, u32[]{:S(2)}) %collective-permute-start.53) | collective-permute-done | bytes 524320 | tf_op jit(solution)/shard_map/ppermute | solution.py:54
  462.3 13.5 %collective-permute-done.57.refs_5_.refs_15_ = bf16[256,2048]{1,0:T(8,128)(2,1)S(1)} collective-permute-done((bf16[256,2048]{1,0:T(8,128)(2,1)S(1)}, bf16[256,2048]{1,0:T(8,128)(2,1)S(1)}, u32[]{:S(2)}, u32[]{:S(2)}) %collective-permute-start.57) | collective-permute-done | bytes 1048608 | tf_op jit(solution)/shard_map/ppermute | solution.py:54
  477.5 5.8 collective-permute-done.55.refs_3_.refs_13_
  487.7 7.2 %back_project.1.do_ref = bf16[2048,128]{1,0:T(8,128)(2,1)} custom-call(bf16[256,2048]{1,0:T(8,128)(2,1)} %copy-done.3, bf16[256,2048]{1,0:T(8,128)(2,1)} %copy-done.2, bf16[256,2048]{1,0:T(8,128)(2,1)} %copy-done.17, bf16[256,2048]{1,0:T(8,128)(2,1)} %copy-done.16, bf16[256,2048]{1,0:T(8,128)(2,1)} %copy-done.15, bf16[256,2048]{1,0:T(8,128)(2,1)} %copy-done.14, ...), custom_call_target="tpu_custom_call" | custom-call | flops 1073741824 | bytes 8388608 | tf_op jit(solution)/shard_map/back_project/pallas_call | solution.py:364
  494.9 4.5 add_convert_fusion.7
  503.9 18.6 %attend_back.1 = (f32[2048,128]{1,0:T(8,128)}, f32[2048,128]{1,0:T(8,128)}, f32[2048,128]{1,0:T(8,128)}) custom-call(bf16[2048,128]{1,0:T(8,128)(2,1)} %get-tuple-element.116.q_ref, bf16[2048,128]{1,0:T(8,128)(2,1)} %back_project.1.do_ref, f32[2048,1]{1,0:T(8,128)} %copy.35.lse_ref, s32[2048,1]{1,0:T(8,128)} %copy.31.pq_ref, ...), custom_call_target="tpu_custom_call" | custom-call | flops 5368709120 | bytes 4194304 | tf_op jit(solution)/shard_map/attend_back/pallas_call | solution.py:400
  525.1 8.1 %back_input.2 = (bf16[1024,384]{1,0:T(8,128)(2,1)}, bf16[512,2048]{1,0:T(8,128)(2,1)}, bf16[512,2048]{1,0:T(8,128)(2,1)}) custom-call(f32[2048,128]{1,0:T(8,128)} %get-tuple-element.165.dq_ref, f32[2048,128]{1,0:T(8,128)} %get-tuple-element.160.dk_ref, f32[2048,128]{1,0:T(8,128)} %get-tuple-element.161.dv_ref, f32[2048,256]{1,0:T(8,128)} %pad_maximum_fusion.refs_9_.t_ref, ...), custom_call_target="tpu_custom_call" | custom-call | flops 1610612736 | bytes 4194304 | tf_op jit(solution)/shard_map/back_input/pallas_call | solution.py:426
  533.3 7.8 %back_input.3 = (bf16[1024,384]{1,0:T(8,128)(2,1)}, bf16[512,2048]{1,0:T(8,128)(2,1)}, bf16[512,2048]{1,0:T(8,128)(2,1)}) custom-call(f32[2048,128]{1,0:T(8,128)} %get-tuple-element.165.dq_ref, f32[2048,128]{1,0:T(8,128)} %get-tuple-element.160.dk_ref, f32[2048,128]{1,0:T(8,128)} %get-tuple-element.161.dv_ref, f32[2048,256]{1,0:T(8,128)} %pad_maximum_fusion.refs_9_.t_ref, ...), custom_call_target="tpu_custom_call" | custom-call | flops 1610612736 | bytes 4194304 | tf_op jit(solution)/shard_map/back_input/pallas_call | solution.py:426
  551.8 13.8 %weight_grads.3 = bf16[2048,512]{1,0:T(8,128)(2,1)} custom-call(bf16[256,2048]{1,0:T(8,128)(2,1)} %copy-done.1, bf16[256,2048]{1,0:T(8,128)(2,1)} %copy-done, bf16[256,2048]{1,0:T(8,128)(2,1)} %collective-permute-done.8.refs_2_, bf16[256,2048]{1,0:T(8,128)(2,1)} %collective-permute-done.9.refs_3_, bf16[256,2048]{1,0:T(8,128)(2,1)} %collective-permute-done.10.refs_4_, ...), custom_call_target="tpu_custom_call" | custom-call | flops 4294967296 | bytes 10485760 | tf_op jit(solution)/shard_map/weight_grads/pallas_call | solution.py:341
  565.6 15.9 %collective-permute-done.62 = bf16[128,2048]{1,0:T(8,128)(2,1)} collective-permute-done((bf16[128,2048]{1,0:T(8,128)(2,1)}, bf16[128,2048]{1,0:T(8,128)(2,1)}, u32[]{:S(2)}, u32[]{:S(2)}) %collective-permute-start.62) | collective-permute-done | bytes 524320 | tf_op jit(solution)/shard_map/ppermute | solution.py:54
  584.1 3.3 convert_add_fusion.1
  594.6 2.5 collective-permute-start.65
  597.1 4.4 collective-permute-done.70
  609.3 11.3 %collective-permute-done.65 = bf16[128,2048]{1,0:T(8,128)(2,1)} collective-permute-done((bf16[128,2048]{1,0:T(8,128)(2,1)}, bf16[128,2048]{1,0:T(8,128)(2,1)}, u32[]{:S(2)}, u32[]{:S(2)}) %collective-permute-start.65) | collective-permute-done | bytes 524320 | tf_op jit(solution)/shard_map/ppermute | solution.py:54
  622.0 20.8 %collective-permute-done.73 = bf16[128,2048]{1,0:T(8,128)(2,1)} collective-permute-done((bf16[128,2048]{1,0:T(8,128)(2,1)}, bf16[128,2048]{1,0:T(8,128)(2,1)}, u32[]{:S(2)}, u32[]{:S(2)}) %collective-permute-start.73) | collective-permute-done | bytes 524320 | tf_op jit(solution)/shard_map/ppermute | solution.py:54
  649.2 2.5 collective-permute-start.79
  651.8 7.3 %collective-permute-done.66 = bf16[64,2048]{1,0:T(8,128)(2,1)S(1)} collective-permute-done((bf16[64,2048]{1,0:T(8,128)(2,1)S(1)}, bf16[64,2048]{1,0:T(8,128)(2,1)S(1)}, u32[]{:S(2)}, u32[]{:S(2)}) %collective-permute-start.66) | collective-permute-done | bytes 262176 | tf_op jit(solution)/shard_map/ppermute | solution.py:54
  659.1 9.2 %collective-permute-done.74 = bf16[64,2048]{1,0:T(8,128)(2,1)S(1)} collective-permute-done((bf16[64,2048]{1,0:T(8,128)(2,1)S(1)}, bf16[64,2048]{1,0:T(8,128)(2,1)S(1)}, u32[]{:S(2)}, u32[]{:S(2)}) %collective-permute-start.74) | collective-permute-done | bytes 262176 | tf_op jit(solution)/shard_map/ppermute | solution.py:54
  676.6 6.8 collective-permute-done.79.refs_2_
  683.5 17.3 %collective-permute-done.80.refs_3_ = bf16[256,1536]{1,0:T(8,128)(2,1)} collective-permute-done((bf16[256,1536]{1,0:T(8,128)(2,1)S(1)}, bf16[256,1536]{1,0:T(8,128)(2,1)}, u32[]{:S(2)}, u32[]{:S(2)}) %collective-permute-start.80) | collective-permute-done | bytes 786464 | tf_op jit(solution)/shard_map/ppermute | solution.py:54
  700.8 5.0 unpack.3
  707.7 2.6 unpack.2
  (374 shorter events, 127.8 us)
Async XLA Ops:
  7.2 70.9 %all-gather.5.cloned.1.call-start = ((), (), s32[]{:S(2)}) async-start(), calls=%async_computation.2 | async-start | bytes 2359296 | tf_op jit(solution)/shard_map/all_gather | solution.py:576
  8.4 20.0 %collective-permute-start = (bf16[64,2048]{1,0:T(8,128)(2,1)S(1)}, bf16[64,2048]{1,0:T(8,128)(2,1)S(1)}, u32[]{:S(2)}, u32[]{:S(2)}) collective-permute-start(bf16[64,2048]{1,0:T(8,128)(2,1)S(1)} %get-tuple-element.245), channel_id=1, source_target_pairs={{0,16},{1,17},{2,18},{3,19},{4,20},{5,21},{6,22},{7,23},{8,24},{9,... | collective-permute-start | bytes 786440 | tf_op jit(solution)/shard_map/ppermute | solution.py:54
  14.7 26.1 %collective-permute-start.2 = (bf16[256,512]{1,0:T(8,128)(2,1)}, bf16[256,512]{1,0:T(8,128)(2,1)S(1)}, u32[]{:S(2)}, u32[]{:S(2)}) collective-permute-start(bf16[256,512]{1,0:T(8,128)(2,1)} %get-tuple-element.98), channel_id=1, source_target_pairs={{0,4},{1,5},{2,6},{3,7},{4,0},{5,1},{6,2},{7,3},{8,12},{9,13},{10,... | collective-permute-start | bytes 786440 | tf_op jit(solution)/shard_map/ppermute | solution.py:54
  16.2 24.6 %collective-permute-start.3 = (bf16[256,512]{1,0:T(8,128)(2,1)}, bf16[256,512]{1,0:T(8,128)(2,1)S(1)}, u32[]{:S(2)}, u32[]{:S(2)}) collective-permute-start(bf16[256,512]{1,0:T(8,128)(2,1)} %get-tuple-element.99), channel_id=1, source_target_pairs={{0,8},{1,9},{2,10},{3,11},{4,12},{5,13},{6,14},{7,15},{8,0},{9,1},... | collective-permute-start | bytes 786440 | tf_op jit(solution)/shard_map/ppermute | solution.py:54
  17.8 26.5 %collective-permute-start.4 = (bf16[256,512]{1,0:T(8,128)(2,1)}, bf16[256,512]{1,0:T(8,128)(2,1)S(1)}, u32[]{:S(2)}, u32[]{:S(2)}) collective-permute-start(bf16[256,512]{1,0:T(8,128)(2,1)} %get-tuple-element.100), channel_id=1, source_target_pairs={{0,12},{1,13},{2,14},{3,15},{4,8},{5,9},{6,10},{7,11},{8,4},{9,5},... | collective-permute-start | bytes 786440 | tf_op jit(solution)/shard_map/ppermute | solution.py:54
  18.3 21.7 %collective-permute-start.5 = (bf16[64,2048]{1,0:T(8,128)(2,1)S(1)}, bf16[64,2048]{1,0:T(8,128)(2,1)S(1)}, u32[]{:S(2)}, u32[]{:S(2)}) collective-permute-start(bf16[64,2048]{1,0:T(8,128)(2,1)S(1)} %get-tuple-element.243), channel_id=1, source_target_pairs={{0,16},{1,17},{2,18},{3,19},{4,20},{5,21},{6,22},{7,23},{8,24},{9,... | collective-permute-start | bytes 786440 | tf_op jit(solution)/shard_map/ppermute | solution.py:54
  22.3 116.2 %all-gather.7.cloned.1.call-start = ((), (), s32[]{:S(2)}) async-start(), calls=%async_computation.3 | async-start | bytes 3145728 | tf_op jit(solution)/shard_map/all_gather | solution.py:576
  29.1 32.9 %collective-permute-start.1 = (bf16[128,2048]{1,0:T(8,128)(2,1)S(1)}, bf16[128,2048]{1,0:T(8,128)(2,1)S(1)}, u32[]{:S(2)}, u32[]{:S(2)}) collective-permute-start(bf16[128,2048]{1,0:T(8,128)(2,1)S(1)} %fusion.4), channel_id=1, source_target_pairs={{0,8},{1,9},{2,10},{3,11},{4,12},{5,13},{6,14},{7,15},{8,0},{9,1},... | collective-permute-start | bytes 1572872 | tf_op jit(solution)/shard_map/ppermute | solution.py:54
  75.1 61.4 %collective-permute-start.14 = (bf16[256,2048]{1,0:T(8,128)(2,1)S(1)}, bf16[256,2048]{1,0:T(8,128)(2,1)S(1)}, u32[]{:S(2)}, u32[]{:S(2)}) collective-permute-start(bf16[256,2048]{1,0:T(8,128)(2,1)S(1)} %pad_maximum_fusion.2.refs_1_), channel_id=1, source_target_pairs={{0,4},{1,5},{2,6},{3,7},{4,0},{5,1},{6,2},{7,3},{8,12},{9,13},{10,... | collective-permute-start | bytes 3145736 | tf_op jit(solution)/shard_map/ppermute | solution.py:54
  78.1 150.4 %all-gather.9.cloned.1.call-start = ((), (), s32[]{:S(2)}) async-start(), calls=%async_computation.4 | async-start | bytes 2359296 | tf_op jit(solution)/shard_map/all_gather | solution.py:576
  78.5 58.1 %collective-permute-start.10 = (bf16[256,2048]{1,0:T(8,128)(2,1)S(1)}, bf16[256,2048]{1,0:T(8,128)(2,1)}, u32[]{:S(2)}, u32[]{:S(2)}) collective-permute-start(bf16[256,2048]{1,0:T(8,128)(2,1)S(1)} %pad_maximum_fusion.1.refs_0_), channel_id=1, source_target_pairs={{0,2},{1,3},{2,0},{3,1},{4,6},{5,7},{6,4},{7,5},{8,10},{9,11},{10,... | collective-permute-start | bytes 3145736 | tf_op jit(solution)/shard_map/ppermute | solution.py:54
  79.0 35.1 %collective-permute-start.13 = (bf16[256,1536]{1,0:T(8,128)(2,1)}, bf16[256,1536]{1,0:T(8,128)(2,1)}, u32[]{:S(2)}, u32[]{:S(2)}) collective-permute-start(bf16[256,1536]{1,0:T(8,128)(2,1)} %get-tuple-element.104), channel_id=1, source_target_pairs={{0,12},{1,13},{2,14},{3,15},{4,8},{5,9},{6,10},{7,11},{8,4},{9,5},... | collective-permute-start | bytes 2359304 | tf_op jit(solution)/shard_map/ppermute | solution.py:54
  81.3 51.4 %collective-permute-start.11 = (bf16[256,1536]{1,0:T(8,128)(2,1)}, bf16[256,1536]{1,0:T(8,128)(2,1)}, u32[]{:S(2)}, u32[]{:S(2)}) collective-permute-start(bf16[256,1536]{1,0:T(8,128)(2,1)} %get-tuple-element.102), channel_id=1, source_target_pairs={{0,4},{1,5},{2,6},{3,7},{4,0},{5,1},{6,2},{7,3},{8,12},{9,13},{10,... | collective-permute-start | bytes 2359304 | tf_op jit(solution)/shard_map/ppermute | solution.py:54
  81.7 54.8 %collective-permute-start.12 = (bf16[256,1536]{1,0:T(8,128)(2,1)}, bf16[256,1536]{1,0:T(8,128)(2,1)}, u32[]{:S(2)}, u32[]{:S(2)}) collective-permute-start(bf16[256,1536]{1,0:T(8,128)(2,1)} %get-tuple-element.103), channel_id=1, source_target_pairs={{0,8},{1,9},{2,10},{3,11},{4,12},{5,13},{6,14},{7,15},{8,0},{9,1},... | collective-permute-start | bytes 2359304 | tf_op jit(solution)/shard_map/ppermute | solution.py:54
  114.1 27.4 %collective-permute-start.9 = (bf16[256,2048]{1,0:T(8,128)(2,1)S(1)}, bf16[256,2048]{1,0:T(8,128)(2,1)}, u32[]{:S(2)}, u32[]{:S(2)}) collective-permute-start(bf16[256,2048]{1,0:T(8,128)(2,1)S(1)} %pad_maximum_fusion.2.refs_1_), channel_id=1, source_target_pairs={{0,1},{1,0},{2,3},{3,2},{4,5},{5,4},{6,7},{7,6},{8,9},{9,8},{10,11... | collective-permute-start | bytes 3145736 | tf_op jit(solution)/shard_map/ppermute | solution.py:54
  162.3 114.7 %all-gather.11.cloned.1.call-start = ((), (), s32[]{:S(2)}) async-start(), calls=%async_computation.5 | async-start | bytes 2359296 | tf_op jit(solution)/shard_map/all_gather | solution.py:576
  162.4 19.4 %collective-permute-start.18 = (bf16[128,2048]{1,0:T(8,128)(2,1)S(1)}, bf16[128,2048]{1,0:T(8,128)(2,1)S(1)}, u32[]{:S(2)}, u32[]{:S(2)}) collective-permute-start(bf16[128,2048]{1,0:T(8,128)(2,1)S(1)} %copy-done.34), channel_id=1, source_target_pairs={{0,8},{1,9},{2,10},{3,11},{4,12},{5,13},{6,14},{7,15},{8,0},{9,1},... | collective-permute-start | bytes 1572872 | tf_op jit(solution)/shard_map/ppermute | solution.py:54
  192.8 35.8 %collective-permute-start.19 = (bf16[512,2048]{1,0:T(8,128)(2,1)}, bf16[512,2048]{1,0:T(8,128)(2,1)}, u32[]{:S(2)}, u32[]{:S(2)}) collective-permute-start(bf16[512,2048]{1,0:T(8,128)(2,1)} %get-tuple-element.118), channel_id=1, source_target_pairs={{0,1},{1,0},{2,3},{3,2},{4,5},{5,4},{6,7},{7,6},{8,9},{9,8},{10,11... | collective-permute-start | bytes 6291464 | tf_op jit(solution)/shard_map/ppermute | solution.py:54
  192.9 56.5 %collective-permute-start.25 = (bf16[256,1536]{1,0:T(8,128)(2,1)}, bf16[256,1536]{1,0:T(8,128)(2,1)}, u32[]{:S(2)}, u32[]{:S(2)}) collective-permute-start(bf16[256,1536]{1,0:T(8,128)(2,1)} %collective-permute-done.13), channel_id=1, source_target_pairs={{0,16},{1,17},{2,18},{3,19},{4,20},{5,21},{6,22},{7,23},{8,24},{9,... | collective-permute-start | bytes 2359304 | tf_op jit(solution)/shard_map/ppermute | solution.py:54
  193.0 399.6 %reduce-scatter.3.cloned.1.call-start = ((), (), s32[]{:S(2)}) async-start(), calls=%async_computation.6 | async-start | bytes 9437184 | tf_op jit(solution)/shard_map/reduce_scatter | solution.py:595
  193.6 34.9 %collective-permute-start.22 = (bf16[256,2048]{1,0:T(8,128)(2,1)}, bf16[256,2048]{1,0:T(8,128)(2,1)}, u32[]{:S(2)}, u32[]{:S(2)}) collective-permute-start(bf16[256,2048]{1,0:T(8,128)(2,1)} %get-tuple-element.209), channel_id=1, source_target_pairs={{0,4},{1,5},{2,6},{3,7},{4,0},{5,1},{6,2},{7,3},{8,12},{9,13},{10,... | collective-permute-start | bytes 3145736 | tf_op jit(solution)/shard_map/ppermute | solution.py:54
  193.7 34.8 %collective-permute-start.20 = (bf16[256,2048]{1,0:T(8,128)(2,1)}, bf16[256,2048]{1,0:T(8,128)(2,1)}, u32[]{:S(2)}, u32[]{:S(2)}) collective-permute-start(bf16[256,2048]{1,0:T(8,128)(2,1)} %get-tuple-element.208), channel_id=1, source_target_pairs={{0,2},{1,3},{2,0},{3,1},{4,6},{5,7},{6,4},{7,5},{8,10},{9,11},{10,... | collective-permute-start | bytes 3145736 | tf_op jit(solution)/shard_map/ppermute | solution.py:54
  196.8 56.0 %collective-permute-start.29 = (bf16[128,2048]{1,0:T(8,128)(2,1)}, bf16[128,2048]{1,0:T(8,128)(2,1)}, u32[]{:S(2)}, u32[]{:S(2)}) collective-permute-start(bf16[128,2048]{1,0:T(8,128)(2,1)} %pad_maximum_fusion.19), channel_id=1, source_target_pairs={{0,2},{1,3},{2,0},{3,1},{4,6},{5,7},{6,4},{7,5},{8,10},{9,11},{10,... | collective-permute-start | bytes 1572872 | tf_op jit(solution)/shard_map/ppermute | solution.py:54
  231.9 15.9 %collective-permute-start.21 = (bf16[128,2048]{1,0:T(8,128)(2,1)S(1)}, bf16[128,2048]{1,0:T(8,128)(2,1)S(1)}, u32[]{:S(2)}, u32[]{:S(2)}) collective-permute-start(bf16[128,2048]{1,0:T(8,128)(2,1)S(1)} %fusion.19), channel_id=1, source_target_pairs={{0,4},{1,5},{2,6},{3,7},{4,0},{5,1},{6,2},{7,3},{8,12},{9,13},{10,... | collective-permute-start | bytes 1572872 | tf_op jit(solution)/shard_map/ppermute | solution.py:54
  235.1 13.9 %collective-permute-start.23 = (bf16[128,2048]{1,0:T(8,128)(2,1)S(1)}, bf16[128,2048]{1,0:T(8,128)(2,1)S(1)}, u32[]{:S(2)}, u32[]{:S(2)}) collective-permute-start(bf16[128,2048]{1,0:T(8,128)(2,1)S(1)} %fusion.18), channel_id=1, source_target_pairs={{0,2},{1,3},{2,0},{3,1},{4,6},{5,7},{6,4},{7,5},{8,10},{9,11},{10,... | collective-permute-start | bytes 1572872 | tf_op jit(solution)/shard_map/ppermute | solution.py:54
  237.8 21.2 %collective-permute-start.27 = (bf16[128,2048]{1,0:T(8,128)(2,1)S(1)}, bf16[128,2048]{1,0:T(8,128)(2,1)S(1)}, u32[]{:S(2)}, u32[]{:S(2)}) collective-permute-start(bf16[128,2048]{1,0:T(8,128)(2,1)S(1)} %pad_maximum_fusion.18), channel_id=1, source_target_pairs={{0,4},{1,5},{2,6},{3,7},{4,0},{5,1},{6,2},{7,3},{8,12},{9,13},{10,... | collective-permute-start | bytes 1572872 | tf_op jit(solution)/shard_map/ppermute | solution.py:54
  249.3 28.4 %collective-permute-start.24 = (bf16[128,2048]{1,0:T(8,128)(2,1)S(1)}, bf16[128,2048]{1,0:T(8,128)(2,1)}, u32[]{:S(2)}, u32[]{:S(2)}) collective-permute-start(bf16[128,2048]{1,0:T(8,128)(2,1)S(1)} %pad_maximum_fusion.17), channel_id=1, source_target_pairs={{0,8},{1,9},{2,10},{3,11},{4,12},{5,13},{6,14},{7,15},{8,0},{9,1},... | collective-permute-start | bytes 1572872 | tf_op jit(solution)/shard_map/ppermute | solution.py:54
  255.0 25.4 %collective-permute-start.30 = (bf16[256,2048]{1,0:T(8,128)(2,1)}, bf16[256,2048]{1,0:T(8,128)(2,1)}, u32[]{:S(2)}, u32[]{:S(2)}) collective-permute-start(bf16[256,2048]{1,0:T(8,128)(2,1)} %pad_maximum_fusion.5.refs_5_.refs_11_), channel_id=1, source_target_pairs={{0,4},{1,5},{2,6},{3,7},{4,0},{5,1},{6,2},{7,3},{8,12},{9,13},{10,... | collective-permute-start | bytes 3145736 | tf_op jit(solution)/shard_map/ppermute | solution.py:54
  260.1 23.8 %collective-permute-start.28 = (bf16[256,2048]{1,0:T(8,128)(2,1)}, bf16[256,2048]{1,0:T(8,128)(2,1)}, u32[]{:S(2)}, u32[]{:S(2)}) collective-permute-start(bf16[256,2048]{1,0:T(8,128)(2,1)} %pad_maximum_fusion.4.refs_4_.refs_10_), channel_id=1, source_target_pairs={{0,2},{1,3},{2,0},{3,1},{4,6},{5,7},{6,4},{7,5},{8,10},{9,11},{10,... | collective-permute-start | bytes 3145736 | tf_op jit(solution)/shard_map/ppermute | solution.py:54
  292.6 14.5 %collective-permute-start.33 = (bf16[256,2048]{1,0:T(8,128)(2,1)}, bf16[256,2048]{1,0:T(8,128)(2,1)S(1)}, u32[]{:S(2)}, u32[]{:S(2)}) collective-permute-start(bf16[256,2048]{1,0:T(8,128)(2,1)} %collective-permute-done.30.refs_5_.refs_15_), channel_id=1, source_target_pairs={{0,1},{1,0},{2,3},{3,2},{4,5},{5,4},{6,7},{7,6},{8,9},{9,8},{10,11... | collective-permute-start | bytes 3145736 | tf_op jit(solution)/shard_map/ppermute | solution.py:54
  292.6 14.4 %collective-permute-start.32 = (bf16[256,2048]{1,0:T(8,128)(2,1)}, bf16[256,2048]{1,0:T(8,128)(2,1)S(1)}, u32[]{:S(2)}, u32[]{:S(2)}) collective-permute-start(bf16[256,2048]{1,0:T(8,128)(2,1)} %collective-permute-done.28.refs_4_.refs_14_), channel_id=1, source_target_pairs={{0,1},{1,0},{2,3},{3,2},{4,5},{5,4},{6,7},{7,6},{8,9},{9,8},{10,11... | collective-permute-start | bytes 3145736 | tf_op jit(solution)/shard_map/ppermute | solution.py:54
  293.1 13.9 %collective-permute-start.34 = (bf16[128,2048]{1,0:T(8,128)(2,1)S(1)}, bf16[128,2048]{1,0:T(8,128)(2,1)S(1)}, u32[]{:S(2)}, u32[]{:S(2)}) collective-permute-start(bf16[128,2048]{1,0:T(8,128)(2,1)S(1)} %pad_maximum_fusion.21), channel_id=1, source_target_pairs={{0,2},{1,3},{2,0},{3,1},{4,6},{5,7},{6,4},{7,5},{8,10},{9,11},{10,... | collective-permute-start | bytes 1572872 | tf_op jit(solution)/shard_map/ppermute | solution.py:54
  294.6 13.6 %collective-permute-start.31 = (bf16[128,2048]{1,0:T(8,128)(2,1)S(1)}, bf16[128,2048]{1,0:T(8,128)(2,1)S(1)}, u32[]{:S(2)}, u32[]{:S(2)}) collective-permute-start(bf16[128,2048]{1,0:T(8,128)(2,1)S(1)} %pad_maximum_fusion.20), channel_id=1, source_target_pairs={{0,4},{1,5},{2,6},{3,7},{4,0},{5,1},{6,2},{7,3},{8,12},{9,13},{10,... | collective-permute-start | bytes 1572872 | tf_op jit(solution)/shard_map/ppermute | solution.py:54
  296.1 14.3 %collective-permute-start.38 = (bf16[256,2048]{1,0:T(8,128)(2,1)}, bf16[256,2048]{1,0:T(8,128)(2,1)S(1)}, u32[]{:S(2)}, u32[]{:S(2)}) collective-permute-start(bf16[256,2048]{1,0:T(8,128)(2,1)} %pad_maximum_fusion.5.refs_5_.refs_11_), channel_id=1, source_target_pairs={{0,1},{1,0},{2,3},{3,2},{4,5},{5,4},{6,7},{7,6},{8,9},{9,8},{10,11... | collective-permute-start | bytes 3145736 | tf_op jit(solution)/shard_map/ppermute | solution.py:54
  308.9 29.4 %collective-permute-start.41 = (bf16[256,2048]{1,0:T(8,128)(2,1)S(1)}, bf16[256,2048]{1,0:T(8,128)(2,1)S(1)}, u32[]{:S(2)}, u32[]{:S(2)}) collective-permute-start(bf16[256,2048]{1,0:T(8,128)(2,1)S(1)} %pad_maximum_fusion.7.refs_1_), channel_id=1, source_target_pairs={{0,4},{1,5},{2,6},{3,7},{4,0},{5,1},{6,2},{7,3},{8,12},{9,13},{10,... | collective-permute-start | bytes 3145736 | tf_op jit(solution)/shard_map/ppermute | solution.py:54
  310.4 28.0 %collective-permute-start.40 = (bf16[256,2048]{1,0:T(8,128)(2,1)S(1)}, bf16[256,2048]{1,0:T(8,128)(2,1)S(1)}, u32[]{:S(2)}, u32[]{:S(2)}) collective-permute-start(bf16[256,2048]{1,0:T(8,128)(2,1)S(1)} %pad_maximum_fusion.6.refs_0_), channel_id=1, source_target_pairs={{0,2},{1,3},{2,0},{3,1},{4,6},{5,7},{6,4},{7,5},{8,10},{9,11},{10,... | collective-permute-start | bytes 3145736 | tf_op jit(solution)/shard_map/ppermute | solution.py:54
  363.0 35.3 %collective-permute-start.39 = (bf16[512,2048]{1,0:T(8,128)(2,1)}, bf16[512,2048]{1,0:T(8,128)(2,1)}, u32[]{:S(2)}, u32[]{:S(2)}) collective-permute-start(bf16[512,2048]{1,0:T(8,128)(2,1)} %get-tuple-element.131), channel_id=1, source_target_pairs={{0,1},{1,0},{2,3},{3,2},{4,5},{5,4},{6,7},{7,6},{8,9},{9,8},{10,11... | collective-permute-start | bytes 6291464 | tf_op jit(solution)/shard_map/ppermute | solution.py:54
  372.5 25.5 %collective-permute-start.47 = (bf16[256,2048]{1,0:T(8,128)(2,1)}, bf16[256,2048]{1,0:T(8,128)(2,1)}, u32[]{:S(2)}, u32[]{:S(2)}) collective-permute-start(bf16[256,2048]{1,0:T(8,128)(2,1)} %get-tuple-element.205), channel_id=1, source_target_pairs={{0,4},{1,5},{2,6},{3,7},{4,0},{5,1},{6,2},{7,3},{8,12},{9,13},{10,... | collective-permute-start | bytes 3145736 | tf_op jit(solution)/shard_map/ppermute | solution.py:54
  373.0 25.2 %collective-permute-start.45 = (bf16[256,2048]{1,0:T(8,128)(2,1)}, bf16[256,2048]{1,0:T(8,128)(2,1)}, u32[]{:S(2)}, u32[]{:S(2)}) collective-permute-start(bf16[256,2048]{1,0:T(8,128)(2,1)} %get-tuple-element.204), channel_id=1, source_target_pairs={{0,2},{1,3},{2,0},{3,1},{4,6},{5,7},{6,4},{7,5},{8,10},{9,11},{10,... | collective-permute-start | bytes 3145736 | tf_op jit(solution)/shard_map/ppermute | solution.py:54
  429.7 15.2 %collective-permute-start.51 = (bf16[128,2048]{1,0:T(8,128)(2,1)S(1)}, bf16[128,2048]{1,0:T(8,128)(2,1)S(1)}, u32[]{:S(2)}, u32[]{:S(2)}) collective-permute-start(bf16[128,2048]{1,0:T(8,128)(2,1)S(1)} %get-tuple-element.190), channel_id=1, source_target_pairs={{0,8},{1,9},{2,10},{3,11},{4,12},{5,13},{6,14},{7,15},{8,0},{9,1},... | collective-permute-start | bytes 1572872 | tf_op jit(solution)/shard_map/ppermute | solution.py:54
  430.1 239.4 %reduce-scatter.5.cloned.1.call-start = ((), (), s32[]{:S(2)}) async-start(), calls=%async_computation.7 | async-start | bytes 3145728 | tf_op jit(solution)/shard_map/reduce_scatter | solution.py:595
  445.1 14.9 %collective-permute-start.53 = (bf16[128,2048]{1,0:T(8,128)(2,1)S(1)}, bf16[128,2048]{1,0:T(8,128)(2,1)S(1)}, u32[]{:S(2)}, u32[]{:S(2)}) collective-permute-start(bf16[128,2048]{1,0:T(8,128)(2,1)S(1)} %pad_maximum_fusion.24), channel_id=1, source_target_pairs={{0,2},{1,3},{2,0},{3,1},{4,6},{5,7},{6,4},{7,5},{8,10},{9,11},{10,... | collective-permute-start | bytes 1572872 | tf_op jit(solution)/shard_map/ppermute | solution.py:54
  445.2 14.9 %collective-permute-start.52 = (bf16[128,2048]{1,0:T(8,128)(2,1)S(1)}, bf16[128,2048]{1,0:T(8,128)(2,1)S(1)}, u32[]{:S(2)}, u32[]{:S(2)}) collective-permute-start(bf16[128,2048]{1,0:T(8,128)(2,1)S(1)} %pad_maximum_fusion.23), channel_id=1, source_target_pairs={{0,4},{1,5},{2,6},{3,7},{4,0},{5,1},{6,2},{7,3},{8,12},{9,13},{10,... | collective-permute-start | bytes 1572872 | tf_op jit(solution)/shard_map/ppermute | solution.py:54
  460.0 15.8 %collective-permute-start.57 = (bf16[256,2048]{1,0:T(8,128)(2,1)S(1)}, bf16[256,2048]{1,0:T(8,128)(2,1)S(1)}, u32[]{:S(2)}, u32[]{:S(2)}) collective-permute-start(bf16[256,2048]{1,0:T(8,128)(2,1)S(1)} %pad_maximum_fusion.10.refs_1_.refs_11_), channel_id=1, source_target_pairs={{0,4},{1,5},{2,6},{3,7},{4,0},{5,1},{6,2},{7,3},{8,12},{9,13},{10,... | collective-permute-start | bytes 3145736 | tf_op jit(solution)/shard_map/ppermute | solution.py:54
  460.2 16.2 %collective-permute-start.56 = (bf16[256,2048]{1,0:T(8,128)(2,1)S(1)}, bf16[256,2048]{1,0:T(8,128)(2,1)S(1)}, u32[]{:S(2)}, u32[]{:S(2)}) collective-permute-start(bf16[256,2048]{1,0:T(8,128)(2,1)S(1)} %pad_maximum_fusion.9.refs_0_.refs_10_), channel_id=1, source_target_pairs={{0,2},{1,3},{2,0},{3,1},{4,6},{5,7},{6,4},{7,5},{8,10},{9,11},{10,... | collective-permute-start | bytes 3145736 | tf_op jit(solution)/shard_map/ppermute | solution.py:54
  476.5 18.4 %collective-permute-start.60 = (bf16[512,2048]{1,0:T(8,128)(2,1)}, bf16[512,2048]{1,0:T(8,128)(2,1)}, u32[]{:S(2)}, u32[]{:S(2)}) collective-permute-start(bf16[512,2048]{1,0:T(8,128)(2,1)} %get-tuple-element.152), channel_id=1, source_target_pairs={{0,1},{1,0},{2,3},{3,2},{4,5},{5,4},{6,7},{7,6},{8,9},{9,8},{10,11... | collective-permute-start | bytes 6291464 | tf_op jit(solution)/shard_map/ppermute | solution.py:54
  499.4 25.4 %collective-permute-start.61 = (bf16[256,2048]{1,0:T(8,128)(2,1)}, bf16[256,2048]{1,0:T(8,128)(2,1)S(1)}, u32[]{:S(2)}, u32[]{:S(2)}) collective-permute-start(bf16[256,2048]{1,0:T(8,128)(2,1)} %get-tuple-element.200), channel_id=1, source_target_pairs={{0,2},{1,3},{2,0},{3,1},{4,6},{5,7},{6,4},{7,5},{8,10},{9,11},{10,... | collective-permute-start | bytes 3145736 | tf_op jit(solution)/shard_map/ppermute | solution.py:54
  500.0 25.1 %collective-permute-start.63 = (bf16[256,2048]{1,0:T(8,128)(2,1)}, bf16[256,2048]{1,0:T(8,128)(2,1)S(1)}, u32[]{:S(2)}, u32[]{:S(2)}) collective-permute-start(bf16[256,2048]{1,0:T(8,128)(2,1)} %get-tuple-element.201), channel_id=1, source_target_pairs={{0,4},{1,5},{2,6},{3,7},{4,0},{5,1},{6,2},{7,3},{8,12},{9,13},{10,... | collective-permute-start | bytes 3145736 | tf_op jit(solution)/shard_map/ppermute | solution.py:54
  503.9 37.6 %collective-permute-start.49 = (bf16[512,2048]{1,0:T(8,128)(2,1)}, bf16[512,2048]{1,0:T(8,128)(2,1)S(1)}, u32[]{:S(2)}, u32[]{:S(2)}) collective-permute-start(bf16[512,2048]{1,0:T(8,128)(2,1)} %get-tuple-element.149), channel_id=1, source_target_pairs={{0,1},{1,0},{2,3},{3,2},{4,5},{5,4},{6,7},{7,6},{8,9},{9,8},{10,11... | collective-permute-start | bytes 6291464 | tf_op jit(solution)/shard_map/ppermute | solution.py:54
  541.2 42.7 %collective-permute-start.67 = (bf16[512,2048]{1,0:T(8,128)(2,1)}, bf16[512,2048]{1,0:T(8,128)(2,1)}, u32[]{:S(2)}, u32[]{:S(2)}) collective-permute-start(bf16[512,2048]{1,0:T(8,128)(2,1)} %get-tuple-element.169), channel_id=1, source_target_pairs={{0,1},{1,0},{2,3},{3,2},{4,5},{5,4},{6,7},{7,6},{8,9},{9,8},{10,11... | collective-permute-start | bytes 6291464 | tf_op jit(solution)/shard_map/ppermute | solution.py:54
  543.7 40.2 %collective-permute-start.69 = (bf16[256,2048]{1,0:T(8,128)(2,1)}, bf16[256,2048]{1,0:T(8,128)(2,1)}, u32[]{:S(2)}, u32[]{:S(2)}) collective-permute-start(bf16[256,2048]{1,0:T(8,128)(2,1)} %get-tuple-element.196), channel_id=1, source_target_pairs={{0,2},{1,3},{2,0},{3,1},{4,6},{5,7},{6,4},{7,5},{8,10},{9,11},{10,... | collective-permute-start | bytes 3145736 | tf_op jit(solution)/shard_map/ppermute | solution.py:54
  545.1 38.8 %collective-permute-start.71 = (bf16[256,2048]{1,0:T(8,128)(2,1)}, bf16[256,2048]{1,0:T(8,128)(2,1)}, u32[]{:S(2)}, u32[]{:S(2)}) collective-permute-start(bf16[256,2048]{1,0:T(8,128)(2,1)} %get-tuple-element.197), channel_id=1, source_target_pairs={{0,4},{1,5},{2,6},{3,7},{4,0},{5,1},{6,2},{7,3},{8,12},{9,13},{10,... | collective-permute-start | bytes 3145736 | tf_op jit(solution)/shard_map/ppermute | solution.py:54
  549.0 32.6 %collective-permute-start.62 = (bf16[128,2048]{1,0:T(8,128)(2,1)}, bf16[128,2048]{1,0:T(8,128)(2,1)}, u32[]{:S(2)}, u32[]{:S(2)}) collective-permute-start(bf16[128,2048]{1,0:T(8,128)(2,1)} %slice.499), channel_id=1, source_target_pairs={{0,4},{1,5},{2,6},{3,7},{4,0},{5,1},{6,2},{7,3},{8,12},{9,13},{10,... | collective-permute-start | bytes 1572872 | tf_op jit(solution)/shard_map/ppermute | solution.py:54
  551.2 32.6 %collective-permute-start.64 = (bf16[128,2048]{1,0:T(8,128)(2,1)}, bf16[128,2048]{1,0:T(8,128)(2,1)}, u32[]{:S(2)}, u32[]{:S(2)}) collective-permute-start(bf16[128,2048]{1,0:T(8,128)(2,1)} %slice.498), channel_id=1, source_target_pairs={{0,2},{1,3},{2,0},{3,1},{4,6},{5,7},{6,4},{7,5},{8,10},{9,11},{10,... | collective-permute-start | bytes 1572872 | tf_op jit(solution)/shard_map/ppermute | solution.py:54
  594.6 26.1 %collective-permute-start.65 = (bf16[128,2048]{1,0:T(8,128)(2,1)}, bf16[128,2048]{1,0:T(8,128)(2,1)}, u32[]{:S(2)}, u32[]{:S(2)}) collective-permute-start(bf16[128,2048]{1,0:T(8,128)(2,1)} %pad_maximum_fusion.25), channel_id=1, source_target_pairs={{0,8},{1,9},{2,10},{3,11},{4,12},{5,13},{6,14},{7,15},{8,0},{9,1},... | collective-permute-start | bytes 1572872 | tf_op jit(solution)/shard_map/ppermute | solution.py:54
  607.1 35.8 %collective-permute-start.73 = (bf16[128,2048]{1,0:T(8,128)(2,1)}, bf16[128,2048]{1,0:T(8,128)(2,1)}, u32[]{:S(2)}, u32[]{:S(2)}) collective-permute-start(bf16[128,2048]{1,0:T(8,128)(2,1)} %pad_maximum_fusion.27), channel_id=1, source_target_pairs={{0,8},{1,9},{2,10},{3,11},{4,12},{5,13},{6,14},{7,15},{8,0},{9,1},... | collective-permute-start | bytes 1572872 | tf_op jit(solution)/shard_map/ppermute | solution.py:54
  621.9 37.2 %collective-permute-start.66 = (bf16[64,2048]{1,0:T(8,128)(2,1)S(1)}, bf16[64,2048]{1,0:T(8,128)(2,1)S(1)}, u32[]{:S(2)}, u32[]{:S(2)}) collective-permute-start(bf16[64,2048]{1,0:T(8,128)(2,1)S(1)} %slice.414), channel_id=1, source_target_pairs={{0,16},{1,17},{2,18},{3,19},{4,20},{5,21},{6,22},{7,23},{8,24},{9,... | collective-permute-start | bytes 786440 | tf_op jit(solution)/shard_map/ppermute | solution.py:54
  644.9 23.5 %collective-permute-start.74 = (bf16[64,2048]{1,0:T(8,128)(2,1)S(1)}, bf16[64,2048]{1,0:T(8,128)(2,1)S(1)}, u32[]{:S(2)}, u32[]{:S(2)}) collective-permute-start(bf16[64,2048]{1,0:T(8,128)(2,1)S(1)} %slice.426), channel_id=1, source_target_pairs={{0,16},{1,17},{2,18},{3,19},{4,20},{5,21},{6,22},{7,23},{8,24},{9,... | collective-permute-start | bytes 786440 | tf_op jit(solution)/shard_map/ppermute | solution.py:54
  647.6 25.5 %collective-permute-start.78 = (bf16[256,1536]{1,0:T(8,128)(2,1)}, bf16[256,1536]{1,0:T(8,128)(2,1)S(1)}, u32[]{:S(2)}, u32[]{:S(2)}) collective-permute-start(bf16[256,1536]{1,0:T(8,128)(2,1)} %get-tuple-element.212), channel_id=1, source_target_pairs={{0,4},{1,5},{2,6},{3,7},{4,0},{5,1},{6,2},{7,3},{8,12},{9,13},{10,... | collective-permute-start | bytes 2359304 | tf_op jit(solution)/shard_map/ppermute | solution.py:54
  649.2 34.2 %collective-permute-start.79 = (bf16[256,1536]{1,0:T(8,128)(2,1)}, bf16[256,1536]{1,0:T(8,128)(2,1)S(1)}, u32[]{:S(2)}, u32[]{:S(2)}) collective-permute-start(bf16[256,1536]{1,0:T(8,128)(2,1)} %get-tuple-element.211), channel_id=1, source_target_pairs={{0,8},{1,9},{2,10},{3,11},{4,12},{5,13},{6,14},{7,15},{8,0},{9,1},... | collective-permute-start | bytes 2359304 | tf_op jit(solution)/shard_map/ppermute | solution.py:54
  651.8 49.0 %collective-permute-start.80 = (bf16[256,1536]{1,0:T(8,128)(2,1)S(1)}, bf16[256,1536]{1,0:T(8,128)(2,1)}, u32[]{:S(2)}, u32[]{:S(2)}) collective-permute-start(bf16[256,1536]{1,0:T(8,128)(2,1)S(1)} %get-tuple-element.210), channel_id=1, source_target_pairs={{0,12},{1,13},{2,14},{3,15},{4,8},{5,9},{6,10},{7,11},{8,4},{9,5},... | collective-permute-start | bytes 2359304 | tf_op jit(solution)/shard_map/ppermute | solution.py:54
  671.5 34.3 %collective-permute-start.75 = (bf16[256,512]{1,0:T(8,128)(2,1)S(1)}, bf16[256,512]{1,0:T(8,128)(2,1)S(1)}, u32[]{:S(2)}, u32[]{:S(2)}) collective-permute-start(bf16[256,512]{1,0:T(8,128)(2,1)S(1)} %get-tuple-element.220), channel_id=1, source_target_pairs={{0,4},{1,5},{2,6},{3,7},{4,0},{5,1},{6,2},{7,3},{8,12},{9,13},{10,... | collective-permute-start | bytes 786440 | tf_op jit(solution)/shard_map/ppermute | solution.py:54
  673.1 32.6 %collective-permute-start.76 = (bf16[256,512]{1,0:T(8,128)(2,1)S(1)}, bf16[256,512]{1,0:T(8,128)(2,1)S(1)}, u32[]{:S(2)}, u32[]{:S(2)}) collective-permute-start(bf16[256,512]{1,0:T(8,128)(2,1)S(1)} %get-tuple-element.219), channel_id=1, source_target_pairs={{0,8},{1,9},{2,10},{3,11},{4,12},{5,13},{6,14},{7,15},{8,0},{9,1},... | collective-permute-start | bytes 786440 | tf_op jit(solution)/shard_map/ppermute | solution.py:54
  673.1 33.9 %collective-permute-start.77 = (bf16[256,512]{1,0:T(8,128)(2,1)S(1)}, bf16[256,512]{1,0:T(8,128)(2,1)S(1)}, u32[]{:S(2)}, u32[]{:S(2)}) collective-permute-start(bf16[256,512]{1,0:T(8,128)(2,1)S(1)} %get-tuple-element.218), channel_id=1, source_target_pairs={{0,12},{1,13},{2,14},{3,15},{4,8},{5,9},{6,10},{7,11},{8,4},{9,5},... | collective-permute-start | bytes 786440 | tf_op jit(solution)/shard_map/ppermute | solution.py:54
  (90 other events, 1112.2 us)
Sparse Core Ops, SparseCore 0:
  22.4 48.2 all-gather.4
  78.2 54.9 all-gather.6
  162.4 66.0 all-gather.8
  229.9 47.0 all-gather.10
  430.2 144.2 reduce-scatter.2
  592.7 76.7 reduce-scatter.4

commit v4 on v3

--- a/solution.py
+++ b/solution.py
@@ -189,8 +189,8 @@
     )(*pieces, weights, table)
 
 
-def row_block(keys):
-    return max(64, 256 * 2048 // keys)
+def row_block(keys, rows):
+    return max(64, rows * 2048 // keys)
 
 
 def split_rows(rows, step, width):
@@ -217,7 +217,7 @@
 
 def attend(q, k, v, weights, pos_q, pos_k, half):
     rows, keys, width = q.shape[0] // 2, k.shape[0], weights.shape[0]
-    bq = min(rows // 2, row_block(keys))
+    bq = min(rows // 2, row_block(keys, 256))
     first = half * rows // bq
     n, split, shapes = split_rows(rows, bq, width)
 
@@ -251,7 +251,7 @@
     rows, width = sum(p.shape[0] for p in tokens), weights.shape[0]
     unit = weights.shape[1] // 3
     count = len(tokens)
-    step = min(256, rows // 2)
+    step = min(512, rows // 2)
 
     def kernel(*refs):
         xs, gs = refs[:count], refs[count : 2 * count]
@@ -317,7 +317,7 @@
 def weight_grads(pairs, width):
     columns = [sides[0].shape[1] for _, sides in pairs]
     total = sum(columns)
-    block = 256
+    block = 512
     flat = []
     for pieces, sides in pairs:
         flat += list(pieces) + list(sides)
@@ -374,7 +374,7 @@
 
 def attend_back(q, do, lse, pos_q, k, v, pos_k):
     rows, keys = q.shape[0], k.shape[0]
-    bq = min(rows, row_block(keys))
+    bq = min(rows, row_block(keys, 512))
 
     def kernel(q_ref, do_ref, lse_ref, pq_ref, k_ref, v_ref, pk_ref, dq_ref, dk_ref, dv_ref):
         @pl.when(pl.program_id(0) == 0)

time: 728 us -> 722 us (level)
  transfers between devices with their start and end apart: 87 -> 87, of which waited for: 49 -> 49; matrix products, arithmetic and copies ran while one was open for 10% -> 10% of each run, Pallas kernels for 20% -> 19%
where the time goes in v4:
time: 722 us; the launch traced here: 716 us
  waiting for transfers between devices  371 us (51%)
  Pallas kernels  177 us (25%)
  starting transfers between devices  65.1 us (9%)
  other arithmetic  62.1 us (9%)
  local copies, waits for them, and re-layouts  24.2 us (3%)
  between operations  15.9 us (2%)
    ppermute x81, waiting for transfers between devices, swap(): return lax.ppermute(value, AXES, pairs)  326 us
    ppermute x81, starting transfers between devices, swap(): return lax.ppermute(value, AXES, pairs)  64.2 us
    all_gather x4, waiting for transfers between devices, to_groups(): lax.all_gather(piece, 'blk', axis=0, tiled=True, axis_index_groups=alike)  44.1 us
    pallas_call x2, Pallas kernels, feed(): call(kernel, [shape(rows, 2 * unit), shape(rows, unit)] + [shape(rows //...  36.3 us
    pallas_call x2, Pallas kernels, weight_grads(): call(kernel, shape(width, total), 'weight_grads', 2 * rows * width * tota...  31.6 us
    pallas_call x2, Pallas kernels, attend(): call(kernel, [shape(rows, HEAD_DIM), shape(rows, 1, F32)] + shapes, 'atte...  20.5 us
    pallas_call x1, Pallas kernels, attend_back(): call(kernel, [shape(rows, HEAD_DIM, F32), shape(keys, HEAD_DIM, F32), sha...  16.7 us
    pallas_call x2, Pallas kernels, back_input(): call(kernel, [shape(rows, 3 * HEAD_DIM)] + shapes, 'back_input', 6 * rows...  15.9 us
  transfers between devices with their start and end apart: 87, of which 49 were waited for; matrix products, arithmetic and copies ran while one was open for 10% of the time, Pallas kernels for 19%

profile of v4, /device:TPU:0, one launch (start us, length us, event | category | flops | bytes accessed | tf_op | source)
XLA Modules:
  0.0 715.6 jit_solution(18209387771212738221)
XLA Ops:
  8.4 4.1 collective-permute-start
  18.4 3.8 pack.3
  22.4 3.7 multiply_cosine_fusion
  31.1 8.9 %collective-permute-done.5 = bf16[64,2048]{1,0:T(8,128)(2,1)S(1)} collective-permute-done((bf16[64,2048]{1,0:T(8,128)(2,1)S(1)}, bf16[64,2048]{1,0:T(8,128)(2,1)S(1)}, u32[]{:S(2)}, u32[]{:S(2)}) %collective-permute-start.5) | collective-permute-done | bytes 262176 | tf_op jit(solution)/shard_map/ppermute | solution.py:54
  40.8 3.4 collective-permute-done.4
  44.3 17.8 %collective-permute-done.1 = bf16[128,2048]{1,0:T(8,128)(2,1)S(1)} collective-permute-done((bf16[128,2048]{1,0:T(8,128)(2,1)S(1)}, bf16[128,2048]{1,0:T(8,128)(2,1)S(1)}, u32[]{:S(2)}, u32[]{:S(2)}) %collective-permute-start.1) | collective-permute-done | bytes 524320 | tf_op jit(solution)/shard_map/ppermute | solution.py:54
  66.6 8.4 %collective-permute-done.7 = bf16[128,2048]{1,0:T(8,128)(2,1)S(1)} collective-permute-done((bf16[128,2048]{1,0:T(8,128)(2,1)S(1)}, bf16[128,2048]{1,0:T(8,128)(2,1)S(1)}, u32[]{:S(2)}, u32[]{:S(2)}) %collective-permute-start.7) | collective-permute-done | bytes 524320 | tf_op jit(solution)/shard_map/ppermute | solution.py:54
  82.4 31.5 %collective-permute-done.13 = bf16[256,1536]{1,0:T(8,128)(2,1)} collective-permute-done((bf16[256,1536]{1,0:T(8,128)(2,1)}, bf16[256,1536]{1,0:T(8,128)(2,1)}, u32[]{:S(2)}, u32[]{:S(2)}) %collective-permute-start.13) | collective-permute-done | bytes 786464 | tf_op jit(solution)/shard_map/ppermute | solution.py:54
  113.9 18.8 %collective-permute-done.11 = bf16[256,1536]{1,0:T(8,128)(2,1)} collective-permute-done((bf16[256,1536]{1,0:T(8,128)(2,1)}, bf16[256,1536]{1,0:T(8,128)(2,1)}, u32[]{:S(2)}, u32[]{:S(2)}) %collective-permute-start.11) | collective-permute-done | bytes 786464 | tf_op jit(solution)/shard_map/ppermute | solution.py:54
  132.7 3.7 collective-permute-done.12
  138.3 3.0 assemble.2.refs_8_.w_ref
  141.4 10.4 %project.1 = (bf16[2048,128]{1,0:T(8,128)(2,1)}, bf16[2048,128]{1,0:T(8,128)(2,1)}, bf16[2048,128]{1,0:T(8,128)(2,1)}) custom-call(bf16[256,2048]{1,0:T(8,128)(2,1)} %copy-done.1, bf16[256,2048]{1,0:T(8,128)(2,1)} %copy-done, bf16[256,2048]{1,0:T(8,128)(2,1)} %collective-permute-done.8.refs_2_, bf16[256,2048]{1,0:T(8,128)(2,1)} %collective-permute-done.9.refs_3_, ...), custom_call_target="tpu_custom_call" | custom-call | flops 3221225472 | bytes 8388608 | tf_op jit(solution)/shard_map/project/pallas_call | solution.py:181
  151.8 10.3 %attend.2 = (bf16[1024,128]{1,0:T(8,128)(2,1)}, f32[1024,1]{1,0:T(8,128)}, bf16[512,2048]{1,0:T(8,128)(2,1)}, bf16[512,2048]{1,0:T(8,128)(2,1)}) custom-call(bf16[2048,128]{1,0:T(8,128)(2,1)} %get-tuple-element.116.q_ref, bf16[2048,128]{1,0:T(8,128)(2,1)} %get-tuple-element.111.k_ref, bf16[2048,128]{1,0:T(8,128)(2,1)} %get-tuple-element.112.v_ref, ...), custom_call_target="tpu_custom_call" | custom-call | flops 1610612736 | bytes 4194304 | tf_op jit(solution)/shard_map/attend/pallas_call | solution.py:238
  162.3 4.1 collective-permute-done.17
  166.5 3.8 add_convert_fusion.15
  170.2 11.4 %collective-permute-done.18 = bf16[128,2048]{1,0:T(8,128)(2,1)S(1)} collective-permute-done((bf16[128,2048]{1,0:T(8,128)(2,1)S(1)}, bf16[128,2048]{1,0:T(8,128)(2,1)S(1)}, u32[]{:S(2)}, u32[]{:S(2)}) %collective-permute-start.18) | collective-permute-done | bytes 524320 | tf_op jit(solution)/shard_map/ppermute | solution.py:54
  182.4 10.2 %attend.3 = (bf16[1024,128]{1,0:T(8,128)(2,1)}, f32[1024,1]{1,0:T(8,128)}, bf16[512,2048]{1,0:T(8,128)(2,1)}, bf16[512,2048]{1,0:T(8,128)(2,1)}) custom-call(bf16[2048,128]{1,0:T(8,128)(2,1)} %get-tuple-element.116.q_ref, bf16[2048,128]{1,0:T(8,128)(2,1)} %get-tuple-element.111.k_ref, bf16[2048,128]{1,0:T(8,128)(2,1)} %get-tuple-element.112.v_ref, ...), custom_call_target="tpu_custom_call" | custom-call | flops 1610612736 | bytes 4194304 | tf_op jit(solution)/shard_map/attend/pallas_call | solution.py:238
  198.4 30.0 %all-gather.9.cloned.1.call-done.refs_1_ = bf16[512,1536]{1,0:T(8,128)(2,1)} async-done(((bf16[256,1536]{1,0:T(8,128)(2,1)}), bf16[512,1536]{1,0:T(8,128)(2,1)}) %all-gather.9.cloned.1.call-update) | async-done | bytes 1572880 | tf_op jit(solution)/shard_map/all_gather | solution.py:576
  228.5 3.3 convert_add_fusion.7
  231.9 3.1 collective-permute-start.21
  235.0 2.7 collective-permute-start.23
  237.9 9.9 %collective-permute-done.21 = bf16[128,2048]{1,0:T(8,128)(2,1)S(1)} collective-permute-done((bf16[128,2048]{1,0:T(8,128)(2,1)S(1)}, bf16[128,2048]{1,0:T(8,128)(2,1)S(1)}, u32[]{:S(2)}, u32[]{:S(2)}) %collective-permute-start.21) | collective-permute-done | bytes 524320 | tf_op jit(solution)/shard_map/ppermute | solution.py:54
  249.3 3.5 maximum_select_fusion.refs_3_
  255.9 3.1 collective-permute-done.27
  260.0 2.7 collective-permute-start.28
  262.8 14.1 %all-gather.11.cloned.1.call-done.refs_2_ = bf16[512,1536]{1,0:T(8,128)(2,1)} async-done(((bf16[256,1536]{1,0:T(8,128)(2,1)}), bf16[512,1536]{1,0:T(8,128)(2,1)}) %all-gather.11.cloned.1.call-update) | async-done | bytes 1572880 | tf_op jit(solution)/shard_map/all_gather | solution.py:576
  280.3 3.6 collective-permute-done.28.refs_4_.refs_14_
  283.8 8.5 %collective-permute-done.26 = bf16[128,2048]{1,0:T(8,128)(2,1)S(1)} collective-permute-done((bf16[128,2048]{1,0:T(8,128)(2,1)S(1)}, bf16[128,2048]{1,0:T(8,128)(2,1)S(1)}, u32[]{:S(2)}, u32[]{:S(2)}) %collective-permute-start.26) | collective-permute-done | bytes 524320 | tf_op jit(solution)/shard_map/ppermute | solution.py:54
  296.0 11.0 %collective-permute-done.34 = bf16[128,2048]{1,0:T(8,128)(2,1)S(1)} collective-permute-done((bf16[128,2048]{1,0:T(8,128)(2,1)S(1)}, bf16[128,2048]{1,0:T(8,128)(2,1)S(1)}, u32[]{:S(2)}, u32[]{:S(2)}) %collective-permute-start.34) | collective-permute-done | bytes 524320 | tf_op jit(solution)/shard_map/ppermute | solution.py:54
  311.8 5.9 assemble.3.refs_8_.w_ref
  318.8 18.3 %feed.2 = (bf16[1024,1024]{1,0:T(8,128)(2,1)}, bf16[1024,512]{1,0:T(8,128)(2,1)}, bf16[512,2048]{1,0:T(8,128)(2,1)}, bf16[512,2048]{1,0:T(8,128)(2,1)}) custom-call(bf16[256,2048]{1,0:T(8,128)(2,1)} %copy-done.40, bf16[256,2048]{1,0:T(8,128)(2,1)} %copy-done.39, bf16[256,2048]{1,0:T(8,128)(2,1)} %collective-permute-done.35.refs_2_, ...), custom_call_target="tpu_custom_call" | custom-call | flops 10737418240 | bytes 4194304 | tf_op jit(solution)/shard_map/feed/pallas_call | solution.py:281
  342.2 18.1 %feed.3 = (bf16[1024,1024]{1,0:T(8,128)(2,1)}, bf16[1024,512]{1,0:T(8,128)(2,1)}, bf16[512,2048]{1,0:T(8,128)(2,1)}, bf16[512,2048]{1,0:T(8,128)(2,1)}) custom-call(bf16[256,2048]{1,0:T(8,128)(2,1)} %copy-done.61, bf16[256,2048]{1,0:T(8,128)(2,1)} %copy-done.60, bf16[256,2048]{1,0:T(8,128)(2,1)} %copy-done.63, bf16[256,2048]{1,0:T(8,128)(2,1)} %copy-done.62, ...), custom_call_target="tpu_custom_call" | custom-call | flops 10737418240 | bytes 4194304 | tf_op jit(solution)/shard_map/feed/pallas_call | solution.py:281
  360.8 5.5 collective-permute-done.44
  366.4 3.6 add_convert_fusion.10
  371.1 19.6 %weight_grads.2 = bf16[2048,1536]{1,0:T(8,128)(2,1)} custom-call(bf16[256,2048]{1,0:T(8,128)(2,1)} %copy-done.40, bf16[256,2048]{1,0:T(8,128)(2,1)} %copy-done.39, bf16[256,2048]{1,0:T(8,128)(2,1)} %collective-permute-done.35.refs_2_, bf16[256,2048]{1,0:T(8,128)(2,1)} %collective-permute-done.36.refs_3_, bf16[256,2048]{1,0:T(8,128)(2,1)} %copy-done.61, ...), custom_call_target="tpu_custom_call" | custom-call | flops 12884901888 | bytes 14680064 | tf_op jit(solution)/shard_map/weight_grads/pallas_call | solution.py:341
  390.6 4.9 collective-permute-done.47
  395.8 3.3 convert_add_fusion.5
  401.4 7.9 %feed_out.2 = (bf16[512,2048]{1,0:T(8,128)(2,1)}, bf16[512,2048]{1,0:T(8,128)(2,1)}) custom-call(bf16[1024,512]{1,0:T(8,128)(2,1)} %get-tuple-element.142.refs_19_.hidden_ref, bf16[2048,1536]{1,0:T(8,128)(2,1)} %assemble.3.refs_8_.w_ref), custom_call_target="tpu_custom_call" | custom-call | flops 2147483648 | bytes 4194304 | tf_op jit(solution)/shard_map/feed_out/pallas_call | solution.py:302
  409.3 2.8 collective-permute-done.46
  413.9 7.9 %feed_out.3 = (bf16[512,2048]{1,0:T(8,128)(2,1)}, bf16[512,2048]{1,0:T(8,128)(2,1)}) custom-call(bf16[1024,512]{1,0:T(8,128)(2,1)} %get-tuple-element.147.refs_18_.hidden_ref, bf16[2048,1536]{1,0:T(8,128)(2,1)} %assemble.3.refs_8_.w_ref), custom_call_target="tpu_custom_call" | custom-call | flops 2147483648 | bytes 4194304 | tf_op jit(solution)/shard_map/feed_out/pallas_call | solution.py:302
  421.9 3.3 collective-permute-done.50
  427.7 15.0 %collective-permute-done.51 = bf16[128,2048]{1,0:T(8,128)(2,1)S(1)} collective-permute-done((bf16[128,2048]{1,0:T(8,128)(2,1)S(1)}, bf16[128,2048]{1,0:T(8,128)(2,1)S(1)}, u32[]{:S(2)}, u32[]{:S(2)}) %collective-permute-start.51) | collective-permute-done | bytes 524320 | tf_op jit(solution)/shard_map/ppermute | solution.py:54
  443.0 14.6 %collective-permute-done.53 = bf16[128,2048]{1,0:T(8,128)(2,1)S(1)} collective-permute-done((bf16[128,2048]{1,0:T(8,128)(2,1)S(1)}, bf16[128,2048]{1,0:T(8,128)(2,1)S(1)}, u32[]{:S(2)}, u32[]{:S(2)}) %collective-permute-start.53) | collective-permute-done | bytes 524320 | tf_op jit(solution)/shard_map/ppermute | solution.py:54
  460.1 13.3 %collective-permute-done.57.refs_5_.refs_15_ = bf16[256,2048]{1,0:T(8,128)(2,1)S(1)} collective-permute-done((bf16[256,2048]{1,0:T(8,128)(2,1)S(1)}, bf16[256,2048]{1,0:T(8,128)(2,1)S(1)}, u32[]{:S(2)}, u32[]{:S(2)}) %collective-permute-start.57) | collective-permute-done | bytes 1048608 | tf_op jit(solution)/shard_map/ppermute | solution.py:54
  475.1 5.8 collective-permute-done.55.refs_3_.refs_13_
  485.3 7.2 %back_project.1.do_ref = bf16[2048,128]{1,0:T(8,128)(2,1)} custom-call(bf16[256,2048]{1,0:T(8,128)(2,1)} %copy-done.3, bf16[256,2048]{1,0:T(8,128)(2,1)} %copy-done.2, bf16[256,2048]{1,0:T(8,128)(2,1)} %copy-done.17, bf16[256,2048]{1,0:T(8,128)(2,1)} %copy-done.16, bf16[256,2048]{1,0:T(8,128)(2,1)} %copy-done.15, bf16[256,2048]{1,0:T(8,128)(2,1)} %copy-done.14, ...), custom_call_target="tpu_custom_call" | custom-call | flops 1073741824 | bytes 8388608 | tf_op jit(solution)/shard_map/back_project/pallas_call | solution.py:364
  492.5 4.5 add_convert_fusion.7
  501.6 16.7 %attend_back.1 = (f32[2048,128]{1,0:T(8,128)}, f32[2048,128]{1,0:T(8,128)}, f32[2048,128]{1,0:T(8,128)}) custom-call(bf16[2048,128]{1,0:T(8,128)(2,1)} %get-tuple-element.116.q_ref, bf16[2048,128]{1,0:T(8,128)(2,1)} %back_project.1.do_ref, f32[2048,1]{1,0:T(8,128)} %copy.35.lse_ref, s32[2048,1]{1,0:T(8,128)} %copy.31.pq_ref, ...), custom_call_target="tpu_custom_call" | custom-call | flops 5368709120 | bytes 4194304 | tf_op jit(solution)/shard_map/attend_back/pallas_call | solution.py:400
  518.3 4.1 collective-permute-done.61
  522.9 8.1 %back_input.2 = (bf16[1024,384]{1,0:T(8,128)(2,1)}, bf16[512,2048]{1,0:T(8,128)(2,1)}, bf16[512,2048]{1,0:T(8,128)(2,1)}) custom-call(f32[2048,128]{1,0:T(8,128)} %get-tuple-element.165.dq_ref, f32[2048,128]{1,0:T(8,128)} %get-tuple-element.160.dk_ref, f32[2048,128]{1,0:T(8,128)} %get-tuple-element.161.dv_ref, f32[2048,256]{1,0:T(8,128)} %pad_maximum_fusion.refs_9_.t_ref, ...), custom_call_target="tpu_custom_call" | custom-call | flops 1610612736 | bytes 4194304 | tf_op jit(solution)/shard_map/back_input/pallas_call | solution.py:426
  531.1 7.8 %back_input.3 = (bf16[1024,384]{1,0:T(8,128)(2,1)}, bf16[512,2048]{1,0:T(8,128)(2,1)}, bf16[512,2048]{1,0:T(8,128)(2,1)}) custom-call(f32[2048,128]{1,0:T(8,128)} %get-tuple-element.165.dq_ref, f32[2048,128]{1,0:T(8,128)} %get-tuple-element.160.dk_ref, f32[2048,128]{1,0:T(8,128)} %get-tuple-element.161.dv_ref, f32[2048,256]{1,0:T(8,128)} %pad_maximum_fusion.refs_9_.t_ref, ...), custom_call_target="tpu_custom_call" | custom-call | flops 1610612736 | bytes 4194304 | tf_op jit(solution)/shard_map/back_input/pallas_call | solution.py:426
  549.6 12.0 %weight_grads.3 = bf16[2048,512]{1,0:T(8,128)(2,1)} custom-call(bf16[256,2048]{1,0:T(8,128)(2,1)} %copy-done.1, bf16[256,2048]{1,0:T(8,128)(2,1)} %copy-done, bf16[256,2048]{1,0:T(8,128)(2,1)} %collective-permute-done.8.refs_2_, bf16[256,2048]{1,0:T(8,128)(2,1)} %collective-permute-done.9.refs_3_, bf16[256,2048]{1,0:T(8,128)(2,1)} %collective-permute-done.10.refs_4_, ...), custom_call_target="tpu_custom_call" | custom-call | flops 4294967296 | bytes 10485760 | tf_op jit(solution)/shard_map/weight_grads/pallas_call | solution.py:341
  561.6 17.5 %collective-permute-done.62 = bf16[128,2048]{1,0:T(8,128)(2,1)} collective-permute-done((bf16[128,2048]{1,0:T(8,128)(2,1)}, bf16[128,2048]{1,0:T(8,128)(2,1)}, u32[]{:S(2)}, u32[]{:S(2)}) %collective-permute-start.62) | collective-permute-done | bytes 524320 | tf_op jit(solution)/shard_map/ppermute | solution.py:54
  581.7 3.3 convert_add_fusion.1
  592.3 2.7 collective-permute-start.65
  595.0 4.2 collective-permute-done.70
  607.2 11.4 %collective-permute-done.65 = bf16[128,2048]{1,0:T(8,128)(2,1)} collective-permute-done((bf16[128,2048]{1,0:T(8,128)(2,1)}, bf16[128,2048]{1,0:T(8,128)(2,1)}, u32[]{:S(2)}, u32[]{:S(2)}) %collective-permute-start.65) | collective-permute-done | bytes 524320 | tf_op jit(solution)/shard_map/ppermute | solution.py:54
  619.9 20.7 %collective-permute-done.73 = bf16[128,2048]{1,0:T(8,128)(2,1)} collective-permute-done((bf16[128,2048]{1,0:T(8,128)(2,1)}, bf16[128,2048]{1,0:T(8,128)(2,1)}, u32[]{:S(2)}, u32[]{:S(2)}) %collective-permute-start.73) | collective-permute-done | bytes 524320 | tf_op jit(solution)/shard_map/ppermute | solution.py:54
  649.6 7.3 %collective-permute-done.66 = bf16[64,2048]{1,0:T(8,128)(2,1)S(1)} collective-permute-done((bf16[64,2048]{1,0:T(8,128)(2,1)S(1)}, bf16[64,2048]{1,0:T(8,128)(2,1)S(1)}, u32[]{:S(2)}, u32[]{:S(2)}) %collective-permute-start.66) | collective-permute-done | bytes 262176 | tf_op jit(solution)/shard_map/ppermute | solution.py:54
  656.9 9.2 %collective-permute-done.74 = bf16[64,2048]{1,0:T(8,128)(2,1)S(1)} collective-permute-done((bf16[64,2048]{1,0:T(8,128)(2,1)S(1)}, bf16[64,2048]{1,0:T(8,128)(2,1)S(1)}, u32[]{:S(2)}, u32[]{:S(2)}) %collective-permute-start.74) | collective-permute-done | bytes 262176 | tf_op jit(solution)/shard_map/ppermute | solution.py:54
  674.4 6.8 collective-permute-done.79.refs_2_
  681.2 17.3 %collective-permute-done.80.refs_3_ = bf16[256,1536]{1,0:T(8,128)(2,1)} collective-permute-done((bf16[256,1536]{1,0:T(8,128)(2,1)S(1)}, bf16[256,1536]{1,0:T(8,128)(2,1)}, u32[]{:S(2)}, u32[]{:S(2)}) %collective-permute-start.80) | collective-permute-done | bytes 786464 | tf_op jit(solution)/shard_map/ppermute | solution.py:54
  698.6 5.0 unpack.3
  705.6 2.6 unpack.2
  (374 shorter events, 128.5 us)
Async XLA Ops:
  7.2 70.9 %all-gather.5.cloned.1.call-start = ((), (), s32[]{:S(2)}) async-start(), calls=%async_computation.2 | async-start | bytes 2359296 | tf_op jit(solution)/shard_map/all_gather | solution.py:576
  8.4 20.0 %collective-permute-start = (bf16[64,2048]{1,0:T(8,128)(2,1)S(1)}, bf16[64,2048]{1,0:T(8,128)(2,1)S(1)}, u32[]{:S(2)}, u32[]{:S(2)}) collective-permute-start(bf16[64,2048]{1,0:T(8,128)(2,1)S(1)} %get-tuple-element.245), channel_id=1, source_target_pairs={{0,16},{1,17},{2,18},{3,19},{4,20},{5,21},{6,22},{7,23},{8,24},{9,... | collective-permute-start | bytes 786440 | tf_op jit(solution)/shard_map/ppermute | solution.py:54
  14.7 26.1 %collective-permute-start.2 = (bf16[256,512]{1,0:T(8,128)(2,1)}, bf16[256,512]{1,0:T(8,128)(2,1)S(1)}, u32[]{:S(2)}, u32[]{:S(2)}) collective-permute-start(bf16[256,512]{1,0:T(8,128)(2,1)} %get-tuple-element.98), channel_id=1, source_target_pairs={{0,4},{1,5},{2,6},{3,7},{4,0},{5,1},{6,2},{7,3},{8,12},{9,13},{10,... | collective-permute-start | bytes 786440 | tf_op jit(solution)/shard_map/ppermute | solution.py:54
  16.2 24.6 %collective-permute-start.3 = (bf16[256,512]{1,0:T(8,128)(2,1)}, bf16[256,512]{1,0:T(8,128)(2,1)S(1)}, u32[]{:S(2)}, u32[]{:S(2)}) collective-permute-start(bf16[256,512]{1,0:T(8,128)(2,1)} %get-tuple-element.99), channel_id=1, source_target_pairs={{0,8},{1,9},{2,10},{3,11},{4,12},{5,13},{6,14},{7,15},{8,0},{9,1},... | collective-permute-start | bytes 786440 | tf_op jit(solution)/shard_map/ppermute | solution.py:54
  17.8 26.5 %collective-permute-start.4 = (bf16[256,512]{1,0:T(8,128)(2,1)}, bf16[256,512]{1,0:T(8,128)(2,1)S(1)}, u32[]{:S(2)}, u32[]{:S(2)}) collective-permute-start(bf16[256,512]{1,0:T(8,128)(2,1)} %get-tuple-element.100), channel_id=1, source_target_pairs={{0,12},{1,13},{2,14},{3,15},{4,8},{5,9},{6,10},{7,11},{8,4},{9,5},... | collective-permute-start | bytes 786440 | tf_op jit(solution)/shard_map/ppermute | solution.py:54
  18.3 21.7 %collective-permute-start.5 = (bf16[64,2048]{1,0:T(8,128)(2,1)S(1)}, bf16[64,2048]{1,0:T(8,128)(2,1)S(1)}, u32[]{:S(2)}, u32[]{:S(2)}) collective-permute-start(bf16[64,2048]{1,0:T(8,128)(2,1)S(1)} %get-tuple-element.243), channel_id=1, source_target_pairs={{0,16},{1,17},{2,18},{3,19},{4,20},{5,21},{6,22},{7,23},{8,24},{9,... | collective-permute-start | bytes 786440 | tf_op jit(solution)/shard_map/ppermute | solution.py:54
  22.3 116.1 %all-gather.7.cloned.1.call-start = ((), (), s32[]{:S(2)}) async-start(), calls=%async_computation.3 | async-start | bytes 3145728 | tf_op jit(solution)/shard_map/all_gather | solution.py:576
  29.1 32.9 %collective-permute-start.1 = (bf16[128,2048]{1,0:T(8,128)(2,1)S(1)}, bf16[128,2048]{1,0:T(8,128)(2,1)S(1)}, u32[]{:S(2)}, u32[]{:S(2)}) collective-permute-start(bf16[128,2048]{1,0:T(8,128)(2,1)S(1)} %fusion.4), channel_id=1, source_target_pairs={{0,8},{1,9},{2,10},{3,11},{4,12},{5,13},{6,14},{7,15},{8,0},{9,1},... | collective-permute-start | bytes 1572872 | tf_op jit(solution)/shard_map/ppermute | solution.py:54
  75.1 61.3 %collective-permute-start.14 = (bf16[256,2048]{1,0:T(8,128)(2,1)S(1)}, bf16[256,2048]{1,0:T(8,128)(2,1)S(1)}, u32[]{:S(2)}, u32[]{:S(2)}) collective-permute-start(bf16[256,2048]{1,0:T(8,128)(2,1)S(1)} %pad_maximum_fusion.2.refs_1_), channel_id=1, source_target_pairs={{0,4},{1,5},{2,6},{3,7},{4,0},{5,1},{6,2},{7,3},{8,12},{9,13},{10,... | collective-permute-start | bytes 3145736 | tf_op jit(solution)/shard_map/ppermute | solution.py:54
  78.1 150.4 %all-gather.9.cloned.1.call-start = ((), (), s32[]{:S(2)}) async-start(), calls=%async_computation.4 | async-start | bytes 2359296 | tf_op jit(solution)/shard_map/all_gather | solution.py:576
  78.4 58.1 %collective-permute-start.10 = (bf16[256,2048]{1,0:T(8,128)(2,1)S(1)}, bf16[256,2048]{1,0:T(8,128)(2,1)}, u32[]{:S(2)}, u32[]{:S(2)}) collective-permute-start(bf16[256,2048]{1,0:T(8,128)(2,1)S(1)} %pad_maximum_fusion.1.refs_0_), channel_id=1, source_target_pairs={{0,2},{1,3},{2,0},{3,1},{4,6},{5,7},{6,4},{7,5},{8,10},{9,11},{10,... | collective-permute-start | bytes 3145736 | tf_op jit(solution)/shard_map/ppermute | solution.py:54
  78.9 35.0 %collective-permute-start.13 = (bf16[256,1536]{1,0:T(8,128)(2,1)}, bf16[256,1536]{1,0:T(8,128)(2,1)}, u32[]{:S(2)}, u32[]{:S(2)}) collective-permute-start(bf16[256,1536]{1,0:T(8,128)(2,1)} %get-tuple-element.104), channel_id=1, source_target_pairs={{0,12},{1,13},{2,14},{3,15},{4,8},{5,9},{6,10},{7,11},{8,4},{9,5},... | collective-permute-start | bytes 2359304 | tf_op jit(solution)/shard_map/ppermute | solution.py:54
  81.2 51.5 %collective-permute-start.11 = (bf16[256,1536]{1,0:T(8,128)(2,1)}, bf16[256,1536]{1,0:T(8,128)(2,1)}, u32[]{:S(2)}, u32[]{:S(2)}) collective-permute-start(bf16[256,1536]{1,0:T(8,128)(2,1)} %get-tuple-element.102), channel_id=1, source_target_pairs={{0,4},{1,5},{2,6},{3,7},{4,0},{5,1},{6,2},{7,3},{8,12},{9,13},{10,... | collective-permute-start | bytes 2359304 | tf_op jit(solution)/shard_map/ppermute | solution.py:54
  81.6 54.8 %collective-permute-start.12 = (bf16[256,1536]{1,0:T(8,128)(2,1)}, bf16[256,1536]{1,0:T(8,128)(2,1)}, u32[]{:S(2)}, u32[]{:S(2)}) collective-permute-start(bf16[256,1536]{1,0:T(8,128)(2,1)} %get-tuple-element.103), channel_id=1, source_target_pairs={{0,8},{1,9},{2,10},{3,11},{4,12},{5,13},{6,14},{7,15},{8,0},{9,1},... | collective-permute-start | bytes 2359304 | tf_op jit(solution)/shard_map/ppermute | solution.py:54
  113.9 27.5 %collective-permute-start.9 = (bf16[256,2048]{1,0:T(8,128)(2,1)S(1)}, bf16[256,2048]{1,0:T(8,128)(2,1)}, u32[]{:S(2)}, u32[]{:S(2)}) collective-permute-start(bf16[256,2048]{1,0:T(8,128)(2,1)S(1)} %pad_maximum_fusion.2.refs_1_), channel_id=1, source_target_pairs={{0,1},{1,0},{2,3},{3,2},{4,5},{5,4},{6,7},{7,6},{8,9},{9,8},{10,11... | collective-permute-start | bytes 3145736 | tf_op jit(solution)/shard_map/ppermute | solution.py:54
  162.2 114.7 %all-gather.11.cloned.1.call-start = ((), (), s32[]{:S(2)}) async-start(), calls=%async_computation.5 | async-start | bytes 2359296 | tf_op jit(solution)/shard_map/all_gather | solution.py:576
  162.2 19.4 %collective-permute-start.18 = (bf16[128,2048]{1,0:T(8,128)(2,1)S(1)}, bf16[128,2048]{1,0:T(8,128)(2,1)S(1)}, u32[]{:S(2)}, u32[]{:S(2)}) collective-permute-start(bf16[128,2048]{1,0:T(8,128)(2,1)S(1)} %copy-done.34), channel_id=1, source_target_pairs={{0,8},{1,9},{2,10},{3,11},{4,12},{5,13},{6,14},{7,15},{8,0},{9,1},... | collective-permute-start | bytes 1572872 | tf_op jit(solution)/shard_map/ppermute | solution.py:54
  192.6 35.9 %collective-permute-start.19 = (bf16[512,2048]{1,0:T(8,128)(2,1)}, bf16[512,2048]{1,0:T(8,128)(2,1)}, u32[]{:S(2)}, u32[]{:S(2)}) collective-permute-start(bf16[512,2048]{1,0:T(8,128)(2,1)} %get-tuple-element.118), channel_id=1, source_target_pairs={{0,1},{1,0},{2,3},{3,2},{4,5},{5,4},{6,7},{7,6},{8,9},{9,8},{10,11... | collective-permute-start | bytes 6291464 | tf_op jit(solution)/shard_map/ppermute | solution.py:54
  192.7 56.6 %collective-permute-start.25 = (bf16[256,1536]{1,0:T(8,128)(2,1)}, bf16[256,1536]{1,0:T(8,128)(2,1)}, u32[]{:S(2)}, u32[]{:S(2)}) collective-permute-start(bf16[256,1536]{1,0:T(8,128)(2,1)} %collective-permute-done.13), channel_id=1, source_target_pairs={{0,16},{1,17},{2,18},{3,19},{4,20},{5,21},{6,22},{7,23},{8,24},{9,... | collective-permute-start | bytes 2359304 | tf_op jit(solution)/shard_map/ppermute | solution.py:54
  192.8 397.4 %reduce-scatter.3.cloned.1.call-start = ((), (), s32[]{:S(2)}) async-start(), calls=%async_computation.6 | async-start | bytes 9437184 | tf_op jit(solution)/shard_map/reduce_scatter | solution.py:595
  193.3 35.2 %collective-permute-start.22 = (bf16[256,2048]{1,0:T(8,128)(2,1)}, bf16[256,2048]{1,0:T(8,128)(2,1)}, u32[]{:S(2)}, u32[]{:S(2)}) collective-permute-start(bf16[256,2048]{1,0:T(8,128)(2,1)} %get-tuple-element.209), channel_id=1, source_target_pairs={{0,4},{1,5},{2,6},{3,7},{4,0},{5,1},{6,2},{7,3},{8,12},{9,13},{10,... | collective-permute-start | bytes 3145736 | tf_op jit(solution)/shard_map/ppermute | solution.py:54
  193.4 35.1 %collective-permute-start.20 = (bf16[256,2048]{1,0:T(8,128)(2,1)}, bf16[256,2048]{1,0:T(8,128)(2,1)}, u32[]{:S(2)}, u32[]{:S(2)}) collective-permute-start(bf16[256,2048]{1,0:T(8,128)(2,1)} %get-tuple-element.208), channel_id=1, source_target_pairs={{0,2},{1,3},{2,0},{3,1},{4,6},{5,7},{6,4},{7,5},{8,10},{9,11},{10,... | collective-permute-start | bytes 3145736 | tf_op jit(solution)/shard_map/ppermute | solution.py:54
  196.5 56.3 %collective-permute-start.29 = (bf16[128,2048]{1,0:T(8,128)(2,1)}, bf16[128,2048]{1,0:T(8,128)(2,1)}, u32[]{:S(2)}, u32[]{:S(2)}) collective-permute-start(bf16[128,2048]{1,0:T(8,128)(2,1)} %pad_maximum_fusion.19), channel_id=1, source_target_pairs={{0,2},{1,3},{2,0},{3,1},{4,6},{5,7},{6,4},{7,5},{8,10},{9,11},{10,... | collective-permute-start | bytes 1572872 | tf_op jit(solution)/shard_map/ppermute | solution.py:54
  231.9 15.9 %collective-permute-start.21 = (bf16[128,2048]{1,0:T(8,128)(2,1)S(1)}, bf16[128,2048]{1,0:T(8,128)(2,1)S(1)}, u32[]{:S(2)}, u32[]{:S(2)}) collective-permute-start(bf16[128,2048]{1,0:T(8,128)(2,1)S(1)} %fusion.19), channel_id=1, source_target_pairs={{0,4},{1,5},{2,6},{3,7},{4,0},{5,1},{6,2},{7,3},{8,12},{9,13},{10,... | collective-permute-start | bytes 1572872 | tf_op jit(solution)/shard_map/ppermute | solution.py:54
  235.0 13.9 %collective-permute-start.23 = (bf16[128,2048]{1,0:T(8,128)(2,1)S(1)}, bf16[128,2048]{1,0:T(8,128)(2,1)S(1)}, u32[]{:S(2)}, u32[]{:S(2)}) collective-permute-start(bf16[128,2048]{1,0:T(8,128)(2,1)S(1)} %fusion.18), channel_id=1, source_target_pairs={{0,2},{1,3},{2,0},{3,1},{4,6},{5,7},{6,4},{7,5},{8,10},{9,11},{10,... | collective-permute-start | bytes 1572872 | tf_op jit(solution)/shard_map/ppermute | solution.py:54
  237.8 21.2 %collective-permute-start.27 = (bf16[128,2048]{1,0:T(8,128)(2,1)S(1)}, bf16[128,2048]{1,0:T(8,128)(2,1)S(1)}, u32[]{:S(2)}, u32[]{:S(2)}) collective-permute-start(bf16[128,2048]{1,0:T(8,128)(2,1)S(1)} %pad_maximum_fusion.18), channel_id=1, source_target_pairs={{0,4},{1,5},{2,6},{3,7},{4,0},{5,1},{6,2},{7,3},{8,12},{9,13},{10,... | collective-permute-start | bytes 1572872 | tf_op jit(solution)/shard_map/ppermute | solution.py:54
  249.2 28.4 %collective-permute-start.24 = (bf16[128,2048]{1,0:T(8,128)(2,1)S(1)}, bf16[128,2048]{1,0:T(8,128)(2,1)}, u32[]{:S(2)}, u32[]{:S(2)}) collective-permute-start(bf16[128,2048]{1,0:T(8,128)(2,1)S(1)} %pad_maximum_fusion.17), channel_id=1, source_target_pairs={{0,8},{1,9},{2,10},{3,11},{4,12},{5,13},{6,14},{7,15},{8,0},{9,1},... | collective-permute-start | bytes 1572872 | tf_op jit(solution)/shard_map/ppermute | solution.py:54
  254.9 25.4 %collective-permute-start.30 = (bf16[256,2048]{1,0:T(8,128)(2,1)}, bf16[256,2048]{1,0:T(8,128)(2,1)}, u32[]{:S(2)}, u32[]{:S(2)}) collective-permute-start(bf16[256,2048]{1,0:T(8,128)(2,1)} %pad_maximum_fusion.5.refs_5_.refs_11_), channel_id=1, source_target_pairs={{0,4},{1,5},{2,6},{3,7},{4,0},{5,1},{6,2},{7,3},{8,12},{9,13},{10,... | collective-permute-start | bytes 3145736 | tf_op jit(solution)/shard_map/ppermute | solution.py:54
  260.0 23.8 %collective-permute-start.28 = (bf16[256,2048]{1,0:T(8,128)(2,1)}, bf16[256,2048]{1,0:T(8,128)(2,1)}, u32[]{:S(2)}, u32[]{:S(2)}) collective-permute-start(bf16[256,2048]{1,0:T(8,128)(2,1)} %pad_maximum_fusion.4.refs_4_.refs_10_), channel_id=1, source_target_pairs={{0,2},{1,3},{2,0},{3,1},{4,6},{5,7},{6,4},{7,5},{8,10},{9,11},{10,... | collective-permute-start | bytes 3145736 | tf_op jit(solution)/shard_map/ppermute | solution.py:54
  292.5 14.5 %collective-permute-start.33 = (bf16[256,2048]{1,0:T(8,128)(2,1)}, bf16[256,2048]{1,0:T(8,128)(2,1)S(1)}, u32[]{:S(2)}, u32[]{:S(2)}) collective-permute-start(bf16[256,2048]{1,0:T(8,128)(2,1)} %collective-permute-done.30.refs_5_.refs_15_), channel_id=1, source_target_pairs={{0,1},{1,0},{2,3},{3,2},{4,5},{5,4},{6,7},{7,6},{8,9},{9,8},{10,11... | collective-permute-start | bytes 3145736 | tf_op jit(solution)/shard_map/ppermute | solution.py:54
  292.6 14.4 %collective-permute-start.32 = (bf16[256,2048]{1,0:T(8,128)(2,1)}, bf16[256,2048]{1,0:T(8,128)(2,1)S(1)}, u32[]{:S(2)}, u32[]{:S(2)}) collective-permute-start(bf16[256,2048]{1,0:T(8,128)(2,1)} %collective-permute-done.28.refs_4_.refs_14_), channel_id=1, source_target_pairs={{0,1},{1,0},{2,3},{3,2},{4,5},{5,4},{6,7},{7,6},{8,9},{9,8},{10,11... | collective-permute-start | bytes 3145736 | tf_op jit(solution)/shard_map/ppermute | solution.py:54
  293.1 13.9 %collective-permute-start.34 = (bf16[128,2048]{1,0:T(8,128)(2,1)S(1)}, bf16[128,2048]{1,0:T(8,128)(2,1)S(1)}, u32[]{:S(2)}, u32[]{:S(2)}) collective-permute-start(bf16[128,2048]{1,0:T(8,128)(2,1)S(1)} %pad_maximum_fusion.21), channel_id=1, source_target_pairs={{0,2},{1,3},{2,0},{3,1},{4,6},{5,7},{6,4},{7,5},{8,10},{9,11},{10,... | collective-permute-start | bytes 1572872 | tf_op jit(solution)/shard_map/ppermute | solution.py:54
  294.6 13.6 %collective-permute-start.31 = (bf16[128,2048]{1,0:T(8,128)(2,1)S(1)}, bf16[128,2048]{1,0:T(8,128)(2,1)S(1)}, u32[]{:S(2)}, u32[]{:S(2)}) collective-permute-start(bf16[128,2048]{1,0:T(8,128)(2,1)S(1)} %pad_maximum_fusion.20), channel_id=1, source_target_pairs={{0,4},{1,5},{2,6},{3,7},{4,0},{5,1},{6,2},{7,3},{8,12},{9,13},{10,... | collective-permute-start | bytes 1572872 | tf_op jit(solution)/shard_map/ppermute | solution.py:54
  296.0 14.3 %collective-permute-start.38 = (bf16[256,2048]{1,0:T(8,128)(2,1)}, bf16[256,2048]{1,0:T(8,128)(2,1)S(1)}, u32[]{:S(2)}, u32[]{:S(2)}) collective-permute-start(bf16[256,2048]{1,0:T(8,128)(2,1)} %pad_maximum_fusion.5.refs_5_.refs_11_), channel_id=1, source_target_pairs={{0,1},{1,0},{2,3},{3,2},{4,5},{5,4},{6,7},{7,6},{8,9},{9,8},{10,11... | collective-permute-start | bytes 3145736 | tf_op jit(solution)/shard_map/ppermute | solution.py:54
  308.8 28.2 %collective-permute-start.41 = (bf16[256,2048]{1,0:T(8,128)(2,1)S(1)}, bf16[256,2048]{1,0:T(8,128)(2,1)S(1)}, u32[]{:S(2)}, u32[]{:S(2)}) collective-permute-start(bf16[256,2048]{1,0:T(8,128)(2,1)S(1)} %pad_maximum_fusion.7.refs_1_), channel_id=1, source_target_pairs={{0,4},{1,5},{2,6},{3,7},{4,0},{5,1},{6,2},{7,3},{8,12},{9,13},{10,... | collective-permute-start | bytes 3145736 | tf_op jit(solution)/shard_map/ppermute | solution.py:54
  310.3 26.8 %collective-permute-start.40 = (bf16[256,2048]{1,0:T(8,128)(2,1)S(1)}, bf16[256,2048]{1,0:T(8,128)(2,1)S(1)}, u32[]{:S(2)}, u32[]{:S(2)}) collective-permute-start(bf16[256,2048]{1,0:T(8,128)(2,1)S(1)} %pad_maximum_fusion.6.refs_0_), channel_id=1, source_target_pairs={{0,2},{1,3},{2,0},{3,1},{4,6},{5,7},{6,4},{7,5},{8,10},{9,11},{10,... | collective-permute-start | bytes 3145736 | tf_op jit(solution)/shard_map/ppermute | solution.py:54
  360.5 35.3 %collective-permute-start.39 = (bf16[512,2048]{1,0:T(8,128)(2,1)}, bf16[512,2048]{1,0:T(8,128)(2,1)}, u32[]{:S(2)}, u32[]{:S(2)}) collective-permute-start(bf16[512,2048]{1,0:T(8,128)(2,1)} %get-tuple-element.131), channel_id=1, source_target_pairs={{0,1},{1,0},{2,3},{3,2},{4,5},{5,4},{6,7},{7,6},{8,9},{9,8},{10,11... | collective-permute-start | bytes 6291464 | tf_op jit(solution)/shard_map/ppermute | solution.py:54
  370.0 25.5 %collective-permute-start.47 = (bf16[256,2048]{1,0:T(8,128)(2,1)}, bf16[256,2048]{1,0:T(8,128)(2,1)}, u32[]{:S(2)}, u32[]{:S(2)}) collective-permute-start(bf16[256,2048]{1,0:T(8,128)(2,1)} %get-tuple-element.205), channel_id=1, source_target_pairs={{0,4},{1,5},{2,6},{3,7},{4,0},{5,1},{6,2},{7,3},{8,12},{9,13},{10,... | collective-permute-start | bytes 3145736 | tf_op jit(solution)/shard_map/ppermute | solution.py:54
  370.5 25.2 %collective-permute-start.45 = (bf16[256,2048]{1,0:T(8,128)(2,1)}, bf16[256,2048]{1,0:T(8,128)(2,1)}, u32[]{:S(2)}, u32[]{:S(2)}) collective-permute-start(bf16[256,2048]{1,0:T(8,128)(2,1)} %get-tuple-element.204), channel_id=1, source_target_pairs={{0,2},{1,3},{2,0},{3,1},{4,6},{5,7},{6,4},{7,5},{8,10},{9,11},{10,... | collective-permute-start | bytes 3145736 | tf_op jit(solution)/shard_map/ppermute | solution.py:54
  427.3 15.5 %collective-permute-start.51 = (bf16[128,2048]{1,0:T(8,128)(2,1)S(1)}, bf16[128,2048]{1,0:T(8,128)(2,1)S(1)}, u32[]{:S(2)}, u32[]{:S(2)}) collective-permute-start(bf16[128,2048]{1,0:T(8,128)(2,1)S(1)} %get-tuple-element.190), channel_id=1, source_target_pairs={{0,8},{1,9},{2,10},{3,11},{4,12},{5,13},{6,14},{7,15},{8,0},{9,1},... | collective-permute-start | bytes 1572872 | tf_op jit(solution)/shard_map/ppermute | solution.py:54
  427.6 239.7 %reduce-scatter.5.cloned.1.call-start = ((), (), s32[]{:S(2)}) async-start(), calls=%async_computation.7 | async-start | bytes 3145728 | tf_op jit(solution)/shard_map/reduce_scatter | solution.py:595
  442.8 14.8 %collective-permute-start.53 = (bf16[128,2048]{1,0:T(8,128)(2,1)S(1)}, bf16[128,2048]{1,0:T(8,128)(2,1)S(1)}, u32[]{:S(2)}, u32[]{:S(2)}) collective-permute-start(bf16[128,2048]{1,0:T(8,128)(2,1)S(1)} %pad_maximum_fusion.24), channel_id=1, source_target_pairs={{0,2},{1,3},{2,0},{3,1},{4,6},{5,7},{6,4},{7,5},{8,10},{9,11},{10,... | collective-permute-start | bytes 1572872 | tf_op jit(solution)/shard_map/ppermute | solution.py:54
  442.9 14.9 %collective-permute-start.52 = (bf16[128,2048]{1,0:T(8,128)(2,1)S(1)}, bf16[128,2048]{1,0:T(8,128)(2,1)S(1)}, u32[]{:S(2)}, u32[]{:S(2)}) collective-permute-start(bf16[128,2048]{1,0:T(8,128)(2,1)S(1)} %pad_maximum_fusion.23), channel_id=1, source_target_pairs={{0,4},{1,5},{2,6},{3,7},{4,0},{5,1},{6,2},{7,3},{8,12},{9,13},{10,... | collective-permute-start | bytes 1572872 | tf_op jit(solution)/shard_map/ppermute | solution.py:54
  457.7 15.6 %collective-permute-start.57 = (bf16[256,2048]{1,0:T(8,128)(2,1)S(1)}, bf16[256,2048]{1,0:T(8,128)(2,1)S(1)}, u32[]{:S(2)}, u32[]{:S(2)}) collective-permute-start(bf16[256,2048]{1,0:T(8,128)(2,1)S(1)} %pad_maximum_fusion.10.refs_1_.refs_11_), channel_id=1, source_target_pairs={{0,4},{1,5},{2,6},{3,7},{4,0},{5,1},{6,2},{7,3},{8,12},{9,13},{10,... | collective-permute-start | bytes 3145736 | tf_op jit(solution)/shard_map/ppermute | solution.py:54
  458.0 16.1 %collective-permute-start.56 = (bf16[256,2048]{1,0:T(8,128)(2,1)S(1)}, bf16[256,2048]{1,0:T(8,128)(2,1)S(1)}, u32[]{:S(2)}, u32[]{:S(2)}) collective-permute-start(bf16[256,2048]{1,0:T(8,128)(2,1)S(1)} %pad_maximum_fusion.9.refs_0_.refs_10_), channel_id=1, source_target_pairs={{0,2},{1,3},{2,0},{3,1},{4,6},{5,7},{6,4},{7,5},{8,10},{9,11},{10,... | collective-permute-start | bytes 3145736 | tf_op jit(solution)/shard_map/ppermute | solution.py:54
  474.1 18.4 %collective-permute-start.60 = (bf16[512,2048]{1,0:T(8,128)(2,1)}, bf16[512,2048]{1,0:T(8,128)(2,1)}, u32[]{:S(2)}, u32[]{:S(2)}) collective-permute-start(bf16[512,2048]{1,0:T(8,128)(2,1)} %get-tuple-element.152), channel_id=1, source_target_pairs={{0,1},{1,0},{2,3},{3,2},{4,5},{5,4},{6,7},{7,6},{8,9},{9,8},{10,11... | collective-permute-start | bytes 6291464 | tf_op jit(solution)/shard_map/ppermute | solution.py:54
  497.0 25.4 %collective-permute-start.61 = (bf16[256,2048]{1,0:T(8,128)(2,1)}, bf16[256,2048]{1,0:T(8,128)(2,1)S(1)}, u32[]{:S(2)}, u32[]{:S(2)}) collective-permute-start(bf16[256,2048]{1,0:T(8,128)(2,1)} %get-tuple-element.200), channel_id=1, source_target_pairs={{0,2},{1,3},{2,0},{3,1},{4,6},{5,7},{6,4},{7,5},{8,10},{9,11},{10,... | collective-permute-start | bytes 3145736 | tf_op jit(solution)/shard_map/ppermute | solution.py:54
  497.8 25.1 %collective-permute-start.63 = (bf16[256,2048]{1,0:T(8,128)(2,1)}, bf16[256,2048]{1,0:T(8,128)(2,1)S(1)}, u32[]{:S(2)}, u32[]{:S(2)}) collective-permute-start(bf16[256,2048]{1,0:T(8,128)(2,1)} %get-tuple-element.201), channel_id=1, source_target_pairs={{0,4},{1,5},{2,6},{3,7},{4,0},{5,1},{6,2},{7,3},{8,12},{9,13},{10,... | collective-permute-start | bytes 3145736 | tf_op jit(solution)/shard_map/ppermute | solution.py:54
  501.6 37.7 %collective-permute-start.49 = (bf16[512,2048]{1,0:T(8,128)(2,1)}, bf16[512,2048]{1,0:T(8,128)(2,1)S(1)}, u32[]{:S(2)}, u32[]{:S(2)}) collective-permute-start(bf16[512,2048]{1,0:T(8,128)(2,1)} %get-tuple-element.149), channel_id=1, source_target_pairs={{0,1},{1,0},{2,3},{3,2},{4,5},{5,4},{6,7},{7,6},{8,9},{9,8},{10,11... | collective-permute-start | bytes 6291464 | tf_op jit(solution)/shard_map/ppermute | solution.py:54
  538.9 42.5 %collective-permute-start.67 = (bf16[512,2048]{1,0:T(8,128)(2,1)}, bf16[512,2048]{1,0:T(8,128)(2,1)}, u32[]{:S(2)}, u32[]{:S(2)}) collective-permute-start(bf16[512,2048]{1,0:T(8,128)(2,1)} %get-tuple-element.169), channel_id=1, source_target_pairs={{0,1},{1,0},{2,3},{3,2},{4,5},{5,4},{6,7},{7,6},{8,9},{9,8},{10,11... | collective-permute-start | bytes 6291464 | tf_op jit(solution)/shard_map/ppermute | solution.py:54
  541.4 40.0 %collective-permute-start.69 = (bf16[256,2048]{1,0:T(8,128)(2,1)}, bf16[256,2048]{1,0:T(8,128)(2,1)}, u32[]{:S(2)}, u32[]{:S(2)}) collective-permute-start(bf16[256,2048]{1,0:T(8,128)(2,1)} %get-tuple-element.196), channel_id=1, source_target_pairs={{0,2},{1,3},{2,0},{3,1},{4,6},{5,7},{6,4},{7,5},{8,10},{9,11},{10,... | collective-permute-start | bytes 3145736 | tf_op jit(solution)/shard_map/ppermute | solution.py:54
  542.7 38.8 %collective-permute-start.71 = (bf16[256,2048]{1,0:T(8,128)(2,1)}, bf16[256,2048]{1,0:T(8,128)(2,1)}, u32[]{:S(2)}, u32[]{:S(2)}) collective-permute-start(bf16[256,2048]{1,0:T(8,128)(2,1)} %get-tuple-element.197), channel_id=1, source_target_pairs={{0,4},{1,5},{2,6},{3,7},{4,0},{5,1},{6,2},{7,3},{8,12},{9,13},{10,... | collective-permute-start | bytes 3145736 | tf_op jit(solution)/shard_map/ppermute | solution.py:54
  546.6 32.5 %collective-permute-start.62 = (bf16[128,2048]{1,0:T(8,128)(2,1)}, bf16[128,2048]{1,0:T(8,128)(2,1)}, u32[]{:S(2)}, u32[]{:S(2)}) collective-permute-start(bf16[128,2048]{1,0:T(8,128)(2,1)} %slice.499), channel_id=1, source_target_pairs={{0,4},{1,5},{2,6},{3,7},{4,0},{5,1},{6,2},{7,3},{8,12},{9,13},{10,... | collective-permute-start | bytes 1572872 | tf_op jit(solution)/shard_map/ppermute | solution.py:54
  548.8 32.6 %collective-permute-start.64 = (bf16[128,2048]{1,0:T(8,128)(2,1)}, bf16[128,2048]{1,0:T(8,128)(2,1)}, u32[]{:S(2)}, u32[]{:S(2)}) collective-permute-start(bf16[128,2048]{1,0:T(8,128)(2,1)} %slice.498), channel_id=1, source_target_pairs={{0,2},{1,3},{2,0},{3,1},{4,6},{5,7},{6,4},{7,5},{8,10},{9,11},{10,... | collective-permute-start | bytes 1572872 | tf_op jit(solution)/shard_map/ppermute | solution.py:54
  592.3 26.2 %collective-permute-start.65 = (bf16[128,2048]{1,0:T(8,128)(2,1)}, bf16[128,2048]{1,0:T(8,128)(2,1)}, u32[]{:S(2)}, u32[]{:S(2)}) collective-permute-start(bf16[128,2048]{1,0:T(8,128)(2,1)} %pad_maximum_fusion.25), channel_id=1, source_target_pairs={{0,8},{1,9},{2,10},{3,11},{4,12},{5,13},{6,14},{7,15},{8,0},{9,1},... | collective-permute-start | bytes 1572872 | tf_op jit(solution)/shard_map/ppermute | solution.py:54
  604.6 36.0 %collective-permute-start.73 = (bf16[128,2048]{1,0:T(8,128)(2,1)}, bf16[128,2048]{1,0:T(8,128)(2,1)}, u32[]{:S(2)}, u32[]{:S(2)}) collective-permute-start(bf16[128,2048]{1,0:T(8,128)(2,1)} %pad_maximum_fusion.27), channel_id=1, source_target_pairs={{0,8},{1,9},{2,10},{3,11},{4,12},{5,13},{6,14},{7,15},{8,0},{9,1},... | collective-permute-start | bytes 1572872 | tf_op jit(solution)/shard_map/ppermute | solution.py:54
  619.8 37.2 %collective-permute-start.66 = (bf16[64,2048]{1,0:T(8,128)(2,1)S(1)}, bf16[64,2048]{1,0:T(8,128)(2,1)S(1)}, u32[]{:S(2)}, u32[]{:S(2)}) collective-permute-start(bf16[64,2048]{1,0:T(8,128)(2,1)S(1)} %slice.414), channel_id=1, source_target_pairs={{0,16},{1,17},{2,18},{3,19},{4,20},{5,21},{6,22},{7,23},{8,24},{9,... | collective-permute-start | bytes 786440 | tf_op jit(solution)/shard_map/ppermute | solution.py:54
  642.7 23.4 %collective-permute-start.74 = (bf16[64,2048]{1,0:T(8,128)(2,1)S(1)}, bf16[64,2048]{1,0:T(8,128)(2,1)S(1)}, u32[]{:S(2)}, u32[]{:S(2)}) collective-permute-start(bf16[64,2048]{1,0:T(8,128)(2,1)S(1)} %slice.426), channel_id=1, source_target_pairs={{0,16},{1,17},{2,18},{3,19},{4,20},{5,21},{6,22},{7,23},{8,24},{9,... | collective-permute-start | bytes 786440 | tf_op jit(solution)/shard_map/ppermute | solution.py:54
  645.4 25.5 %collective-permute-start.78 = (bf16[256,1536]{1,0:T(8,128)(2,1)}, bf16[256,1536]{1,0:T(8,128)(2,1)S(1)}, u32[]{:S(2)}, u32[]{:S(2)}) collective-permute-start(bf16[256,1536]{1,0:T(8,128)(2,1)} %get-tuple-element.212), channel_id=1, source_target_pairs={{0,4},{1,5},{2,6},{3,7},{4,0},{5,1},{6,2},{7,3},{8,12},{9,13},{10,... | collective-permute-start | bytes 2359304 | tf_op jit(solution)/shard_map/ppermute | solution.py:54
  647.0 34.2 %collective-permute-start.79 = (bf16[256,1536]{1,0:T(8,128)(2,1)}, bf16[256,1536]{1,0:T(8,128)(2,1)S(1)}, u32[]{:S(2)}, u32[]{:S(2)}) collective-permute-start(bf16[256,1536]{1,0:T(8,128)(2,1)} %get-tuple-element.211), channel_id=1, source_target_pairs={{0,8},{1,9},{2,10},{3,11},{4,12},{5,13},{6,14},{7,15},{8,0},{9,1},... | collective-permute-start | bytes 2359304 | tf_op jit(solution)/shard_map/ppermute | solution.py:54
  649.6 48.9 %collective-permute-start.80 = (bf16[256,1536]{1,0:T(8,128)(2,1)S(1)}, bf16[256,1536]{1,0:T(8,128)(2,1)}, u32[]{:S(2)}, u32[]{:S(2)}) collective-permute-start(bf16[256,1536]{1,0:T(8,128)(2,1)S(1)} %get-tuple-element.210), channel_id=1, source_target_pairs={{0,12},{1,13},{2,14},{3,15},{4,8},{5,9},{6,10},{7,11},{8,4},{9,5},... | collective-permute-start | bytes 2359304 | tf_op jit(solution)/shard_map/ppermute | solution.py:54
  669.2 34.3 %collective-permute-start.75 = (bf16[256,512]{1,0:T(8,128)(2,1)S(1)}, bf16[256,512]{1,0:T(8,128)(2,1)S(1)}, u32[]{:S(2)}, u32[]{:S(2)}) collective-permute-start(bf16[256,512]{1,0:T(8,128)(2,1)S(1)} %get-tuple-element.220), channel_id=1, source_target_pairs={{0,4},{1,5},{2,6},{3,7},{4,0},{5,1},{6,2},{7,3},{8,12},{9,13},{10,... | collective-permute-start | bytes 786440 | tf_op jit(solution)/shard_map/ppermute | solution.py:54
  670.9 32.7 %collective-permute-start.76 = (bf16[256,512]{1,0:T(8,128)(2,1)S(1)}, bf16[256,512]{1,0:T(8,128)(2,1)S(1)}, u32[]{:S(2)}, u32[]{:S(2)}) collective-permute-start(bf16[256,512]{1,0:T(8,128)(2,1)S(1)} %get-tuple-element.219), channel_id=1, source_target_pairs={{0,8},{1,9},{2,10},{3,11},{4,12},{5,13},{6,14},{7,15},{8,0},{9,1},... | collective-permute-start | bytes 786440 | tf_op jit(solution)/shard_map/ppermute | solution.py:54
  670.9 34.0 %collective-permute-start.77 = (bf16[256,512]{1,0:T(8,128)(2,1)S(1)}, bf16[256,512]{1,0:T(8,128)(2,1)S(1)}, u32[]{:S(2)}, u32[]{:S(2)}) collective-permute-start(bf16[256,512]{1,0:T(8,128)(2,1)S(1)} %get-tuple-element.218), channel_id=1, source_target_pairs={{0,12},{1,13},{2,14},{3,15},{4,8},{5,9},{6,10},{7,11},{8,4},{9,5},... | collective-permute-start | bytes 786440 | tf_op jit(solution)/shard_map/ppermute | solution.py:54
  (90 other events, 1114.1 us)
Sparse Core Ops, SparseCore 0:
  22.4 48.2 all-gather.4
  78.2 54.9 all-gather.6
  162.3 66.1 all-gather.8
  229.9 46.9 all-gather.10
  427.7 144.2 reduce-scatter.2
  590.4 76.8 reduce-scatter.4

commit v5 on v4

--- a/solution.py
+++ b/solution.py
@@ -372,20 +372,26 @@
     )(*pieces, weights)
 
 
-def attend_back(q, do, lse, pos_q, k, v, pos_k):
+def attend_back(q, dos, lses, pos_q, k, v, pos_k):
     rows, keys = q.shape[0], k.shape[0]
-    bq = min(rows, row_block(keys, 512))
-
-    def kernel(q_ref, do_ref, lse_ref, pq_ref, k_ref, v_ref, pk_ref, dq_ref, dk_ref, dv_ref):
+    bq = min(rows // 2, row_block(keys, 512))
+    n = rows // 2 // bq
+
+    def kernel(q_ref, *refs):
+        do0, do1, lse0, lse1, pq_ref, k_ref, v_ref, pk_ref, dq_ref, dk_ref, dv_ref = refs
+        near = pl.program_id(0) < n
+
         @pl.when(pl.program_id(0) == 0)
         def _():
             dk_ref[...] = jnp.zeros_like(dk_ref)
             dv_ref[...] = jnp.zeros_like(dv_ref)
 
-        q, k, v, do = q_ref[...], k_ref[...], v_ref[...], do_ref[...]
+        q, k, v = q_ref[...], k_ref[...], v_ref[...]
+        do = jnp.where(near, do0[...], do1[...])
+        lse = jnp.where(near, lse0[...], lse1[...])
         scores = dot(q, k, NT)
         probs = jnp.where(
-            pk_ref[...] <= pq_ref[...], jnp.exp(scores * SCALE - lse_ref[...]), 0.0
+            pk_ref[...] <= pq_ref[...], jnp.exp(scores * SCALE - lse), 0.0
         )
         dots = dot(do, v, NT)
         delta = jnp.sum(probs * dots, axis=-1, keepdims=True)
@@ -395,6 +401,10 @@
         dv_ref[...] += dot(probs.astype(BF16), do, TN)
 
     row = lambda w: pl.BlockSpec((bq, w), lambda i: (i, 0))
+    halves = lambda w: [
+        pl.BlockSpec((bq, w), lambda i: (jnp.minimum(i, n - 1), 0)),
+        pl.BlockSpec((bq, w), lambda i: (jnp.maximum(i - n, 0), 0)),
+    ]
     whole = lambda s: pl.BlockSpec(s, lambda i: (0, 0))
     kv = whole((keys, HEAD_DIM))
     return call(
@@ -404,9 +414,9 @@
         10 * rows * keys * HEAD_DIM,
         16 * rows * HEAD_DIM,
         grid=(rows // bq,),
-        in_specs=[row(HEAD_DIM), row(HEAD_DIM), row(1), row(1), kv, kv, whole((1, keys))],
+        in_specs=[row(HEAD_DIM)] + halves(HEAD_DIM) + halves(1) + [row(1), kv, kv, whole((1, keys))],
         out_specs=[row(HEAD_DIM), kv, kv],
-    )(q, do, lse, pos_q, k, v, pos_k)
+    )(q, *dos, *lses, pos_q, k, v, pos_k)
 
 
 def back_input(dq, dk, dv, table, weights, half):
@@ -690,12 +700,18 @@
     back_attn = turned[0] + turned[1]
 
     finishing = Scatter(*(after(o, *turned[1][:2]) for o in out1))
-    back_attended = back_project(back_attn, w_attn)
-    finishing.open(back_attended)
+    back_near = back_project(turned[0], w_attn)
+    back_far = back_project([after(turned[1][0], back_near)] + turned[1][1:], w_attn)
+    finishing.open(back_far)
     finishing.near(*out0)
-    lse = jnp.concatenate([lse0, lse1], axis=0)
     back_q, back_k, back_v = attend_back(
-        query, after(back_attended, *finishing.far), lse, pos_q, keys, values, pos_k
+        query,
+        (back_near, after(back_far, *finishing.far)),
+        (lse0, lse1),
+        pos_q,
+        keys,
+        values,
+        pos_k,
     )
     finishing.take_near(back_q)
     finishing.take()

time: 722 us -> 719 us (level)
  local copies, waits for them, and re-layouts: 24.2 us -> 16.3 us
  transfers between devices with their start and end apart: 87 -> 87, of which waited for: 49 -> 48; matrix products, arithmetic and copies ran while one was open for 10% -> 9% of each run, Pallas kernels for 19% -> 20%
where the time goes in v5:
time: 719 us; the launch traced here: 712 us
  waiting for transfers between devices  373 us (52%)
  Pallas kernels  181 us (25%)
  starting transfers between devices  63.6 us (9%)
  other arithmetic  61.5 us (9%)
  local copies, waits for them, and re-layouts  16.3 us (2%)
  between operations  16 us (2%)
    ppermute x81, waiting for transfers between devices, swap(): return lax.ppermute(value, AXES, pairs)  326 us
    ppermute x81, starting transfers between devices, swap(): return lax.ppermute(value, AXES, pairs)  62.7 us
    all_gather x4, waiting for transfers between devices, to_groups(): lax.all_gather(piece, 'blk', axis=0, tiled=True, axis_index_groups=alike)  44.9 us
    pallas_call x2, Pallas kernels, feed(): call(kernel, [shape(rows, 2 * unit), shape(rows, unit)] + [shape(rows //...  36.3 us
    pallas_call x2, Pallas kernels, weight_grads(): call(kernel, shape(width, total), 'weight_grads', 2 * rows * width * tota...  32 us
    pallas_call x2, Pallas kernels, attend(): call(kernel, [shape(rows, HEAD_DIM), shape(rows, 1, F32)] + shapes, 'atte...  20.6 us
    pallas_call x1, Pallas kernels, attend_back(): call(kernel, [shape(rows, HEAD_DIM, F32), shape(keys, HEAD_DIM, F32), sha...  17.6 us
    pallas_call x2, Pallas kernels, back_input(): call(kernel, [shape(rows, 3 * HEAD_DIM)] + shapes, 'back_input', 6 * rows...  16.1 us
  transfers between devices with their start and end apart: 87, of which 48 were waited for; matrix products, arithmetic and copies ran while one was open for 9% of the time, Pallas kernels for 20%

profile of v5, /device:TPU:0, one launch (start us, length us, event | category | flops | bytes accessed | tf_op | source)
XLA Modules:
  0.0 712.1 jit_solution(9139258513814728303)
XLA Ops:
  8.4 4.1 collective-permute-start
  18.4 3.8 pack.3
  22.4 3.7 multiply_cosine_fusion
  31.1 8.9 %collective-permute-done.5 = bf16[64,2048]{1,0:T(8,128)(2,1)S(1)} collective-permute-done((bf16[64,2048]{1,0:T(8,128)(2,1)S(1)}, bf16[64,2048]{1,0:T(8,128)(2,1)S(1)}, u32[]{:S(2)}, u32[]{:S(2)}) %collective-permute-start.5) | collective-permute-done | bytes 262176 | tf_op jit(solution)/shard_map/ppermute | solution.py:54
  40.8 3.4 collective-permute-done.4
  44.3 17.8 %collective-permute-done.1 = bf16[128,2048]{1,0:T(8,128)(2,1)S(1)} collective-permute-done((bf16[128,2048]{1,0:T(8,128)(2,1)S(1)}, bf16[128,2048]{1,0:T(8,128)(2,1)S(1)}, u32[]{:S(2)}, u32[]{:S(2)}) %collective-permute-start.1) | collective-permute-done | bytes 524320 | tf_op jit(solution)/shard_map/ppermute | solution.py:54
  66.6 8.4 %collective-permute-done.7 = bf16[128,2048]{1,0:T(8,128)(2,1)S(1)} collective-permute-done((bf16[128,2048]{1,0:T(8,128)(2,1)S(1)}, bf16[128,2048]{1,0:T(8,128)(2,1)S(1)}, u32[]{:S(2)}, u32[]{:S(2)}) %collective-permute-start.7) | collective-permute-done | bytes 524320 | tf_op jit(solution)/shard_map/ppermute | solution.py:54
  82.4 31.5 %collective-permute-done.13 = bf16[256,1536]{1,0:T(8,128)(2,1)} collective-permute-done((bf16[256,1536]{1,0:T(8,128)(2,1)}, bf16[256,1536]{1,0:T(8,128)(2,1)}, u32[]{:S(2)}, u32[]{:S(2)}) %collective-permute-start.13) | collective-permute-done | bytes 786464 | tf_op jit(solution)/shard_map/ppermute | solution.py:54
  113.9 18.8 %collective-permute-done.11 = bf16[256,1536]{1,0:T(8,128)(2,1)} collective-permute-done((bf16[256,1536]{1,0:T(8,128)(2,1)}, bf16[256,1536]{1,0:T(8,128)(2,1)}, u32[]{:S(2)}, u32[]{:S(2)}) %collective-permute-start.11) | collective-permute-done | bytes 786464 | tf_op jit(solution)/shard_map/ppermute | solution.py:54
  132.7 3.7 collective-permute-done.12
  138.3 3.0 assemble.2.refs_8_.w_ref.refs_4_
  141.4 10.4 %project.1 = (bf16[2048,128]{1,0:T(8,128)(2,1)}, bf16[2048,128]{1,0:T(8,128)(2,1)}, bf16[2048,128]{1,0:T(8,128)(2,1)}) custom-call(bf16[256,2048]{1,0:T(8,128)(2,1)} %copy-done.1, bf16[256,2048]{1,0:T(8,128)(2,1)} %copy-done, bf16[256,2048]{1,0:T(8,128)(2,1)} %collective-permute-done.8.refs_2_, bf16[256,2048]{1,0:T(8,128)(2,1)} %collective-permute-done.9.refs_3_, ...), custom_call_target="tpu_custom_call" | custom-call | flops 3221225472 | bytes 8388608 | tf_op jit(solution)/shard_map/project/pallas_call | solution.py:181
  151.8 10.3 %attend.2 = (bf16[1024,128]{1,0:T(8,128)(2,1)}, f32[1024,1]{1,0:T(8,128)}, bf16[512,2048]{1,0:T(8,128)(2,1)}, bf16[512,2048]{1,0:T(8,128)(2,1)}) custom-call(bf16[2048,128]{1,0:T(8,128)(2,1)} %get-tuple-element.117.q_ref, bf16[2048,128]{1,0:T(8,128)(2,1)} %get-tuple-element.112.k_ref.refs_5_, bf16[2048,128]{1,0:T(8,128)(2,1)} %get-tuple-element.113.v_ref.refs_6_, ...), custom_call_target="tpu_custom_call" | custom-call | flops 1610612736 | bytes 4194304 | tf_op jit(solution)/shard_map/attend/pallas_call | solution.py:238
  162.3 4.1 collective-permute-done.17
  166.5 3.8 add_convert_fusion.15
  170.2 11.4 %collective-permute-done.18 = bf16[128,2048]{1,0:T(8,128)(2,1)S(1)} collective-permute-done((bf16[128,2048]{1,0:T(8,128)(2,1)S(1)}, bf16[128,2048]{1,0:T(8,128)(2,1)S(1)}, u32[]{:S(2)}, u32[]{:S(2)}) %collective-permute-start.18) | collective-permute-done | bytes 524320 | tf_op jit(solution)/shard_map/ppermute | solution.py:54
  182.5 10.3 %attend.3 = (bf16[1024,128]{1,0:T(8,128)(2,1)}, f32[1024,1]{1,0:T(8,128)}, bf16[512,2048]{1,0:T(8,128)(2,1)}, bf16[512,2048]{1,0:T(8,128)(2,1)}) custom-call(bf16[2048,128]{1,0:T(8,128)(2,1)} %get-tuple-element.117.q_ref, bf16[2048,128]{1,0:T(8,128)(2,1)} %get-tuple-element.112.k_ref.refs_5_, bf16[2048,128]{1,0:T(8,128)(2,1)} %get-tuple-element.113.v_ref.refs_6_, ...), custom_call_target="tpu_custom_call" | custom-call | flops 1610612736 | bytes 4194304 | tf_op jit(solution)/shard_map/attend/pallas_call | solution.py:238
  197.6 30.8 %all-gather.9.cloned.1.call-done.refs_1_ = bf16[512,1536]{1,0:T(8,128)(2,1)} async-done(((bf16[256,1536]{1,0:T(8,128)(2,1)}), bf16[512,1536]{1,0:T(8,128)(2,1)}) %all-gather.9.cloned.1.call-update) | async-done | bytes 1572880 | tf_op jit(solution)/shard_map/all_gather | solution.py:586
  228.4 3.3 convert_add_fusion.7
  231.7 3.1 collective-permute-start.21
  234.9 2.7 collective-permute-start.23
  237.8 9.9 %collective-permute-done.21 = bf16[128,2048]{1,0:T(8,128)(2,1)S(1)} collective-permute-done((bf16[128,2048]{1,0:T(8,128)(2,1)S(1)}, bf16[128,2048]{1,0:T(8,128)(2,1)S(1)}, u32[]{:S(2)}, u32[]{:S(2)}) %collective-permute-start.21) | collective-permute-done | bytes 524320 | tf_op jit(solution)/shard_map/ppermute | solution.py:54
  249.2 3.5 maximum_select_fusion.refs_3_
  255.8 3.1 collective-permute-done.27
  259.9 2.7 collective-permute-start.28
  262.7 14.1 %all-gather.11.cloned.1.call-done.refs_2_ = bf16[512,1536]{1,0:T(8,128)(2,1)} async-done(((bf16[256,1536]{1,0:T(8,128)(2,1)}), bf16[512,1536]{1,0:T(8,128)(2,1)}) %all-gather.11.cloned.1.call-update) | async-done | bytes 1572880 | tf_op jit(solution)/shard_map/all_gather | solution.py:586
  280.1 3.6 collective-permute-done.28.refs_4_.refs_14_
  283.7 8.5 %collective-permute-done.26 = bf16[128,2048]{1,0:T(8,128)(2,1)S(1)} collective-permute-done((bf16[128,2048]{1,0:T(8,128)(2,1)S(1)}, bf16[128,2048]{1,0:T(8,128)(2,1)S(1)}, u32[]{:S(2)}, u32[]{:S(2)}) %collective-permute-start.26) | collective-permute-done | bytes 524320 | tf_op jit(solution)/shard_map/ppermute | solution.py:54
  295.9 11.0 %collective-permute-done.34 = bf16[128,2048]{1,0:T(8,128)(2,1)S(1)} collective-permute-done((bf16[128,2048]{1,0:T(8,128)(2,1)S(1)}, bf16[128,2048]{1,0:T(8,128)(2,1)S(1)}, u32[]{:S(2)}, u32[]{:S(2)}) %collective-permute-start.34) | collective-permute-done | bytes 524320 | tf_op jit(solution)/shard_map/ppermute | solution.py:54
  311.7 5.9 assemble.3.refs_8_.w_ref
  317.6 18.3 %feed.2 = (bf16[1024,1024]{1,0:T(8,128)(2,1)}, bf16[1024,512]{1,0:T(8,128)(2,1)}, bf16[512,2048]{1,0:T(8,128)(2,1)}, bf16[512,2048]{1,0:T(8,128)(2,1)}) custom-call(bf16[256,2048]{1,0:T(8,128)(2,1)} %copy-done.37, bf16[256,2048]{1,0:T(8,128)(2,1)} %copy-done.36, bf16[256,2048]{1,0:T(8,128)(2,1)} %collective-permute-done.35.refs_2_, ...), custom_call_target="tpu_custom_call" | custom-call | flops 10737418240 | bytes 4194304 | tf_op jit(solution)/shard_map/feed/pallas_call | solution.py:281
  341.1 18.1 %feed.3 = (bf16[1024,1024]{1,0:T(8,128)(2,1)}, bf16[1024,512]{1,0:T(8,128)(2,1)}, bf16[512,2048]{1,0:T(8,128)(2,1)}, bf16[512,2048]{1,0:T(8,128)(2,1)}) custom-call(bf16[256,2048]{1,0:T(8,128)(2,1)} %copy-done.57, bf16[256,2048]{1,0:T(8,128)(2,1)} %copy-done.56, bf16[256,2048]{1,0:T(8,128)(2,1)} %copy-done.59, bf16[256,2048]{1,0:T(8,128)(2,1)} %copy-done.58, ...), custom_call_target="tpu_custom_call" | custom-call | flops 10737418240 | bytes 4194304 | tf_op jit(solution)/shard_map/feed/pallas_call | solution.py:281
  359.7 5.5 collective-permute-done.44
  365.3 3.7 add_convert_fusion.10
  370.0 19.8 %weight_grads.2 = bf16[2048,1536]{1,0:T(8,128)(2,1)} custom-call(bf16[256,2048]{1,0:T(8,128)(2,1)} %copy-done.37, bf16[256,2048]{1,0:T(8,128)(2,1)} %copy-done.36, bf16[256,2048]{1,0:T(8,128)(2,1)} %collective-permute-done.35.refs_2_, bf16[256,2048]{1,0:T(8,128)(2,1)} %collective-permute-done.36.refs_3_, bf16[256,2048]{1,0:T(8,128)(2,1)} %copy-done.57, ...), custom_call_target="tpu_custom_call" | custom-call | flops 12884901888 | bytes 14680064 | tf_op jit(solution)/shard_map/weight_grads/pallas_call | solution.py:341
  389.8 4.5 collective-permute-done.47
  394.7 3.6 convert_add_fusion.5
  401.4 8.0 %feed_out.2 = (bf16[512,2048]{1,0:T(8,128)(2,1)}, bf16[512,2048]{1,0:T(8,128)(2,1)}) custom-call(bf16[1024,512]{1,0:T(8,128)(2,1)} %get-tuple-element.143.refs_19_.hidden_ref, bf16[2048,1536]{1,0:T(8,128)(2,1)} %assemble.3.refs_8_.w_ref), custom_call_target="tpu_custom_call" | custom-call | flops 2147483648 | bytes 4194304 | tf_op jit(solution)/shard_map/feed_out/pallas_call | solution.py:302
  414.1 8.0 %feed_out.3 = (bf16[512,2048]{1,0:T(8,128)(2,1)}, bf16[512,2048]{1,0:T(8,128)(2,1)}) custom-call(bf16[1024,512]{1,0:T(8,128)(2,1)} %get-tuple-element.148.refs_18_.hidden_ref, bf16[2048,1536]{1,0:T(8,128)(2,1)} %assemble.3.refs_8_.w_ref), custom_call_target="tpu_custom_call" | custom-call | flops 2147483648 | bytes 4194304 | tf_op jit(solution)/shard_map/feed_out/pallas_call | solution.py:302
  422.2 3.3 collective-permute-done.50
  427.9 14.9 %collective-permute-done.51 = bf16[128,2048]{1,0:T(8,128)(2,1)S(1)} collective-permute-done((bf16[128,2048]{1,0:T(8,128)(2,1)S(1)}, bf16[128,2048]{1,0:T(8,128)(2,1)S(1)}, u32[]{:S(2)}, u32[]{:S(2)}) %collective-permute-start.51) | collective-permute-done | bytes 524320 | tf_op jit(solution)/shard_map/ppermute | solution.py:54
  443.1 14.7 %collective-permute-done.53 = bf16[128,2048]{1,0:T(8,128)(2,1)S(1)} collective-permute-done((bf16[128,2048]{1,0:T(8,128)(2,1)S(1)}, bf16[128,2048]{1,0:T(8,128)(2,1)S(1)}, u32[]{:S(2)}, u32[]{:S(2)}) %collective-permute-start.53) | collective-permute-done | bytes 524320 | tf_op jit(solution)/shard_map/ppermute | solution.py:54
  460.2 13.4 %collective-permute-done.57.refs_1_.refs_15_ = bf16[256,2048]{1,0:T(8,128)(2,1)S(1)} collective-permute-done((bf16[256,2048]{1,0:T(8,128)(2,1)S(1)}, bf16[256,2048]{1,0:T(8,128)(2,1)S(1)}, u32[]{:S(2)}, u32[]{:S(2)}) %collective-permute-start.57) | collective-permute-done | bytes 1048608 | tf_op jit(solution)/shard_map/ppermute | solution.py:54
  475.3 5.8 collective-permute-done.55.refs_3_.refs_13_
  482.1 4.8 back_project.2.refs_0_
  486.9 4.9 back_project.3.refs_1_
  491.9 3.4 add_convert_fusion.7
  496.1 17.6 %attend_back.1 = (f32[2048,128]{1,0:T(8,128)}, f32[2048,128]{1,0:T(8,128)}, f32[2048,128]{1,0:T(8,128)}) custom-call(bf16[2048,128]{1,0:T(8,128)(2,1)} %get-tuple-element.117.q_ref, bf16[1024,128]{1,0:T(8,128)(2,1)} %back_project.2.refs_0_, bf16[1024,128]{1,0:T(8,128)(2,1)} %back_project.3.refs_1_, f32[1024,1]{1,0:T(8,128)} %get-tuple-element.157.refs_2_, ...), custom_call_target="tpu_custom_call" | custom-call | flops 5368709120 | bytes 4194304 | tf_op jit(solution)/shard_map/attend_back/pallas_call | solution.py:410
  513.7 7.2 %collective-permute-done.61 = bf16[256,2048]{1,0:T(8,128)(2,1)S(1)} collective-permute-done((bf16[256,2048]{1,0:T(8,128)(2,1)}, bf16[256,2048]{1,0:T(8,128)(2,1)S(1)}, u32[]{:S(2)}, u32[]{:S(2)}) %collective-permute-start.61) | collective-permute-done | bytes 1048608 | tf_op jit(solution)/shard_map/ppermute | solution.py:54
  521.1 8.0 %back_input.2 = (bf16[1024,384]{1,0:T(8,128)(2,1)}, bf16[512,2048]{1,0:T(8,128)(2,1)}, bf16[512,2048]{1,0:T(8,128)(2,1)}) custom-call(f32[2048,128]{1,0:T(8,128)} %get-tuple-element.167.dq_ref, f32[2048,128]{1,0:T(8,128)} %get-tuple-element.162.dk_ref, f32[2048,128]{1,0:T(8,128)} %get-tuple-element.163.dv_ref, f32[2048,256]{1,0:T(8,128)} %pad_maximum_fusion.refs_9_.t_ref, ...), custom_call_target="tpu_custom_call" | custom-call | flops 1610612736 | bytes 4194304 | tf_op jit(solution)/shard_map/back_input/pallas_call | solution.py:436
  529.3 8.1 %back_input.3 = (bf16[1024,384]{1,0:T(8,128)(2,1)}, bf16[512,2048]{1,0:T(8,128)(2,1)}, bf16[512,2048]{1,0:T(8,128)(2,1)}) custom-call(f32[2048,128]{1,0:T(8,128)} %get-tuple-element.167.dq_ref, f32[2048,128]{1,0:T(8,128)} %get-tuple-element.162.dk_ref, f32[2048,128]{1,0:T(8,128)} %get-tuple-element.163.dv_ref, f32[2048,256]{1,0:T(8,128)} %pad_maximum_fusion.refs_9_.t_ref, ...), custom_call_target="tpu_custom_call" | custom-call | flops 1610612736 | bytes 4194304 | tf_op jit(solution)/shard_map/back_input/pallas_call | solution.py:436
  537.5 3.9 add_convert_fusion.2
  547.7 12.2 %weight_grads.3 = bf16[2048,512]{1,0:T(8,128)(2,1)} custom-call(bf16[256,2048]{1,0:T(8,128)(2,1)} %copy-done.1, bf16[256,2048]{1,0:T(8,128)(2,1)} %copy-done, bf16[256,2048]{1,0:T(8,128)(2,1)} %collective-permute-done.8.refs_2_, bf16[256,2048]{1,0:T(8,128)(2,1)} %collective-permute-done.9.refs_3_, bf16[256,2048]{1,0:T(8,128)(2,1)} %collective-permute-done.10.refs_4_, ...), custom_call_target="tpu_custom_call" | custom-call | flops 4294967296 | bytes 10485760 | tf_op jit(solution)/shard_map/weight_grads/pallas_call | solution.py:341
  559.9 19.6 %collective-permute-done.62 = bf16[128,2048]{1,0:T(8,128)(2,1)} collective-permute-done((bf16[128,2048]{1,0:T(8,128)(2,1)S(1)}, bf16[128,2048]{1,0:T(8,128)(2,1)}, u32[]{:S(2)}, u32[]{:S(2)}) %collective-permute-start.62) | collective-permute-done | bytes 524320 | tf_op jit(solution)/shard_map/ppermute | solution.py:54
  581.1 3.5 convert_add_fusion.1
  591.6 7.2 %collective-permute-done.70 = bf16[128,2048]{1,0:T(8,128)(2,1)} collective-permute-done((bf16[128,2048]{1,0:T(8,128)(2,1)}, bf16[128,2048]{1,0:T(8,128)(2,1)}, u32[]{:S(2)}, u32[]{:S(2)}) %collective-permute-start.70) | collective-permute-done | bytes 524320 | tf_op jit(solution)/shard_map/ppermute | solution.py:54
  605.7 9.5 %collective-permute-done.65 = bf16[128,2048]{1,0:T(8,128)(2,1)} collective-permute-done((bf16[128,2048]{1,0:T(8,128)(2,1)}, bf16[128,2048]{1,0:T(8,128)(2,1)}, u32[]{:S(2)}, u32[]{:S(2)}) %collective-permute-start.65) | collective-permute-done | bytes 524320 | tf_op jit(solution)/shard_map/ppermute | solution.py:54
  616.7 21.1 %collective-permute-done.73 = bf16[128,2048]{1,0:T(8,128)(2,1)} collective-permute-done((bf16[128,2048]{1,0:T(8,128)(2,1)}, bf16[128,2048]{1,0:T(8,128)(2,1)}, u32[]{:S(2)}, u32[]{:S(2)}) %collective-permute-start.73) | collective-permute-done | bytes 524320 | tf_op jit(solution)/shard_map/ppermute | solution.py:54
  646.5 7.1 collective-permute-done.66
  653.7 9.6 %collective-permute-done.74 = bf16[64,2048]{1,0:T(8,128)(2,1)S(1)} collective-permute-done((bf16[64,2048]{1,0:T(8,128)(2,1)S(1)}, bf16[64,2048]{1,0:T(8,128)(2,1)S(1)}, u32[]{:S(2)}, u32[]{:S(2)}) %collective-permute-start.74) | collective-permute-done | bytes 262176 | tf_op jit(solution)/shard_map/ppermute | solution.py:54
  672.5 6.1 collective-permute-done.79.refs_2_
  678.6 17.3 %collective-permute-done.80.refs_3_ = bf16[256,1536]{1,0:T(8,128)(2,1)} collective-permute-done((bf16[256,1536]{1,0:T(8,128)(2,1)S(1)}, bf16[256,1536]{1,0:T(8,128)(2,1)}, u32[]{:S(2)}, u32[]{:S(2)}) %collective-permute-start.80) | collective-permute-done | bytes 786464 | tf_op jit(solution)/shard_map/ppermute | solution.py:54
  695.9 5.0 unpack.3
  702.1 2.6 unpack.2
  (363 shorter events, 116.0 us)
Async XLA Ops:
  7.2 70.9 %all-gather.5.cloned.1.call-start = ((), (), s32[]{:S(2)}) async-start(), calls=%async_computation.2 | async-start | bytes 2359296 | tf_op jit(solution)/shard_map/all_gather | solution.py:586
  8.4 20.0 %collective-permute-start = (bf16[64,2048]{1,0:T(8,128)(2,1)S(1)}, bf16[64,2048]{1,0:T(8,128)(2,1)S(1)}, u32[]{:S(2)}, u32[]{:S(2)}) collective-permute-start(bf16[64,2048]{1,0:T(8,128)(2,1)S(1)} %get-tuple-element.247), channel_id=1, source_target_pairs={{0,16},{1,17},{2,18},{3,19},{4,20},{5,21},{6,22},{7,23},{8,24},{9,... | collective-permute-start | bytes 786440 | tf_op jit(solution)/shard_map/ppermute | solution.py:54
  14.7 26.1 %collective-permute-start.2 = (bf16[256,512]{1,0:T(8,128)(2,1)}, bf16[256,512]{1,0:T(8,128)(2,1)S(1)}, u32[]{:S(2)}, u32[]{:S(2)}) collective-permute-start(bf16[256,512]{1,0:T(8,128)(2,1)} %get-tuple-element.99), channel_id=1, source_target_pairs={{0,4},{1,5},{2,6},{3,7},{4,0},{5,1},{6,2},{7,3},{8,12},{9,13},{10,... | collective-permute-start | bytes 786440 | tf_op jit(solution)/shard_map/ppermute | solution.py:54
  16.2 24.6 %collective-permute-start.3 = (bf16[256,512]{1,0:T(8,128)(2,1)}, bf16[256,512]{1,0:T(8,128)(2,1)S(1)}, u32[]{:S(2)}, u32[]{:S(2)}) collective-permute-start(bf16[256,512]{1,0:T(8,128)(2,1)} %get-tuple-element.100), channel_id=1, source_target_pairs={{0,8},{1,9},{2,10},{3,11},{4,12},{5,13},{6,14},{7,15},{8,0},{9,1},... | collective-permute-start | bytes 786440 | tf_op jit(solution)/shard_map/ppermute | solution.py:54
  17.8 26.5 %collective-permute-start.4 = (bf16[256,512]{1,0:T(8,128)(2,1)}, bf16[256,512]{1,0:T(8,128)(2,1)S(1)}, u32[]{:S(2)}, u32[]{:S(2)}) collective-permute-start(bf16[256,512]{1,0:T(8,128)(2,1)} %get-tuple-element.101), channel_id=1, source_target_pairs={{0,12},{1,13},{2,14},{3,15},{4,8},{5,9},{6,10},{7,11},{8,4},{9,5},... | collective-permute-start | bytes 786440 | tf_op jit(solution)/shard_map/ppermute | solution.py:54
  18.3 21.7 %collective-permute-start.5 = (bf16[64,2048]{1,0:T(8,128)(2,1)S(1)}, bf16[64,2048]{1,0:T(8,128)(2,1)S(1)}, u32[]{:S(2)}, u32[]{:S(2)}) collective-permute-start(bf16[64,2048]{1,0:T(8,128)(2,1)S(1)} %get-tuple-element.245), channel_id=1, source_target_pairs={{0,16},{1,17},{2,18},{3,19},{4,20},{5,21},{6,22},{7,23},{8,24},{9,... | collective-permute-start | bytes 786440 | tf_op jit(solution)/shard_map/ppermute | solution.py:54
  22.3 116.1 %all-gather.7.cloned.1.call-start = ((), (), s32[]{:S(2)}) async-start(), calls=%async_computation.3 | async-start | bytes 3145728 | tf_op jit(solution)/shard_map/all_gather | solution.py:586
  29.1 32.9 %collective-permute-start.1 = (bf16[128,2048]{1,0:T(8,128)(2,1)S(1)}, bf16[128,2048]{1,0:T(8,128)(2,1)S(1)}, u32[]{:S(2)}, u32[]{:S(2)}) collective-permute-start(bf16[128,2048]{1,0:T(8,128)(2,1)S(1)} %fusion.4), channel_id=1, source_target_pairs={{0,8},{1,9},{2,10},{3,11},{4,12},{5,13},{6,14},{7,15},{8,0},{9,1},... | collective-permute-start | bytes 1572872 | tf_op jit(solution)/shard_map/ppermute | solution.py:54
  75.1 61.3 %collective-permute-start.14 = (bf16[256,2048]{1,0:T(8,128)(2,1)S(1)}, bf16[256,2048]{1,0:T(8,128)(2,1)S(1)}, u32[]{:S(2)}, u32[]{:S(2)}) collective-permute-start(bf16[256,2048]{1,0:T(8,128)(2,1)S(1)} %pad_maximum_fusion.2.refs_1_), channel_id=1, source_target_pairs={{0,4},{1,5},{2,6},{3,7},{4,0},{5,1},{6,2},{7,3},{8,12},{9,13},{10,... | collective-permute-start | bytes 3145736 | tf_op jit(solution)/shard_map/ppermute | solution.py:54
  78.1 150.2 %all-gather.9.cloned.1.call-start = ((), (), s32[]{:S(2)}) async-start(), calls=%async_computation.4 | async-start | bytes 2359296 | tf_op jit(solution)/shard_map/all_gather | solution.py:586
  78.4 58.1 %collective-permute-start.10 = (bf16[256,2048]{1,0:T(8,128)(2,1)S(1)}, bf16[256,2048]{1,0:T(8,128)(2,1)}, u32[]{:S(2)}, u32[]{:S(2)}) collective-permute-start(bf16[256,2048]{1,0:T(8,128)(2,1)S(1)} %pad_maximum_fusion.1.refs_0_), channel_id=1, source_target_pairs={{0,2},{1,3},{2,0},{3,1},{4,6},{5,7},{6,4},{7,5},{8,10},{9,11},{10,... | collective-permute-start | bytes 3145736 | tf_op jit(solution)/shard_map/ppermute | solution.py:54
  78.9 35.0 %collective-permute-start.13 = (bf16[256,1536]{1,0:T(8,128)(2,1)}, bf16[256,1536]{1,0:T(8,128)(2,1)}, u32[]{:S(2)}, u32[]{:S(2)}) collective-permute-start(bf16[256,1536]{1,0:T(8,128)(2,1)} %get-tuple-element.105), channel_id=1, source_target_pairs={{0,12},{1,13},{2,14},{3,15},{4,8},{5,9},{6,10},{7,11},{8,4},{9,5},... | collective-permute-start | bytes 2359304 | tf_op jit(solution)/shard_map/ppermute | solution.py:54
  81.2 51.5 %collective-permute-start.11 = (bf16[256,1536]{1,0:T(8,128)(2,1)}, bf16[256,1536]{1,0:T(8,128)(2,1)}, u32[]{:S(2)}, u32[]{:S(2)}) collective-permute-start(bf16[256,1536]{1,0:T(8,128)(2,1)} %get-tuple-element.103), channel_id=1, source_target_pairs={{0,4},{1,5},{2,6},{3,7},{4,0},{5,1},{6,2},{7,3},{8,12},{9,13},{10,... | collective-permute-start | bytes 2359304 | tf_op jit(solution)/shard_map/ppermute | solution.py:54
  81.6 54.8 %collective-permute-start.12 = (bf16[256,1536]{1,0:T(8,128)(2,1)}, bf16[256,1536]{1,0:T(8,128)(2,1)}, u32[]{:S(2)}, u32[]{:S(2)}) collective-permute-start(bf16[256,1536]{1,0:T(8,128)(2,1)} %get-tuple-element.104), channel_id=1, source_target_pairs={{0,8},{1,9},{2,10},{3,11},{4,12},{5,13},{6,14},{7,15},{8,0},{9,1},... | collective-permute-start | bytes 2359304 | tf_op jit(solution)/shard_map/ppermute | solution.py:54
  113.9 27.5 %collective-permute-start.9 = (bf16[256,2048]{1,0:T(8,128)(2,1)S(1)}, bf16[256,2048]{1,0:T(8,128)(2,1)}, u32[]{:S(2)}, u32[]{:S(2)}) collective-permute-start(bf16[256,2048]{1,0:T(8,128)(2,1)S(1)} %pad_maximum_fusion.2.refs_1_), channel_id=1, source_target_pairs={{0,1},{1,0},{2,3},{3,2},{4,5},{5,4},{6,7},{7,6},{8,9},{9,8},{10,11... | collective-permute-start | bytes 3145736 | tf_op jit(solution)/shard_map/ppermute | solution.py:54
  162.2 114.6 %all-gather.11.cloned.1.call-start = ((), (), s32[]{:S(2)}) async-start(), calls=%async_computation.5 | async-start | bytes 2359296 | tf_op jit(solution)/shard_map/all_gather | solution.py:586
  162.3 19.4 %collective-permute-start.18 = (bf16[128,2048]{1,0:T(8,128)(2,1)S(1)}, bf16[128,2048]{1,0:T(8,128)(2,1)S(1)}, u32[]{:S(2)}, u32[]{:S(2)}) collective-permute-start(bf16[128,2048]{1,0:T(8,128)(2,1)S(1)} %copy-done.32), channel_id=1, source_target_pairs={{0,8},{1,9},{2,10},{3,11},{4,12},{5,13},{6,14},{7,15},{8,0},{9,1},... | collective-permute-start | bytes 1572872 | tf_op jit(solution)/shard_map/ppermute | solution.py:54
  192.8 35.6 %collective-permute-start.19 = (bf16[512,2048]{1,0:T(8,128)(2,1)}, bf16[512,2048]{1,0:T(8,128)(2,1)}, u32[]{:S(2)}, u32[]{:S(2)}) collective-permute-start(bf16[512,2048]{1,0:T(8,128)(2,1)} %get-tuple-element.119), channel_id=1, source_target_pairs={{0,1},{1,0},{2,3},{3,2},{4,5},{5,4},{6,7},{7,6},{8,9},{9,8},{10,11... | collective-permute-start | bytes 6291464 | tf_op jit(solution)/shard_map/ppermute | solution.py:54
  192.9 56.3 %collective-permute-start.25 = (bf16[256,1536]{1,0:T(8,128)(2,1)}, bf16[256,1536]{1,0:T(8,128)(2,1)}, u32[]{:S(2)}, u32[]{:S(2)}) collective-permute-start(bf16[256,1536]{1,0:T(8,128)(2,1)} %collective-permute-done.13), channel_id=1, source_target_pairs={{0,16},{1,17},{2,18},{3,19},{4,20},{5,21},{6,22},{7,23},{8,24},{9,... | collective-permute-start | bytes 2359304 | tf_op jit(solution)/shard_map/ppermute | solution.py:54
  193.0 395.2 %reduce-scatter.3.cloned.1.call-start = ((), (), s32[]{:S(2)}) async-start(), calls=%async_computation.6 | async-start | bytes 9437184 | tf_op jit(solution)/shard_map/reduce_scatter | solution.py:605
  193.4 34.9 %collective-permute-start.22 = (bf16[256,2048]{1,0:T(8,128)(2,1)}, bf16[256,2048]{1,0:T(8,128)(2,1)}, u32[]{:S(2)}, u32[]{:S(2)}) collective-permute-start(bf16[256,2048]{1,0:T(8,128)(2,1)} %get-tuple-element.211), channel_id=1, source_target_pairs={{0,4},{1,5},{2,6},{3,7},{4,0},{5,1},{6,2},{7,3},{8,12},{9,13},{10,... | collective-permute-start | bytes 3145736 | tf_op jit(solution)/shard_map/ppermute | solution.py:54
  193.5 34.8 %collective-permute-start.20 = (bf16[256,2048]{1,0:T(8,128)(2,1)}, bf16[256,2048]{1,0:T(8,128)(2,1)}, u32[]{:S(2)}, u32[]{:S(2)}) collective-permute-start(bf16[256,2048]{1,0:T(8,128)(2,1)} %get-tuple-element.210), channel_id=1, source_target_pairs={{0,2},{1,3},{2,0},{3,1},{4,6},{5,7},{6,4},{7,5},{8,10},{9,11},{10,... | collective-permute-start | bytes 3145736 | tf_op jit(solution)/shard_map/ppermute | solution.py:54
  195.6 57.0 %collective-permute-start.29 = (bf16[128,2048]{1,0:T(8,128)(2,1)}, bf16[128,2048]{1,0:T(8,128)(2,1)}, u32[]{:S(2)}, u32[]{:S(2)}) collective-permute-start(bf16[128,2048]{1,0:T(8,128)(2,1)} %pad_maximum_fusion.19), channel_id=1, source_target_pairs={{0,2},{1,3},{2,0},{3,1},{4,6},{5,7},{6,4},{7,5},{8,10},{9,11},{10,... | collective-permute-start | bytes 1572872 | tf_op jit(solution)/shard_map/ppermute | solution.py:54
  231.7 15.9 %collective-permute-start.21 = (bf16[128,2048]{1,0:T(8,128)(2,1)S(1)}, bf16[128,2048]{1,0:T(8,128)(2,1)S(1)}, u32[]{:S(2)}, u32[]{:S(2)}) collective-permute-start(bf16[128,2048]{1,0:T(8,128)(2,1)S(1)} %fusion.19), channel_id=1, source_target_pairs={{0,4},{1,5},{2,6},{3,7},{4,0},{5,1},{6,2},{7,3},{8,12},{9,13},{10,... | collective-permute-start | bytes 1572872 | tf_op jit(solution)/shard_map/ppermute | solution.py:54
  234.9 13.9 %collective-permute-start.23 = (bf16[128,2048]{1,0:T(8,128)(2,1)S(1)}, bf16[128,2048]{1,0:T(8,128)(2,1)S(1)}, u32[]{:S(2)}, u32[]{:S(2)}) collective-permute-start(bf16[128,2048]{1,0:T(8,128)(2,1)S(1)} %fusion.18), channel_id=1, source_target_pairs={{0,2},{1,3},{2,0},{3,1},{4,6},{5,7},{6,4},{7,5},{8,10},{9,11},{10,... | collective-permute-start | bytes 1572872 | tf_op jit(solution)/shard_map/ppermute | solution.py:54
  237.7 21.2 %collective-permute-start.27 = (bf16[128,2048]{1,0:T(8,128)(2,1)S(1)}, bf16[128,2048]{1,0:T(8,128)(2,1)S(1)}, u32[]{:S(2)}, u32[]{:S(2)}) collective-permute-start(bf16[128,2048]{1,0:T(8,128)(2,1)S(1)} %pad_maximum_fusion.18), channel_id=1, source_target_pairs={{0,4},{1,5},{2,6},{3,7},{4,0},{5,1},{6,2},{7,3},{8,12},{9,13},{10,... | collective-permute-start | bytes 1572872 | tf_op jit(solution)/shard_map/ppermute | solution.py:54
  249.1 28.4 %collective-permute-start.24 = (bf16[128,2048]{1,0:T(8,128)(2,1)S(1)}, bf16[128,2048]{1,0:T(8,128)(2,1)}, u32[]{:S(2)}, u32[]{:S(2)}) collective-permute-start(bf16[128,2048]{1,0:T(8,128)(2,1)S(1)} %pad_maximum_fusion.17), channel_id=1, source_target_pairs={{0,8},{1,9},{2,10},{3,11},{4,12},{5,13},{6,14},{7,15},{8,0},{9,1},... | collective-permute-start | bytes 1572872 | tf_op jit(solution)/shard_map/ppermute | solution.py:54
  254.7 25.4 %collective-permute-start.30 = (bf16[256,2048]{1,0:T(8,128)(2,1)}, bf16[256,2048]{1,0:T(8,128)(2,1)}, u32[]{:S(2)}, u32[]{:S(2)}) collective-permute-start(bf16[256,2048]{1,0:T(8,128)(2,1)} %pad_maximum_fusion.5.refs_5_.refs_11_), channel_id=1, source_target_pairs={{0,4},{1,5},{2,6},{3,7},{4,0},{5,1},{6,2},{7,3},{8,12},{9,13},{10,... | collective-permute-start | bytes 3145736 | tf_op jit(solution)/shard_map/ppermute | solution.py:54
  259.9 23.8 %collective-permute-start.28 = (bf16[256,2048]{1,0:T(8,128)(2,1)}, bf16[256,2048]{1,0:T(8,128)(2,1)}, u32[]{:S(2)}, u32[]{:S(2)}) collective-permute-start(bf16[256,2048]{1,0:T(8,128)(2,1)} %pad_maximum_fusion.4.refs_4_.refs_10_), channel_id=1, source_target_pairs={{0,2},{1,3},{2,0},{3,1},{4,6},{5,7},{6,4},{7,5},{8,10},{9,11},{10,... | collective-permute-start | bytes 3145736 | tf_op jit(solution)/shard_map/ppermute | solution.py:54
  292.4 14.5 %collective-permute-start.33 = (bf16[256,2048]{1,0:T(8,128)(2,1)}, bf16[256,2048]{1,0:T(8,128)(2,1)S(1)}, u32[]{:S(2)}, u32[]{:S(2)}) collective-permute-start(bf16[256,2048]{1,0:T(8,128)(2,1)} %collective-permute-done.30.refs_5_.refs_15_), channel_id=1, source_target_pairs={{0,1},{1,0},{2,3},{3,2},{4,5},{5,4},{6,7},{7,6},{8,9},{9,8},{10,11... | collective-permute-start | bytes 3145736 | tf_op jit(solution)/shard_map/ppermute | solution.py:54
  292.5 14.4 %collective-permute-start.32 = (bf16[256,2048]{1,0:T(8,128)(2,1)}, bf16[256,2048]{1,0:T(8,128)(2,1)S(1)}, u32[]{:S(2)}, u32[]{:S(2)}) collective-permute-start(bf16[256,2048]{1,0:T(8,128)(2,1)} %collective-permute-done.28.refs_4_.refs_14_), channel_id=1, source_target_pairs={{0,1},{1,0},{2,3},{3,2},{4,5},{5,4},{6,7},{7,6},{8,9},{9,8},{10,11... | collective-permute-start | bytes 3145736 | tf_op jit(solution)/shard_map/ppermute | solution.py:54
  293.0 13.9 %collective-permute-start.34 = (bf16[128,2048]{1,0:T(8,128)(2,1)S(1)}, bf16[128,2048]{1,0:T(8,128)(2,1)S(1)}, u32[]{:S(2)}, u32[]{:S(2)}) collective-permute-start(bf16[128,2048]{1,0:T(8,128)(2,1)S(1)} %pad_maximum_fusion.21), channel_id=1, source_target_pairs={{0,2},{1,3},{2,0},{3,1},{4,6},{5,7},{6,4},{7,5},{8,10},{9,11},{10,... | collective-permute-start | bytes 1572872 | tf_op jit(solution)/shard_map/ppermute | solution.py:54
  294.4 13.6 %collective-permute-start.31 = (bf16[128,2048]{1,0:T(8,128)(2,1)S(1)}, bf16[128,2048]{1,0:T(8,128)(2,1)S(1)}, u32[]{:S(2)}, u32[]{:S(2)}) collective-permute-start(bf16[128,2048]{1,0:T(8,128)(2,1)S(1)} %pad_maximum_fusion.20), channel_id=1, source_target_pairs={{0,4},{1,5},{2,6},{3,7},{4,0},{5,1},{6,2},{7,3},{8,12},{9,13},{10,... | collective-permute-start | bytes 1572872 | tf_op jit(solution)/shard_map/ppermute | solution.py:54
  295.9 14.3 %collective-permute-start.38 = (bf16[256,2048]{1,0:T(8,128)(2,1)}, bf16[256,2048]{1,0:T(8,128)(2,1)S(1)}, u32[]{:S(2)}, u32[]{:S(2)}) collective-permute-start(bf16[256,2048]{1,0:T(8,128)(2,1)} %pad_maximum_fusion.5.refs_5_.refs_11_), channel_id=1, source_target_pairs={{0,1},{1,0},{2,3},{3,2},{4,5},{5,4},{6,7},{7,6},{8,9},{9,8},{10,11... | collective-permute-start | bytes 3145736 | tf_op jit(solution)/shard_map/ppermute | solution.py:54
  308.7 27.2 %collective-permute-start.41 = (bf16[256,2048]{1,0:T(8,128)(2,1)S(1)}, bf16[256,2048]{1,0:T(8,128)(2,1)S(1)}, u32[]{:S(2)}, u32[]{:S(2)}) collective-permute-start(bf16[256,2048]{1,0:T(8,128)(2,1)S(1)} %pad_maximum_fusion.7.refs_1_), channel_id=1, source_target_pairs={{0,4},{1,5},{2,6},{3,7},{4,0},{5,1},{6,2},{7,3},{8,12},{9,13},{10,... | collective-permute-start | bytes 3145736 | tf_op jit(solution)/shard_map/ppermute | solution.py:54
  310.2 25.8 %collective-permute-start.40 = (bf16[256,2048]{1,0:T(8,128)(2,1)S(1)}, bf16[256,2048]{1,0:T(8,128)(2,1)S(1)}, u32[]{:S(2)}, u32[]{:S(2)}) collective-permute-start(bf16[256,2048]{1,0:T(8,128)(2,1)S(1)} %pad_maximum_fusion.6.refs_0_), channel_id=1, source_target_pairs={{0,2},{1,3},{2,0},{3,1},{4,6},{5,7},{6,4},{7,5},{8,10},{9,11},{10,... | collective-permute-start | bytes 3145736 | tf_op jit(solution)/shard_map/ppermute | solution.py:54
  359.4 35.4 %collective-permute-start.39 = (bf16[512,2048]{1,0:T(8,128)(2,1)}, bf16[512,2048]{1,0:T(8,128)(2,1)}, u32[]{:S(2)}, u32[]{:S(2)}) collective-permute-start(bf16[512,2048]{1,0:T(8,128)(2,1)} %get-tuple-element.132), channel_id=1, source_target_pairs={{0,1},{1,0},{2,3},{3,2},{4,5},{5,4},{6,7},{7,6},{8,9},{9,8},{10,11... | collective-permute-start | bytes 6291464 | tf_op jit(solution)/shard_map/ppermute | solution.py:54
  368.9 25.4 %collective-permute-start.47 = (bf16[256,2048]{1,0:T(8,128)(2,1)}, bf16[256,2048]{1,0:T(8,128)(2,1)S(1)}, u32[]{:S(2)}, u32[]{:S(2)}) collective-permute-start(bf16[256,2048]{1,0:T(8,128)(2,1)} %get-tuple-element.207), channel_id=1, source_target_pairs={{0,4},{1,5},{2,6},{3,7},{4,0},{5,1},{6,2},{7,3},{8,12},{9,13},{10,... | collective-permute-start | bytes 3145736 | tf_op jit(solution)/shard_map/ppermute | solution.py:54
  369.5 25.2 %collective-permute-start.45 = (bf16[256,2048]{1,0:T(8,128)(2,1)}, bf16[256,2048]{1,0:T(8,128)(2,1)}, u32[]{:S(2)}, u32[]{:S(2)}) collective-permute-start(bf16[256,2048]{1,0:T(8,128)(2,1)} %get-tuple-element.206), channel_id=1, source_target_pairs={{0,2},{1,3},{2,0},{3,1},{4,6},{5,7},{6,4},{7,5},{8,10},{9,11},{10,... | collective-permute-start | bytes 3145736 | tf_op jit(solution)/shard_map/ppermute | solution.py:54
  427.5 15.3 %collective-permute-start.51 = (bf16[128,2048]{1,0:T(8,128)(2,1)S(1)}, bf16[128,2048]{1,0:T(8,128)(2,1)S(1)}, u32[]{:S(2)}, u32[]{:S(2)}) collective-permute-start(bf16[128,2048]{1,0:T(8,128)(2,1)S(1)} %get-tuple-element.192), channel_id=1, source_target_pairs={{0,8},{1,9},{2,10},{3,11},{4,12},{5,13},{6,14},{7,15},{8,0},{9,1},... | collective-permute-start | bytes 1572872 | tf_op jit(solution)/shard_map/ppermute | solution.py:54
  427.8 237.5 %reduce-scatter.5.cloned.1.call-start = ((), (), s32[]{:S(2)}) async-start(), calls=%async_computation.7 | async-start | bytes 3145728 | tf_op jit(solution)/shard_map/reduce_scatter | solution.py:605
  442.9 14.9 %collective-permute-start.53 = (bf16[128,2048]{1,0:T(8,128)(2,1)S(1)}, bf16[128,2048]{1,0:T(8,128)(2,1)S(1)}, u32[]{:S(2)}, u32[]{:S(2)}) collective-permute-start(bf16[128,2048]{1,0:T(8,128)(2,1)S(1)} %pad_maximum_fusion.24), channel_id=1, source_target_pairs={{0,2},{1,3},{2,0},{3,1},{4,6},{5,7},{6,4},{7,5},{8,10},{9,11},{10,... | collective-permute-start | bytes 1572872 | tf_op jit(solution)/shard_map/ppermute | solution.py:54
  443.0 14.9 %collective-permute-start.52 = (bf16[128,2048]{1,0:T(8,128)(2,1)S(1)}, bf16[128,2048]{1,0:T(8,128)(2,1)S(1)}, u32[]{:S(2)}, u32[]{:S(2)}) collective-permute-start(bf16[128,2048]{1,0:T(8,128)(2,1)S(1)} %pad_maximum_fusion.23), channel_id=1, source_target_pairs={{0,4},{1,5},{2,6},{3,7},{4,0},{5,1},{6,2},{7,3},{8,12},{9,13},{10,... | collective-permute-start | bytes 1572872 | tf_op jit(solution)/shard_map/ppermute | solution.py:54
  457.9 15.7 %collective-permute-start.57 = (bf16[256,2048]{1,0:T(8,128)(2,1)S(1)}, bf16[256,2048]{1,0:T(8,128)(2,1)S(1)}, u32[]{:S(2)}, u32[]{:S(2)}) collective-permute-start(bf16[256,2048]{1,0:T(8,128)(2,1)S(1)} %pad_maximum_fusion.10.refs_1_.refs_11_), channel_id=1, source_target_pairs={{0,4},{1,5},{2,6},{3,7},{4,0},{5,1},{6,2},{7,3},{8,12},{9,13},{10,... | collective-permute-start | bytes 3145736 | tf_op jit(solution)/shard_map/ppermute | solution.py:54
  458.1 16.2 %collective-permute-start.56 = (bf16[256,2048]{1,0:T(8,128)(2,1)S(1)}, bf16[256,2048]{1,0:T(8,128)(2,1)S(1)}, u32[]{:S(2)}, u32[]{:S(2)}) collective-permute-start(bf16[256,2048]{1,0:T(8,128)(2,1)S(1)} %pad_maximum_fusion.9.refs_0_.refs_10_), channel_id=1, source_target_pairs={{0,2},{1,3},{2,0},{3,1},{4,6},{5,7},{6,4},{7,5},{8,10},{9,11},{10,... | collective-permute-start | bytes 3145736 | tf_op jit(solution)/shard_map/ppermute | solution.py:54
  474.3 17.6 %collective-permute-start.60 = (bf16[512,2048]{1,0:T(8,128)(2,1)}, bf16[512,2048]{1,0:T(8,128)(2,1)}, u32[]{:S(2)}, u32[]{:S(2)}) collective-permute-start(bf16[512,2048]{1,0:T(8,128)(2,1)} %get-tuple-element.154), channel_id=1, source_target_pairs={{0,1},{1,0},{2,3},{3,2},{4,5},{5,4},{6,7},{7,6},{8,9},{9,8},{10,11... | collective-permute-start | bytes 6291464 | tf_op jit(solution)/shard_map/ppermute | solution.py:54
  495.3 25.6 %collective-permute-start.61 = (bf16[256,2048]{1,0:T(8,128)(2,1)}, bf16[256,2048]{1,0:T(8,128)(2,1)S(1)}, u32[]{:S(2)}, u32[]{:S(2)}) collective-permute-start(bf16[256,2048]{1,0:T(8,128)(2,1)} %get-tuple-element.202), channel_id=1, source_target_pairs={{0,2},{1,3},{2,0},{3,1},{4,6},{5,7},{6,4},{7,5},{8,10},{9,11},{10,... | collective-permute-start | bytes 3145736 | tf_op jit(solution)/shard_map/ppermute | solution.py:54
  496.0 25.1 %collective-permute-start.63 = (bf16[256,2048]{1,0:T(8,128)(2,1)S(1)}, bf16[256,2048]{1,0:T(8,128)(2,1)S(1)}, u32[]{:S(2)}, u32[]{:S(2)}) collective-permute-start(bf16[256,2048]{1,0:T(8,128)(2,1)S(1)} %get-tuple-element.203), channel_id=1, source_target_pairs={{0,4},{1,5},{2,6},{3,7},{4,0},{5,1},{6,2},{7,3},{8,12},{9,13},{10,... | collective-permute-start | bytes 3145736 | tf_op jit(solution)/shard_map/ppermute | solution.py:54
  496.1 41.4 %collective-permute-start.49 = (bf16[512,2048]{1,0:T(8,128)(2,1)}, bf16[512,2048]{1,0:T(8,128)(2,1)S(1)}, u32[]{:S(2)}, u32[]{:S(2)}) collective-permute-start(bf16[512,2048]{1,0:T(8,128)(2,1)} %get-tuple-element.150), channel_id=1, source_target_pairs={{0,1},{1,0},{2,3},{3,2},{4,5},{5,4},{6,7},{7,6},{8,9},{9,8},{10,11... | collective-permute-start | bytes 6291464 | tf_op jit(solution)/shard_map/ppermute | solution.py:54
  537.3 43.7 %collective-permute-start.67 = (bf16[512,2048]{1,0:T(8,128)(2,1)}, bf16[512,2048]{1,0:T(8,128)(2,1)}, u32[]{:S(2)}, u32[]{:S(2)}) collective-permute-start(bf16[512,2048]{1,0:T(8,128)(2,1)} %get-tuple-element.171), channel_id=1, source_target_pairs={{0,1},{1,0},{2,3},{3,2},{4,5},{5,4},{6,7},{7,6},{8,9},{9,8},{10,11... | collective-permute-start | bytes 6291464 | tf_op jit(solution)/shard_map/ppermute | solution.py:54
  541.4 39.6 %collective-permute-start.69 = (bf16[256,2048]{1,0:T(8,128)(2,1)}, bf16[256,2048]{1,0:T(8,128)(2,1)}, u32[]{:S(2)}, u32[]{:S(2)}) collective-permute-start(bf16[256,2048]{1,0:T(8,128)(2,1)} %get-tuple-element.198), channel_id=1, source_target_pairs={{0,2},{1,3},{2,0},{3,1},{4,6},{5,7},{6,4},{7,5},{8,10},{9,11},{10,... | collective-permute-start | bytes 3145736 | tf_op jit(solution)/shard_map/ppermute | solution.py:54
  542.8 38.2 %collective-permute-start.71 = (bf16[256,2048]{1,0:T(8,128)(2,1)}, bf16[256,2048]{1,0:T(8,128)(2,1)}, u32[]{:S(2)}, u32[]{:S(2)}) collective-permute-start(bf16[256,2048]{1,0:T(8,128)(2,1)} %get-tuple-element.199), channel_id=1, source_target_pairs={{0,4},{1,5},{2,6},{3,7},{4,0},{5,1},{6,2},{7,3},{8,12},{9,13},{10,... | collective-permute-start | bytes 3145736 | tf_op jit(solution)/shard_map/ppermute | solution.py:54
  544.9 34.6 %collective-permute-start.62 = (bf16[128,2048]{1,0:T(8,128)(2,1)S(1)}, bf16[128,2048]{1,0:T(8,128)(2,1)}, u32[]{:S(2)}, u32[]{:S(2)}) collective-permute-start(bf16[128,2048]{1,0:T(8,128)(2,1)S(1)} %slice.499), channel_id=1, source_target_pairs={{0,4},{1,5},{2,6},{3,7},{4,0},{5,1},{6,2},{7,3},{8,12},{9,13},{10,... | collective-permute-start | bytes 1572872 | tf_op jit(solution)/shard_map/ppermute | solution.py:54
  547.1 33.9 %collective-permute-start.64 = (bf16[128,2048]{1,0:T(8,128)(2,1)}, bf16[128,2048]{1,0:T(8,128)(2,1)S(1)}, u32[]{:S(2)}, u32[]{:S(2)}) collective-permute-start(bf16[128,2048]{1,0:T(8,128)(2,1)} %slice.498), channel_id=1, source_target_pairs={{0,2},{1,3},{2,0},{3,1},{4,6},{5,7},{6,4},{7,5},{8,10},{9,11},{10,... | collective-permute-start | bytes 1572872 | tf_op jit(solution)/shard_map/ppermute | solution.py:54
  589.1 26.2 %collective-permute-start.65 = (bf16[128,2048]{1,0:T(8,128)(2,1)}, bf16[128,2048]{1,0:T(8,128)(2,1)}, u32[]{:S(2)}, u32[]{:S(2)}) collective-permute-start(bf16[128,2048]{1,0:T(8,128)(2,1)} %pad_maximum_fusion.25), channel_id=1, source_target_pairs={{0,8},{1,9},{2,10},{3,11},{4,12},{5,13},{6,14},{7,15},{8,0},{9,1},... | collective-permute-start | bytes 1572872 | tf_op jit(solution)/shard_map/ppermute | solution.py:54
  604.0 33.8 %collective-permute-start.73 = (bf16[128,2048]{1,0:T(8,128)(2,1)}, bf16[128,2048]{1,0:T(8,128)(2,1)}, u32[]{:S(2)}, u32[]{:S(2)}) collective-permute-start(bf16[128,2048]{1,0:T(8,128)(2,1)} %pad_maximum_fusion.27), channel_id=1, source_target_pairs={{0,8},{1,9},{2,10},{3,11},{4,12},{5,13},{6,14},{7,15},{8,0},{9,1},... | collective-permute-start | bytes 1572872 | tf_op jit(solution)/shard_map/ppermute | solution.py:54
  616.6 37.1 %collective-permute-start.66 = (bf16[64,2048]{1,0:T(8,128)(2,1)S(1)}, bf16[64,2048]{1,0:T(8,128)(2,1)S(1)}, u32[]{:S(2)}, u32[]{:S(2)}) collective-permute-start(bf16[64,2048]{1,0:T(8,128)(2,1)S(1)} %slice.414), channel_id=1, source_target_pairs={{0,16},{1,17},{2,18},{3,19},{4,20},{5,21},{6,22},{7,23},{8,24},{9,... | collective-permute-start | bytes 786440 | tf_op jit(solution)/shard_map/ppermute | solution.py:54
  639.8 23.5 %collective-permute-start.74 = (bf16[64,2048]{1,0:T(8,128)(2,1)S(1)}, bf16[64,2048]{1,0:T(8,128)(2,1)S(1)}, u32[]{:S(2)}, u32[]{:S(2)}) collective-permute-start(bf16[64,2048]{1,0:T(8,128)(2,1)S(1)} %slice.426), channel_id=1, source_target_pairs={{0,16},{1,17},{2,18},{3,19},{4,20},{5,21},{6,22},{7,23},{8,24},{9,... | collective-permute-start | bytes 786440 | tf_op jit(solution)/shard_map/ppermute | solution.py:54
  642.5 26.2 %collective-permute-start.78 = (bf16[256,1536]{1,0:T(8,128)(2,1)}, bf16[256,1536]{1,0:T(8,128)(2,1)S(1)}, u32[]{:S(2)}, u32[]{:S(2)}) collective-permute-start(bf16[256,1536]{1,0:T(8,128)(2,1)} %get-tuple-element.214), channel_id=1, source_target_pairs={{0,4},{1,5},{2,6},{3,7},{4,0},{5,1},{6,2},{7,3},{8,12},{9,13},{10,... | collective-permute-start | bytes 2359304 | tf_op jit(solution)/shard_map/ppermute | solution.py:54
  643.3 35.3 %collective-permute-start.79 = (bf16[256,1536]{1,0:T(8,128)(2,1)}, bf16[256,1536]{1,0:T(8,128)(2,1)S(1)}, u32[]{:S(2)}, u32[]{:S(2)}) collective-permute-start(bf16[256,1536]{1,0:T(8,128)(2,1)} %get-tuple-element.213), channel_id=1, source_target_pairs={{0,8},{1,9},{2,10},{3,11},{4,12},{5,13},{6,14},{7,15},{8,0},{9,1},... | collective-permute-start | bytes 2359304 | tf_op jit(solution)/shard_map/ppermute | solution.py:54
  645.8 50.1 %collective-permute-start.80 = (bf16[256,1536]{1,0:T(8,128)(2,1)S(1)}, bf16[256,1536]{1,0:T(8,128)(2,1)}, u32[]{:S(2)}, u32[]{:S(2)}) collective-permute-start(bf16[256,1536]{1,0:T(8,128)(2,1)S(1)} %get-tuple-element.212), channel_id=1, source_target_pairs={{0,12},{1,13},{2,14},{3,15},{4,8},{5,9},{6,10},{7,11},{8,4},{9,5},... | collective-permute-start | bytes 2359304 | tf_op jit(solution)/shard_map/ppermute | solution.py:54
  667.3 33.6 %collective-permute-start.75 = (bf16[256,512]{1,0:T(8,128)(2,1)S(1)}, bf16[256,512]{1,0:T(8,128)(2,1)S(1)}, u32[]{:S(2)}, u32[]{:S(2)}) collective-permute-start(bf16[256,512]{1,0:T(8,128)(2,1)S(1)} %get-tuple-element.222), channel_id=1, source_target_pairs={{0,4},{1,5},{2,6},{3,7},{4,0},{5,1},{6,2},{7,3},{8,12},{9,13},{10,... | collective-permute-start | bytes 786440 | tf_op jit(solution)/shard_map/ppermute | solution.py:54
  668.8 32.1 %collective-permute-start.76 = (bf16[256,512]{1,0:T(8,128)(2,1)S(1)}, bf16[256,512]{1,0:T(8,128)(2,1)S(1)}, u32[]{:S(2)}, u32[]{:S(2)}) collective-permute-start(bf16[256,512]{1,0:T(8,128)(2,1)S(1)} %get-tuple-element.221), channel_id=1, source_target_pairs={{0,8},{1,9},{2,10},{3,11},{4,12},{5,13},{6,14},{7,15},{8,0},{9,1},... | collective-permute-start | bytes 786440 | tf_op jit(solution)/shard_map/ppermute | solution.py:54
  668.8 32.6 %collective-permute-start.77 = (bf16[256,512]{1,0:T(8,128)(2,1)S(1)}, bf16[256,512]{1,0:T(8,128)(2,1)S(1)}, u32[]{:S(2)}, u32[]{:S(2)}) collective-permute-start(bf16[256,512]{1,0:T(8,128)(2,1)S(1)} %get-tuple-element.220), channel_id=1, source_target_pairs={{0,12},{1,13},{2,14},{3,15},{4,8},{5,9},{6,10},{7,11},{8,4},{9,5},... | collective-permute-start | bytes 786440 | tf_op jit(solution)/shard_map/ppermute | solution.py:54
  (86 other events, 1059.1 us)
Sparse Core Ops, SparseCore 0:
  22.4 48.2 all-gather.4
  78.3 54.9 all-gather.6
  162.3 65.9 all-gather.8
  229.7 47.0 all-gather.10
  427.9 144.2 reduce-scatter.2
  588.4 76.9 reduce-scatter.4
